TPU v7x, 128 devices: a whole 4x4x4 slice. The times are simulated.
128 devices in a mesh: gx: 16 (over z, y_hi, core), gy: 8 (over x, y_lo).
Axes of the slice: x: 4, y: 4 (y_hi: 2, y_lo: 2; y = y_hi * 2 + y_lo), z: 4, core: 2. Of those that a mesh axis runs over, the one named last changes fastest.
Arguments:
- obj_field: float32 [2, 2, 4096, 8192], P(None, None, 'gy', 'gx'), may hold values from -0.8 to 0.8
- probe_modes: float32 [2, 2, 256, 256], P(None, None, 'gx'), may hold values from -6 to 6
- positions: int32 [8, 16, 6, 2], P('gy', 'gx'), may hold values from 0 to 511
- counts: int32 [8, 16], P('gy', 'gx'), may hold values from 1 to 6, as said below
- amplitudes: float32 [8, 16, 6, 256, 256], P('gy', 'gx'), may hold values from 0.6 to 1.8
Outputs:
- obj_grad: float32 [2, 2, 4096, 8192], P(None, None, 'gy', 'gx')
- probe_grad: float32 [2, 2, 256, 256], P(None, None, 'gx')
Inputs may be any that keep to these rules, and one draw needn't show every extreme that they name: `counts`: each tile has between 1 and 6 used slots and at least one tile uses all 6.
All inputs are finite; a program needn't handle non-finite values.
Results may differ from a plain program's by a relative error of at most 0.00014.
Values sent between devices are 32-bit elements; how exact they have to be, the bound alone decides.
No kernel may reach another device: no remote copies, remote signals or barrier semaphores. Data moves between devices by JAX's collectives and lax.ppermute only.
A program may use at most 128 MiB of HBM per device.

v0:
```python
import math

import jax
import jax.numpy as jnp
from jax import lax
from jax.sharding import PartitionSpec as P

BAND = 48


def shifted(x, axis, by):
    length = lax.axis_size(axis)
    pairs = [(i, i + by) for i in range(length) if 0 <= i + by < length]
    return lax.ppermute(x, axis, pairs)


def tables_for(probe_len):
    indices = jnp.arange(probe_len, dtype=jnp.int32)
    offsets = (indices[:, None] - indices[None, :]).astype(jnp.float32)
    chirp = math.pi * offsets * offsets / (2.0 * BAND)
    inside = jnp.where(jnp.abs(offsets) <= BAND, 1.0, 0.0).astype(jnp.float32) / math.sqrt(
        2.0 * BAND + 1.0
    )
    cycles = (indices[:, None] * indices[None, :] % probe_len).astype(jnp.float32)
    angles = -2.0 * math.pi * cycles / probe_len
    scaling = 1.0 / math.sqrt(probe_len)
    return (
        jnp.cos(chirp) * inside,
        jnp.sin(chirp) * inside,
        jnp.cos(angles) * scaling,
        jnp.sin(angles) * scaling,
    )


def left_apply(mat_re, mat_im, wave_re, wave_im):
    highest = lax.Precision.HIGHEST
    out_re = jnp.einsum("ab,mbc->mac", mat_re, wave_re, precision=highest) - jnp.einsum(
        "ab,mbc->mac", mat_im, wave_im, precision=highest
    )
    out_im = jnp.einsum("ab,mbc->mac", mat_re, wave_im, precision=highest) + jnp.einsum(
        "ab,mbc->mac", mat_im, wave_re, precision=highest
    )
    return (out_re, out_im)


def right_apply(mat_re, mat_im, wave_re, wave_im):
    highest = lax.Precision.HIGHEST
    out_re = jnp.einsum("mab,bc->mac", wave_re, mat_re, precision=highest) - jnp.einsum(
        "mab,bc->mac", wave_im, mat_im, precision=highest
    )
    out_im = jnp.einsum("mab,bc->mac", wave_im, mat_re, precision=highest) + jnp.einsum(
        "mab,bc->mac", wave_re, mat_im, precision=highest
    )
    return (out_re, out_im)


def position_loss(window, mode_set, amplitude, weight, tables):
    prop_re, prop_im, four_re, four_im = tables
    wave_re = mode_set[:, 0] * window[0, 0] - mode_set[:, 1] * window[0, 1]
    wave_im = mode_set[:, 0] * window[0, 1] + mode_set[:, 1] * window[0, 0]
    wave_re, wave_im = left_apply(prop_re, prop_im, wave_re, wave_im)
    wave_re, wave_im = right_apply(prop_re, prop_im, wave_re, wave_im)
    trans_re = window[1, 0]
    trans_im = window[1, 1]
    wave_re, wave_im = (
        wave_re * trans_re - wave_im * trans_im,
        wave_re * trans_im + wave_im * trans_re,
    )
    far_re, far_im = left_apply(four_re, four_im, wave_re, wave_im)
    far_re, far_im = right_apply(four_re, four_im, far_re, far_im)
    intensity = jnp.sum(far_re * far_re + far_im * far_im, axis=0)
    misfit = jnp.sqrt(intensity + 1.0) - amplitude
    return weight * jnp.sum(misfit * misfit)


def on_device(obj_field, probe_modes, positions, counts, amplitudes):
    probe_full = lax.all_gather(probe_modes, "gx", axis=2, tiled=True)
    probe_len = probe_full.shape[3]
    tile_len = obj_field.shape[2]
    layers = obj_field.shape[0]
    slot_total = amplitudes.shape[2]
    tables = tables_for(probe_len)
    right_part = shifted(obj_field[:, :, :, :probe_len], "gx", -1)
    lower_part = shifted(obj_field[:, :, :probe_len, :], "gy", -1)
    corner_step = shifted(obj_field[:, :, :probe_len, :probe_len], "gx", -1)
    corner_part = shifted(corner_step, "gy", -1)
    upper_half = jnp.concatenate([obj_field, right_part], axis=3)
    lower_half = jnp.concatenate([lower_part, corner_part], axis=3)
    extended = jnp.concatenate([upper_half, lower_half], axis=2)
    active = counts[0, 0]
    anchor = jnp.int32(0)
    block_shape = (layers, 2, probe_len, probe_len)

    def starts_of(number):
        return (anchor, anchor, positions[0, 0, number, 0], positions[0, 0, number, 1])

    def visit(number, running, weight):
        grad_ext, grad_probe = running
        starts = starts_of(number)
        window = lax.dynamic_slice(extended, starts, block_shape)
        window_grad, modes_grad = jax.grad(position_loss, argnums=(0, 1))(
            window, probe_full, amplitudes[0, 0, number], weight, tables
        )
        current = lax.dynamic_slice(grad_ext, starts, block_shape)
        grad_ext = lax.dynamic_update_slice(grad_ext, current + window_grad, starts)
        return (grad_ext, grad_probe + modes_grad)

    initial = (jnp.zeros_like(extended), jnp.zeros_like(probe_full))

    def masked_visit(number, running):
        weight = jnp.where(number < active, 1.0, 0.0).astype(jnp.float32)
        return visit(number, running, weight)

    grad_ext, grad_probe = lax.fori_loop(0, slot_total, masked_visit, initial)
    back_right = shifted(grad_ext[:, :, :tile_len, tile_len:], "gx", 1)
    back_lower = shifted(grad_ext[:, :, tile_len:, :tile_len], "gy", 1)
    corner_back = shifted(grad_ext[:, :, tile_len:, tile_len:], "gx", 1)
    back_corner = shifted(corner_back, "gy", 1)
    obj_grad = grad_ext[:, :, :tile_len, :tile_len]
    obj_grad = obj_grad.at[:, :, :, :probe_len].add(back_right)
    obj_grad = obj_grad.at[:, :, :probe_len, :].add(back_lower)
    obj_grad = obj_grad.at[:, :, :probe_len, :probe_len].add(back_corner)
    column_sum = lax.psum(grad_probe, "gy")
    probe_grad = lax.psum_scatter(column_sum, "gx", scatter_dimension=2, tiled=True)
    return (obj_grad, probe_grad)


def solution(mesh):
    return jax.shard_map(
        on_device,
        mesh=mesh,
        in_specs=(
            P(None, None, "gy", "gx"),
            P(None, None, "gx", None),
            P("gy", "gx", None, None),
            P("gy", "gx"),
            P("gy", "gx", None, None, None),
        ),
        out_specs=(P(None, None, "gy", "gx"), P(None, None, "gx", None)),
        check_vma=False,
    )
```

profile of v0, /device:TPU:0, one launch (start us, length us, event | category | flops | bytes accessed | tf_op | source)
XLA Modules:
  0.0 898.1 jit_solution(7615137868655429804)
XLA Ops:
  10.1 3.1 slice.161
  19.5 127.2 %all-gather.2.cloned.1.call-done = f32[2,2,256,256]{3,1,0,2:T(2,128)} async-done(((f32[2,2,16,256]{3,1,0,2:T(2,128)}), f32[2,2,256,256]{3,1,0,2:T(2,128)}) %all-gather.2.cloned.1.call-update) | async-done | bytes 1048592 | tf_op jit(solution)/shard_map/all_gather | solution.py:77
  148.2 6.1 maximum_maximum_fusion
  154.3 4.5 broadcast_in_dim.94
  158.8 528.7 %while.20 = (s32[]{:T(128)}, f32[2,2,768,768]{3,2,1,0:T(8,128)}, f32[2,2,256,256]{2,3,0,1:T(8,128)}, s32[1,1,6,2]{2,3,1,0:T(2,128)S(1)}, f32[2,2,256,256]{2,3,0,...) while((s32[]{:T(128)}, f32[2,2,768,768]{3,2,1,0:T(8,128)}, ...), condition=%wide.region_10.11_spmd.clone.clone, body=%wide.region_0.10_spmd.clone.clone.sunk | while | flops 12925992960 | bytes 81264944 | solution.py:114
  222.3 3.8 multiply_bitcast_fusion.5
  234.3 11.9 %dynamic_update_slice.10 = f32[2,2,768,768]{3,2,1,0:T(8,128)} dynamic-update-slice(f32[2,2,768,768]{3,2,1,0:T(8,128)} %get-tuple-element.593, f32[2,2,256,256]{3,2,1,0:T(8,128)S(1)} %add_add_fusion.2, s32[]{:T(128)} %constant.155.clone.1..sunk, s32[]{:T(128)} %constant.155.clone.1..sunk, s32[]{:T(128)S(6)} %select_n.311, s32[]{:T(128)S(6)} %select_n.312) | dynamic-update-slice | bytes 2097156 | tf_op jit(solution)/shard_map/while/body/eval_jaxpr/dynamic_update_slice | solution.py:105
  309.7 3.8 multiply_bitcast_fusion.5
  319.2 2.7 select_add_fusion.2
  322.0 11.8 %dynamic_update_slice.10 = f32[2,2,768,768]{3,2,1,0:T(8,128)} dynamic-update-slice(f32[2,2,768,768]{3,2,1,0:T(8,128)} %get-tuple-element.593, f32[2,2,256,256]{3,2,1,0:T(8,128)S(1)} %add_add_fusion.2, s32[]{:T(128)} %constant.155.clone.1..sunk, s32[]{:T(128)} %constant.155.clone.1..sunk, s32[]{:T(128)S(6)} %select_n.311, s32[]{:T(128)S(6)} %select_n.312) | dynamic-update-slice | bytes 2097156 | tf_op jit(solution)/shard_map/while/body/eval_jaxpr/dynamic_update_slice | solution.py:105
  397.4 3.8 multiply_bitcast_fusion.5
  407.0 2.7 select_add_fusion.2
  409.7 11.5 %dynamic_update_slice.10 = f32[2,2,768,768]{3,2,1,0:T(8,128)} dynamic-update-slice(f32[2,2,768,768]{3,2,1,0:T(8,128)} %get-tuple-element.593, f32[2,2,256,256]{3,2,1,0:T(8,128)S(1)} %add_add_fusion.2, s32[]{:T(128)} %constant.155.clone.1..sunk, s32[]{:T(128)} %constant.155.clone.1..sunk, s32[]{:T(128)S(6)} %select_n.311, s32[]{:T(128)S(6)} %select_n.312) | dynamic-update-slice | bytes 2097156 | tf_op jit(solution)/shard_map/while/body/eval_jaxpr/dynamic_update_slice | solution.py:105
  484.9 3.8 multiply_bitcast_fusion.5
  494.4 2.7 select_add_fusion.2
  497.2 12.3 %dynamic_update_slice.10 = f32[2,2,768,768]{3,2,1,0:T(8,128)} dynamic-update-slice(f32[2,2,768,768]{3,2,1,0:T(8,128)} %get-tuple-element.593, f32[2,2,256,256]{3,2,1,0:T(8,128)S(1)} %add_add_fusion.2, s32[]{:T(128)} %constant.155.clone.1..sunk, s32[]{:T(128)} %constant.155.clone.1..sunk, s32[]{:T(128)S(6)} %select_n.311, s32[]{:T(128)S(6)} %select_n.312) | dynamic-update-slice | bytes 2097156 | tf_op jit(solution)/shard_map/while/body/eval_jaxpr/dynamic_update_slice | solution.py:105
  573.0 3.8 multiply_bitcast_fusion.5
  582.5 2.7 select_add_fusion.2
  585.2 12.0 %dynamic_update_slice.10 = f32[2,2,768,768]{3,2,1,0:T(8,128)} dynamic-update-slice(f32[2,2,768,768]{3,2,1,0:T(8,128)} %get-tuple-element.593, f32[2,2,256,256]{3,2,1,0:T(8,128)S(1)} %add_add_fusion.2, s32[]{:T(128)} %constant.155.clone.1..sunk, s32[]{:T(128)} %constant.155.clone.1..sunk, s32[]{:T(128)S(6)} %select_n.311, s32[]{:T(128)S(6)} %select_n.312) | dynamic-update-slice | bytes 2097156 | tf_op jit(solution)/shard_map/while/body/eval_jaxpr/dynamic_update_slice | solution.py:105
  660.9 3.8 multiply_bitcast_fusion.5
  670.5 2.7 select_add_fusion.2
  673.2 11.5 %dynamic_update_slice.10 = f32[2,2,768,768]{3,2,1,0:T(8,128)} dynamic-update-slice(f32[2,2,768,768]{3,2,1,0:T(8,128)} %get-tuple-element.593, f32[2,2,256,256]{3,2,1,0:T(8,128)S(1)} %add_add_fusion.2, s32[]{:T(128)} %constant.155.clone.1..sunk, s32[]{:T(128)} %constant.155.clone.1..sunk, s32[]{:T(128)S(6)} %select_n.311, s32[]{:T(128)S(6)} %select_n.312) | dynamic-update-slice | bytes 2097156 | tf_op jit(solution)/shard_map/while/body/eval_jaxpr/dynamic_update_slice | solution.py:105
  687.5 3.2 slice.165
  690.7 4.2 collective-permute-start.4
  694.9 3.1 slice.167
  698.0 3.8 collective-permute-start.5
  708.4 3.0 collective-permute-start.7
  711.4 4.7 slice.163
  716.2 90.7 %reduce-scatter.2.cloned.1.call-done = f32[2,2,16,256]{3,2,1,0:T(8,128)} async-done(((f32[2,2,256,256]{3,2,1,0:T(8,128)}), f32[2,2,16,256]{3,2,1,0:T(8,128)}) %reduce-scatter.2.cloned.1.call-update) | async-done | bytes 65552 | tf_op jit(solution)/shard_map/reduce_scatter | solution.py:124
  806.9 3.2 add_dynamic-update-slice_fusion
  810.1 4.3 constant_dynamic-update-slice_fusion
  815.6 74.3 %all-reduce.12.cloned.1.call-done = f32[2,2,16,256]{3,2,1,0:T(8,128)} async-done(((f32[2,2,16,256]{3,2,1,0:T(8,128)}), f32[2,2,16,256]{3,2,1,0:T(8,128)}) %all-reduce.12.cloned.1.call-update) | async-done | bytes 65552 | tf_op jit(solution)/shard_map/psum | solution.py:123
  (289 shorter events, 408.4 us)
Async XLA Ops:
  7.2 139.5 %all-gather.2.cloned.1.call-start = ((), (), s32[]{:S(2)}) async-start(), calls=%async_computation.1 | async-start | bytes 1114112 | tf_op jit(solution)/shard_map/all_gather | solution.py:77
  7.2 7.3 copy-start.1
  8.7 8.7 copy-start.2
  8.7 9.5 %collective-permute-start.2 = (f32[2,2,256,256]{3,2,1,0:T(8,128)S(1)}, f32[2,2,256,256]{3,2,1,0:T(8,128)}, u32[]{:S(2)}, u32[]{:S(2)}) collective-permute-start(f32[2,2,256,256]{3,2,1,0:T(8,128)S(1)} %slice.162), channel_id=1, source_target_pairs={{8,0},{16,8},{24,16},{32,24},{40,32},{48,40},{56,48},{64,56},{72,6... | collective-permute-start | bytes 3145736 | tf_op jit(solution)/shard_map/ppermute | solution.py:14
  13.2 134.9 %collective-permute-start.1 = (f32[2,2,256,512]{3,2,1,0:T(8,128)}, f32[2,2,256,512]{3,2,1,0:T(8,128)S(1)}, u32[]{:S(2)}, u32[]{:S(2)}) collective-permute-start(f32[2,2,256,512]{3,2,1,0:T(8,128)} %slice.161), channel_id=1, source_target_pairs={{1,0},{2,1},{3,2},{4,3},{5,4},{6,5},{7,6},{9,8},{10,9},{11,10},{12... | collective-permute-start | bytes 6291464 | tf_op jit(solution)/shard_map/ppermute | solution.py:14
  16.1 132.0 %collective-permute-start = (f32[2,2,512,256]{3,2,1,0:T(8,128)}, f32[2,2,512,256]{3,2,1,0:T(8,128)}, u32[]{:S(2)}, u32[]{:S(2)}) collective-permute-start(f32[2,2,512,256]{3,2,1,0:T(8,128)} %slice.160), channel_id=1, source_target_pairs={{8,0},{16,8},{24,16},{32,24},{40,32},{48,40},{56,48},{64,56},{72,6... | collective-permute-start | bytes 6291464 | tf_op jit(solution)/shard_map/ppermute | solution.py:14
  18.1 788.7 %reduce-scatter.2.cloned.1.call-start = ((), (), s32[]{:S(2)}) async-start(), calls=%async_computation.2 | async-start | bytes 1114112 | tf_op jit(solution)/shard_map/reduce_scatter | solution.py:124
  18.2 130.0 %collective-permute-start.3 = (f32[2,2,256,256]{3,2,1,0:T(8,128)}, f32[2,2,256,256]{3,2,1,0:T(8,128)}, u32[]{:S(2)}, u32[]{:S(2)}) collective-permute-start(f32[2,2,256,256]{3,2,1,0:T(8,128)} %collective-permute-done.2), channel_id=1, source_target_pairs={{1,0},{2,1},{3,2},{4,3},{5,4},{6,5},{7,6},{9,8},{10,9},{11,10},{12... | collective-permute-start | bytes 3145736 | tf_op jit(solution)/shard_map/ppermute | solution.py:14
  154.3 4.5 copy-start.3
  687.5 14.3 %copy-start = (f32[2,2,256,256]{2,3,0,1:T(8,128)S(1)}, f32[2,2,256,256]{2,3,0,1:T(8,128)}, u32[]{:S(2)}) copy-start(f32[2,2,256,256]{2,3,0,1:T(8,128)} %get-tuple-element.323) | copy-start | bytes 3145732
  690.7 116.2 %collective-permute-start.4 = (f32[2,2,512,256]{3,2,1,0:T(8,128)}, f32[2,2,512,256]{3,2,1,0:T(8,128)S(1)}, u32[]{:S(2)}, u32[]{:S(2)}) collective-permute-start(f32[2,2,512,256]{3,2,1,0:T(8,128)} %slice.165), channel_id=1, source_target_pairs={{0,8},{8,16},{16,24},{24,32},{32,40},{40,48},{48,56},{56,64},{64,7... | collective-permute-start | bytes 6291464 | tf_op jit(solution)/shard_map/ppermute | solution.py:14
  698.0 112.1 %collective-permute-start.5 = (f32[2,2,256,512]{3,2,1,0:T(8,128)}, f32[2,2,256,512]{3,2,1,0:T(8,128)}, u32[]{:S(2)}, u32[]{:S(2)}) collective-permute-start(f32[2,2,256,512]{3,2,1,0:T(8,128)} %slice.167), channel_id=1, source_target_pairs={{0,1},{1,2},{2,3},{3,4},{4,5},{5,6},{6,7},{8,9},{9,10},{10,11},{11... | collective-permute-start | bytes 6291464 | tf_op jit(solution)/shard_map/ppermute | solution.py:14
  703.1 186.7 %all-reduce.12.cloned.1.call-start = ((), (), s32[]{:S(2)}) async-start(), calls=%async_computation.3 | async-start | bytes 131072 | tf_op jit(solution)/shard_map/psum | solution.py:123
  704.5 3.9 collective-permute-start.6
  708.4 106.0 %collective-permute-start.7 = (f32[2,2,256,256]{3,2,1,0:T(8,128)}, f32[2,2,256,256]{3,2,1,0:T(8,128)S(1)}, u32[]{:S(2)}, u32[]{:S(2)}) collective-permute-start(f32[2,2,256,256]{3,2,1,0:T(8,128)} %collective-permute-done.6), channel_id=1, source_target_pairs={{0,1},{1,2},{2,3},{3,4},{4,5},{5,6},{6,7},{8,9},{9,10},{10,11},{11... | collective-permute-start | bytes 3145736 | tf_op jit(solution)/shard_map/ppermute | solution.py:14
Sparse Core Ops, SparseCore 0:
  18.2 128.3 all-gather.1
  703.2 103.5 reduce-scatter.1
  809.5 80.2 all-reduce.11
where the time goes:
time: 904 us; the launch traced here: 898 us
  matrix products  347 us (38%)
  waiting for transfers between devices  294 us (33%)
  local copies, waits for them, and re-layouts  136 us (15%)
  other arithmetic  55.7 us (6%)
  loops' own time  33 us (4%)
  starting transfers between devices  18.8 us (2%)
  between operations  14.2 us (2%)
    all_gather x1, waiting for transfers between devices, on_device(): probe_full = lax.all_gather(probe_modes, 'gx', axis=2, tiled=True)  127 us
    reduce_scatter x1, waiting for transfers between devices, on_device(): lax.psum_scatter(column_sum, 'gx', scatter_dimension=2, tiled=True)  90.7 us
    psum x1, waiting for transfers between devices, on_device(): column_sum = lax.psum(grad_probe, 'gy')  74.3 us
    dynamic_update_slice x6, local copies, waits for them, and re-layouts, visit(): grad_ext = lax.dynamic_update_slice(grad_ext, current + window_grad, starts)  71 us
    dot_general x24, matrix products, left_apply(): jnp.einsum('ab,mbc->mac', mat_im, wave_im, precision=highest)  54.9 us
    dot_general x24, matrix products, right_apply(): jnp.einsum('mab,bc->mac', wave_im, mat_re, precision=highest)  43.6 us
    dot_general x24, matrix products, right_apply(): jnp.einsum('mab,bc->mac', wave_im, mat_im, precision=highest)  42.4 us
    dot_general x24, matrix products, left_apply(): jnp.einsum('ab,mbc->mac', mat_re, wave_re, precision=highest)  42 us
  transfers between devices with their start and end apart: 11, of which 4 were waited for; matrix products, arithmetic and copies ran while one was open for 3% of the time, Pallas kernels for 0%

commit v1 on v0

v1 whole, which is shorter than its diff:
```python
import functools
import math

import jax
import jax.numpy as jnp
import numpy as np
from jax import lax
from jax.experimental import pallas as pl
from jax.experimental.pallas import tpu as pltpu
from jax.sharding import PartitionSpec as P

BAND = 48
PROBE = 256
HALF = 128
TILE = 512
SLOTS = 6
F32 = jnp.float32
BF16 = jnp.bfloat16
VMEM_LIMIT = 48 * 1024 * 1024


def split_table(mat):
    hi = mat.astype(BF16)
    lo = (mat - hi.astype(np.float64)).astype(BF16)
    return hi, lo


def left_table(mat):
    hi, lo = split_table(mat)
    return np.concatenate([hi, lo, hi], axis=1)


def right_table(mat):
    hi, lo = split_table(mat)
    return np.concatenate([hi, lo, hi], axis=0)


def make_tables():
    index = np.arange(PROBE)
    offset = (index[:, None] - index[None, :]).astype(np.float64)
    prop = np.where(np.abs(offset) <= BAND, np.exp(1j * np.pi * offset**2 / (2 * BAND)), 0)
    prop = prop / math.sqrt(2 * BAND + 1)
    half = np.arange(HALF)
    four = np.exp(-2j * np.pi * ((half[:, None] * half[None, :]) % HALF) / HALF) / math.sqrt(PROBE)
    twist = np.exp(-2j * np.pi * half / PROBE)

    def from_left(mat):
        return np.block([[mat.real, -mat.imag], [mat.imag, mat.real]])

    def from_right(mat):
        return from_left(mat).T

    order = np.concatenate([np.arange(0, PROBE, 2), np.arange(1, PROBE, 2)])
    perm = np.zeros((PROBE, PROBE))
    perm[np.arange(PROBE), order] = 1
    return {
        "prop_l": left_table(from_left(prop)),
        "prop_r": right_table(from_right(prop)),
        "back_l": left_table(from_left(prop.conj())),
        "back_r": right_table(from_right(prop.conj())),
        "four_l": left_table(from_left(four)),
        "four_r": right_table(from_right(four)),
        "ruof_l": left_table(from_left(four.conj())),
        "ruof_r": right_table(from_right(four.conj())),
        "tw_row": np.stack(
            [
                np.broadcast_to(twist.real[:, None], (HALF, PROBE)),
                np.broadcast_to(twist.imag[:, None], (HALF, PROBE)),
            ]
        ).astype(np.float32),
        "tw_col": np.stack(
            [
                np.broadcast_to(twist.real[None, :], (8, HALF)),
                np.broadcast_to(twist.imag[None, :], (8, HALF)),
            ]
        ).astype(np.float32),
        "perm_l": np.concatenate([perm] * 3, axis=1).astype(BF16),
        "perm_r": np.concatenate([perm.T] * 3, axis=0).astype(BF16),
    }


def parted(x):
    hi = x.astype(BF16)
    return hi, (x - hi.astype(F32)).astype(BF16)


def lmul(table, x):
    hi, lo = parted(x)
    return jnp.dot(table, jnp.concatenate([hi, hi, lo], axis=0), preferred_element_type=F32)


def rmul(x, table):
    hi, lo = parted(x)
    return jnp.dot(jnp.concatenate([hi, hi, lo], axis=1), table, preferred_element_type=F32)


def exact_parts(x):
    hi = x.astype(BF16)
    rest = x - hi.astype(F32)
    mid = rest.astype(BF16)
    return hi, mid, (rest - mid.astype(F32)).astype(BF16)


def both_sides(re, im, table_l, table_r):
    x = jnp.concatenate(
        [jnp.concatenate(re, axis=1), jnp.concatenate(im, axis=1)], axis=0
    )
    y = lmul(table_l, x)
    n = PROBE
    x = jnp.concatenate(
        [jnp.concatenate([y[:n, m * n : (m + 1) * n], y[n:, m * n : (m + 1) * n]], axis=1) for m in (0, 1)],
        axis=0,
    )
    y = rmul(x, table_r)
    return [y[m * n : (m + 1) * n, :n] for m in (0, 1)], [y[m * n : (m + 1) * n, n:] for m in (0, 1)]


def place_of(scalars, slot):
    row = scalars[2 * slot]
    col = scalars[2 * slot + 1]
    row_base = pl.multiple_of(row // 8 * 8, 8)
    col_base = pl.multiple_of(col // 128 * 128, 128)
    return row_base, row - row_base, col_base, col - col_base


def window_of(field, part, place):
    row_base, row_off, col_base, col_off = place
    x = field[part, pl.ds(row_base, PROBE + 8), pl.ds(col_base, PROBE + 128)]
    x = pltpu.roll(x, (PROBE + 128 - col_off) % (PROBE + 128), 1)[:, :PROBE]
    return pltpu.roll(x, (PROBE + 8 - row_off) % (PROBE + 8), 0)[:PROBE]


def add_window(field, part, place, x):
    row_base, row_off, col_base, col_off = place
    x = jnp.concatenate([x, jnp.zeros((8, PROBE), F32)], axis=0)
    x = pltpu.roll(x, row_off, 0)
    x = jnp.concatenate([x, jnp.zeros((PROBE + 8, 128), F32)], axis=1)
    x = pltpu.roll(x, col_off, 1)
    at = (part, pl.ds(row_base, PROBE + 8), pl.ds(col_base, PROBE + 128))
    field[at] = field[at] + x


def fetch_field(layer, core, obj, right, low_a, low_b, diag, side, field, sems):
    n, t = PROBE, TILE
    copies = [
        pltpu.make_async_copy(obj.at[layer], field.at[:, :t, :t], sems.at[0]),
        pltpu.make_async_copy(right, field.at[:, :t, t:], sems.at[1]),
        pltpu.make_async_copy(low_a, field.at[:, t:, :n], sems.at[2]),
        pltpu.make_async_copy(low_b, field.at[:, t:, n:t], sems.at[3]),
    ]
    for copy in copies:
        copy.start()

    @pl.when(core == 0)
    def _():
        copy = pltpu.make_async_copy(side, field.at[:, t:, t:], sems.at[4])
        copy.start()
        copy.wait()

    @pl.when(core != 0)
    def _():
        copy = pltpu.make_async_copy(diag, field.at[:, t:, t:], sems.at[4])
        copy.start()
        copy.wait()

    for copy in copies:
        copy.wait()


def store_field(field, main, right, low_a, low_b, corner, sems):
    n, t = PROBE, TILE
    copies = [
        pltpu.make_async_copy(field.at[:, :t, t:], right, sems.at[0]),
        pltpu.make_async_copy(field.at[:, t:, n:t], low_b, sems.at[1]),
        pltpu.make_async_copy(field.at[:, t:, :n], low_a, sems.at[2]),
        pltpu.make_async_copy(field.at[:, t:, t:], corner, sems.at[3]),
        pltpu.make_async_copy(field.at[:, :t, :t], main, sems.at[4]),
    ]
    for copy in copies:
        copy.start()
    for copy in copies:
        copy.wait()


def amp_kernel(amp, perm_l, perm_r, out):
    hi, mid, lo = exact_parts(amp[0])
    y = jnp.dot(perm_l[...], jnp.concatenate([hi, mid, lo], axis=0), preferred_element_type=F32)
    hi, mid, lo = exact_parts(y)
    out[0] = jnp.dot(jnp.concatenate([hi, mid, lo], axis=1), perm_r[...], preferred_element_type=F32)


def out_kernel(scalars, obj, right, low_a, low_b, diag, side, probe, table_l, table_r, psi, win, field, sems):
    slot = pl.program_id(0)

    @pl.when(slot == 0)
    def _():
        fetch_field(0, scalars[13], obj, right, low_a, low_b, diag, side, field, sems)

    @pl.when(slot < scalars[12])
    def _():
        place = place_of(scalars, slot)
        w_re = window_of(field, 0, place)
        w_im = window_of(field, 1, place)
        win[0, 0] = w_re
        win[0, 1] = w_im
        re = [probe[m, 0] * w_re - probe[m, 1] * w_im for m in (0, 1)]
        im = [probe[m, 0] * w_im + probe[m, 1] * w_re for m in (0, 1)]
        re, im = both_sides(re, im, table_l[...], table_r[...])
        for m in (0, 1):
            psi[0, m, 0] = re[m]
            psi[0, m, 1] = im[m]


def far_kernel(
    scalars, obj, right, low_a, low_b, diag, side, psi, amp, four_l, four_r, ruof_l, ruof_r, tw_row, tw_col,
    g_psi, g_main, g_right, g_low_a, g_low_b, g_corner, field, grad, sems,
):
    slot = pl.program_id(0)
    h, n = HALF, PROBE

    @pl.when(slot == 0)
    def _():
        fetch_field(1, scalars[13], obj, right, low_a, low_b, diag, side, field, sems)
        grad[...] = jnp.zeros_like(grad)

    @pl.when(slot < scalars[12])
    def _():
        place = place_of(scalars, slot)
        w_re = window_of(field, 0, place)
        w_im = window_of(field, 1, place)
        tr, ti = tw_row[0], tw_row[1]
        cr, ci = tw_col[0, 0:1], tw_col[1, 0:1]
        outs = []
        for m in (0, 1):
            p_re, p_im = psi[0, m, 0], psi[0, m, 1]
            re = p_re * w_re - p_im * w_im
            im = p_re * w_im + p_im * w_re
            d_re, d_im = re[:h] - re[h:], im[:h] - im[h:]
            top = jnp.concatenate([re[:h] + re[h:], d_re * tr - d_im * ti], axis=1)
            bottom = jnp.concatenate([im[:h] + im[h:], d_re * ti + d_im * tr], axis=1)
            y = lmul(four_l[...], jnp.concatenate([top, bottom], axis=0))
            re = jnp.concatenate([y[:h, :n], y[:h, n:]], axis=0)
            im = jnp.concatenate([y[h:, :n], y[h:, n:]], axis=0)
            d_re, d_im = re[:, :h] - re[:, h:], im[:, :h] - im[:, h:]
            even = jnp.concatenate([re[:, :h] + re[:, h:], im[:, :h] + im[:, h:]], axis=1)
            odd = jnp.concatenate([d_re * cr - d_im * ci, d_re * ci + d_im * cr], axis=1)
            outs.append(rmul(jnp.concatenate([even, odd], axis=0), four_r[...]))
        sq = outs[0] * outs[0] + outs[1] * outs[1]
        total = sq[:, :h] + sq[:, h:] + 1.0
        both = jnp.concatenate([amp[0, :, :h], amp[0, :, h:]], axis=0)
        slope = 2.0 - 2.0 * both * lax.rsqrt(total)
        slope = jnp.concatenate([slope, slope], axis=1)
        gw_re = gw_im = None
        for m in (0, 1):
            y = rmul(outs[m] * slope, ruof_r[...])
            q_re = y[n:, :h] * cr + y[n:, h:] * ci
            q_im = y[n:, h:] * cr - y[n:, :h] * ci
            re = jnp.concatenate([y[:n, :h] + q_re, y[:n, :h] - q_re], axis=1)
            im = jnp.concatenate([y[:n, h:] + q_im, y[:n, h:] - q_im], axis=1)
            x = jnp.concatenate(
                [
                    jnp.concatenate([re[:h], re[h:]], axis=1),
                    jnp.concatenate([im[:h], im[h:]], axis=1),
                ],
                axis=0,
            )
            y = lmul(ruof_l[...], x)
            q_re = y[:h, n:] * tr + y[h:, n:] * ti
            q_im = y[h:, n:] * tr - y[:h, n:] * ti
            re = jnp.concatenate([y[:h, :n] + q_re, y[:h, :n] - q_re], axis=0)
            im = jnp.concatenate([y[h:, :n] + q_im, y[h:, :n] - q_im], axis=0)
            g_psi[0, m, 0] = w_re * re + w_im * im
            g_psi[0, m, 1] = w_re * im - w_im * re
            p_re, p_im = psi[0, m, 0], psi[0, m, 1]
            a_re = p_re * re + p_im * im
            a_im = p_re * im - p_im * re
            gw_re = a_re if m == 0 else gw_re + a_re
            gw_im = a_im if m == 0 else gw_im + a_im
        add_window(grad, 0, place, gw_re)
        add_window(grad, 1, place, gw_im)

    @pl.when(slot == pl.num_programs(0) - 1)
    def _():
        store_field(grad, g_main, g_right, g_low_a, g_low_b, g_corner, sems)


def home_kernel(
    scalars, win, g_psi, probe, table_l, table_r,
    g_probe, g_main, g_right, g_low_a, g_low_b, g_corner, grad, sems,
):
    slot = pl.program_id(0)

    @pl.when(slot == 0)
    def _():
        grad[...] = jnp.zeros_like(grad)
        g_probe[...] = jnp.zeros_like(g_probe)

    @pl.when(slot < scalars[12])
    def _():
        place = place_of(scalars, slot)
        re = [g_psi[0, m, 0] for m in (0, 1)]
        im = [g_psi[0, m, 1] for m in (0, 1)]
        re, im = both_sides(re, im, table_l[...], table_r[...])
        w_re, w_im = win[0, 0], win[0, 1]
        gw_re = gw_im = None
        for m in (0, 1):
            p_re, p_im = probe[m, 0], probe[m, 1]
            a_re = p_re * re[m] + p_im * im[m]
            a_im = p_re * im[m] - p_im * re[m]
            gw_re = a_re if m == 0 else gw_re + a_re
            gw_im = a_im if m == 0 else gw_im + a_im
            g_probe[m, 0] += w_re * re[m] + w_im * im[m]
            g_probe[m, 1] += w_re * im[m] - w_im * re[m]
        add_window(grad, 0, place, gw_re)
        add_window(grad, 1, place, gw_im)

    @pl.when(slot == pl.num_programs(0) - 1)
    def _():
        store_field(grad, g_main, g_right, g_low_a, g_low_b, g_corner, sems)


def join_kernel(main, right, low_a, low_b, diag, *rest):
    out = rest[-1]
    n, h = PROBE, HALF
    i = pl.program_id(0)

    @pl.when(i < 2)
    def _():
        out[0, :, :, :n] = main[:, :, :n] + right[...] + low_a[...] + diag[...]
        out[0, :, :, n:] = main[:, :, n:] + low_b[...]

    @pl.when(i >= 2)
    def _():
        out[0, :, :, :n] = main[:, :, :n] + right[...]
        out[0, :, :, n:] = main[:, :, n:]


def whole(shape):
    return pl.BlockSpec(shape, lambda j, s: (0,) * len(shape))


def any_spec():
    return pl.BlockSpec(memory_space=pl.ANY)


def of_slot(shape):
    return pl.BlockSpec(
        (1,) + shape, lambda j, s: (jnp.minimum(j, s[12] - 1),) + (0,) * len(shape)
    )


def cost(flops, data):
    return pl.CostEstimate(flops=int(flops), bytes_accessed=int(data), transcendentals=0)


def params():
    return pltpu.CompilerParams(vmem_limit_bytes=VMEM_LIMIT)


FIELD_PARTS = [(2, TILE, TILE), (2, TILE, PROBE), (2, PROBE, PROBE), (2, PROBE, PROBE), (2, PROBE, PROBE)]


def sds(shape):
    return jax.ShapeDtypeStruct(shape, F32)


def permute_amplitudes(amp, tables):
    n = PROBE
    return pl.pallas_call(
        amp_kernel,
        grid=(SLOTS,),
        in_specs=[
            pl.BlockSpec((1, n, n), lambda j: (j, 0, 0)),
            pl.BlockSpec((n, 3 * n), lambda j: (0, 0)),
            pl.BlockSpec((3 * n, n), lambda j: (0, 0)),
        ],
        out_specs=pl.BlockSpec((1, n, n), lambda j: (j, 0, 0)),
        out_shape=sds((SLOTS, n, n)),
        compiler_params=params(),
        cost_estimate=cost(1.2e9, 4e6),
        name="order_amplitudes",
    )(amp, tables["perm_l"], tables["perm_r"])


def run_out(scalars, obj, halo, probe, tables):
    n = PROBE
    return pl.pallas_call(
        out_kernel,
        grid_spec=pltpu.PrefetchScalarGridSpec(
            num_scalar_prefetch=1,
            grid=(SLOTS,),
            in_specs=[any_spec()] * 6
            + [whole((2, 2, n, n)), whole((2 * n, 6 * n)), whole((6 * n, 2 * n))],
            out_specs=[of_slot((2, 2, n, n)), of_slot((2, n, n))],
            scratch_shapes=[pltpu.VMEM((2, 3 * n, 3 * n), F32), pltpu.SemaphoreType.DMA((5,))],
        ),
        out_shape=[sds((SLOTS, 2, 2, n, n)), sds((SLOTS, 2, n, n))],
        compiler_params=params(),
        cost_estimate=cost(1e10, 2e7),
        name="propagate_out",
    )(scalars, obj, *halo, probe, tables["prop_l"], tables["prop_r"])


def run_far(scalars, obj, halo, psi, amp, tables):
    n = PROBE
    return pl.pallas_call(
        far_kernel,
        grid_spec=pltpu.PrefetchScalarGridSpec(
            num_scalar_prefetch=1,
            grid=(SLOTS,),
            in_specs=[any_spec()] * 6
            + [of_slot((2, 2, n, n)), of_slot((n, n))]
            + [whole((n, 3 * n)), whole((3 * n, n))] * 2
            + [whole((2, HALF, n)), whole((2, 8, HALF))],
            out_specs=[of_slot((2, 2, n, n))] + [any_spec()] * 5,
            scratch_shapes=[
                pltpu.VMEM((2, 3 * n, 3 * n), F32),
                pltpu.VMEM((2, 3 * n, 3 * n), F32),
                pltpu.SemaphoreType.DMA((5,)),
            ],
        ),
        out_shape=[sds((SLOTS, 2, 2, n, n))] + [sds(s) for s in FIELD_PARTS],
        compiler_params=params(),
        cost_estimate=cost(1e10, 2e7),
        name="far_field",
    )(
        scalars, obj, *halo, psi, amp,
        tables["four_l"], tables["four_r"], tables["ruof_l"], tables["ruof_r"],
        tables["tw_row"], tables["tw_col"],
    )


def run_home(scalars, win, g_psi, probe, tables):
    n = PROBE
    return pl.pallas_call(
        home_kernel,
        grid_spec=pltpu.PrefetchScalarGridSpec(
            num_scalar_prefetch=1,
            grid=(SLOTS,),
            in_specs=[
                of_slot((2, n, n)),
                of_slot((2, 2, n, n)),
                whole((2, 2, n, n)),
                whole((2 * n, 6 * n)),
                whole((6 * n, 2 * n)),
            ],
            out_specs=[whole((2, 2, n, n))] + [any_spec()] * 5,
            scratch_shapes=[pltpu.VMEM((2, 3 * n, 3 * n), F32), pltpu.SemaphoreType.DMA((5,))],
        ),
        out_shape=[sds((2, 2, n, n))] + [sds(s) for s in FIELD_PARTS],
        compiler_params=params(),
        cost_estimate=cost(1e10, 2e7),
        name="propagate_home",
    )(scalars, win, g_psi, probe, tables["back_l"], tables["back_r"])


def run_join(layer, main, arrived, into):
    n, h = PROBE, HALF
    top = lambda i: (0, jnp.minimum(i, 1), 0)
    extra = [] if into is None else [into]
    return pl.pallas_call(
        join_kernel,
        grid=(4,),
        in_specs=[
            pl.BlockSpec((2, h, TILE), lambda i: (0, i, 0)),
            pl.BlockSpec((2, h, n), lambda i: (0, i, 0)),
            pl.BlockSpec((2, h, n), top),
            pl.BlockSpec((2, h, n), top),
            pl.BlockSpec((2, h, n), top),
        ]
        + [pl.BlockSpec(memory_space=pl.ANY)] * len(extra),
        out_specs=pl.BlockSpec((1, 2, h, TILE), lambda i: (layer, 0, i, 0)),
        out_shape=sds((2, 2, TILE, TILE)),
        input_output_aliases={} if into is None else {5: 0},
        compiler_params=params(),
        cost_estimate=cost(1e6, 6e6),
        name="join_gradients",
    )(main, *arrived, *extra)


def solution(mesh):
    n_gx, n_gy = mesh.shape["gx"], mesh.shape["gy"]
    axes = tuple(mesh.axis_names)
    tables = make_tables()

    def number(gx, gy):
        return gx * n_gy + gy if axes == ("gx", "gy") else gy * n_gx + gx

    def send(x, target):
        pairs = []
        for gx in range(n_gx):
            for gy in range(n_gy):
                to = target(gx, gy)
                if to is not None and 0 <= to[0] < n_gx and 0 <= to[1] < n_gy:
                    pairs.append((number(gx, gy), number(*to)))
        return lax.ppermute(x, axes, pairs)

    def flip(gx_bits, gy_bits):
        return lambda gx, gy: (gx ^ gx_bits, gy ^ gy_bits)

    def bring(obj, layer):
        n = PROBE
        low_a = send(obj[layer, :, :n, :n], lambda gx, gy: (gx, gy - 1))
        right = send(obj[layer, :, :, :n], lambda gx, gy: (gx - 1, gy))
        low_b = send(obj[layer, :, :n, n:], lambda gx, gy: (gx, gy - 1))
        diag = send(obj[layer, :, :n, :n], lambda gx, gy: (gx - 1, gy - 1) if gx % 2 == 0 else None)
        side = send(low_a, lambda gx, gy: (gx - 1, gy) if gx % 2 == 1 else None)
        return right, low_a, low_b, diag, side

    def take_back(right, low_a, low_b, corner):
        side = send(corner, lambda gx, gy: (gx + 1, gy) if gx % 2 == 0 else None)
        right = send(right, lambda gx, gy: (gx + 1, gy))
        low_b = send(low_b, lambda gx, gy: (gx, gy + 1))
        diag = send(corner, lambda gx, gy: (gx + 1, gy + 1) if gx % 2 == 1 else None)
        low_a = send(low_a + side, lambda gx, gy: (gx, gy + 1))
        return right, low_a, low_b, diag

    def gather_probe(probe):
        gx = lax.axis_index("gx")
        core, y_hi, z = gx % 2, gx // 2 % 2, gx // 4
        parts = [probe] + [send(probe, flip(4 * k, 0)) for k in (1, 2, 3)]
        stack = jnp.stack(parts)
        stack = jnp.stack([stack[k ^ 0] for k in range(4)])
        ordered = [
            jnp.where(z == 0, stack[k], jnp.where(z == 1, stack[k ^ 1], jnp.where(z == 2, stack[k ^ 2], stack[k ^ 3])))
            for k in range(4)
        ]
        mine = jnp.stack(ordered)
        other = send(mine, flip(2, 1))
        mine = jnp.where(y_hi == 0, jnp.stack([mine, other]), jnp.stack([other, mine]))
        other = send(mine, flip(1, 0))
        mine = jnp.where(core == 0, jnp.stack([mine, other]), jnp.stack([other, mine]))
        rows = probe.shape[2]
        full = jnp.transpose(mine, (3, 4, 2, 1, 0, 5, 6))
        return full.reshape(2, 2, n_gx * rows, PROBE)

    def reduce_probe(grad):
        gx = lax.axis_index("gx")
        core, y_hi, z = gx % 2, gx // 2 % 2, gx // 4
        rows = PROBE // n_gx
        parts = jnp.transpose(grad.reshape(2, 2, 4, 2, 2, rows, PROBE), (4, 2, 3, 0, 1, 5, 6))
        keep = jnp.where(core == 0, parts[0], parts[1])
        give = jnp.where(core == 0, parts[1], parts[0])
        part = keep + send(give, flip(1, 0))

        def at_z(k):
            return lax.dynamic_index_in_dim(part, z ^ k, 0, keepdims=False)

        got = [send(at_z(k), flip(4 * k, 0)) for k in (1, 2, 3)]
        part = (at_z(0) + got[0]) + (got[1] + got[2])
        keep = jnp.where(y_hi == 0, part[0], part[1])
        give = jnp.where(y_hi == 0, part[1], part[0])
        near = send(keep, flip(0, 1))
        far = send(give, flip(2, 0))
        across = send(give, flip(2, 1))
        part = (keep + near) + (far + across)
        got = [send(part, flip(0, 2 * k)) for k in (1, 2, 3)]
        return (part + got[0]) + (got[1] + got[2])

    def on_device(obj, probe, positions, counts, amplitudes):
        core = lax.axis_index("gx") % 2
        scalars = jnp.concatenate(
            [positions.reshape(2 * SLOTS), counts.reshape(1), core.astype(jnp.int32).reshape(1)]
        )
        halo_0 = bring(obj, 0)
        probe_full = gather_probe(probe)
        amp = permute_amplitudes(amplitudes[0, 0], tables)
        obj_late, halo_0 = lax.optimization_barrier((obj, halo_0))
        halo_1 = bring(obj_late, 1)
        psi, win = run_out(scalars, obj, halo_0, probe_full, tables)
        g_psi, main_1, *edges_1 = run_far(scalars, obj, halo_1, psi, amp, tables)
        back_1 = take_back(*edges_1)
        g_probe, main_0, *edges_0 = run_home(scalars, win, g_psi, probe_full, tables)
        edges_0, back_1 = lax.optimization_barrier((edges_0, back_1))
        back_0 = take_back(*edges_0)
        grad = run_join(1, main_1, back_1, None)
        probe_grad = reduce_probe(g_probe)
        grad = run_join(0, main_0, back_0, grad)
        return grad, probe_grad

    return jax.shard_map(
        on_device,
        mesh=mesh,
        in_specs=(
            P(None, None, "gy", "gx"),
            P(None, None, "gx", None),
            P("gy", "gx", None, None),
            P("gy", "gx"),
            P("gy", "gx", None, None, None),
        ),
        out_specs=(P(None, None, "gy", "gx"), P(None, None, "gx", None)),
        check_vma=False,
    )
```

time: 904 us -> 247 us (0.27)
  the two profiles are of different devices: /device:TPU:0 before, /device:TPU:41 now
where the time goes in v1:
time: 247 us; the launch traced here: 246 us
  starting transfers between devices  123 us (50%)
  Pallas kernels  54 us (22%)
  waiting for transfers between devices  49.3 us (20%)
  other arithmetic  8.5 us (3%)
  local copies, waits for them, and re-layouts  8.45 us (3%)
    ppermute x35, starting transfers between devices, send(): return lax.ppermute(x, axes, pairs)  123 us
    ppermute x35, waiting for transfers between devices, send(): return lax.ppermute(x, axes, pairs)  49.3 us
    pallas_call x1, Pallas kernels, run_far(): pl.pallas_call(far_kernel, grid_spec=pltpu.PrefetchScalarGridSpec(num_sca...  19.8 us
    pallas_call x1, Pallas kernels, run_out(): pl.pallas_call(out_kernel, grid_spec=pltpu.PrefetchScalarGridSpec(num_sca...  12.3 us
    pallas_call x1, Pallas kernels, run_home(): pl.pallas_call(home_kernel, grid_spec=pltpu.PrefetchScalarGridSpec(num_sc...  11.9 us
    pallas_call x2, Pallas kernels, run_join(): pl.pallas_call(join_kernel, grid=(4,), in_specs=[pl.BlockSpec((2, h, TILE...  6.33 us
  transfers between devices with their start and end apart: 35, of which 10 were waited for; matrix products, arithmetic and copies ran while one was open for 5% of the time, Pallas kernels for 13%

profile of v1, /device:TPU:41, one launch (start us, length us, event | category | flops | bytes accessed | tf_op | source)
XLA Modules:
  0.0 245.8 jit_solution(12140459673141070522)
XLA Ops:
  0.7 2.5 %slice_bitcast_fusion.4 = (f32[2,256,256]{2,1,0:T(8,128)}, f32[2,256,256]{2,1,0:T(8,128)}) fusion(f32[2,2,512,512]{3,2,1,0:T(8,128)} %obj.3), kind=kLoop, calls=%fused_computation.12 | loop fusion | bytes 2097152 | tf_op jit(solution)/shard_map/squeeze | solution.py:505
  3.1 2.1 collective-permute-start.1
  5.2 2.3 slice_bitcast_fusion.1
  7.5 2.9 %collective-permute-start = (f32[2,512,256]{2,1,0:T(8,128)}, f32[2,512,256]{2,1,0:T(8,128)S(1)}, u32[]{:S(2)}, u32[]{:S(2)}) collective-permute-start(f32[2,512,256]{2,1,0:T(8,128)} %slice_bitcast_fusion.1), channel_id=1, source_target_pairs={{8,0},{9,1},{10,2},{11,3},{12,4},{13,5},{14,6},{15,7},{16,8},{17,9... | collective-permute-start | bytes 3145736 | tf_op jit(solution)/shard_map/ppermute | solution.py:496
  10.4 2.8 %collective-permute-start.6 = (f32[2,2,16,256]{3,2,1,0:T(8,128)}, f32[2,2,16,256]{3,2,1,0:T(8,128)}, u32[]{:S(2)}, u32[]{:S(2)}) collective-permute-start(f32[2,2,16,256]{3,2,1,0:T(8,128)} %param.18), channel_id=1, source_target_pairs={{0,64},{1,65},{2,66},{3,67},{4,68},{5,69},{6,70},{7,71},{8,72},{9,... | collective-permute-start | bytes 196616 | tf_op jit(solution)/shard_map/ppermute | solution.py:496
  18.9 4.3 %collective-permute-start.4 = (f32[2,256,256]{2,1,0:T(8,128)S(1)}, f32[2,256,256]{2,1,0:T(8,128)}, u32[]{:S(2)}, u32[]{:S(2)}) collective-permute-start(f32[2,256,256]{2,1,0:T(8,128)S(1)} %collective-permute-done.1.low_a), channel_id=1, source_target_pairs={{8,0},{9,1},{10,2},{11,3},{12,4},{13,5},{14,6},{15,7},{24,16},{25,... | collective-permute-start | bytes 1572872 | tf_op jit(solution)/shard_map/ppermute | solution.py:496
  27.5 3.7 %order_amplitudes.1.amp = f32[6,256,256]{2,1,0:T(8,128)S(1)} custom-call(f32[6,256,256]{2,1,0:T(8,128)S(1)} %bitcast.76, bf16[256,768]{1,0:T(8,128)(2,1)S(1)} %copy-done.15, bf16[768,256]{1,0:T(8,128)(2,1)S(1)} %copy-done.16), custom_call_target="tpu_custom_call" | custom-call | flops 1200000000 | bytes 4000000 | tf_op jit(solution)/shard_map/order_amplitudes/pallas_call | solution.py:369
  32.3 10.3 %collective-permute-done.8 = f32[4,2,2,16,256]{4,3,2,1,0:T(8,128)} collective-permute-done((f32[4,2,2,16,256]{4,3,2,1,0:T(8,128)}, f32[4,2,2,16,256]{4,3,2,1,0:T(8,128)}, u32[]{:S(2)}, u32[]{:S(2)}) %collective-permute-start.8) | collective-permute-done | bytes 262176 | tf_op jit(solution)/shard_map/ppermute | solution.py:496
  44.5 2.5 %collective-permute-start.11 = (f32[2,256,256]{2,1,0:T(8,128)S(1)}, f32[2,256,256]{2,1,0:T(8,128)S(1)}, u32[]{:S(2)}, u32[]{:S(2)}) collective-permute-start(f32[2,256,256]{2,1,0:T(8,128)S(1)} %get-tuple-element.59), channel_id=1, source_target_pairs={{1,0},{2,1},{3,2},{4,3},{5,4},{6,5},{7,6},{9,8},{10,9},{11,10},{12... | collective-permute-start | bytes 1572872 | tf_op jit(solution)/shard_map/ppermute | solution.py:496
  48.3 1.9 collective-permute-start.10
  53.7 7.2 %collective-permute-done.11.low_a = f32[2,256,256]{2,1,0:T(8,128)S(1)} collective-permute-done((f32[2,256,256]{2,1,0:T(8,128)S(1)}, f32[2,256,256]{2,1,0:T(8,128)S(1)}, u32[]{:S(2)}, u32[]{:S(2)}) %collective-permute-start.11) | collective-permute-done | bytes 524320 | tf_op jit(solution)/shard_map/ppermute | solution.py:496
  60.9 3.5 %collective-permute-start.14 = (f32[2,256,256]{2,1,0:T(8,128)S(1)}, f32[2,256,256]{2,1,0:T(8,128)S(1)}, u32[]{:S(2)}, u32[]{:S(2)}) collective-permute-start(f32[2,256,256]{2,1,0:T(8,128)S(1)} %collective-permute-done.11.low_a), channel_id=1, source_target_pairs={{8,0},{9,1},{10,2},{11,3},{12,4},{13,5},{14,6},{15,7},{24,16},{25,... | collective-permute-start | bytes 1572872 | tf_op jit(solution)/shard_map/ppermute | solution.py:496
  64.5 12.3 %propagate_out.1 = (f32[6,2,2,256,256]{4,3,2,1,0:T(8,128)}, f32[6,2,256,256]{3,2,1,0:T(8,128)}) custom-call(s32[14]{0:T(128)S(1)} %pad_add_fusion.scalars, f32[2,2,512,512]{3,2,1,0:T(8,128)} %obj.3, f32[2,512,256]{2,1,0:T(8,128)S(1)} %collective-permute-done.right, f32[2,256,256]{2,1,0:T(8,128)S(1)} %collective-permute-done.1.low_a, ...), custom_call_target="tpu_custom_call" | custom-call | flops 10000000000 | bytes 20000000 | tf_op jit(solution)/shard_map/propagate_out/pallas_call | solution.py:387
  79.5 19.8 %far_field.1 = (f32[6,2,2,256,256]{4,3,2,1,0:T(8,128)}, f32[2,512,512]{2,1,0:T(8,128)}, f32[2,512,256]{2,1,0:T(8,128)}, f32[2,256,256]{2,1,0:T(8,128)S(1)}, f32[...) custom-call(s32[14]{0:T(128)S(1)} %pad_add_fusion.scalars, f32[2,2,512,512]{3,2,1,0:T(8,128)} %obj.3, ...), custom_call_target="tpu_custom_call" | custom-call | flops 10000000000 | bytes 20000000 | tf_op jit(solution)/shard_map/far_field/pallas_call | solution.py:406
  99.3 3.3 %collective-permute-start.15 = (f32[2,512,256]{2,1,0:T(8,128)}, f32[2,512,256]{2,1,0:T(8,128)}, u32[]{:S(2)}, u32[]{:S(2)}) collective-permute-start(f32[2,512,256]{2,1,0:T(8,128)} %get-tuple-element.44), channel_id=1, source_target_pairs={{0,8},{1,9},{2,10},{3,11},{4,12},{5,13},{6,14},{7,15},{8,16},{9,17... | collective-permute-start | bytes 3145736 | tf_op jit(solution)/shard_map/ppermute | solution.py:496
  104.0 11.9 %propagate_home.1 = (f32[2,2,256,256]{3,2,1,0:T(8,128)S(1)}, f32[2,512,512]{2,1,0:T(8,128)}, f32[2,512,256]{2,1,0:T(8,128)S(1)}, f32[2,256,256]{2,1,0:T(8,128)S(...) custom-call(s32[14]{0:T(128)S(1)} %pad_add_fusion.scalars, f32[6,2,256,256]{3,2,1,0:T(8,128)} %get-tuple-element.35.win, ...), custom_call_target="tpu_custom_call" | custom-call | flops 10000000000 | bytes 20000000 | tf_op jit(solution)/shard_map/propagate_home/pallas_call | solution.py:435
  117.0 4.1 %collective-permute-start.18 = (f32[2,256,256]{2,1,0:T(8,128)}, f32[2,256,256]{2,1,0:T(8,128)}, u32[]{:S(2)}, u32[]{:S(2)}) collective-permute-start(f32[2,256,256]{2,1,0:T(8,128)} %get-tuple-element.47), channel_id=1, source_target_pairs={{0,1},{1,2},{2,3},{3,4},{4,5},{5,6},{6,7},{8,9},{9,10},{10,11},{11... | collective-permute-start | bytes 1572872 | tf_op jit(solution)/shard_map/ppermute | solution.py:496
  121.0 27.4 %collective-permute-start.19 = (f32[2,256,256]{2,1,0:T(8,128)}, f32[2,256,256]{2,1,0:T(8,128)}, u32[]{:S(2)}, u32[]{:S(2)}) collective-permute-start(f32[2,256,256]{2,1,0:T(8,128)} %get-tuple-element.46), channel_id=1, source_target_pairs={{8,17},{9,18},{10,19},{11,20},{12,21},{13,22},{14,23},{24,33},{25,... | collective-permute-start | bytes 1572872 | tf_op jit(solution)/shard_map/ppermute | solution.py:496
  149.4 9.3 %collective-permute-start.17 = (f32[2,256,256]{2,1,0:T(8,128)}, f32[2,256,256]{2,1,0:T(8,128)}, u32[]{:S(2)}, u32[]{:S(2)}) collective-permute-start(f32[2,256,256]{2,1,0:T(8,128)} %add.63), channel_id=1, source_target_pairs={{0,1},{1,2},{2,3},{3,4},{4,5},{5,6},{6,7},{8,9},{9,10},{10,11},{11... | collective-permute-start | bytes 1572872 | tf_op jit(solution)/shard_map/ppermute | solution.py:496
  160.4 8.5 %collective-permute-start.28 = (f32[2,2,2,16,256]{4,3,2,1,0:T(8,128)S(1)}, f32[2,2,2,16,256]{4,3,2,1,0:T(8,128)S(1)}, u32[]{:S(2)}, u32[]{:S(2)}) collective-permute-start(f32[2,2,2,16,256]{4,3,2,1,0:T(8,128)S(1)} %bitcast.79), channel_id=1, source_target_pairs={{0,96},{1,97},{2,98},{3,99},{4,100},{5,101},{6,102},{7,103},{8,104... | collective-permute-start | bytes 393224 | tf_op jit(solution)/shard_map/ppermute | solution.py:496
  168.9 4.0 %collective-permute-start.20 = (f32[2,512,256]{2,1,0:T(8,128)}, f32[2,512,256]{2,1,0:T(8,128)S(1)}, u32[]{:S(2)}, u32[]{:S(2)}) collective-permute-start(f32[2,512,256]{2,1,0:T(8,128)} %copy-done.5), channel_id=1, source_target_pairs={{0,8},{1,9},{2,10},{3,11},{4,12},{5,13},{6,14},{7,15},{8,16},{9,17... | collective-permute-start | bytes 3145736 | tf_op jit(solution)/shard_map/ppermute | solution.py:496
  174.3 4.5 %collective-permute-start.30 = (f32[2,2,16,256]{3,2,1,0:T(8,128)S(1)}, f32[2,2,16,256]{3,2,1,0:T(8,128)S(1)}, u32[]{:S(2)}, u32[]{:S(2)}) collective-permute-start(f32[2,2,16,256]{3,2,1,0:T(8,128)S(1)} %get-tuple-element.74), channel_id=1, source_target_pairs={{0,16},{1,17},{2,18},{3,19},{4,20},{5,21},{6,22},{7,23},{8,24},{9,... | collective-permute-start | bytes 196616 | tf_op jit(solution)/shard_map/ppermute | solution.py:496
  179.8 9.1 %collective-permute-start.24 = (f32[2,256,256]{2,1,0:T(8,128)S(1)}, f32[2,256,256]{2,1,0:T(8,128)S(1)}, u32[]{:S(2)}, u32[]{:S(2)}) collective-permute-start(f32[2,256,256]{2,1,0:T(8,128)S(1)} %copy-done.7), channel_id=1, source_target_pairs={{8,17},{9,18},{10,19},{11,20},{12,21},{13,22},{14,23},{24,33},{25,... | collective-permute-start | bytes 1572872 | tf_op jit(solution)/shard_map/ppermute | solution.py:496
  189.0 3.1 %collective-permute-done.30 = f32[2,2,16,256]{3,2,1,0:T(8,128)S(1)} collective-permute-done((f32[2,2,16,256]{3,2,1,0:T(8,128)S(1)}, f32[2,2,16,256]{3,2,1,0:T(8,128)S(1)}, u32[]{:S(2)}, u32[]{:S(2)}) %collective-permute-start.30) | collective-permute-done | bytes 65568 | tf_op jit(solution)/shard_map/ppermute | solution.py:496
  192.1 7.9 %collective-permute-start.23 = (f32[2,256,256]{2,1,0:T(8,128)S(1)}, f32[2,256,256]{2,1,0:T(8,128)S(1)}, u32[]{:S(2)}, u32[]{:S(2)}) collective-permute-start(f32[2,256,256]{2,1,0:T(8,128)S(1)} %copy-done.9), channel_id=1, source_target_pairs={{0,1},{1,2},{2,3},{3,4},{4,5},{5,6},{6,7},{8,9},{9,10},{10,11},{11... | collective-permute-start | bytes 1572872 | tf_op jit(solution)/shard_map/ppermute | solution.py:496
  200.1 5.3 %collective-permute-start.22 = (f32[2,256,256]{2,1,0:T(8,128)S(1)}, f32[2,256,256]{2,1,0:T(8,128)S(1)}, u32[]{:S(2)}, u32[]{:S(2)}) collective-permute-start(f32[2,256,256]{2,1,0:T(8,128)S(1)} %add.64), channel_id=1, source_target_pairs={{0,1},{1,2},{2,3},{3,4},{4,5},{5,6},{6,7},{8,9},{9,10},{10,11},{11... | collective-permute-start | bytes 1572872 | tf_op jit(solution)/shard_map/ppermute | solution.py:496
  205.5 8.7 %collective-permute-start.33 = (f32[2,2,16,256]{3,2,1,0:T(8,128)S(1)}, f32[2,2,16,256]{3,2,1,0:T(8,128)S(1)}, u32[]{:S(2)}, u32[]{:S(2)}) collective-permute-start(f32[2,2,16,256]{3,2,1,0:T(8,128)S(1)} %add_add_fusion.1), channel_id=1, source_target_pairs={{0,4},{1,5},{2,6},{3,7},{4,0},{5,1},{6,2},{7,3},{8,12},{9,13},{10,... | collective-permute-start | bytes 196616 | tf_op jit(solution)/shard_map/ppermute | solution.py:496
  214.2 17.1 %collective-permute-done.33 = f32[2,2,16,256]{3,2,1,0:T(8,128)S(1)} collective-permute-done((f32[2,2,16,256]{3,2,1,0:T(8,128)S(1)}, f32[2,2,16,256]{3,2,1,0:T(8,128)S(1)}, u32[]{:S(2)}, u32[]{:S(2)}) %collective-permute-start.33) | collective-permute-done | bytes 65568 | tf_op jit(solution)/shard_map/ppermute | solution.py:496
  231.3 4.3 %collective-permute-done.34 = f32[2,2,16,256]{3,2,1,0:T(8,128)S(1)} collective-permute-done((f32[2,2,16,256]{3,2,1,0:T(8,128)S(1)}, f32[2,2,16,256]{3,2,1,0:T(8,128)S(1)}, u32[]{:S(2)}, u32[]{:S(2)}) %collective-permute-start.34) | collective-permute-done | bytes 65568 | tf_op jit(solution)/shard_map/ppermute | solution.py:496
  235.6 3.1 %collective-permute-done.32 = f32[2,2,16,256]{3,2,1,0:T(8,128)S(1)} collective-permute-done((f32[2,2,16,256]{3,2,1,0:T(8,128)S(1)}, f32[2,2,16,256]{3,2,1,0:T(8,128)S(1)}, u32[]{:S(2)}, u32[]{:S(2)}) %collective-permute-start.32) | collective-permute-done | bytes 65568 | tf_op jit(solution)/shard_map/ppermute | solution.py:496
  239.4 4.1 %join_gradients.2.rest_0_ = f32[2,2,512,512]{3,2,1,0:T(8,128)} custom-call(f32[2,512,512]{2,1,0:T(8,128)S(1)} %copy-done, f32[2,512,256]{2,1,0:T(8,128)} %collective-permute-done.15.right, f32[2,256,256]{2,1,0:T(8,128)} %collective-permute-done.17.low_a, f32[2,256,256]{2,1,0:T(8,128)} %collective-permute-done.18.low_b, ...), custom_call_target="tpu_custom_call" | custom-call | flops 1000000 | bytes 6000000 | tf_op jit(solution)/shard_map/join_gradients/pallas_call | solution.py:461
  243.5 2.2 join_gradients.3
  (117 shorter events, 27.7 us)
Async XLA Ops:
  3.1 15.8 %collective-permute-start.1 = (f32[2,256,256]{2,1,0:T(8,128)}, f32[2,256,256]{2,1,0:T(8,128)S(1)}, u32[]{:S(2)}, u32[]{:S(2)}) collective-permute-start(f32[2,256,256]{2,1,0:T(8,128)} %get-tuple-element.61), channel_id=1, source_target_pairs={{1,0},{2,1},{3,2},{4,3},{5,4},{6,5},{7,6},{9,8},{10,9},{11,10},{12... | collective-permute-start | bytes 1572872 | tf_op jit(solution)/shard_map/ppermute | solution.py:496
  7.5 36.9 %collective-permute-start = (f32[2,512,256]{2,1,0:T(8,128)}, f32[2,512,256]{2,1,0:T(8,128)S(1)}, u32[]{:S(2)}, u32[]{:S(2)}) collective-permute-start(f32[2,512,256]{2,1,0:T(8,128)} %slice_bitcast_fusion.1), channel_id=1, source_target_pairs={{8,0},{9,1},{10,2},{11,3},{12,4},{13,5},{14,6},{15,7},{16,8},{17,9... | collective-permute-start | bytes 3145736 | tf_op jit(solution)/shard_map/ppermute | solution.py:496
  10.4 5.7 %collective-permute-start.6 = (f32[2,2,16,256]{3,2,1,0:T(8,128)}, f32[2,2,16,256]{3,2,1,0:T(8,128)}, u32[]{:S(2)}, u32[]{:S(2)}) collective-permute-start(f32[2,2,16,256]{3,2,1,0:T(8,128)} %param.18), channel_id=1, source_target_pairs={{0,64},{1,65},{2,66},{3,67},{4,68},{5,69},{6,70},{7,71},{8,72},{9,... | collective-permute-start | bytes 196616 | tf_op jit(solution)/shard_map/ppermute | solution.py:496
  13.2 10.1 %collective-permute-start.7 = (f32[2,2,16,256]{3,2,1,0:T(8,128)}, f32[2,2,16,256]{3,2,1,0:T(8,128)}, u32[]{:S(2)}, u32[]{:S(2)}) collective-permute-start(f32[2,2,16,256]{3,2,1,0:T(8,128)} %param.18), channel_id=1, source_target_pairs={{0,96},{1,97},{2,98},{3,99},{4,100},{5,101},{6,102},{7,103},{8,104... | collective-permute-start | bytes 196616 | tf_op jit(solution)/shard_map/ppermute | solution.py:496
  14.0 30.4 %collective-permute-start.3 = (f32[2,256,256]{2,1,0:T(8,128)}, f32[2,256,256]{2,1,0:T(8,128)}, u32[]{:S(2)}, u32[]{:S(2)}) collective-permute-start(f32[2,256,256]{2,1,0:T(8,128)} %get-tuple-element.61), channel_id=1, source_target_pairs={{17,8},{18,9},{19,10},{20,11},{21,12},{22,13},{23,14},{33,24},{34,... | collective-permute-start | bytes 1572872 | tf_op jit(solution)/shard_map/ppermute | solution.py:496
  16.1 28.3 %collective-permute-start.2 = (f32[2,256,256]{2,1,0:T(8,128)}, f32[2,256,256]{2,1,0:T(8,128)}, u32[]{:S(2)}, u32[]{:S(2)}) collective-permute-start(f32[2,256,256]{2,1,0:T(8,128)} %get-tuple-element.60), channel_id=1, source_target_pairs={{1,0},{2,1},{3,2},{4,3},{5,4},{6,5},{7,6},{9,8},{10,9},{11,10},{12... | collective-permute-start | bytes 1572872 | tf_op jit(solution)/shard_map/ppermute | solution.py:496
  18.9 25.5 %collective-permute-start.4 = (f32[2,256,256]{2,1,0:T(8,128)S(1)}, f32[2,256,256]{2,1,0:T(8,128)}, u32[]{:S(2)}, u32[]{:S(2)}) collective-permute-start(f32[2,256,256]{2,1,0:T(8,128)S(1)} %collective-permute-done.1.low_a), channel_id=1, source_target_pairs={{8,0},{9,1},{10,2},{11,3},{12,4},{13,5},{14,6},{15,7},{24,16},{25,... | collective-permute-start | bytes 1572872 | tf_op jit(solution)/shard_map/ppermute | solution.py:496
  25.3 17.4 %collective-permute-start.8 = (f32[4,2,2,16,256]{4,3,2,1,0:T(8,128)}, f32[4,2,2,16,256]{4,3,2,1,0:T(8,128)}, u32[]{:S(2)}, u32[]{:S(2)}) collective-permute-start(f32[4,2,2,16,256]{4,3,2,1,0:T(8,128)} %get-tuple-element.68), channel_id=1, source_target_pairs={{0,17},{1,16},{2,19},{3,18},{4,21},{5,20},{6,23},{7,22},{8,25},{9,... | collective-permute-start | bytes 786440 | tf_op jit(solution)/shard_map/ppermute | solution.py:496
  43.9 6.3 %collective-permute-start.9 = (f32[2,4,2,2,16,256]{5,4,3,2,1,0:T(8,128)S(1)}, f32[2,4,2,2,16,256]{5,4,3,2,1,0:T(8,128)S(1)}, u32[]{:S(2)}, u32[]{:S(2)}) collective-permute-start(f32[2,4,2,2,16,256]{5,4,3,2,1,0:T(8,128)S(1)} %maximum_select_fusion.2), channel_id=1, source_target_pairs={{0,8},{1,9},{2,10},{3,11},{4,12},{5,13},{6,14},{7,15},{8,0},{9,1},... | collective-permute-start | bytes 1572872 | tf_op jit(solution)/shard_map/ppermute | solution.py:496
  44.5 16.4 %collective-permute-start.11 = (f32[2,256,256]{2,1,0:T(8,128)S(1)}, f32[2,256,256]{2,1,0:T(8,128)S(1)}, u32[]{:S(2)}, u32[]{:S(2)}) collective-permute-start(f32[2,256,256]{2,1,0:T(8,128)S(1)} %get-tuple-element.59), channel_id=1, source_target_pairs={{1,0},{2,1},{3,2},{4,3},{5,4},{6,5},{7,6},{9,8},{10,9},{11,10},{12... | collective-permute-start | bytes 1572872 | tf_op jit(solution)/shard_map/ppermute | solution.py:496
  48.3 30.2 %collective-permute-start.10 = (f32[2,512,256]{2,1,0:T(8,128)S(1)}, f32[2,512,256]{2,1,0:T(8,128)S(1)}, u32[]{:S(2)}, u32[]{:S(2)}) collective-permute-start(f32[2,512,256]{2,1,0:T(8,128)S(1)} %slice_bitcast_fusion), channel_id=1, source_target_pairs={{8,0},{9,1},{10,2},{11,3},{12,4},{13,5},{14,6},{15,7},{16,8},{17,9... | collective-permute-start | bytes 3145736 | tf_op jit(solution)/shard_map/ppermute | solution.py:496
  50.5 26.3 %collective-permute-start.13 = (f32[2,256,256]{2,1,0:T(8,128)S(1)}, f32[2,256,256]{2,1,0:T(8,128)S(1)}, u32[]{:S(2)}, u32[]{:S(2)}) collective-permute-start(f32[2,256,256]{2,1,0:T(8,128)S(1)} %get-tuple-element.59), channel_id=1, source_target_pairs={{17,8},{18,9},{19,10},{20,11},{21,12},{22,13},{23,14},{33,24},{34,... | collective-permute-start | bytes 1572872 | tf_op jit(solution)/shard_map/ppermute | solution.py:496
  51.8 25.0 %collective-permute-start.12 = (f32[2,256,256]{2,1,0:T(8,128)S(1)}, f32[2,256,256]{2,1,0:T(8,128)S(1)}, u32[]{:S(2)}, u32[]{:S(2)}) collective-permute-start(f32[2,256,256]{2,1,0:T(8,128)S(1)} %get-tuple-element.58), channel_id=1, source_target_pairs={{1,0},{2,1},{3,2},{4,3},{5,4},{6,5},{7,6},{9,8},{10,9},{11,10},{12... | collective-permute-start | bytes 1572872 | tf_op jit(solution)/shard_map/ppermute | solution.py:496
  60.9 17.6 %collective-permute-start.14 = (f32[2,256,256]{2,1,0:T(8,128)S(1)}, f32[2,256,256]{2,1,0:T(8,128)S(1)}, u32[]{:S(2)}, u32[]{:S(2)}) collective-permute-start(f32[2,256,256]{2,1,0:T(8,128)S(1)} %collective-permute-done.11.low_a), channel_id=1, source_target_pairs={{8,0},{9,1},{10,2},{11,3},{12,4},{13,5},{14,6},{15,7},{24,16},{25,... | collective-permute-start | bytes 1572872 | tf_op jit(solution)/shard_map/ppermute | solution.py:496
  99.3 69.7 %collective-permute-start.15 = (f32[2,512,256]{2,1,0:T(8,128)}, f32[2,512,256]{2,1,0:T(8,128)}, u32[]{:S(2)}, u32[]{:S(2)}) collective-permute-start(f32[2,512,256]{2,1,0:T(8,128)} %get-tuple-element.44), channel_id=1, source_target_pairs={{0,8},{1,9},{2,10},{3,11},{4,12},{5,13},{6,14},{7,15},{8,16},{9,17... | collective-permute-start | bytes 3145736 | tf_op jit(solution)/shard_map/ppermute | solution.py:496
  102.6 45.9 %collective-permute-start.16 = (f32[2,256,256]{2,1,0:T(8,128)}, f32[2,256,256]{2,1,0:T(8,128)S(1)}, u32[]{:S(2)}, u32[]{:S(2)}) collective-permute-start(f32[2,256,256]{2,1,0:T(8,128)} %get-tuple-element.46), channel_id=1, source_target_pairs={{0,8},{1,9},{2,10},{3,11},{4,12},{5,13},{6,14},{7,15},{16,24},{17,... | collective-permute-start | bytes 1572872 | tf_op jit(solution)/shard_map/ppermute | solution.py:496
  117.0 41.8 %collective-permute-start.25 = (f32[4,2,2,2,16,256]{5,4,1,0,3,2:T(8,128)}, f32[4,2,2,2,16,256]{5,4,1,0,3,2:T(8,128)}, u32[]{:S(2)}, u32[]{:S(2)}) collective-permute-start(f32[4,2,2,2,16,256]{5,4,1,0,3,2:T(8,128)} %select_bitcast_fusion), channel_id=1, source_target_pairs={{0,8},{1,9},{2,10},{3,11},{4,12},{5,13},{6,14},{7,15},{8,0},{9,1},... | collective-permute-start | bytes 1572872 | tf_op jit(solution)/shard_map/ppermute | solution.py:496
  117.0 43.3 %collective-permute-start.18 = (f32[2,256,256]{2,1,0:T(8,128)}, f32[2,256,256]{2,1,0:T(8,128)}, u32[]{:S(2)}, u32[]{:S(2)}) collective-permute-start(f32[2,256,256]{2,1,0:T(8,128)} %get-tuple-element.47), channel_id=1, source_target_pairs={{0,1},{1,2},{2,3},{3,4},{4,5},{5,6},{6,7},{8,9},{9,10},{10,11},{11... | collective-permute-start | bytes 1572872 | tf_op jit(solution)/shard_map/ppermute | solution.py:496
  121.0 39.4 %collective-permute-start.19 = (f32[2,256,256]{2,1,0:T(8,128)}, f32[2,256,256]{2,1,0:T(8,128)}, u32[]{:S(2)}, u32[]{:S(2)}) collective-permute-start(f32[2,256,256]{2,1,0:T(8,128)} %get-tuple-element.46), channel_id=1, source_target_pairs={{8,17},{9,18},{10,19},{11,20},{12,21},{13,22},{14,23},{24,33},{25,... | collective-permute-start | bytes 1572872 | tf_op jit(solution)/shard_map/ppermute | solution.py:496
  149.4 19.6 %collective-permute-start.17 = (f32[2,256,256]{2,1,0:T(8,128)}, f32[2,256,256]{2,1,0:T(8,128)}, u32[]{:S(2)}, u32[]{:S(2)}) collective-permute-start(f32[2,256,256]{2,1,0:T(8,128)} %add.63), channel_id=1, source_target_pairs={{0,1},{1,2},{2,3},{3,4},{4,5},{5,6},{6,7},{8,9},{9,10},{10,11},{11... | collective-permute-start | bytes 1572872 | tf_op jit(solution)/shard_map/ppermute | solution.py:496
  160.1 14.1 %collective-permute-start.26 = (f32[2,2,2,16,256]{4,3,2,1,0:T(8,128)S(1)}, f32[2,2,2,16,256]{4,3,2,1,0:T(8,128)S(1)}, u32[]{:S(2)}, u32[]{:S(2)}) collective-permute-start(f32[2,2,2,16,256]{4,3,2,1,0:T(8,128)S(1)} %bitcast.78), channel_id=1, source_target_pairs={{0,32},{1,33},{2,34},{3,35},{4,36},{5,37},{6,38},{7,39},{8,40},{9,... | collective-permute-start | bytes 393224 | tf_op jit(solution)/shard_map/ppermute | solution.py:496
  160.3 14.0 %collective-permute-start.27 = (f32[2,2,2,16,256]{4,3,2,1,0:T(8,128)S(1)}, f32[2,2,2,16,256]{4,3,2,1,0:T(8,128)S(1)}, u32[]{:S(2)}, u32[]{:S(2)}) collective-permute-start(f32[2,2,2,16,256]{4,3,2,1,0:T(8,128)S(1)} %bitcast.80), channel_id=1, source_target_pairs={{0,64},{1,65},{2,66},{3,67},{4,68},{5,69},{6,70},{7,71},{8,72},{9,... | collective-permute-start | bytes 393224 | tf_op jit(solution)/shard_map/ppermute | solution.py:496
  160.4 13.9 %collective-permute-start.28 = (f32[2,2,2,16,256]{4,3,2,1,0:T(8,128)S(1)}, f32[2,2,2,16,256]{4,3,2,1,0:T(8,128)S(1)}, u32[]{:S(2)}, u32[]{:S(2)}) collective-permute-start(f32[2,2,2,16,256]{4,3,2,1,0:T(8,128)S(1)} %bitcast.79), channel_id=1, source_target_pairs={{0,96},{1,97},{2,98},{3,99},{4,100},{5,101},{6,102},{7,103},{8,104... | collective-permute-start | bytes 393224 | tf_op jit(solution)/shard_map/ppermute | solution.py:496
  168.9 74.6 %collective-permute-start.20 = (f32[2,512,256]{2,1,0:T(8,128)}, f32[2,512,256]{2,1,0:T(8,128)S(1)}, u32[]{:S(2)}, u32[]{:S(2)}) collective-permute-start(f32[2,512,256]{2,1,0:T(8,128)} %copy-done.5), channel_id=1, source_target_pairs={{0,8},{1,9},{2,10},{3,11},{4,12},{5,13},{6,14},{7,15},{8,16},{9,17... | collective-permute-start | bytes 3145736 | tf_op jit(solution)/shard_map/ppermute | solution.py:496
  172.9 6.9 %collective-permute-start.21 = (f32[2,256,256]{2,1,0:T(8,128)}, f32[2,256,256]{2,1,0:T(8,128)S(1)}, u32[]{:S(2)}, u32[]{:S(2)}) collective-permute-start(f32[2,256,256]{2,1,0:T(8,128)} %copy-done.6), channel_id=1, source_target_pairs={{0,8},{1,9},{2,10},{3,11},{4,12},{5,13},{6,14},{7,15},{16,24},{17,... | collective-permute-start | bytes 1572872 | tf_op jit(solution)/shard_map/ppermute | solution.py:496
  174.3 17.8 %collective-permute-start.30 = (f32[2,2,16,256]{3,2,1,0:T(8,128)S(1)}, f32[2,2,16,256]{3,2,1,0:T(8,128)S(1)}, u32[]{:S(2)}, u32[]{:S(2)}) collective-permute-start(f32[2,2,16,256]{3,2,1,0:T(8,128)S(1)} %get-tuple-element.74), channel_id=1, source_target_pairs={{0,16},{1,17},{2,18},{3,19},{4,20},{5,21},{6,22},{7,23},{8,24},{9,... | collective-permute-start | bytes 196616 | tf_op jit(solution)/shard_map/ppermute | solution.py:496
  178.8 21.3 %collective-permute-start.31 = (f32[2,2,16,256]{3,2,1,0:T(8,128)S(1)}, f32[2,2,16,256]{3,2,1,0:T(8,128)S(1)}, u32[]{:S(2)}, u32[]{:S(2)}) collective-permute-start(f32[2,2,16,256]{3,2,1,0:T(8,128)S(1)} %get-tuple-element.74), channel_id=1, source_target_pairs={{0,17},{1,16},{2,19},{3,18},{4,21},{5,20},{6,23},{7,22},{8,25},{9,... | collective-permute-start | bytes 196616 | tf_op jit(solution)/shard_map/ppermute | solution.py:496
  178.8 26.6 %collective-permute-start.29 = (f32[2,2,16,256]{3,2,1,0:T(8,128)S(1)}, f32[2,2,16,256]{3,2,1,0:T(8,128)S(1)}, u32[]{:S(2)}, u32[]{:S(2)}) collective-permute-start(f32[2,2,16,256]{3,2,1,0:T(8,128)S(1)} %get-tuple-element.73), channel_id=1, source_target_pairs={{0,1},{1,0},{2,3},{3,2},{4,5},{5,4},{6,7},{7,6},{8,9},{9,8},{10,11... | collective-permute-start | bytes 196616 | tf_op jit(solution)/shard_map/ppermute | solution.py:496
  179.8 63.7 %collective-permute-start.24 = (f32[2,256,256]{2,1,0:T(8,128)S(1)}, f32[2,256,256]{2,1,0:T(8,128)S(1)}, u32[]{:S(2)}, u32[]{:S(2)}) collective-permute-start(f32[2,256,256]{2,1,0:T(8,128)S(1)} %copy-done.7), channel_id=1, source_target_pairs={{8,17},{9,18},{10,19},{11,20},{12,21},{13,22},{14,23},{24,33},{25,... | collective-permute-start | bytes 1572872 | tf_op jit(solution)/shard_map/ppermute | solution.py:496
  192.1 51.4 %collective-permute-start.23 = (f32[2,256,256]{2,1,0:T(8,128)S(1)}, f32[2,256,256]{2,1,0:T(8,128)S(1)}, u32[]{:S(2)}, u32[]{:S(2)}) collective-permute-start(f32[2,256,256]{2,1,0:T(8,128)S(1)} %copy-done.9), channel_id=1, source_target_pairs={{0,1},{1,2},{2,3},{3,4},{4,5},{5,6},{6,7},{8,9},{9,10},{10,11},{11... | collective-permute-start | bytes 1572872 | tf_op jit(solution)/shard_map/ppermute | solution.py:496
  200.1 43.4 %collective-permute-start.22 = (f32[2,256,256]{2,1,0:T(8,128)S(1)}, f32[2,256,256]{2,1,0:T(8,128)S(1)}, u32[]{:S(2)}, u32[]{:S(2)}) collective-permute-start(f32[2,256,256]{2,1,0:T(8,128)S(1)} %add.64), channel_id=1, source_target_pairs={{0,1},{1,2},{2,3},{3,4},{4,5},{5,6},{6,7},{8,9},{9,10},{10,11},{11... | collective-permute-start | bytes 1572872 | tf_op jit(solution)/shard_map/ppermute | solution.py:496
  205.5 25.8 %collective-permute-start.33 = (f32[2,2,16,256]{3,2,1,0:T(8,128)S(1)}, f32[2,2,16,256]{3,2,1,0:T(8,128)S(1)}, u32[]{:S(2)}, u32[]{:S(2)}) collective-permute-start(f32[2,2,16,256]{3,2,1,0:T(8,128)S(1)} %add_add_fusion.1), channel_id=1, source_target_pairs={{0,4},{1,5},{2,6},{3,7},{4,0},{5,1},{6,2},{7,3},{8,12},{9,13},{10,... | collective-permute-start | bytes 196616 | tf_op jit(solution)/shard_map/ppermute | solution.py:496
  (27 other events, 550.4 us)

commit v2 on v1

--- a/solution.py
+++ b/solution.py
@@ -189,12 +189,31 @@
     out[0] = jnp.dot(jnp.concatenate([hi, mid, lo], axis=1), perm_r[...], preferred_element_type=F32)
 
 
-def out_kernel(scalars, obj, right, low_a, low_b, diag, side, probe, table_l, table_r, psi, win, field, sems):
+def out_kernel(
+    scalars, obj, right, low_a, low_b, diag, side, mine, across, mine_other, across_other, table_l, table_r,
+    psi, win, probe_rows, field, sems, probe_sem,
+):
     slot = pl.program_id(0)
+    probe = probe_rows.reshape(2, 2, PROBE, PROBE)
 
     @pl.when(slot == 0)
     def _():
-        fetch_field(0, scalars[13], obj, right, low_a, low_b, diag, side, field, sems)
+        core, y_hi, z = scalars[13], scalars[14], scalars[15]
+        copies = [
+            pltpu.make_async_copy(src.at[k], probe_rows.at[:, :, z ^ k, y, c], probe_sem)
+            for src, y, c in (
+                (mine, y_hi, core),
+                (across, 1 - y_hi, core),
+                (mine_other, y_hi, 1 - core),
+                (across_other, 1 - y_hi, 1 - core),
+            )
+            for k in range(4)
+        ]
+        for copy in copies:
+            copy.start()
+        fetch_field(0, core, obj, right, low_a, low_b, diag, side, field, sems)
+        for copy in copies:
+            copy.wait()
 
     @pl.when(slot < scalars[12])
     def _():
@@ -213,74 +232,109 @@
 
 def far_kernel(
     scalars, obj, right, low_a, low_b, diag, side, psi, amp, four_l, four_r, ruof_l, ruof_r, tw_row, tw_col,
-    g_psi, g_main, g_right, g_low_a, g_low_b, g_corner, field, grad, sems,
+    g_psi, g_main, g_right, g_low_a, g_low_b, g_corner, field, grad, win, gwin, sems,
 ):
     slot = pl.program_id(0)
     h, n = HALF, PROBE
+    used = scalars[12]
+
+    def load_window(at):
+        place = place_of(scalars, at)
+        win[0] = window_of(field, 0, place)
+        win[1] = window_of(field, 1, place)
+
+    def flush(at):
+        place = place_of(scalars, at)
+        add_window(grad, 0, place, gwin[0])
+        add_window(grad, 1, place, gwin[1])
 
     @pl.when(slot == 0)
     def _():
+        grad[...] = jnp.zeros_like(grad)
+        gwin[...] = jnp.zeros_like(gwin)
         fetch_field(1, scalars[13], obj, right, low_a, low_b, diag, side, field, sems)
-        grad[...] = jnp.zeros_like(grad)
-
-    @pl.when(slot < scalars[12])
-    def _():
-        place = place_of(scalars, slot)
-        w_re = window_of(field, 0, place)
-        w_im = window_of(field, 1, place)
+        load_window(0)
+
+    @pl.when(slot < used)
+    def _():
+        w_re, w_im = win[0], win[1]
         tr, ti = tw_row[0], tw_row[1]
         cr, ci = tw_col[0, 0:1], tw_col[1, 0:1]
-        outs = []
-        for m in (0, 1):
-            p_re, p_im = psi[0, m, 0], psi[0, m, 1]
-            re = p_re * w_re - p_im * w_im
-            im = p_re * w_im + p_im * w_re
-            d_re, d_im = re[:h] - re[h:], im[:h] - im[h:]
-            top = jnp.concatenate([re[:h] + re[h:], d_re * tr - d_im * ti], axis=1)
-            bottom = jnp.concatenate([im[:h] + im[h:], d_re * ti + d_im * tr], axis=1)
-            y = lmul(four_l[...], jnp.concatenate([top, bottom], axis=0))
-            re = jnp.concatenate([y[:h, :n], y[:h, n:]], axis=0)
-            im = jnp.concatenate([y[h:, :n], y[h:, n:]], axis=0)
+        chi = {}
+
+        def left(m, odd):
+            if m not in chi:
+                p_re, p_im = psi[0, m, 0], psi[0, m, 1]
+                chi[m] = (p_re * w_re - p_im * w_im, p_re * w_im + p_im * w_re)
+            re, im = chi[m]
+            if odd:
+                d_re, d_im = re[:h] - re[h:], im[:h] - im[h:]
+                x = [d_re * tr - d_im * ti, d_re * ti + d_im * tr]
+            else:
+                x = [re[:h] + re[h:], im[:h] + im[h:]]
+            return lmul(four_l[...], jnp.concatenate(x, axis=0))
+
+        def across(y):
+            re, im = y[:h], y[h:]
             d_re, d_im = re[:, :h] - re[:, h:], im[:, :h] - im[:, h:]
             even = jnp.concatenate([re[:, :h] + re[:, h:], im[:, :h] + im[:, h:]], axis=1)
             odd = jnp.concatenate([d_re * cr - d_im * ci, d_re * ci + d_im * cr], axis=1)
-            outs.append(rmul(jnp.concatenate([even, odd], axis=0), four_r[...]))
-        sq = outs[0] * outs[0] + outs[1] * outs[1]
-        total = sq[:, :h] + sq[:, h:] + 1.0
-        both = jnp.concatenate([amp[0, :, :h], amp[0, :, h:]], axis=0)
-        slope = 2.0 - 2.0 * both * lax.rsqrt(total)
-        slope = jnp.concatenate([slope, slope], axis=1)
-        gw_re = gw_im = None
-        for m in (0, 1):
-            y = rmul(outs[m] * slope, ruof_r[...])
-            q_re = y[n:, :h] * cr + y[n:, h:] * ci
-            q_im = y[n:, h:] * cr - y[n:, :h] * ci
-            re = jnp.concatenate([y[:n, :h] + q_re, y[:n, :h] - q_re], axis=1)
-            im = jnp.concatenate([y[:n, h:] + q_im, y[:n, h:] - q_im], axis=1)
-            x = jnp.concatenate(
-                [
-                    jnp.concatenate([re[:h], re[h:]], axis=1),
-                    jnp.concatenate([im[:h], im[h:]], axis=1),
-                ],
-                axis=0,
-            )
-            y = lmul(ruof_l[...], x)
-            q_re = y[:h, n:] * tr + y[h:, n:] * ti
-            q_im = y[h:, n:] * tr - y[:h, n:] * ti
-            re = jnp.concatenate([y[:h, :n] + q_re, y[:h, :n] - q_re], axis=0)
-            im = jnp.concatenate([y[h:, :n] + q_im, y[h:, :n] - q_im], axis=0)
+            return rmul(jnp.concatenate([even, odd], axis=0), four_r[...])
+
+        def slope_of(z0, z1, rows):
+            sq = z0 * z0 + z1 * z1
+            total = sq[:, :h] + sq[:, h:] + 1.0
+            both = jnp.concatenate([amp[0, rows, :h], amp[0, rows, h:]], axis=0)
+            slope = 2.0 - 2.0 * both * lax.rsqrt(total)
+            return jnp.concatenate([slope, slope], axis=1)
+
+        def back_across(z):
+            y = rmul(z, ruof_r[...])
+            q_re = y[h:, :h] * cr + y[h:, h:] * ci
+            q_im = y[h:, h:] * cr - y[h:, :h] * ci
+            re = jnp.concatenate([y[:h, :h] + q_re, y[:h, :h] - q_re], axis=1)
+            im = jnp.concatenate([y[:h, h:] + q_im, y[:h, h:] - q_im], axis=1)
+            return jnp.concatenate([re, im], axis=0)
+
+        def finish(m, y_even, y_odd):
+            q_re = y_odd[:h] * tr + y_odd[h:] * ti
+            q_im = y_odd[h:] * tr - y_odd[:h] * ti
+            re = jnp.concatenate([y_even[:h] + q_re, y_even[:h] - q_re], axis=0)
+            im = jnp.concatenate([y_even[h:] + q_im, y_even[h:] - q_im], axis=0)
             g_psi[0, m, 0] = w_re * re + w_im * im
             g_psi[0, m, 1] = w_re * im - w_im * re
             p_re, p_im = psi[0, m, 0], psi[0, m, 1]
-            a_re = p_re * re + p_im * im
-            a_im = p_re * im - p_im * re
-            gw_re = a_re if m == 0 else gw_re + a_re
-            gw_im = a_im if m == 0 else gw_im + a_im
-        add_window(grad, 0, place, gw_re)
-        add_window(grad, 1, place, gw_im)
+            return p_re * re + p_im * im, p_re * im - p_im * re
+
+        back = ruof_l[...]
+        l0e = left(0, 0)
+        l1e = left(1, 0)
+        l0o = left(0, 1)
+        z0e = across(l0e)
+        l1o = left(1, 1)
+        z1e = across(l1e)
+        slope_e = slope_of(z0e, z1e, slice(0, h))
+        z0o = across(l0o)
+        b0e = back_across(z0e * slope_e)
+        z1o = across(l1o)
+        flush(jnp.maximum(slot - 1, 0))
+        slope_o = slope_of(z0o, z1o, slice(h, n))
+        load_window(jnp.minimum(slot + 1, SLOTS - 1))
+        b1e = back_across(z1e * slope_e)
+        a0e = lmul(back, b0e)
+        b0o = back_across(z0o * slope_o)
+        a1e = lmul(back, b1e)
+        b1o = back_across(z1o * slope_o)
+        a0o = lmul(back, b0o)
+        a1o = lmul(back, b1o)
+        u_re, u_im = finish(0, a0e, a0o)
+        v_re, v_im = finish(1, a1e, a1o)
+        gwin[0] = u_re + v_re
+        gwin[1] = u_im + v_im
 
     @pl.when(slot == pl.num_programs(0) - 1)
     def _():
+        flush(used - 1)
         store_field(grad, g_main, g_right, g_low_a, g_low_b, g_corner, sems)
 
 
@@ -339,6 +393,10 @@
     return pl.BlockSpec(shape, lambda j, s: (0,) * len(shape))
 
 
+def held():
+    return pl.BlockSpec(memory_space=pltpu.VMEM)
+
+
 def any_spec():
     return pl.BlockSpec(memory_space=pl.ANY)
 
@@ -389,16 +447,19 @@
         grid_spec=pltpu.PrefetchScalarGridSpec(
             num_scalar_prefetch=1,
             grid=(SLOTS,),
-            in_specs=[any_spec()] * 6
-            + [whole((2, 2, n, n)), whole((2 * n, 6 * n)), whole((6 * n, 2 * n))],
-            out_specs=[of_slot((2, 2, n, n)), of_slot((2, n, n))],
-            scratch_shapes=[pltpu.VMEM((2, 3 * n, 3 * n), F32), pltpu.SemaphoreType.DMA((5,))],
+            in_specs=[any_spec()] * 10 + [held()] * 2,
+            out_specs=[of_slot((2, 2, n, n)), of_slot((2, n, n)), whole((2, 2, 4, 2, 2, 16, n))],
+            scratch_shapes=[
+                pltpu.VMEM((2, 3 * n, 3 * n), F32),
+                pltpu.SemaphoreType.DMA((5,)),
+                pltpu.SemaphoreType.DMA,
+            ],
         ),
-        out_shape=[sds((SLOTS, 2, 2, n, n)), sds((SLOTS, 2, n, n))],
+        out_shape=[sds((SLOTS, 2, 2, n, n)), sds((SLOTS, 2, n, n)), sds((2, 2, 4, 2, 2, 16, n))],
         compiler_params=params(),
-        cost_estimate=cost(1e10, 2e7),
+        cost_estimate=cost(6e10, 2e7),
         name="propagate_out",
-    )(scalars, obj, *halo, probe, tables["prop_l"], tables["prop_r"])
+    )(scalars, obj, *halo, *probe, tables["prop_l"], tables["prop_r"])
 
 
 def run_far(scalars, obj, halo, psi, amp, tables):
@@ -410,18 +471,19 @@
             grid=(SLOTS,),
             in_specs=[any_spec()] * 6
             + [of_slot((2, 2, n, n)), of_slot((n, n))]
-            + [whole((n, 3 * n)), whole((3 * n, n))] * 2
-            + [whole((2, HALF, n)), whole((2, 8, HALF))],
+            + [held()] * 6,
             out_specs=[of_slot((2, 2, n, n))] + [any_spec()] * 5,
             scratch_shapes=[
                 pltpu.VMEM((2, 3 * n, 3 * n), F32),
                 pltpu.VMEM((2, 3 * n, 3 * n), F32),
+                pltpu.VMEM((2, n, n), F32),
+                pltpu.VMEM((2, n, n), F32),
                 pltpu.SemaphoreType.DMA((5,)),
             ],
         ),
         out_shape=[sds((SLOTS, 2, 2, n, n))] + [sds(s) for s in FIELD_PARTS],
         compiler_params=params(),
-        cost_estimate=cost(1e10, 2e7),
+        cost_estimate=cost(6e10, 2e7),
         name="far_field",
     )(
         scalars, obj, *halo, psi, amp,
@@ -440,16 +502,16 @@
             in_specs=[
                 of_slot((2, n, n)),
                 of_slot((2, 2, n, n)),
-                whole((2, 2, n, n)),
-                whole((2 * n, 6 * n)),
-                whole((6 * n, 2 * n)),
+                held(),
+                held(),
+                held(),
             ],
             out_specs=[whole((2, 2, n, n))] + [any_spec()] * 5,
             scratch_shapes=[pltpu.VMEM((2, 3 * n, 3 * n), F32), pltpu.SemaphoreType.DMA((5,))],
         ),
         out_shape=[sds((2, 2, n, n))] + [sds(s) for s in FIELD_PARTS],
         compiler_params=params(),
-        cost_estimate=cost(1e10, 2e7),
+        cost_estimate=cost(6e10, 2e7),
         name="propagate_home",
     )(scalars, win, g_psi, probe, tables["back_l"], tables["back_r"])
 
@@ -498,12 +560,15 @@
     def flip(gx_bits, gy_bits):
         return lambda gx, gy: (gx ^ gx_bits, gy ^ gy_bits)
 
-    def bring(obj, layer):
+    def pieces(obj, layer):
         n = PROBE
-        low_a = send(obj[layer, :, :n, :n], lambda gx, gy: (gx, gy - 1))
-        right = send(obj[layer, :, :, :n], lambda gx, gy: (gx - 1, gy))
-        low_b = send(obj[layer, :, :n, n:], lambda gx, gy: (gx, gy - 1))
-        diag = send(obj[layer, :, :n, :n], lambda gx, gy: (gx - 1, gy - 1) if gx % 2 == 0 else None)
+        return obj[layer, :, :n, :n], obj[layer, :, :, :n], obj[layer, :, :n, n:]
+
+    def bring(corner, edge, low):
+        low_a = send(corner, lambda gx, gy: (gx, gy - 1))
+        right = send(edge, lambda gx, gy: (gx - 1, gy))
+        low_b = send(low, lambda gx, gy: (gx, gy - 1))
+        diag = send(corner, lambda gx, gy: (gx - 1, gy - 1) if gx % 2 == 0 else None)
         side = send(low_a, lambda gx, gy: (gx - 1, gy) if gx % 2 == 1 else None)
         return right, low_a, low_b, diag, side
 
@@ -516,23 +581,8 @@
         return right, low_a, low_b, diag
 
     def gather_probe(probe):
-        gx = lax.axis_index("gx")
-        core, y_hi, z = gx % 2, gx // 2 % 2, gx // 4
-        parts = [probe] + [send(probe, flip(4 * k, 0)) for k in (1, 2, 3)]
-        stack = jnp.stack(parts)
-        stack = jnp.stack([stack[k ^ 0] for k in range(4)])
-        ordered = [
-            jnp.where(z == 0, stack[k], jnp.where(z == 1, stack[k ^ 1], jnp.where(z == 2, stack[k ^ 2], stack[k ^ 3])))
-            for k in range(4)
-        ]
-        mine = jnp.stack(ordered)
-        other = send(mine, flip(2, 1))
-        mine = jnp.where(y_hi == 0, jnp.stack([mine, other]), jnp.stack([other, mine]))
-        other = send(mine, flip(1, 0))
-        mine = jnp.where(core == 0, jnp.stack([mine, other]), jnp.stack([other, mine]))
-        rows = probe.shape[2]
-        full = jnp.transpose(mine, (3, 4, 2, 1, 0, 5, 6))
-        return full.reshape(2, 2, n_gx * rows, PROBE)
+        mine = jnp.stack([probe] + [send(probe, flip(4 * k, 0)) for k in (1, 2, 3)])
+        return mine, send(mine, flip(2, 1))
 
     def reduce_probe(grad):
         gx = lax.axis_index("gx")
@@ -558,20 +608,22 @@
         return (part + got[0]) + (got[1] + got[2])
 
     def on_device(obj, probe, positions, counts, amplitudes):
-        core = lax.axis_index("gx") % 2
+        gx = lax.axis_index("gx").astype(jnp.int32)
         scalars = jnp.concatenate(
-            [positions.reshape(2 * SLOTS), counts.reshape(1), core.astype(jnp.int32).reshape(1)]
+            [positions.reshape(2 * SLOTS), counts.reshape(1), jnp.stack([gx & 1, gx >> 1 & 1, gx >> 2])]
         )
-        halo_0 = bring(obj, 0)
-        probe_full = gather_probe(probe)
+        halo_0 = bring(*pieces(obj, 0))
+        probe_parts = gather_probe(probe)
         amp = permute_amplitudes(amplitudes[0, 0], tables)
-        obj_late, halo_0 = lax.optimization_barrier((obj, halo_0))
-        halo_1 = bring(obj_late, 1)
-        psi, win = run_out(scalars, obj, halo_0, probe_full, tables)
+        pieces_1, halo_0, amp, probe_parts = lax.optimization_barrier((pieces(obj, 1), halo_0, amp, probe_parts))
+        probe_parts = [*probe_parts, *(send(x, flip(1, 0)) for x in probe_parts)]
+        halo_1 = bring(*pieces_1)
+        psi, win, probe_rows = run_out(scalars, obj, halo_0, probe_parts, tables)
+        probe_full = probe_rows.reshape(2, 2, PROBE, PROBE)
         g_psi, main_1, *edges_1 = run_far(scalars, obj, halo_1, psi, amp, tables)
         back_1 = take_back(*edges_1)
         g_probe, main_0, *edges_0 = run_home(scalars, win, g_psi, probe_full, tables)
-        edges_0, back_1 = lax.optimization_barrier((edges_0, back_1))
+        edges_0, g_probe, back_1 = lax.optimization_barrier((edges_0, g_probe, back_1))
         back_0 = take_back(*edges_0)
         grad = run_join(1, main_1, back_1, None)
         probe_grad = reduce_probe(g_probe)

time: 247 us -> 243 us (0.984)
  the two profiles are of different devices: /device:TPU:41 before, /device:TPU:9 now
where the time goes in v2:
time: 243 us; the launch traced here: 242 us
  starting transfers between devices  126 us (52%)
  waiting for transfers between devices  42.2 us (17%)
  Pallas kernels  42.2 us (17%)
  local copies, waits for them, and re-layouts  26 us (11%)
  other arithmetic  4.02 us (2%)
    ppermute x36, starting transfers between devices, send(): return lax.ppermute(x, axes, pairs)  126 us
    ppermute x36, waiting for transfers between devices, send(): return lax.ppermute(x, axes, pairs)  42.2 us
    unnamed x77, local copies, waits for them, and re-layouts  21.7 us
    pallas_call x1, Pallas kernels, run_far(): pl.pallas_call(far_kernel, grid_spec=pltpu.PrefetchScalarGridSpec(num_sca...  14 us
    pallas_call x1, Pallas kernels, run_out(): pl.pallas_call(out_kernel, grid_spec=pltpu.PrefetchScalarGridSpec(num_sca...  10.5 us
    pallas_call x1, Pallas kernels, run_home(): pl.pallas_call(home_kernel, grid_spec=pltpu.PrefetchScalarGridSpec(num_sc...  9.56 us
  transfers between devices with their start and end apart: 36, of which 12 were waited for; matrix products, arithmetic and copies ran while one was open for 1% of the time, Pallas kernels for 11%

profile of v2, /device:TPU:9, one launch (start us, length us, event | category | flops | bytes accessed | tf_op | source)
XLA Modules:
  0.0 242.2 jit_solution(12204315627322363399)
XLA Ops:
  0.6 2.8 %slice_bitcast_fusion.2 = (f32[2,256,256]{2,1,0:T(8,128)S(1)}, f32[2,256,256]{2,1,0:T(8,128)S(1)}, f32[2,256,256]{2,1,0:T(8,128)}, f32[2,256,256]{2,1,0:T(8,128)}) fusion(f32[2,2,512,512]{3,2,1,0:T(8,128)} %obj.3), kind=kLoop, calls=%fused_computation.6 | loop fusion | bytes 4194304 | tf_op jit(solution)/shard_map/squeeze | solution.py:565
  3.5 2.1 collective-permute-start.1
  6.8 3.1 %collective-permute-start = (f32[2,512,256]{2,1,0:T(8,128)S(1)}, f32[2,512,256]{2,1,0:T(8,128)S(1)}, u32[]{:S(2)}, u32[]{:S(2)}) collective-permute-start(f32[2,512,256]{2,1,0:T(8,128)S(1)} %get-tuple-element.76), channel_id=1, source_target_pairs={{8,0},{9,1},{10,2},{11,3},{12,4},{13,5},{14,6},{15,7},{16,8},{17,9... | collective-permute-start | bytes 3145736 | tf_op jit(solution)/shard_map/ppermute | solution.py:558
  14.9 4.3 %collective-permute-done.1.low_a = f32[2,256,256]{2,1,0:T(8,128)S(1)} collective-permute-done((f32[2,256,256]{2,1,0:T(8,128)S(1)}, f32[2,256,256]{2,1,0:T(8,128)S(1)}, u32[]{:S(2)}, u32[]{:S(2)}) %collective-permute-start.1) | collective-permute-done | bytes 524320 | tf_op jit(solution)/shard_map/ppermute | solution.py:558
  19.2 4.6 %collective-permute-start.4 = (f32[2,256,256]{2,1,0:T(8,128)S(1)}, f32[2,256,256]{2,1,0:T(8,128)S(1)}, u32[]{:S(2)}, u32[]{:S(2)}) collective-permute-start(f32[2,256,256]{2,1,0:T(8,128)S(1)} %collective-permute-done.1.low_a), channel_id=1, source_target_pairs={{8,0},{9,1},{10,2},{11,3},{12,4},{13,5},{14,6},{15,7},{24,16},{25,... | collective-permute-start | bytes 1572872 | tf_op jit(solution)/shard_map/ppermute | solution.py:558
  23.9 3.8 %collective-permute-start.6 = (f32[2,2,16,256]{3,2,1,0:T(8,128)S(1)}, f32[2,2,16,256]{3,2,1,0:T(8,128)S(1)}, u32[]{:S(2)}, u32[]{:S(2)}) collective-permute-start(f32[2,2,16,256]{3,2,1,0:T(8,128)S(1)} %copy-done.35), channel_id=1, source_target_pairs={{0,64},{1,65},{2,66},{3,67},{4,68},{5,69},{6,70},{7,71},{8,72},{9,... | collective-permute-start | bytes 196616 | tf_op jit(solution)/shard_map/ppermute | solution.py:558
  29.5 3.5 %collective-permute-start.7 = (f32[2,2,16,256]{3,2,1,0:T(8,128)S(1)}, f32[2,2,16,256]{3,2,1,0:T(8,128)S(1)}, u32[]{:S(2)}, u32[]{:S(2)}) collective-permute-start(f32[2,2,16,256]{3,2,1,0:T(8,128)S(1)} %copy-done.35), channel_id=1, source_target_pairs={{0,96},{1,97},{2,98},{3,99},{4,100},{5,101},{6,102},{7,103},{8,104... | collective-permute-start | bytes 196616 | tf_op jit(solution)/shard_map/ppermute | solution.py:558
  33.0 2.1 collective-permute-done.7
  37.0 3.7 %order_amplitudes.1.amp = f32[6,256,256]{2,1,0:T(8,128)S(1)} custom-call(f32[6,256,256]{2,1,0:T(8,128)S(1)} %bitcast.63, bf16[256,768]{1,0:T(8,128)(2,1)S(1)} %copy-done.29, bf16[768,256]{1,0:T(8,128)(2,1)S(1)} %copy-done.30), custom_call_target="tpu_custom_call" | custom-call | flops 1200000000 | bytes 4000000 | tf_op jit(solution)/shard_map/order_amplitudes/pallas_call | solution.py:427
  41.8 2.1 collective-permute-done.8.across
  45.6 11.6 %collective-permute-start.12 = (f32[2,256,256]{2,1,0:T(8,128)}, f32[2,256,256]{2,1,0:T(8,128)}, u32[]{:S(2)}, u32[]{:S(2)}) collective-permute-start(f32[2,256,256]{2,1,0:T(8,128)} %get-tuple-element.46), channel_id=1, source_target_pairs={{1,0},{2,1},{3,2},{4,3},{5,4},{6,5},{7,6},{9,8},{10,9},{11,10},{12... | collective-permute-start | bytes 1572872 | tf_op jit(solution)/shard_map/ppermute | solution.py:558
  66.0 3.2 %collective-permute-done.12.low_a = f32[2,256,256]{2,1,0:T(8,128)} collective-permute-done((f32[2,256,256]{2,1,0:T(8,128)}, f32[2,256,256]{2,1,0:T(8,128)}, u32[]{:S(2)}, u32[]{:S(2)}) %collective-permute-start.12) | collective-permute-done | bytes 524320 | tf_op jit(solution)/shard_map/ppermute | solution.py:558
  69.2 5.1 %collective-permute-start.15 = (f32[2,256,256]{2,1,0:T(8,128)}, f32[2,256,256]{2,1,0:T(8,128)S(1)}, u32[]{:S(2)}, u32[]{:S(2)}) collective-permute-start(f32[2,256,256]{2,1,0:T(8,128)} %collective-permute-done.12.low_a), channel_id=1, source_target_pairs={{8,0},{9,1},{10,2},{11,3},{12,4},{13,5},{14,6},{15,7},{24,16},{25,... | collective-permute-start | bytes 1572872 | tf_op jit(solution)/shard_map/ppermute | solution.py:558
  79.0 10.5 %propagate_out.1 = (f32[6,2,2,256,256]{4,3,2,1,0:T(8,128)}, f32[6,2,256,256]{3,2,1,0:T(8,128)}, f32[2,2,4,2,2,16,256]{6,5,4,3,2,1,0:T(8,128)S(1)}) custom-call(s32[16]{0:T(128)S(1)} %concatenate.3.scalars, f32[2,2,512,512]{3,2,1,0:T(8,128)} %obj.3, f32[2,512,256]{2,1,0:T(8,128)S(1)} %collective-permute-done.right, ...), custom_call_target="tpu_custom_call" | custom-call | flops 60000002048 | bytes 20000000 | tf_op jit(solution)/shard_map/propagate_out/pallas_call | solution.py:445
  91.4 14.0 %far_field.1 = (f32[6,2,2,256,256]{4,3,2,1,0:T(8,128)}, f32[2,512,512]{2,1,0:T(8,128)}, f32[2,512,256]{2,1,0:T(8,128)}, f32[2,256,256]{2,1,0:T(8,128)S(1)}, f32[...) custom-call(s32[16]{0:T(128)S(1)} %concatenate.3.scalars, f32[2,2,512,512]{3,2,1,0:T(8,128)} %obj.3, ...), custom_call_target="tpu_custom_call" | custom-call | flops 60000002048 | bytes 20000000 | tf_op jit(solution)/shard_map/far_field/pallas_call | solution.py:467
  106.7 11.0 %collective-permute-start.20 = (f32[2,256,256]{2,1,0:T(8,128)}, f32[2,256,256]{2,1,0:T(8,128)S(1)}, u32[]{:S(2)}, u32[]{:S(2)}) collective-permute-start(f32[2,256,256]{2,1,0:T(8,128)} %get-tuple-element.60), channel_id=1, source_target_pairs={{8,17},{9,18},{10,19},{11,20},{12,21},{13,22},{14,23},{24,33},{25,... | collective-permute-start | bytes 1572872 | tf_op jit(solution)/shard_map/ppermute | solution.py:558
  119.6 3.4 %collective-permute-start.19 = (f32[2,256,256]{2,1,0:T(8,128)}, f32[2,256,256]{2,1,0:T(8,128)S(1)}, u32[]{:S(2)}, u32[]{:S(2)}) collective-permute-start(f32[2,256,256]{2,1,0:T(8,128)} %get-tuple-element.61), channel_id=1, source_target_pairs={{0,1},{1,2},{2,3},{3,4},{4,5},{5,6},{6,7},{8,9},{9,10},{10,11},{11... | collective-permute-start | bytes 1572872 | tf_op jit(solution)/shard_map/ppermute | solution.py:558
  123.2 16.2 %collective-permute-start.18 = (f32[2,256,256]{2,1,0:T(8,128)S(1)}, f32[2,256,256]{2,1,0:T(8,128)S(1)}, u32[]{:S(2)}, u32[]{:S(2)}) collective-permute-start(f32[2,256,256]{2,1,0:T(8,128)S(1)} %add.58), channel_id=1, source_target_pairs={{0,1},{1,2},{2,3},{3,4},{4,5},{5,6},{6,7},{8,9},{9,10},{10,11},{11... | collective-permute-start | bytes 1572872 | tf_op jit(solution)/shard_map/ppermute | solution.py:558
  140.6 9.6 %propagate_home.1 = (f32[2,2,256,256]{3,2,1,0:T(8,128)S(1)}, f32[2,512,512]{2,1,0:T(8,128)}, f32[2,512,256]{2,1,0:T(8,128)S(1)}, f32[2,256,256]{2,1,0:T(8,128)S(...) custom-call(s32[16]{0:T(128)S(1)} %concatenate.3.scalars, f32[6,2,256,256]{3,2,1,0:T(8,128)} %get-tuple-element.44.win, ...), custom_call_target="tpu_custom_call" | custom-call | flops 60000002048 | bytes 20000000 | tf_op jit(solution)/shard_map/propagate_home/pallas_call | solution.py:497
  157.9 2.2 collective-permute-done.26
  161.4 12.8 %collective-permute-start.27 = (f32[2,2,2,16,256]{4,3,2,1,0:T(8,128)S(1)}, f32[2,2,2,16,256]{4,3,2,1,0:T(8,128)S(1)}, u32[]{:S(2)}, u32[]{:S(2)}) collective-permute-start(f32[2,2,2,16,256]{4,3,2,1,0:T(8,128)S(1)} %bitcast.65), channel_id=1, source_target_pairs={{0,32},{1,33},{2,34},{3,35},{4,36},{5,37},{6,38},{7,39},{8,40},{9,... | collective-permute-start | bytes 393224 | tf_op jit(solution)/shard_map/ppermute | solution.py:558
  178.1 3.8 %collective-permute-start.21 = (f32[2,512,256]{2,1,0:T(8,128)}, f32[2,512,256]{2,1,0:T(8,128)S(1)}, u32[]{:S(2)}, u32[]{:S(2)}) collective-permute-start(f32[2,512,256]{2,1,0:T(8,128)} %copy-done.12), channel_id=1, source_target_pairs={{0,8},{1,9},{2,10},{3,11},{4,12},{5,13},{6,14},{7,15},{8,16},{9,17... | collective-permute-start | bytes 3145736 | tf_op jit(solution)/shard_map/ppermute | solution.py:558
  182.3 2.7 %collective-permute-done.29 = f32[2,2,2,16,256]{4,3,2,1,0:T(8,128)S(1)} collective-permute-done((f32[2,2,2,16,256]{4,3,2,1,0:T(8,128)S(1)}, f32[2,2,2,16,256]{4,3,2,1,0:T(8,128)S(1)}, u32[]{:S(2)}, u32[]{:S(2)}) %collective-permute-start.29) | collective-permute-done | bytes 131104 | tf_op jit(solution)/shard_map/ppermute | solution.py:558
  185.4 2.4 collective-permute-start.32
  187.8 7.6 %collective-permute-start.25 = (f32[2,256,256]{2,1,0:T(8,128)}, f32[2,256,256]{2,1,0:T(8,128)S(1)}, u32[]{:S(2)}, u32[]{:S(2)}) collective-permute-start(f32[2,256,256]{2,1,0:T(8,128)} %copy-done.13), channel_id=1, source_target_pairs={{8,17},{9,18},{10,19},{11,20},{12,21},{13,22},{14,23},{24,33},{25,... | collective-permute-start | bytes 1572872 | tf_op jit(solution)/shard_map/ppermute | solution.py:558
  197.3 7.2 %collective-permute-start.24 = (f32[2,256,256]{2,1,0:T(8,128)}, f32[2,256,256]{2,1,0:T(8,128)S(1)}, u32[]{:S(2)}, u32[]{:S(2)}) collective-permute-start(f32[2,256,256]{2,1,0:T(8,128)} %copy-done.14), channel_id=1, source_target_pairs={{0,1},{1,2},{2,3},{3,4},{4,5},{5,6},{6,7},{8,9},{9,10},{10,11},{11... | collective-permute-start | bytes 1572872 | tf_op jit(solution)/shard_map/ppermute | solution.py:558
  204.5 1.9 collective-permute-start.23
  206.5 3.4 %collective-permute-start.33 = (f32[2,2,16,256]{3,2,1,0:T(8,128)S(1)}, f32[2,2,16,256]{3,2,1,0:T(8,128)S(1)}, u32[]{:S(2)}, u32[]{:S(2)}) collective-permute-start(f32[2,2,16,256]{3,2,1,0:T(8,128)S(1)} %add_add_fusion.1), channel_id=1, source_target_pairs={{0,2},{1,3},{2,0},{3,1},{4,6},{5,7},{6,4},{7,5},{8,10},{9,11},{10,... | collective-permute-start | bytes 196616 | tf_op jit(solution)/shard_map/ppermute | solution.py:558
  209.9 16.9 %collective-permute-done.33 = f32[2,2,16,256]{3,2,1,0:T(8,128)S(1)} collective-permute-done((f32[2,2,16,256]{3,2,1,0:T(8,128)S(1)}, f32[2,2,16,256]{3,2,1,0:T(8,128)S(1)}, u32[]{:S(2)}, u32[]{:S(2)}) %collective-permute-start.33) | collective-permute-done | bytes 65568 | tf_op jit(solution)/shard_map/ppermute | solution.py:558
  226.8 4.6 %collective-permute-done.34 = f32[2,2,16,256]{3,2,1,0:T(8,128)S(1)} collective-permute-done((f32[2,2,16,256]{3,2,1,0:T(8,128)S(1)}, f32[2,2,16,256]{3,2,1,0:T(8,128)S(1)}, u32[]{:S(2)}, u32[]{:S(2)}) %collective-permute-start.34) | collective-permute-done | bytes 65568 | tf_op jit(solution)/shard_map/ppermute | solution.py:558
  237.1 2.2 join_gradients.2.rest_0_
  240.0 2.2 join_gradients.3
  (140 shorter events, 53.7 us)
Async XLA Ops:
  3.5 15.7 %collective-permute-start.1 = (f32[2,256,256]{2,1,0:T(8,128)S(1)}, f32[2,256,256]{2,1,0:T(8,128)S(1)}, u32[]{:S(2)}, u32[]{:S(2)}) collective-permute-start(f32[2,256,256]{2,1,0:T(8,128)S(1)} %get-tuple-element.73), channel_id=1, source_target_pairs={{1,0},{2,1},{3,2},{4,3},{5,4},{6,5},{7,6},{9,8},{10,9},{11,10},{12... | collective-permute-start | bytes 1572872 | tf_op jit(solution)/shard_map/ppermute | solution.py:558
  6.8 38.7 %collective-permute-start = (f32[2,512,256]{2,1,0:T(8,128)S(1)}, f32[2,512,256]{2,1,0:T(8,128)S(1)}, u32[]{:S(2)}, u32[]{:S(2)}) collective-permute-start(f32[2,512,256]{2,1,0:T(8,128)S(1)} %get-tuple-element.76), channel_id=1, source_target_pairs={{8,0},{9,1},{10,2},{11,3},{12,4},{13,5},{14,6},{15,7},{16,8},{17,9... | collective-permute-start | bytes 3145736 | tf_op jit(solution)/shard_map/ppermute | solution.py:558
  9.9 13.9 %collective-permute-start.5 = (f32[2,2,16,256]{3,2,1,0:T(8,128)S(1)}, f32[2,2,16,256]{3,2,1,0:T(8,128)S(1)}, u32[]{:S(2)}, u32[]{:S(2)}) collective-permute-start(f32[2,2,16,256]{3,2,1,0:T(8,128)S(1)} %copy-done.35), channel_id=1, source_target_pairs={{0,32},{1,33},{2,34},{3,35},{4,36},{5,37},{6,38},{7,39},{8,40},{9,... | collective-permute-start | bytes 196616 | tf_op jit(solution)/shard_map/ppermute | solution.py:558
  11.7 32.3 %collective-permute-start.3 = (f32[2,256,256]{2,1,0:T(8,128)S(1)}, f32[2,256,256]{2,1,0:T(8,128)S(1)}, u32[]{:S(2)}, u32[]{:S(2)}) collective-permute-start(f32[2,256,256]{2,1,0:T(8,128)S(1)} %get-tuple-element.73), channel_id=1, source_target_pairs={{17,8},{18,9},{19,10},{20,11},{21,12},{22,13},{23,14},{33,24},{34,... | collective-permute-start | bytes 1572872 | tf_op jit(solution)/shard_map/ppermute | solution.py:558
  13.0 31.0 %collective-permute-start.2 = (f32[2,256,256]{2,1,0:T(8,128)S(1)}, f32[2,256,256]{2,1,0:T(8,128)S(1)}, u32[]{:S(2)}, u32[]{:S(2)}) collective-permute-start(f32[2,256,256]{2,1,0:T(8,128)S(1)} %get-tuple-element.72), channel_id=1, source_target_pairs={{1,0},{2,1},{3,2},{4,3},{5,4},{6,5},{7,6},{9,8},{10,9},{11,10},{12... | collective-permute-start | bytes 1572872 | tf_op jit(solution)/shard_map/ppermute | solution.py:558
  19.2 25.6 %collective-permute-start.4 = (f32[2,256,256]{2,1,0:T(8,128)S(1)}, f32[2,256,256]{2,1,0:T(8,128)S(1)}, u32[]{:S(2)}, u32[]{:S(2)}) collective-permute-start(f32[2,256,256]{2,1,0:T(8,128)S(1)} %collective-permute-done.1.low_a), channel_id=1, source_target_pairs={{8,0},{9,1},{10,2},{11,3},{12,4},{13,5},{14,6},{15,7},{24,16},{25,... | collective-permute-start | bytes 1572872 | tf_op jit(solution)/shard_map/ppermute | solution.py:558
  35.2 8.8 %collective-permute-start.8 = (f32[4,2,2,16,256]{4,3,2,1,0:T(8,128)S(1)}, f32[4,2,2,16,256]{4,3,2,1,0:T(8,128)S(1)}, u32[]{:S(2)}, u32[]{:S(2)}) collective-permute-start(f32[4,2,2,16,256]{4,3,2,1,0:T(8,128)S(1)} %pad_maximum_fusion.mine), channel_id=1, source_target_pairs={{0,17},{1,16},{2,19},{3,18},{4,21},{5,20},{6,23},{7,22},{8,25},{9,... | collective-permute-start | bytes 786440 | tf_op jit(solution)/shard_map/ppermute | solution.py:558
  45.6 23.6 %collective-permute-start.12 = (f32[2,256,256]{2,1,0:T(8,128)}, f32[2,256,256]{2,1,0:T(8,128)}, u32[]{:S(2)}, u32[]{:S(2)}) collective-permute-start(f32[2,256,256]{2,1,0:T(8,128)} %get-tuple-element.46), channel_id=1, source_target_pairs={{1,0},{2,1},{3,2},{4,3},{5,4},{6,5},{7,6},{9,8},{10,9},{11,10},{12... | collective-permute-start | bytes 1572872 | tf_op jit(solution)/shard_map/ppermute | solution.py:558
  57.2 6.1 %collective-permute-start.10 = (f32[4,2,2,16,256]{4,3,2,1,0:T(8,128)S(1)}, f32[4,2,2,16,256]{4,3,2,1,0:T(8,128)S(1)}, u32[]{:S(2)}, u32[]{:S(2)}) collective-permute-start(f32[4,2,2,16,256]{4,3,2,1,0:T(8,128)S(1)} %collective-permute-done.8.across), channel_id=1, source_target_pairs={{0,8},{1,9},{2,10},{3,11},{4,12},{5,13},{6,14},{7,15},{8,0},{9,1},... | collective-permute-start | bytes 786440 | tf_op jit(solution)/shard_map/ppermute | solution.py:558
  59.1 15.2 %collective-permute-start.9 = (f32[4,2,2,16,256]{4,3,2,1,0:T(8,128)S(1)}, f32[4,2,2,16,256]{4,3,2,1,0:T(8,128)S(1)}, u32[]{:S(2)}, u32[]{:S(2)}) collective-permute-start(f32[4,2,2,16,256]{4,3,2,1,0:T(8,128)S(1)} %pad_maximum_fusion.mine), channel_id=1, source_target_pairs={{0,8},{1,9},{2,10},{3,11},{4,12},{5,13},{6,14},{7,15},{8,0},{9,1},... | collective-permute-start | bytes 786440 | tf_op jit(solution)/shard_map/ppermute | solution.py:558
  60.1 29.4 %collective-permute-start.14 = (f32[2,256,256]{2,1,0:T(8,128)}, f32[2,256,256]{2,1,0:T(8,128)S(1)}, u32[]{:S(2)}, u32[]{:S(2)}) collective-permute-start(f32[2,256,256]{2,1,0:T(8,128)} %get-tuple-element.46), channel_id=1, source_target_pairs={{17,8},{18,9},{19,10},{20,11},{21,12},{22,13},{23,14},{33,24},{34,... | collective-permute-start | bytes 1572872 | tf_op jit(solution)/shard_map/ppermute | solution.py:558
  61.4 29.0 %collective-permute-start.11 = (f32[2,512,256]{2,1,0:T(8,128)}, f32[2,512,256]{2,1,0:T(8,128)S(1)}, u32[]{:S(2)}, u32[]{:S(2)}) collective-permute-start(f32[2,512,256]{2,1,0:T(8,128)} %get-tuple-element.45), channel_id=1, source_target_pairs={{8,0},{9,1},{10,2},{11,3},{12,4},{13,5},{14,6},{15,7},{16,8},{17,9... | collective-permute-start | bytes 3145736 | tf_op jit(solution)/shard_map/ppermute | solution.py:558
  64.1 25.5 %collective-permute-start.13 = (f32[2,256,256]{2,1,0:T(8,128)}, f32[2,256,256]{2,1,0:T(8,128)S(1)}, u32[]{:S(2)}, u32[]{:S(2)}) collective-permute-start(f32[2,256,256]{2,1,0:T(8,128)} %get-tuple-element.47), channel_id=1, source_target_pairs={{1,0},{2,1},{3,2},{4,3},{5,4},{6,5},{7,6},{9,8},{10,9},{11,10},{12... | collective-permute-start | bytes 1572872 | tf_op jit(solution)/shard_map/ppermute | solution.py:558
  69.2 20.3 %collective-permute-start.15 = (f32[2,256,256]{2,1,0:T(8,128)}, f32[2,256,256]{2,1,0:T(8,128)S(1)}, u32[]{:S(2)}, u32[]{:S(2)}) collective-permute-start(f32[2,256,256]{2,1,0:T(8,128)} %collective-permute-done.12.low_a), channel_id=1, source_target_pairs={{8,0},{9,1},{10,2},{11,3},{12,4},{13,5},{14,6},{15,7},{24,16},{25,... | collective-permute-start | bytes 1572872 | tf_op jit(solution)/shard_map/ppermute | solution.py:558
  105.4 17.7 %collective-permute-start.17 = (f32[2,256,256]{2,1,0:T(8,128)}, f32[2,256,256]{2,1,0:T(8,128)S(1)}, u32[]{:S(2)}, u32[]{:S(2)}) collective-permute-start(f32[2,256,256]{2,1,0:T(8,128)} %get-tuple-element.60), channel_id=1, source_target_pairs={{0,8},{1,9},{2,10},{3,11},{4,12},{5,13},{6,14},{7,15},{16,24},{17,... | collective-permute-start | bytes 1572872 | tf_op jit(solution)/shard_map/ppermute | solution.py:558
  106.7 47.7 %collective-permute-start.20 = (f32[2,256,256]{2,1,0:T(8,128)}, f32[2,256,256]{2,1,0:T(8,128)S(1)}, u32[]{:S(2)}, u32[]{:S(2)}) collective-permute-start(f32[2,256,256]{2,1,0:T(8,128)} %get-tuple-element.60), channel_id=1, source_target_pairs={{8,17},{9,18},{10,19},{11,20},{12,21},{13,22},{14,23},{24,33},{25,... | collective-permute-start | bytes 1572872 | tf_op jit(solution)/shard_map/ppermute | solution.py:558
  117.7 37.5 %collective-permute-start.16 = (f32[2,512,256]{2,1,0:T(8,128)}, f32[2,512,256]{2,1,0:T(8,128)S(1)}, u32[]{:S(2)}, u32[]{:S(2)}) collective-permute-start(f32[2,512,256]{2,1,0:T(8,128)} %get-tuple-element.58), channel_id=1, source_target_pairs={{0,8},{1,9},{2,10},{3,11},{4,12},{5,13},{6,14},{7,15},{8,16},{9,17... | collective-permute-start | bytes 3145736 | tf_op jit(solution)/shard_map/ppermute | solution.py:558
  119.6 34.0 %collective-permute-start.19 = (f32[2,256,256]{2,1,0:T(8,128)}, f32[2,256,256]{2,1,0:T(8,128)S(1)}, u32[]{:S(2)}, u32[]{:S(2)}) collective-permute-start(f32[2,256,256]{2,1,0:T(8,128)} %get-tuple-element.61), channel_id=1, source_target_pairs={{0,1},{1,2},{2,3},{3,4},{4,5},{5,6},{6,7},{8,9},{9,10},{10,11},{11... | collective-permute-start | bytes 1572872 | tf_op jit(solution)/shard_map/ppermute | solution.py:558
  123.2 33.1 %collective-permute-start.18 = (f32[2,256,256]{2,1,0:T(8,128)S(1)}, f32[2,256,256]{2,1,0:T(8,128)S(1)}, u32[]{:S(2)}, u32[]{:S(2)}) collective-permute-start(f32[2,256,256]{2,1,0:T(8,128)S(1)} %add.58), channel_id=1, source_target_pairs={{0,1},{1,2},{2,3},{3,4},{4,5},{5,6},{6,7},{8,9},{9,10},{10,11},{11... | collective-permute-start | bytes 1572872 | tf_op jit(solution)/shard_map/ppermute | solution.py:558
  161.4 20.5 %collective-permute-start.27 = (f32[2,2,2,16,256]{4,3,2,1,0:T(8,128)S(1)}, f32[2,2,2,16,256]{4,3,2,1,0:T(8,128)S(1)}, u32[]{:S(2)}, u32[]{:S(2)}) collective-permute-start(f32[2,2,2,16,256]{4,3,2,1,0:T(8,128)S(1)} %bitcast.65), channel_id=1, source_target_pairs={{0,32},{1,33},{2,34},{3,35},{4,36},{5,37},{6,38},{7,39},{8,40},{9,... | collective-permute-start | bytes 393224 | tf_op jit(solution)/shard_map/ppermute | solution.py:558
  174.3 8.0 %collective-permute-start.28 = (f32[2,2,2,16,256]{4,3,2,1,0:T(8,128)S(1)}, f32[2,2,2,16,256]{4,3,2,1,0:T(8,128)S(1)}, u32[]{:S(2)}, u32[]{:S(2)}) collective-permute-start(f32[2,2,2,16,256]{4,3,2,1,0:T(8,128)S(1)} %bitcast.66), channel_id=1, source_target_pairs={{0,64},{1,65},{2,66},{3,67},{4,68},{5,69},{6,70},{7,71},{8,72},{9,... | collective-permute-start | bytes 393224 | tf_op jit(solution)/shard_map/ppermute | solution.py:558
  176.1 8.9 %collective-permute-start.29 = (f32[2,2,2,16,256]{4,3,2,1,0:T(8,128)S(1)}, f32[2,2,2,16,256]{4,3,2,1,0:T(8,128)S(1)}, u32[]{:S(2)}, u32[]{:S(2)}) collective-permute-start(f32[2,2,2,16,256]{4,3,2,1,0:T(8,128)S(1)} %bitcast.67), channel_id=1, source_target_pairs={{0,96},{1,97},{2,98},{3,99},{4,100},{5,101},{6,102},{7,103},{8,104... | collective-permute-start | bytes 393224 | tf_op jit(solution)/shard_map/ppermute | solution.py:558
  176.9 10.9 %collective-permute-start.22 = (f32[2,256,256]{2,1,0:T(8,128)}, f32[2,256,256]{2,1,0:T(8,128)S(1)}, u32[]{:S(2)}, u32[]{:S(2)}) collective-permute-start(f32[2,256,256]{2,1,0:T(8,128)} %copy-done.13), channel_id=1, source_target_pairs={{0,8},{1,9},{2,10},{3,11},{4,12},{5,13},{6,14},{7,15},{16,24},{17,... | collective-permute-start | bytes 1572872 | tf_op jit(solution)/shard_map/ppermute | solution.py:558
  178.1 61.8 %collective-permute-start.21 = (f32[2,512,256]{2,1,0:T(8,128)}, f32[2,512,256]{2,1,0:T(8,128)S(1)}, u32[]{:S(2)}, u32[]{:S(2)}) collective-permute-start(f32[2,512,256]{2,1,0:T(8,128)} %copy-done.12), channel_id=1, source_target_pairs={{0,8},{1,9},{2,10},{3,11},{4,12},{5,13},{6,14},{7,15},{8,16},{9,17... | collective-permute-start | bytes 3145736 | tf_op jit(solution)/shard_map/ppermute | solution.py:558
  185.1 12.2 %collective-permute-start.30 = (f32[2,2,16,256]{3,2,1,0:T(8,128)S(1)}, f32[2,2,16,256]{3,2,1,0:T(8,128)S(1)}, u32[]{:S(2)}, u32[]{:S(2)}) collective-permute-start(f32[2,2,16,256]{3,2,1,0:T(8,128)S(1)} %get-tuple-element.82), channel_id=1, source_target_pairs={{0,1},{1,0},{2,3},{3,2},{4,5},{5,4},{6,7},{7,6},{8,9},{9,8},{10,11... | collective-permute-start | bytes 196616 | tf_op jit(solution)/shard_map/ppermute | solution.py:558
  185.1 19.3 %collective-permute-start.31 = (f32[2,2,16,256]{3,2,1,0:T(8,128)S(1)}, f32[2,2,16,256]{3,2,1,0:T(8,128)S(1)}, u32[]{:S(2)}, u32[]{:S(2)}) collective-permute-start(f32[2,2,16,256]{3,2,1,0:T(8,128)S(1)} %get-tuple-element.83), channel_id=1, source_target_pairs={{0,16},{1,17},{2,18},{3,19},{4,20},{5,21},{6,22},{7,23},{8,24},{9,... | collective-permute-start | bytes 196616 | tf_op jit(solution)/shard_map/ppermute | solution.py:558
  185.4 21.1 %collective-permute-start.32 = (f32[2,2,16,256]{3,2,1,0:T(8,128)S(1)}, f32[2,2,16,256]{3,2,1,0:T(8,128)S(1)}, u32[]{:S(2)}, u32[]{:S(2)}) collective-permute-start(f32[2,2,16,256]{3,2,1,0:T(8,128)S(1)} %get-tuple-element.83), channel_id=1, source_target_pairs={{0,17},{1,16},{2,19},{3,18},{4,21},{5,20},{6,23},{7,22},{8,25},{9,... | collective-permute-start | bytes 196616 | tf_op jit(solution)/shard_map/ppermute | solution.py:558
  187.8 52.2 %collective-permute-start.25 = (f32[2,256,256]{2,1,0:T(8,128)}, f32[2,256,256]{2,1,0:T(8,128)S(1)}, u32[]{:S(2)}, u32[]{:S(2)}) collective-permute-start(f32[2,256,256]{2,1,0:T(8,128)} %copy-done.13), channel_id=1, source_target_pairs={{8,17},{9,18},{10,19},{11,20},{12,21},{13,22},{14,23},{24,33},{25,... | collective-permute-start | bytes 1572872 | tf_op jit(solution)/shard_map/ppermute | solution.py:558
  197.3 42.7 %collective-permute-start.24 = (f32[2,256,256]{2,1,0:T(8,128)}, f32[2,256,256]{2,1,0:T(8,128)S(1)}, u32[]{:S(2)}, u32[]{:S(2)}) collective-permute-start(f32[2,256,256]{2,1,0:T(8,128)} %copy-done.14), channel_id=1, source_target_pairs={{0,1},{1,2},{2,3},{3,4},{4,5},{5,6},{6,7},{8,9},{9,10},{10,11},{11... | collective-permute-start | bytes 1572872 | tf_op jit(solution)/shard_map/ppermute | solution.py:558
  204.5 35.5 %collective-permute-start.23 = (f32[2,256,256]{2,1,0:T(8,128)S(1)}, f32[2,256,256]{2,1,0:T(8,128)S(1)}, u32[]{:S(2)}, u32[]{:S(2)}) collective-permute-start(f32[2,256,256]{2,1,0:T(8,128)S(1)} %add.59), channel_id=1, source_target_pairs={{0,1},{1,2},{2,3},{3,4},{4,5},{5,6},{6,7},{8,9},{9,10},{10,11},{11... | collective-permute-start | bytes 1572872 | tf_op jit(solution)/shard_map/ppermute | solution.py:558
  206.5 20.3 %collective-permute-start.33 = (f32[2,2,16,256]{3,2,1,0:T(8,128)S(1)}, f32[2,2,16,256]{3,2,1,0:T(8,128)S(1)}, u32[]{:S(2)}, u32[]{:S(2)}) collective-permute-start(f32[2,2,16,256]{3,2,1,0:T(8,128)S(1)} %add_add_fusion.1), channel_id=1, source_target_pairs={{0,2},{1,3},{2,0},{3,1},{4,6},{5,7},{6,4},{7,5},{8,10},{9,11},{10,... | collective-permute-start | bytes 196616 | tf_op jit(solution)/shard_map/ppermute | solution.py:558
  231.4 7.9 %collective-permute-start.35 = (f32[2,2,16,256]{3,2,1,0:T(8,128)S(1)}, f32[2,2,16,256]{3,2,1,0:T(8,128)S(1)}, u32[]{:S(2)}, u32[]{:S(2)}) collective-permute-start(f32[2,2,16,256]{3,2,1,0:T(8,128)S(1)} %add_add_fusion.1), channel_id=1, source_target_pairs={{0,6},{1,7},{2,4},{3,5},{4,2},{5,3},{6,0},{7,1},{8,14},{9,15},{10,... | collective-permute-start | bytes 196616 | tf_op jit(solution)/shard_map/ppermute | solution.py:558
  (42 other events, 390.6 us)

commit v3 on v2

--- a/solution.py
+++ b/solution.py
@@ -50,14 +50,28 @@
     def from_right(mat):
         return from_left(mat).T
 
+    near = np.arange(PROBE) < HALF
+    edge = (np.arange(PROBE) + HALF // 2) // HALF == 1
+    cross = np.where(near[:, None] != near[None, :], prop, 0)
+    assert not cross[~edge].any() and not cross[:, ~edge].any()
+
+    def pair(table, embed, mat):
+        other = np.zeros((HALF, HALF), complex)
+        for a in range(HALF):
+            for b in range(HALF):
+                to, of = (a + HALF, b) if a < HALF // 2 else (a, b + HALF)
+                if (b >= HALF // 2) == (a < HALF // 2):
+                    other[a, b] = mat[to, of]
+        return np.stack([table(embed(mat[:HALF, :HALF])), table(embed(other))])
+
     order = np.concatenate([np.arange(0, PROBE, 2), np.arange(1, PROBE, 2)])
     perm = np.zeros((PROBE, PROBE))
     perm[np.arange(PROBE), order] = 1
     return {
-        "prop_l": left_table(from_left(prop)),
-        "prop_r": right_table(from_right(prop)),
-        "back_l": left_table(from_left(prop.conj())),
-        "back_r": right_table(from_right(prop.conj())),
+        "prop_l": pair(left_table, from_left, prop),
+        "prop_r": pair(right_table, from_right, prop),
+        "back_l": pair(left_table, from_left, prop.conj()),
+        "back_r": pair(right_table, from_right, prop.conj()),
         "four_l": left_table(from_left(four)),
         "four_r": right_table(from_right(four)),
         "ruof_l": left_table(from_left(four.conj())),
@@ -101,18 +115,36 @@
     return hi, mid, (rest - mid.astype(F32)).astype(BF16)
 
 
-def both_sides(re, im, table_l, table_r):
+def prop_left(re, im, table):
+    h, q = HALF, HALF // 2
     x = jnp.concatenate(
-        [jnp.concatenate(re, axis=1), jnp.concatenate(im, axis=1)], axis=0
+        [jnp.concatenate([re[:h], im[:h]], axis=0), jnp.concatenate([re[h:], im[h:]], axis=0)], axis=1
     )
-    y = lmul(table_l, x)
+    y = lmul(table[0], x)
+    v = lmul(table[1], jnp.concatenate([re[h : h + q], re[q:h], im[h : h + q], im[q:h]], axis=0))
     n = PROBE
+    re = [y[:q, :n], y[q:h, :n] + v[q:h], y[:q, n:] + v[:q], y[q:h, n:]]
+    im = [y[h : h + q, :n], y[h + q :, :n] + v[h + q :], y[h : h + q, n:] + v[h : h + q], y[h + q :, n:]]
+    return jnp.concatenate(re, axis=0), jnp.concatenate(im, axis=0)
+
+
+def prop_right(re, im, table):
+    h, n = HALF, PROBE
+    low = lax.broadcasted_iota(jnp.int32, (1, h), 1) < h // 2
     x = jnp.concatenate(
-        [jnp.concatenate([y[:n, m * n : (m + 1) * n], y[n:, m * n : (m + 1) * n]], axis=1) for m in (0, 1)],
-        axis=0,
+        [jnp.concatenate([re[:, :h], im[:, :h]], axis=1), jnp.concatenate([re[:, h:], im[:, h:]], axis=1)], axis=0
     )
-    y = rmul(x, table_r)
-    return [y[m * n : (m + 1) * n, :n] for m in (0, 1)], [y[m * n : (m + 1) * n, n:] for m in (0, 1)]
+    y = rmul(x, table[0])
+    u = [jnp.where(low, z[:, h:], z[:, :h]) for z in (re, im)]
+    v = rmul(jnp.concatenate(u, axis=1), table[1])
+    out = []
+    for at in (slice(0, h), slice(h, n)):
+        out.append(
+            jnp.concatenate(
+                [y[:n, at] + jnp.where(low, 0.0, v[:, at]), y[n:, at] + jnp.where(low, v[:, at], 0.0)], axis=1
+            )
+        )
+    return out
 
 
 def place_of(scalars, slot):
@@ -140,7 +172,7 @@
     field[at] = field[at] + x
 
 
-def fetch_field(layer, core, obj, right, low_a, low_b, diag, side, field, sems):
+def fetch_field(layer, core, obj, right, low_a, low_b, diag, side, field, sems, meanwhile=None):
     n, t = PROBE, TILE
     copies = [
         pltpu.make_async_copy(obj.at[layer], field.at[:, :t, :t], sems.at[0]),
@@ -150,6 +182,8 @@
     ]
     for copy in copies:
         copy.start()
+    if meanwhile is not None:
+        meanwhile()
 
     @pl.when(core == 0)
     def _():
@@ -222,12 +256,15 @@
         w_im = window_of(field, 1, place)
         win[0, 0] = w_re
         win[0, 1] = w_im
-        re = [probe[m, 0] * w_re - probe[m, 1] * w_im for m in (0, 1)]
-        im = [probe[m, 0] * w_im + probe[m, 1] * w_re for m in (0, 1)]
-        re, im = both_sides(re, im, table_l[...], table_r[...])
+        x = []
         for m in (0, 1):
-            psi[0, m, 0] = re[m]
-            psi[0, m, 1] = im[m]
+            re = probe[m, 0] * w_re - probe[m, 1] * w_im
+            im = probe[m, 0] * w_im + probe[m, 1] * w_re
+            x.append(prop_left(re, im, table_l))
+        for m in (0, 1):
+            re, im = prop_right(*x[m], table_r)
+            psi[0, m, 0] = re
+            psi[0, m, 1] = im
 
 
 def far_kernel(
@@ -250,9 +287,11 @@
 
     @pl.when(slot == 0)
     def _():
-        grad[...] = jnp.zeros_like(grad)
-        gwin[...] = jnp.zeros_like(gwin)
-        fetch_field(1, scalars[13], obj, right, low_a, low_b, diag, side, field, sems)
+        def clear():
+            grad[...] = jnp.zeros_like(grad)
+            gwin[...] = jnp.zeros_like(gwin)
+
+        fetch_field(1, scalars[13], obj, right, low_a, low_b, diag, side, field, sems, clear)
         load_window(0)
 
     @pl.when(slot < used)
@@ -352,19 +391,18 @@
     @pl.when(slot < scalars[12])
     def _():
         place = place_of(scalars, slot)
-        re = [g_psi[0, m, 0] for m in (0, 1)]
-        im = [g_psi[0, m, 1] for m in (0, 1)]
-        re, im = both_sides(re, im, table_l[...], table_r[...])
+        x = [prop_left(g_psi[0, m, 0], g_psi[0, m, 1], table_l) for m in (0, 1)]
         w_re, w_im = win[0, 0], win[0, 1]
         gw_re = gw_im = None
         for m in (0, 1):
+            re, im = prop_right(*x[m], table_r)
             p_re, p_im = probe[m, 0], probe[m, 1]
-            a_re = p_re * re[m] + p_im * im[m]
-            a_im = p_re * im[m] - p_im * re[m]
+            a_re = p_re * re + p_im * im
+            a_im = p_re * im - p_im * re
             gw_re = a_re if m == 0 else gw_re + a_re
             gw_im = a_im if m == 0 else gw_im + a_im
-            g_probe[m, 0] += w_re * re[m] + w_im * im[m]
-            g_probe[m, 1] += w_re * im[m] - w_im * re[m]
+            g_probe[m, 0] += w_re * re + w_im * im
+            g_probe[m, 1] += w_re * im - w_im * re
         add_window(grad, 0, place, gw_re)
         add_window(grad, 1, place, gw_im)
 
@@ -581,39 +619,45 @@
         return right, low_a, low_b, diag
 
     def gather_probe(probe):
-        mine = jnp.stack([probe] + [send(probe, flip(4 * k, 0)) for k in (1, 2, 3)])
-        return mine, send(mine, flip(2, 1))
-
-    def reduce_probe(grad):
+        return jnp.stack([probe] + [send(probe, flip(4 * k, 0)) for k in (1, 2, 3)])
+
+    def reduce_chip(grad):
         gx = lax.axis_index("gx")
-        core, y_hi, z = gx % 2, gx // 2 % 2, gx // 4
+        core, z = gx % 2, gx // 4
         rows = PROBE // n_gx
         parts = jnp.transpose(grad.reshape(2, 2, 4, 2, 2, rows, PROBE), (4, 2, 3, 0, 1, 5, 6))
         keep = jnp.where(core == 0, parts[0], parts[1])
         give = jnp.where(core == 0, parts[1], parts[0])
-        part = keep + send(give, flip(1, 0))
-
-        def at_z(k):
-            return lax.dynamic_index_in_dim(part, z ^ k, 0, keepdims=False)
-
-        got = [send(at_z(k), flip(4 * k, 0)) for k in (1, 2, 3)]
-        part = (at_z(0) + got[0]) + (got[1] + got[2])
-        keep = jnp.where(y_hi == 0, part[0], part[1])
-        give = jnp.where(y_hi == 0, part[1], part[0])
-        near = send(keep, flip(0, 1))
-        far = send(give, flip(2, 0))
-        across = send(give, flip(2, 1))
-        part = (keep + near) + (far + across)
-        got = [send(part, flip(0, 2 * k)) for k in (1, 2, 3)]
-        return (part + got[0]) + (got[1] + got[2])
+        return keep + send(give, flip(1, 0))
+
+    def halved(part, bit, there):
+        keep = jnp.where(bit == 0, part[0], part[1])
+        give = jnp.where(bit == 0, part[1], part[0])
+        return keep + send(give, there)
+
+    def halved(part, bit, there):
+        keep = jnp.where(bit == 0, part[0], part[1])
+        give = jnp.where(bit == 0, part[1], part[0])
+        return keep + send(give, there)
+
+    def reduce_rest(part):
+        gx = lax.axis_index("gx")
+        z = gx // 4
+        part = halved(part.reshape(2, 2, *part.shape[1:]), z // 2, flip(8, 0))
+        part = halved(part, z % 2, flip(4, 0))
+        for bit in (2, 4):
+            part = part + send(part, flip(0, bit))
+        part = halved(part, gx // 2 % 2, flip(2, 1))
+        return part + send(part, flip(0, 1))
 
     def on_device(obj, probe, positions, counts, amplitudes):
         gx = lax.axis_index("gx").astype(jnp.int32)
         scalars = jnp.concatenate(
             [positions.reshape(2 * SLOTS), counts.reshape(1), jnp.stack([gx & 1, gx >> 1 & 1, gx >> 2])]
         )
-        halo_0 = bring(*pieces(obj, 0))
-        probe_parts = gather_probe(probe)
+        pieces_0, mine = lax.optimization_barrier((pieces(obj, 0), gather_probe(probe)))
+        halo_0 = bring(*pieces_0)
+        probe_parts = mine, send(mine, flip(2, 1))
         amp = permute_amplitudes(amplitudes[0, 0], tables)
         pieces_1, halo_0, amp, probe_parts = lax.optimization_barrier((pieces(obj, 1), halo_0, amp, probe_parts))
         probe_parts = [*probe_parts, *(send(x, flip(1, 0)) for x in probe_parts)]
@@ -622,11 +666,27 @@
         probe_full = probe_rows.reshape(2, 2, PROBE, PROBE)
         g_psi, main_1, *edges_1 = run_far(scalars, obj, halo_1, psi, amp, tables)
         back_1 = take_back(*edges_1)
-        g_probe, main_0, *edges_0 = run_home(scalars, win, g_psi, probe_full, tables)
-        edges_0, g_probe, back_1 = lax.optimization_barrier((edges_0, g_probe, back_1))
+        used = counts[0, 0] > 0
+
+        def home(operands):
+            g_probe, *fields = run_home(*operands, tables)
+            return reduce_chip(g_probe), *fields
+
+        def idle(operands):
+            return tuple(jnp.zeros(x.shape, x.dtype) for x in jax.eval_shape(home, operands))
+
+        part, main_0, *edges_0 = lax.cond(used, home, idle, (scalars, win, g_psi, probe_full))
+        edges_0, part, back_1 = lax.optimization_barrier((edges_0, part, back_1))
         back_0 = take_back(*edges_0)
-        grad = run_join(1, main_1, back_1, None)
-        probe_grad = reduce_probe(g_probe)
+
+        def rest(operands):
+            part, main, back = operands
+            return reduce_rest(part), run_join(1, main, back, None)
+
+        def nothing(operands):
+            return tuple(jnp.zeros(x.shape, x.dtype) for x in jax.eval_shape(rest, operands))
+
+        probe_grad, grad = lax.cond(used, rest, nothing, (part, main_1, back_1))
         grad = run_join(0, main_0, back_0, grad)
         return grad, probe_grad
 

time: 243 us -> 224 us (0.922)
  the two profiles are of different devices: /device:TPU:9 before, /device:TPU:0 now
where the time goes in v3:
time: 224 us; the launch traced here: 222 us
  starting transfers between devices  98.8 us (44%)
  waiting for transfers between devices  55.8 us (25%)
  Pallas kernels  48.6 us (22%)
  local copies, waits for them, and re-layouts  14.2 us (6%)
  other arithmetic  2.87 us (1%)
    ppermute x33, starting transfers between devices, send(): return lax.ppermute(x, axes, pairs)  98.8 us
    ppermute x33, waiting for transfers between devices, send(): return lax.ppermute(x, axes, pairs)  55.8 us
    pallas_call x1, Pallas kernels, run_far(): pl.pallas_call(far_kernel, grid_spec=pltpu.PrefetchScalarGridSpec(num_sca...  16 us
    pallas_call x1, Pallas kernels, run_home(): pl.pallas_call(home_kernel, grid_spec=pltpu.PrefetchScalarGridSpec(num_sc...  10.4 us
    pallas_call x1, Pallas kernels, run_out(): pl.pallas_call(out_kernel, grid_spec=pltpu.PrefetchScalarGridSpec(num_sca...  10.3 us
    pallas_call x2, Pallas kernels, run_join(): pl.pallas_call(join_kernel, grid=(4,), in_specs=[pl.BlockSpec((2, h, TILE...  8.08 us
    unnamed x37, local copies, waits for them, and re-layouts  6.36 us
    squeeze x2, local copies, waits for them, and re-layouts, pieces(): return (obj[layer, :, :n, :n], obj[layer, :, :, :n], obj[layer, :, :n, n:])  5.31 us
  transfers between devices with their start and end apart: 33, of which 10 were waited for; matrix products, arithmetic and copies ran while one was open for 4% of the time, Pallas kernels for 13%

profile of v3, /device:TPU:0, one launch (start us, length us, event | category | flops | bytes accessed | tf_op | source)
XLA Modules:
  0.0 222.4 jit_solution(4747957916318281104)
XLA Ops:
  2.8 2.5 %collective-permute-start.9 = (f32[2,2,16,256]{3,2,1,0:T(8,128)}, f32[2,2,16,256]{3,2,1,0:T(8,128)S(1)}, u32[]{:S(2)}, u32[]{:S(2)}) collective-permute-start(f32[2,2,16,256]{3,2,1,0:T(8,128)} %param.22), channel_id=1, source_target_pairs={{0,96},{1,97},{2,98},{3,99},{4,100},{5,101},{6,102},{7,103},{8,104... | collective-permute-start | bytes 196616 | tf_op jit(solution)/shard_map/ppermute | solution.py:596
  6.3 2.6 %slice_bitcast_fusion = (f32[2,512,256]{2,1,0:T(8,128)S(1)}, f32[2,512,256]{2,1,0:T(8,128)}) fusion(f32[2,2,512,512]{3,2,1,0:T(8,128)} %obj.3), kind=kLoop, calls=%fused_computation.9 | loop fusion | bytes 4194304 | tf_op jit(solution)/shard_map/squeeze | solution.py:603
  9.0 2.7 %slice_bitcast_fusion.2 = (f32[2,256,256]{2,1,0:T(8,128)S(1)}, f32[2,256,256]{2,1,0:T(8,128)S(1)}, f32[2,256,256]{2,1,0:T(8,128)}, f32[2,256,256]{2,1,0:T(8,128)}) fusion(f32[2,2,512,512]{3,2,1,0:T(8,128)} %obj.3), kind=kLoop, calls=%fused_computation.11 | loop fusion | bytes 4194304 | tf_op jit(solution)/shard_map/squeeze | solution.py:603
  16.3 12.2 %collective-permute-done.11.low_a = f32[2,256,256]{2,1,0:T(8,128)S(1)} collective-permute-done((f32[2,256,256]{2,1,0:T(8,128)S(1)}, f32[2,256,256]{2,1,0:T(8,128)S(1)}, u32[]{:S(2)}, u32[]{:S(2)}) %collective-permute-start.11) | collective-permute-done | bytes 524320 | tf_op jit(solution)/shard_map/ppermute | solution.py:596
  29.8 4.1 %collective-permute-start.15 = (f32[4,2,2,16,256]{4,3,2,1,0:T(8,128)S(1)}, f32[4,2,2,16,256]{4,3,2,1,0:T(8,128)}, u32[]{:S(2)}, u32[]{:S(2)}) collective-permute-start(f32[4,2,2,16,256]{4,3,2,1,0:T(8,128)S(1)} %pad_maximum_fusion.mine), channel_id=1, source_target_pairs={{0,17},{1,16},{2,19},{3,18},{4,21},{5,20},{6,23},{7,22},{8,25},{9,... | collective-permute-start | bytes 786440 | tf_op jit(solution)/shard_map/ppermute | solution.py:596
  33.9 3.7 %order_amplitudes.1.amp = f32[6,256,256]{2,1,0:T(8,128)S(1)} custom-call(f32[6,256,256]{2,1,0:T(8,128)S(1)} %bitcast.41, bf16[256,768]{1,0:T(8,128)(2,1)S(1)} %copy-done.12, bf16[768,256]{1,0:T(8,128)(2,1)S(1)} %copy-done.11), custom_call_target="tpu_custom_call" | custom-call | flops 1200000000 | bytes 4000000 | tf_op jit(solution)/shard_map/order_amplitudes/pallas_call | solution.py:465
  38.7 7.2 %collective-permute-done.15.across = f32[4,2,2,16,256]{4,3,2,1,0:T(8,128)} collective-permute-done((f32[4,2,2,16,256]{4,3,2,1,0:T(8,128)S(1)}, f32[4,2,2,16,256]{4,3,2,1,0:T(8,128)}, u32[]{:S(2)}, u32[]{:S(2)}) %collective-permute-start.15) | collective-permute-done | bytes 262176 | tf_op jit(solution)/shard_map/ppermute | solution.py:596
  48.0 5.8 %collective-permute-start.16 = (f32[4,2,2,16,256]{4,3,2,1,0:T(8,128)S(1)}, f32[4,2,2,16,256]{4,3,2,1,0:T(8,128)}, u32[]{:S(2)}, u32[]{:S(2)}) collective-permute-start(f32[4,2,2,16,256]{4,3,2,1,0:T(8,128)S(1)} %pad_maximum_fusion.mine), channel_id=1, source_target_pairs={{0,8},{1,9},{2,10},{3,11},{4,12},{5,13},{6,14},{7,15},{8,0},{9,1},... | collective-permute-start | bytes 786440 | tf_op jit(solution)/shard_map/ppermute | solution.py:596
  58.1 11.5 %collective-permute-done.19.low_a = f32[2,256,256]{2,1,0:T(8,128)S(1)} collective-permute-done((f32[2,256,256]{2,1,0:T(8,128)}, f32[2,256,256]{2,1,0:T(8,128)S(1)}, u32[]{:S(2)}, u32[]{:S(2)}) %collective-permute-start.19) | collective-permute-done | bytes 524320 | tf_op jit(solution)/shard_map/ppermute | solution.py:596
  74.3 10.3 %propagate_out.1 = (f32[6,2,2,256,256]{4,3,2,1,0:T(8,128)}, f32[6,2,256,256]{3,2,1,0:T(8,128)}, f32[2,2,4,2,2,16,256]{6,5,4,3,2,1,0:T(8,128)}) custom-call(s32[16]{0:T(128)S(1)} %concatenate.3.scalars, f32[2,2,512,512]{3,2,1,0:T(8,128)} %obj.3, f32[2,512,256]{2,1,0:T(8,128)S(1)} %collective-permute-done.10.right, ...), custom_call_target="tpu_custom_call" | custom-call | flops 60000002048 | bytes 20000000 | tf_op jit(solution)/shard_map/propagate_out/pallas_call | solution.py:483
  85.7 16.0 %far_field.1 = (f32[6,2,2,256,256]{4,3,2,1,0:T(8,128)}, f32[2,512,512]{2,1,0:T(8,128)}, f32[2,512,256]{2,1,0:T(8,128)}, f32[2,256,256]{2,1,0:T(8,128)S(1)}, f32[...) custom-call(s32[16]{0:T(128)S(1)} %concatenate.3.scalars, f32[2,2,512,512]{3,2,1,0:T(8,128)} %obj.3, ...), custom_call_target="tpu_custom_call" | custom-call | flops 60000002048 | bytes 20000000 | tf_op jit(solution)/shard_map/far_field/pallas_call | solution.py:505
  101.7 3.3 %collective-permute-start.24 = (f32[2,256,256]{2,1,0:T(8,128)S(1)}, f32[2,256,256]{2,1,0:T(8,128)S(1)}, u32[]{:S(2)}, u32[]{:S(2)}) collective-permute-start(f32[2,256,256]{2,1,0:T(8,128)S(1)} %get-tuple-element.113), channel_id=1, source_target_pairs={{0,8},{1,9},{2,10},{3,11},{4,12},{5,13},{6,14},{7,15},{16,24},{17,... | collective-permute-start | bytes 1572872 | tf_op jit(solution)/shard_map/ppermute | solution.py:596
  105.1 2.3 %collective-permute-start.23 = (f32[2,512,256]{2,1,0:T(8,128)}, f32[2,512,256]{2,1,0:T(8,128)}, u32[]{:S(2)}, u32[]{:S(2)}) collective-permute-start(f32[2,512,256]{2,1,0:T(8,128)} %get-tuple-element.111), channel_id=1, source_target_pairs={{0,8},{1,9},{2,10},{3,11},{4,12},{5,13},{6,14},{7,15},{8,16},{9,17... | collective-permute-start | bytes 3145736 | tf_op jit(solution)/shard_map/ppermute | solution.py:596
  108.9 5.8 %collective-permute-start.26 = (f32[2,256,256]{2,1,0:T(8,128)S(1)}, f32[2,256,256]{2,1,0:T(8,128)}, u32[]{:S(2)}, u32[]{:S(2)}) collective-permute-start(f32[2,256,256]{2,1,0:T(8,128)S(1)} %get-tuple-element.114), channel_id=1, source_target_pairs={{0,1},{1,2},{2,3},{3,4},{4,5},{5,6},{6,7},{8,9},{9,10},{10,11},{11... | collective-permute-start | bytes 1572872 | tf_op jit(solution)/shard_map/ppermute | solution.py:596
  117.7 17.5 %conditional.2 = (f32[4,2,2,2,16,256]{5,4,1,0,3,2:T(8,128)S(1)}, f32[2,512,512]{2,1,0:T(8,128)}, f32[2,512,256]{2,1,0:T(8,128)}, f32[2,256,256]{2,1,0:T(8,128)S(...) conditional(s32[]{:T(128)} %bitcast.9, () %tuple.27, (f32[2,2,4,2,2,16,256]{6,5,4,3,2,1,0:T(8,128)}, ...), branch_computations={%region_0.0_spmd, %region_1.2_spmd} | conditional | flops 60000395264 | bytes 34156064 | solution.py:678
  119.9 10.4 %propagate_home.1 = (f32[2,2,256,256]{3,2,1,0:T(8,128)S(1)}, f32[2,512,512]{2,1,0:T(8,128)}, f32[2,512,256]{2,1,0:T(8,128)}, f32[2,256,256]{2,1,0:T(8,128)S(1)},...) custom-call(s32[16]{0:T(128)S(1)} %get-tuple-element.25.scalars, f32[6,2,256,256]{3,2,1,0:T(8,128)} %get-tuple-element.26.win, ...), custom_call_target="tpu_custom_call" | custom-call | flops 60000002048 | bytes 20000000 | tf_op jit(solution)/shard_map/cond/branch_1_fun/propagate_home/pallas_call | solution.py:535
  130.6 2.7 %collective-permute-start = (f32[4,2,2,2,16,256]{5,4,1,0,3,2:T(8,128)S(1)}, f32[4,2,2,2,16,256]{5,4,1,0,3,2:T(8,128)S(1)}, u32[]{:S(2)}, u32[]{:S(2)}) collective-permute-start(f32[4,2,2,2,16,256]{5,4,1,0,3,2:T(8,128)S(1)} %select_bitcast_fusion), channel_id=1, source_target_pairs={{0,8},{1,9},{2,10},{3,11},{4,12},{5,13},{6,14},{7,15},{8,0},{9,1},... | collective-permute-start | bytes 1572872 | tf_op jit(solution)/shard_map/cond/branch_1_fun/ppermute | solution.py:596
  135.2 15.6 %collective-permute-start.29 = (f32[2,256,256]{2,1,0:T(8,128)}, f32[2,256,256]{2,1,0:T(8,128)S(1)}, u32[]{:S(2)}, u32[]{:S(2)}) collective-permute-start(f32[2,256,256]{2,1,0:T(8,128)} %get-tuple-element.117), channel_id=1, source_target_pairs={{0,8},{1,9},{2,10},{3,11},{4,12},{5,13},{6,14},{7,15},{16,24},{17,... | collective-permute-start | bytes 1572872 | tf_op jit(solution)/shard_map/ppermute | solution.py:596
  152.9 4.1 %collective-permute-start.31 = (f32[2,256,256]{2,1,0:T(8,128)}, f32[2,256,256]{2,1,0:T(8,128)S(1)}, u32[]{:S(2)}, u32[]{:S(2)}) collective-permute-start(f32[2,256,256]{2,1,0:T(8,128)} %get-tuple-element.118), channel_id=1, source_target_pairs={{0,1},{1,2},{2,3},{3,4},{4,5},{5,6},{6,7},{8,9},{9,10},{10,11},{11... | collective-permute-start | bytes 1572872 | tf_op jit(solution)/shard_map/ppermute | solution.py:596
  159.8 58.6 %conditional.3 = (f32[2,2,16,256]{3,2,1,0:T(8,128)S(1)}, f32[2,2,512,512]{3,2,1,0:T(8,128)}) conditional(s32[]{:T(128)} %bitcast.9, () %tuple.32, (f32[4,2,2,2,16,256]{5,4,1,0,3,2:T(8,128)S(1)}, f32[2,512,512]{2,1,0:T(8,128)}, f32[2,512,256]{2,1,0:T(8,128)}, f32[2,256,256]{2,1,0:T(8,128)}, f32[2,256,256]{2,1,0:T(8,128)}, ...), branch_computations={%region_2.3_spmd, %region_3.4_spmd} | conditional | flops 1426045 | bytes 13340902 | solution.py:689
  160.6 5.9 %collective-permute-start.1 = (f32[2,2,2,2,16,256]{5,4,3,2,1,0:T(8,128)}, f32[2,2,2,2,16,256]{5,4,3,2,1,0:T(8,128)S(1)}, u32[]{:S(2)}, u32[]{:S(2)}) collective-permute-start(f32[2,2,2,2,16,256]{5,4,3,2,1,0:T(8,128)} %slice_select_fusion), channel_id=1, source_target_pairs={{0,64},{1,65},{2,66},{3,67},{4,68},{5,69},{6,70},{7,71},{8,72},{9,... | collective-permute-start | bytes 786440 | tf_op jit(solution)/shard_map/cond/branch_1_fun/ppermute | solution.py:596
  166.5 9.0 %collective-permute-done.1 = f32[2,2,2,2,16,256]{5,4,3,2,1,0:T(8,128)S(1)} collective-permute-done((f32[2,2,2,2,16,256]{5,4,3,2,1,0:T(8,128)}, f32[2,2,2,2,16,256]{5,4,3,2,1,0:T(8,128)S(1)}, u32[]{:S(2)}, u32[]{:S(2)}) %collective-permute-start.1) | collective-permute-done | bytes 262176 | tf_op jit(solution)/shard_map/cond/branch_1_fun/ppermute | solution.py:596
  175.5 5.5 %collective-permute-start.2 = (f32[2,2,2,16,256]{4,3,2,1,0:T(8,128)S(1)}, f32[2,2,2,16,256]{4,3,2,1,0:T(8,128)S(1)}, u32[]{:S(2)}, u32[]{:S(2)}) collective-permute-start(f32[2,2,2,16,256]{4,3,2,1,0:T(8,128)S(1)} %select_bitcast_fusion.1), channel_id=1, source_target_pairs={{0,32},{1,33},{2,34},{3,35},{4,36},{5,37},{6,38},{7,39},{8,40},{9,... | collective-permute-start | bytes 393224 | tf_op jit(solution)/shard_map/cond/branch_1_fun/ppermute | solution.py:596
  181.0 2.9 %collective-permute-done.2 = f32[2,2,2,16,256]{4,3,2,1,0:T(8,128)S(1)} collective-permute-done((f32[2,2,2,16,256]{4,3,2,1,0:T(8,128)S(1)}, f32[2,2,2,16,256]{4,3,2,1,0:T(8,128)S(1)}, u32[]{:S(2)}, u32[]{:S(2)}) %collective-permute-start.2) | collective-permute-done | bytes 131104 | tf_op jit(solution)/shard_map/cond/branch_1_fun/ppermute | solution.py:596
  184.0 10.6 %collective-permute-start.3 = (f32[2,2,2,16,256]{4,3,2,1,0:T(8,128)S(1)}, f32[2,2,2,16,256]{4,3,2,1,0:T(8,128)S(1)}, u32[]{:S(2)}, u32[]{:S(2)}) collective-permute-start(f32[2,2,2,16,256]{4,3,2,1,0:T(8,128)S(1)} %bitcast_add_fusion.1), channel_id=1, source_target_pairs={{0,2},{1,3},{2,0},{3,1},{4,6},{5,7},{6,4},{7,5},{8,10},{9,11},{10,... | collective-permute-start | bytes 393224 | tf_op jit(solution)/shard_map/cond/branch_1_fun/ppermute | solution.py:596
  194.6 2.9 %collective-permute-done.3 = f32[2,2,2,16,256]{4,3,2,1,0:T(8,128)S(1)} collective-permute-done((f32[2,2,2,16,256]{4,3,2,1,0:T(8,128)S(1)}, f32[2,2,2,16,256]{4,3,2,1,0:T(8,128)S(1)}, u32[]{:S(2)}, u32[]{:S(2)}) %collective-permute-start.3) | collective-permute-done | bytes 131104 | tf_op jit(solution)/shard_map/cond/branch_1_fun/ppermute | solution.py:596
  197.6 5.9 %collective-permute-start.4 = (f32[2,2,2,16,256]{4,3,2,1,0:T(8,128)S(1)}, f32[2,2,2,16,256]{4,3,2,1,0:T(8,128)S(1)}, u32[]{:S(2)}, u32[]{:S(2)}) collective-permute-start(f32[2,2,2,16,256]{4,3,2,1,0:T(8,128)S(1)} %add.34), channel_id=1, source_target_pairs={{0,4},{1,5},{2,6},{3,7},{4,0},{5,1},{6,2},{7,3},{8,12},{9,13},{10,... | collective-permute-start | bytes 393224 | tf_op jit(solution)/shard_map/cond/branch_1_fun/ppermute | solution.py:596
  203.5 2.9 %collective-permute-done.4 = f32[2,2,2,16,256]{4,3,2,1,0:T(8,128)S(1)} collective-permute-done((f32[2,2,2,16,256]{4,3,2,1,0:T(8,128)S(1)}, f32[2,2,2,16,256]{4,3,2,1,0:T(8,128)S(1)}, u32[]{:S(2)}, u32[]{:S(2)}) %collective-permute-start.4) | collective-permute-done | bytes 131104 | tf_op jit(solution)/shard_map/cond/branch_1_fun/ppermute | solution.py:596
  206.6 5.5 %collective-permute-done.5 = f32[2,2,16,256]{3,2,1,0:T(8,128)S(1)} collective-permute-done((f32[2,2,16,256]{3,2,1,0:T(8,128)S(1)}, f32[2,2,16,256]{3,2,1,0:T(8,128)S(1)}, u32[]{:S(2)}, u32[]{:S(2)}) %collective-permute-start.5) | collective-permute-done | bytes 65568 | tf_op jit(solution)/shard_map/cond/branch_1_fun/ppermute | solution.py:596
  212.1 2.1 collective-permute-start.6
  214.2 4.2 %join_gradients.2 = f32[2,2,512,512]{3,2,1,0:T(8,128)} custom-call(f32[2,512,512]{2,1,0:T(8,128)} %get-tuple-element.38.main, f32[2,512,256]{2,1,0:T(8,128)} %get-tuple-element.39.right, f32[2,256,256]{2,1,0:T(8,128)} %get-tuple-element.40.low_a, f32[2,256,256]{2,1,0:T(8,128)} %get-tuple-element.41.low_b, f32[2,256,256]{2,1,0:T(8,128)} %get-tuple-element.42.diag), custom_call_target="tpu_custom_call" | custom-call | flops 1000000 | bytes 6000000 | tf_op jit(solution)/shard_map/cond/branch_1_fun/join_gradients/pallas_call | solution.py:561
  218.5 3.9 %join_gradients.3 = f32[2,2,512,512]{3,2,1,0:T(8,128)} custom-call(f32[2,512,512]{2,1,0:T(8,128)} %get-tuple-element.105.main, f32[2,512,256]{2,1,0:T(8,128)S(1)} %collective-permute-done.28.right, f32[2,256,256]{2,1,0:T(8,128)S(1)} %collective-permute-done.30.low_a, ...), custom_call_target="tpu_custom_call", output_to_operand_aliasing={{}: (5, {})} | custom-call | flops 1000000 | bytes 6000000 | tf_op jit(solution)/shard_map/join_gradients/pallas_call | solution.py:561
  (102 shorter events, 35.9 us)
Async XLA Ops:
  0.7 11.0 %collective-permute-start.7 = (f32[2,2,16,256]{3,2,1,0:T(8,128)}, f32[2,2,16,256]{3,2,1,0:T(8,128)S(1)}, u32[]{:S(2)}, u32[]{:S(2)}) collective-permute-start(f32[2,2,16,256]{3,2,1,0:T(8,128)} %param.22), channel_id=1, source_target_pairs={{0,32},{1,33},{2,34},{3,35},{4,36},{5,37},{6,38},{7,39},{8,40},{9,... | collective-permute-start | bytes 196616 | tf_op jit(solution)/shard_map/ppermute | solution.py:596
  2.8 8.9 %collective-permute-start.9 = (f32[2,2,16,256]{3,2,1,0:T(8,128)}, f32[2,2,16,256]{3,2,1,0:T(8,128)S(1)}, u32[]{:S(2)}, u32[]{:S(2)}) collective-permute-start(f32[2,2,16,256]{3,2,1,0:T(8,128)} %param.22), channel_id=1, source_target_pairs={{0,96},{1,97},{2,98},{3,99},{4,100},{5,101},{6,102},{7,103},{8,104... | collective-permute-start | bytes 196616 | tf_op jit(solution)/shard_map/ppermute | solution.py:596
  5.3 6.4 %collective-permute-start.8 = (f32[2,2,16,256]{3,2,1,0:T(8,128)}, f32[2,2,16,256]{3,2,1,0:T(8,128)S(1)}, u32[]{:S(2)}, u32[]{:S(2)}) collective-permute-start(f32[2,2,16,256]{3,2,1,0:T(8,128)} %param.22), channel_id=1, source_target_pairs={{0,64},{1,65},{2,66},{3,67},{4,68},{5,69},{6,70},{7,71},{8,72},{9,... | collective-permute-start | bytes 196616 | tf_op jit(solution)/shard_map/ppermute | solution.py:596
  11.7 16.8 %collective-permute-start.11 = (f32[2,256,256]{2,1,0:T(8,128)S(1)}, f32[2,256,256]{2,1,0:T(8,128)S(1)}, u32[]{:S(2)}, u32[]{:S(2)}) collective-permute-start(f32[2,256,256]{2,1,0:T(8,128)S(1)} %get-tuple-element.87), channel_id=1, source_target_pairs={{1,0},{2,1},{3,2},{4,3},{5,4},{6,5},{7,6},{9,8},{10,9},{11,10},{12... | collective-permute-start | bytes 1572872 | tf_op jit(solution)/shard_map/ppermute | solution.py:596
  13.0 33.7 %collective-permute-start.10 = (f32[2,512,256]{2,1,0:T(8,128)S(1)}, f32[2,512,256]{2,1,0:T(8,128)S(1)}, u32[]{:S(2)}, u32[]{:S(2)}) collective-permute-start(f32[2,512,256]{2,1,0:T(8,128)S(1)} %get-tuple-element.86), channel_id=1, source_target_pairs={{8,0},{9,1},{10,2},{11,3},{12,4},{13,5},{14,6},{15,7},{16,8},{17,9... | collective-permute-start | bytes 3145736 | tf_op jit(solution)/shard_map/ppermute | solution.py:596
  14.3 31.6 %collective-permute-start.13 = (f32[2,256,256]{2,1,0:T(8,128)S(1)}, f32[2,256,256]{2,1,0:T(8,128)S(1)}, u32[]{:S(2)}, u32[]{:S(2)}) collective-permute-start(f32[2,256,256]{2,1,0:T(8,128)S(1)} %get-tuple-element.87), channel_id=1, source_target_pairs={{17,8},{18,9},{19,10},{20,11},{21,12},{22,13},{23,14},{33,24},{34,... | collective-permute-start | bytes 1572872 | tf_op jit(solution)/shard_map/ppermute | solution.py:596
  15.0 30.9 %collective-permute-start.12 = (f32[2,256,256]{2,1,0:T(8,128)S(1)}, f32[2,256,256]{2,1,0:T(8,128)S(1)}, u32[]{:S(2)}, u32[]{:S(2)}) collective-permute-start(f32[2,256,256]{2,1,0:T(8,128)S(1)} %get-tuple-element.88), channel_id=1, source_target_pairs={{1,0},{2,1},{3,2},{4,3},{5,4},{6,5},{7,6},{9,8},{10,9},{11,10},{12... | collective-permute-start | bytes 1572872 | tf_op jit(solution)/shard_map/ppermute | solution.py:596
  28.5 17.4 %collective-permute-start.14 = (f32[2,256,256]{2,1,0:T(8,128)S(1)}, f32[2,256,256]{2,1,0:T(8,128)S(1)}, u32[]{:S(2)}, u32[]{:S(2)}) collective-permute-start(f32[2,256,256]{2,1,0:T(8,128)S(1)} %collective-permute-done.11.low_a), channel_id=1, source_target_pairs={{8,0},{9,1},{10,2},{11,3},{12,4},{13,5},{14,6},{15,7},{24,16},{25,... | collective-permute-start | bytes 1572872 | tf_op jit(solution)/shard_map/ppermute | solution.py:596
  29.8 16.1 %collective-permute-start.15 = (f32[4,2,2,16,256]{4,3,2,1,0:T(8,128)S(1)}, f32[4,2,2,16,256]{4,3,2,1,0:T(8,128)}, u32[]{:S(2)}, u32[]{:S(2)}) collective-permute-start(f32[4,2,2,16,256]{4,3,2,1,0:T(8,128)S(1)} %pad_maximum_fusion.mine), channel_id=1, source_target_pairs={{0,17},{1,16},{2,19},{3,18},{4,21},{5,20},{6,23},{7,22},{8,25},{9,... | collective-permute-start | bytes 786440 | tf_op jit(solution)/shard_map/ppermute | solution.py:596
  46.7 22.9 %collective-permute-start.19 = (f32[2,256,256]{2,1,0:T(8,128)}, f32[2,256,256]{2,1,0:T(8,128)S(1)}, u32[]{:S(2)}, u32[]{:S(2)}) collective-permute-start(f32[2,256,256]{2,1,0:T(8,128)} %get-tuple-element.100), channel_id=1, source_target_pairs={{1,0},{2,1},{3,2},{4,3},{5,4},{6,5},{7,6},{9,8},{10,9},{11,10},{12... | collective-permute-start | bytes 1572872 | tf_op jit(solution)/shard_map/ppermute | solution.py:596
  48.0 8.8 %collective-permute-start.16 = (f32[4,2,2,16,256]{4,3,2,1,0:T(8,128)S(1)}, f32[4,2,2,16,256]{4,3,2,1,0:T(8,128)}, u32[]{:S(2)}, u32[]{:S(2)}) collective-permute-start(f32[4,2,2,16,256]{4,3,2,1,0:T(8,128)S(1)} %pad_maximum_fusion.mine), channel_id=1, source_target_pairs={{0,8},{1,9},{2,10},{3,11},{4,12},{5,13},{6,14},{7,15},{8,0},{9,1},... | collective-permute-start | bytes 786440 | tf_op jit(solution)/shard_map/ppermute | solution.py:596
  53.8 17.2 %collective-permute-start.17 = (f32[4,2,2,16,256]{4,3,2,1,0:T(8,128)}, f32[4,2,2,16,256]{4,3,2,1,0:T(8,128)}, u32[]{:S(2)}, u32[]{:S(2)}) collective-permute-start(f32[4,2,2,16,256]{4,3,2,1,0:T(8,128)} %collective-permute-done.15.across), channel_id=1, source_target_pairs={{0,8},{1,9},{2,10},{3,11},{4,12},{5,13},{6,14},{7,15},{8,0},{9,1},... | collective-permute-start | bytes 786440 | tf_op jit(solution)/shard_map/ppermute | solution.py:596
  54.8 29.9 %collective-permute-start.21 = (f32[2,256,256]{2,1,0:T(8,128)}, f32[2,256,256]{2,1,0:T(8,128)S(1)}, u32[]{:S(2)}, u32[]{:S(2)}) collective-permute-start(f32[2,256,256]{2,1,0:T(8,128)} %get-tuple-element.100), channel_id=1, source_target_pairs={{17,8},{18,9},{19,10},{20,11},{21,12},{22,13},{23,14},{33,24},{34,... | collective-permute-start | bytes 1572872 | tf_op jit(solution)/shard_map/ppermute | solution.py:596
  55.5 29.1 %collective-permute-start.20 = (f32[2,256,256]{2,1,0:T(8,128)}, f32[2,256,256]{2,1,0:T(8,128)S(1)}, u32[]{:S(2)}, u32[]{:S(2)}) collective-permute-start(f32[2,256,256]{2,1,0:T(8,128)} %get-tuple-element.101), channel_id=1, source_target_pairs={{1,0},{2,1},{3,2},{4,3},{5,4},{6,5},{7,6},{9,8},{10,9},{11,10},{12... | collective-permute-start | bytes 1572872 | tf_op jit(solution)/shard_map/ppermute | solution.py:596
  56.8 27.9 %collective-permute-start.18 = (f32[2,512,256]{2,1,0:T(8,128)}, f32[2,512,256]{2,1,0:T(8,128)S(1)}, u32[]{:S(2)}, u32[]{:S(2)}) collective-permute-start(f32[2,512,256]{2,1,0:T(8,128)} %get-tuple-element.99), channel_id=1, source_target_pairs={{8,0},{9,1},{10,2},{11,3},{12,4},{13,5},{14,6},{15,7},{16,8},{17,9... | collective-permute-start | bytes 3145736 | tf_op jit(solution)/shard_map/ppermute | solution.py:596
  69.6 15.0 %collective-permute-start.22 = (f32[2,256,256]{2,1,0:T(8,128)S(1)}, f32[2,256,256]{2,1,0:T(8,128)S(1)}, u32[]{:S(2)}, u32[]{:S(2)}) collective-permute-start(f32[2,256,256]{2,1,0:T(8,128)S(1)} %collective-permute-done.19.low_a), channel_id=1, source_target_pairs={{8,0},{9,1},{10,2},{11,3},{12,4},{13,5},{14,6},{15,7},{24,16},{25,... | collective-permute-start | bytes 1572872 | tf_op jit(solution)/shard_map/ppermute | solution.py:596
  101.7 13.0 %collective-permute-start.24 = (f32[2,256,256]{2,1,0:T(8,128)S(1)}, f32[2,256,256]{2,1,0:T(8,128)S(1)}, u32[]{:S(2)}, u32[]{:S(2)}) collective-permute-start(f32[2,256,256]{2,1,0:T(8,128)S(1)} %get-tuple-element.113), channel_id=1, source_target_pairs={{0,8},{1,9},{2,10},{3,11},{4,12},{5,13},{6,14},{7,15},{16,24},{17,... | collective-permute-start | bytes 1572872 | tf_op jit(solution)/shard_map/ppermute | solution.py:596
  105.1 30.1 %collective-permute-start.23 = (f32[2,512,256]{2,1,0:T(8,128)}, f32[2,512,256]{2,1,0:T(8,128)}, u32[]{:S(2)}, u32[]{:S(2)}) collective-permute-start(f32[2,512,256]{2,1,0:T(8,128)} %get-tuple-element.111), channel_id=1, source_target_pairs={{0,8},{1,9},{2,10},{3,11},{4,12},{5,13},{6,14},{7,15},{8,16},{9,17... | collective-permute-start | bytes 3145736 | tf_op jit(solution)/shard_map/ppermute | solution.py:596
  107.4 27.8 %collective-permute-start.27 = (f32[2,256,256]{2,1,0:T(8,128)S(1)}, f32[2,256,256]{2,1,0:T(8,128)}, u32[]{:S(2)}, u32[]{:S(2)}) collective-permute-start(f32[2,256,256]{2,1,0:T(8,128)S(1)} %get-tuple-element.113), channel_id=1, source_target_pairs={{8,17},{9,18},{10,19},{11,20},{12,21},{13,22},{14,23},{24,33},{25,... | collective-permute-start | bytes 1572872 | tf_op jit(solution)/shard_map/ppermute | solution.py:596
  108.9 26.3 %collective-permute-start.26 = (f32[2,256,256]{2,1,0:T(8,128)S(1)}, f32[2,256,256]{2,1,0:T(8,128)}, u32[]{:S(2)}, u32[]{:S(2)}) collective-permute-start(f32[2,256,256]{2,1,0:T(8,128)S(1)} %get-tuple-element.114), channel_id=1, source_target_pairs={{0,1},{1,2},{2,3},{3,4},{4,5},{5,6},{6,7},{8,9},{9,10},{10,11},{11... | collective-permute-start | bytes 1572872 | tf_op jit(solution)/shard_map/ppermute | solution.py:596
  115.6 19.7 %collective-permute-start.25 = (f32[2,256,256]{2,1,0:T(8,128)}, f32[2,256,256]{2,1,0:T(8,128)}, u32[]{:S(2)}, u32[]{:S(2)}) collective-permute-start(f32[2,256,256]{2,1,0:T(8,128)} %add.40), channel_id=1, source_target_pairs={{0,1},{1,2},{2,3},{3,4},{4,5},{5,6},{6,7},{8,9},{9,10},{10,11},{11... | collective-permute-start | bytes 1572872 | tf_op jit(solution)/shard_map/ppermute | solution.py:596
  135.2 21.8 %collective-permute-start.29 = (f32[2,256,256]{2,1,0:T(8,128)}, f32[2,256,256]{2,1,0:T(8,128)S(1)}, u32[]{:S(2)}, u32[]{:S(2)}) collective-permute-start(f32[2,256,256]{2,1,0:T(8,128)} %get-tuple-element.117), channel_id=1, source_target_pairs={{0,8},{1,9},{2,10},{3,11},{4,12},{5,13},{6,14},{7,15},{16,24},{17,... | collective-permute-start | bytes 1572872 | tf_op jit(solution)/shard_map/ppermute | solution.py:596
  150.8 67.7 %collective-permute-start.28 = (f32[2,512,256]{2,1,0:T(8,128)}, f32[2,512,256]{2,1,0:T(8,128)S(1)}, u32[]{:S(2)}, u32[]{:S(2)}) collective-permute-start(f32[2,512,256]{2,1,0:T(8,128)} %get-tuple-element.115), channel_id=1, source_target_pairs={{0,8},{1,9},{2,10},{3,11},{4,12},{5,13},{6,14},{7,15},{8,16},{9,17... | collective-permute-start | bytes 3145736 | tf_op jit(solution)/shard_map/ppermute | solution.py:596
  152.2 66.3 %collective-permute-start.32 = (f32[2,256,256]{2,1,0:T(8,128)}, f32[2,256,256]{2,1,0:T(8,128)S(1)}, u32[]{:S(2)}, u32[]{:S(2)}) collective-permute-start(f32[2,256,256]{2,1,0:T(8,128)} %get-tuple-element.117), channel_id=1, source_target_pairs={{8,17},{9,18},{10,19},{11,20},{12,21},{13,22},{14,23},{24,33},{25,... | collective-permute-start | bytes 1572872 | tf_op jit(solution)/shard_map/ppermute | solution.py:596
  152.9 65.6 %collective-permute-start.31 = (f32[2,256,256]{2,1,0:T(8,128)}, f32[2,256,256]{2,1,0:T(8,128)S(1)}, u32[]{:S(2)}, u32[]{:S(2)}) collective-permute-start(f32[2,256,256]{2,1,0:T(8,128)} %get-tuple-element.118), channel_id=1, source_target_pairs={{0,1},{1,2},{2,3},{3,4},{4,5},{5,6},{6,7},{8,9},{9,10},{10,11},{11... | collective-permute-start | bytes 1572872 | tf_op jit(solution)/shard_map/ppermute | solution.py:596
  157.9 60.6 %collective-permute-start.30 = (f32[2,256,256]{2,1,0:T(8,128)}, f32[2,256,256]{2,1,0:T(8,128)S(1)}, u32[]{:S(2)}, u32[]{:S(2)}) collective-permute-start(f32[2,256,256]{2,1,0:T(8,128)} %add.41), channel_id=1, source_target_pairs={{0,1},{1,2},{2,3},{3,4},{4,5},{5,6},{6,7},{8,9},{9,10},{10,11},{11... | collective-permute-start | bytes 1572872 | tf_op jit(solution)/shard_map/ppermute | solution.py:596
  160.6 14.8 %collective-permute-start.1 = (f32[2,2,2,2,16,256]{5,4,3,2,1,0:T(8,128)}, f32[2,2,2,2,16,256]{5,4,3,2,1,0:T(8,128)S(1)}, u32[]{:S(2)}, u32[]{:S(2)}) collective-permute-start(f32[2,2,2,2,16,256]{5,4,3,2,1,0:T(8,128)} %slice_select_fusion), channel_id=1, source_target_pairs={{0,64},{1,65},{2,66},{3,67},{4,68},{5,69},{6,70},{7,71},{8,72},{9,... | collective-permute-start | bytes 786440 | tf_op jit(solution)/shard_map/cond/branch_1_fun/ppermute | solution.py:596
  175.5 8.4 %collective-permute-start.2 = (f32[2,2,2,16,256]{4,3,2,1,0:T(8,128)S(1)}, f32[2,2,2,16,256]{4,3,2,1,0:T(8,128)S(1)}, u32[]{:S(2)}, u32[]{:S(2)}) collective-permute-start(f32[2,2,2,16,256]{4,3,2,1,0:T(8,128)S(1)} %select_bitcast_fusion.1), channel_id=1, source_target_pairs={{0,32},{1,33},{2,34},{3,35},{4,36},{5,37},{6,38},{7,39},{8,40},{9,... | collective-permute-start | bytes 393224 | tf_op jit(solution)/shard_map/cond/branch_1_fun/ppermute | solution.py:596
  184.0 13.6 %collective-permute-start.3 = (f32[2,2,2,16,256]{4,3,2,1,0:T(8,128)S(1)}, f32[2,2,2,16,256]{4,3,2,1,0:T(8,128)S(1)}, u32[]{:S(2)}, u32[]{:S(2)}) collective-permute-start(f32[2,2,2,16,256]{4,3,2,1,0:T(8,128)S(1)} %bitcast_add_fusion.1), channel_id=1, source_target_pairs={{0,2},{1,3},{2,0},{3,1},{4,6},{5,7},{6,4},{7,5},{8,10},{9,11},{10,... | collective-permute-start | bytes 393224 | tf_op jit(solution)/shard_map/cond/branch_1_fun/ppermute | solution.py:596
  197.6 8.9 %collective-permute-start.4 = (f32[2,2,2,16,256]{4,3,2,1,0:T(8,128)S(1)}, f32[2,2,2,16,256]{4,3,2,1,0:T(8,128)S(1)}, u32[]{:S(2)}, u32[]{:S(2)}) collective-permute-start(f32[2,2,2,16,256]{4,3,2,1,0:T(8,128)S(1)} %add.34), channel_id=1, source_target_pairs={{0,4},{1,5},{2,6},{3,7},{4,0},{5,1},{6,2},{7,3},{8,12},{9,13},{10,... | collective-permute-start | bytes 393224 | tf_op jit(solution)/shard_map/cond/branch_1_fun/ppermute | solution.py:596
  206.5 5.6 %collective-permute-start.5 = (f32[2,2,16,256]{3,2,1,0:T(8,128)S(1)}, f32[2,2,16,256]{3,2,1,0:T(8,128)S(1)}, u32[]{:S(2)}, u32[]{:S(2)}) collective-permute-start(f32[2,2,16,256]{3,2,1,0:T(8,128)S(1)} %select_bitcast_fusion.2), channel_id=1, source_target_pairs={{0,17},{1,16},{2,19},{3,18},{4,21},{5,20},{6,23},{7,22},{8,25},{9,... | collective-permute-start | bytes 196616 | tf_op jit(solution)/shard_map/cond/branch_1_fun/ppermute | solution.py:596
  212.1 6.3 %collective-permute-start.6 = (f32[2,2,16,256]{3,2,1,0:T(8,128)S(1)}, f32[2,2,16,256]{3,2,1,0:T(8,128)S(1)}, u32[]{:S(2)}, u32[]{:S(2)}) collective-permute-start(f32[2,2,16,256]{3,2,1,0:T(8,128)S(1)} %bitcast_add_fusion.2), channel_id=1, source_target_pairs={{0,1},{1,0},{2,3},{3,2},{4,5},{5,4},{6,7},{7,6},{8,9},{9,8},{10,11... | collective-permute-start | bytes 196616 | tf_op jit(solution)/shard_map/cond/branch_1_fun/ppermute | solution.py:596
  (21 other events, 260.9 us)

commit v4 on v3

--- a/solution.py
+++ b/solution.py
@@ -16,7 +16,7 @@
 SLOTS = 6
 F32 = jnp.float32
 BF16 = jnp.bfloat16
-VMEM_LIMIT = 48 * 1024 * 1024
+VMEM_LIMIT = 60 * 1024 * 1024
 
 
 def split_table(mat):
@@ -607,8 +607,10 @@
         right = send(edge, lambda gx, gy: (gx - 1, gy))
         low_b = send(low, lambda gx, gy: (gx, gy - 1))
         diag = send(corner, lambda gx, gy: (gx - 1, gy - 1) if gx % 2 == 0 else None)
-        side = send(low_a, lambda gx, gy: (gx - 1, gy) if gx % 2 == 1 else None)
-        return right, low_a, low_b, diag, side
+        return right, low_a, low_b, diag
+
+    def bring_side(low_a):
+        return send(low_a, lambda gx, gy: (gx - 1, gy) if gx % 2 == 1 else None)
 
     def take_back(right, low_a, low_b, corner):
         side = send(corner, lambda gx, gy: (gx + 1, gy) if gx % 2 == 0 else None)
@@ -643,7 +645,6 @@
     def reduce_rest(part):
         gx = lax.axis_index("gx")
         z = gx // 4
-        part = halved(part.reshape(2, 2, *part.shape[1:]), z // 2, flip(8, 0))
         part = halved(part, z % 2, flip(4, 0))
         for bit in (2, 4):
             part = part + send(part, flip(0, bit))
@@ -658,11 +659,15 @@
         pieces_0, mine = lax.optimization_barrier((pieces(obj, 0), gather_probe(probe)))
         halo_0 = bring(*pieces_0)
         probe_parts = mine, send(mine, flip(2, 1))
+        obj_late, low_a = lax.optimization_barrier((obj, halo_0[1]))
+        halo_0 = (halo_0[0], low_a, *halo_0[2:], bring_side(low_a))
         amp = permute_amplitudes(amplitudes[0, 0], tables)
-        pieces_1, halo_0, amp, probe_parts = lax.optimization_barrier((pieces(obj, 1), halo_0, amp, probe_parts))
+        pieces_1, halo_0, amp, probe_parts = lax.optimization_barrier((pieces(obj_late, 1), halo_0, amp, probe_parts))
         probe_parts = [*probe_parts, *(send(x, flip(1, 0)) for x in probe_parts)]
-        halo_1 = bring(*pieces_1)
+        right, low_a, *others = bring(*pieces_1)
         psi, win, probe_rows = run_out(scalars, obj, halo_0, probe_parts, tables)
+        low_a, psi = lax.optimization_barrier((low_a, psi))
+        halo_1 = (right, low_a, *others, bring_side(low_a))
         probe_full = probe_rows.reshape(2, 2, PROBE, PROBE)
         g_psi, main_1, *edges_1 = run_far(scalars, obj, halo_1, psi, amp, tables)
         back_1 = take_back(*edges_1)
@@ -670,7 +675,9 @@
 
         def home(operands):
             g_probe, *fields = run_home(*operands, tables)
-            return reduce_chip(g_probe), *fields
+            part = reduce_chip(g_probe)
+            part = part.reshape(2, 2, *part.shape[1:])
+            return halved(part, lax.axis_index("gx") // 8, flip(8, 0)), *fields
 
         def idle(operands):
             return tuple(jnp.zeros(x.shape, x.dtype) for x in jax.eval_shape(home, operands))

time: 224 us -> 230 us (1.027); the launches traced: 222 us -> 225 us
  Pallas kernels: 48.6 us -> 56.1 us
  local copies, waits for them, and re-layouts: 14.2 us -> 9.7 us
  other arithmetic: 2.87 us -> 6.16 us
    unnamed x37 -> x21, local copies, waits for them, and re-layouts: 6.36 us -> 2.24 us
    pallas_call x1, Pallas kernels: 3.67 us -> 6.52 us  [permute_amplitudes(): pl.pallas_call(amp_kernel, grid=(SLOTS,), in_specs=[pl.BlockSpec((1, n, n...]
    squeeze x2 -> x4, local copies, waits for them, and re-layouts: 5.31 us -> 5.99 us  [pieces(): return (obj[layer, :, :n, :n], obj[layer, :, :, :n], obj[layer, :, :n, n:])]
  transfers between devices with their start and end apart: 33 -> 33, of which waited for: 10 -> 10; matrix products, arithmetic and copies ran while one was open for 4% -> 6% of each run, Pallas kernels for 13% -> 15%
where the time goes in v4:
time: 230 us; the launch traced here: 225 us
  starting transfers between devices  97.8 us (43%)
  Pallas kernels  56.1 us (24%)
  waiting for transfers between devices  53.8 us (23%)
  local copies, waits for them, and re-layouts  9.7 us (4%)
  other arithmetic  6.16 us (3%)
    ppermute x33, starting transfers between devices, send(): return lax.ppermute(x, axes, pairs)  97.8 us
    ppermute x33, waiting for transfers between devices, send(): return lax.ppermute(x, axes, pairs)  53.8 us
    pallas_call x1, Pallas kernels, run_far(): pl.pallas_call(far_kernel, grid_spec=pltpu.PrefetchScalarGridSpec(num_sca...  17.5 us
    pallas_call x1, Pallas kernels, run_out(): pl.pallas_call(out_kernel, grid_spec=pltpu.PrefetchScalarGridSpec(num_sca...  12.4 us
    pallas_call x1, Pallas kernels, run_home(): pl.pallas_call(home_kernel, grid_spec=pltpu.PrefetchScalarGridSpec(num_sc...  11.5 us
    pallas_call x2, Pallas kernels, run_join(): pl.pallas_call(join_kernel, grid=(4,), in_specs=[pl.BlockSpec((2, h, TILE...  8.17 us
    pallas_call x1, Pallas kernels, permute_amplitudes(): pl.pallas_call(amp_kernel, grid=(SLOTS,), in_specs=[pl.BlockSpec((1, n, n...  6.52 us
    squeeze x4, local copies, waits for them, and re-layouts, pieces(): return (obj[layer, :, :n, :n], obj[layer, :, :, :n], obj[layer, :, :n, n:])  5.99 us
  transfers between devices with their start and end apart: 33, of which 10 were waited for; matrix products, arithmetic and copies ran while one was open for 6% of the time, Pallas kernels for 15%

profile of v4, /device:TPU:0, one launch (start us, length us, event | category | flops | bytes accessed | tf_op | source)
XLA Modules:
  0.0 225.5 jit_solution(5549279628787000481)
XLA Ops:
  0.6 2.1 collective-permute-start.7
  2.7 2.5 %collective-permute-start.9 = (f32[2,2,16,256]{3,2,1,0:T(8,128)}, f32[2,2,16,256]{3,2,1,0:T(8,128)S(1)}, u32[]{:S(2)}, u32[]{:S(2)}) collective-permute-start(f32[2,2,16,256]{3,2,1,0:T(8,128)} %param.22), channel_id=1, source_target_pairs={{0,96},{1,97},{2,98},{3,99},{4,100},{5,101},{6,102},{7,103},{8,104... | collective-permute-start | bytes 196616 | tf_op jit(solution)/shard_map/ppermute | solution.py:596
  7.6 2.1 slice_bitcast_fusion.4
  13.9 6.5 %order_amplitudes.1.amp = f32[6,256,256]{2,1,0:T(8,128)} custom-call(f32[6,256,256]{2,1,0:T(8,128)} %bitcast.47, bf16[256,768]{1,0:T(8,128)(2,1)} %constant.120.clone.perm_l, bf16[768,256]{1,0:T(8,128)(2,1)} %constant.121.clone.perm_r), custom_call_target="tpu_custom_call" | custom-call | flops 1200000000 | bytes 4000000 | tf_op jit(solution)/shard_map/order_amplitudes/pallas_call | solution.py:465
  21.1 5.7 %collective-permute-start.15 = (f32[4,2,2,16,256]{4,3,2,1,0:T(8,128)S(1)}, f32[4,2,2,16,256]{4,3,2,1,0:T(8,128)}, u32[]{:S(2)}, u32[]{:S(2)}) collective-permute-start(f32[4,2,2,16,256]{4,3,2,1,0:T(8,128)S(1)} %pad_maximum_fusion.mine), channel_id=1, source_target_pairs={{0,17},{1,16},{2,19},{3,18},{4,21},{5,20},{6,23},{7,22},{8,25},{9,... | collective-permute-start | bytes 786440 | tf_op jit(solution)/shard_map/ppermute | solution.py:596
  32.0 15.4 %collective-permute-done.15.across = f32[4,2,2,16,256]{4,3,2,1,0:T(8,128)} collective-permute-done((f32[4,2,2,16,256]{4,3,2,1,0:T(8,128)S(1)}, f32[4,2,2,16,256]{4,3,2,1,0:T(8,128)}, u32[]{:S(2)}, u32[]{:S(2)}) %collective-permute-start.15) | collective-permute-done | bytes 262176 | tf_op jit(solution)/shard_map/ppermute | solution.py:596
  47.5 3.4 %collective-permute-start.16 = (f32[4,2,2,16,256]{4,3,2,1,0:T(8,128)S(1)}, f32[4,2,2,16,256]{4,3,2,1,0:T(8,128)}, u32[]{:S(2)}, u32[]{:S(2)}) collective-permute-start(f32[4,2,2,16,256]{4,3,2,1,0:T(8,128)S(1)} %pad_maximum_fusion.mine), channel_id=1, source_target_pairs={{0,8},{1,9},{2,10},{3,11},{4,12},{5,13},{6,14},{7,15},{8,0},{9,1},... | collective-permute-start | bytes 786440 | tf_op jit(solution)/shard_map/ppermute | solution.py:596
  56.5 12.4 %propagate_out.1 = (f32[6,2,2,256,256]{4,3,2,1,0:T(8,128)}, f32[6,2,256,256]{3,2,1,0:T(8,128)}, f32[2,2,4,2,2,16,256]{6,5,4,3,2,1,0:T(8,128)}) custom-call(s32[16]{0:T(128)S(1)} %concatenate.3.scalars, f32[2,2,512,512]{3,2,1,0:T(8,128)} %obj.3, f32[2,512,256]{2,1,0:T(8,128)} %collective-permute-done.11.right, f32[2,256,256]{2,1,0:T(8,128)} %collective-permute-done.10.low_a, ...), custom_call_target="tpu_custom_call" | custom-call | flops 60000002048 | bytes 20000000 | tf_op jit(solution)/shard_map/propagate_out/pallas_call | solution.py:483
  70.6 9.9 %collective-permute-done.20.low_b = f32[2,256,256]{2,1,0:T(8,128)} collective-permute-done((f32[2,256,256]{2,1,0:T(8,128)S(1)}, f32[2,256,256]{2,1,0:T(8,128)}, u32[]{:S(2)}, u32[]{:S(2)}) %collective-permute-start.20) | collective-permute-done | bytes 524320 | tf_op jit(solution)/shard_map/ppermute | solution.py:596
  81.8 17.5 %far_field.1 = (f32[6,2,2,256,256]{4,3,2,1,0:T(8,128)}, f32[2,512,512]{2,1,0:T(8,128)}, f32[2,512,256]{2,1,0:T(8,128)}, f32[2,256,256]{2,1,0:T(8,128)}, f32[2,256,256]{2,1,0:T(8,128)}, /*index=5*/f32[2,256,256]{2,1,0:T(8,128)}) custom-call(s32[16]{0:T(128)S(1)} %concatenate.3.scalars, f32[2,2,512,512]{3,2,1,0:T(8,128)} %obj.3, f32[2,512,256]{2,1,0:T(8,128)} %copy-done.5, ...), custom_call_target="tpu_custom_call" | custom-call | flops 60000002048 | bytes 20000000 | tf_op jit(solution)/shard_map/far_field/pallas_call | solution.py:505
  99.3 12.6 %collective-permute-start.24 = (f32[2,256,256]{2,1,0:T(8,128)}, f32[2,256,256]{2,1,0:T(8,128)S(1)}, u32[]{:S(2)}, u32[]{:S(2)}) collective-permute-start(f32[2,256,256]{2,1,0:T(8,128)} %get-tuple-element.121), channel_id=1, source_target_pairs={{0,8},{1,9},{2,10},{3,11},{4,12},{5,13},{6,14},{7,15},{16,24},{17,... | collective-permute-start | bytes 1572872 | tf_op jit(solution)/shard_map/ppermute | solution.py:596
  111.8 2.3 %collective-permute-start.23 = (f32[2,512,256]{2,1,0:T(8,128)}, f32[2,512,256]{2,1,0:T(8,128)}, u32[]{:S(2)}, u32[]{:S(2)}) collective-permute-start(f32[2,512,256]{2,1,0:T(8,128)} %get-tuple-element.119), channel_id=1, source_target_pairs={{0,8},{1,9},{2,10},{3,11},{4,12},{5,13},{6,14},{7,15},{8,16},{9,17... | collective-permute-start | bytes 3145736 | tf_op jit(solution)/shard_map/ppermute | solution.py:596
  115.6 2.1 collective-permute-start.26
  117.7 1.9 add.40
  119.6 4.2 %collective-permute-start.25 = (f32[2,256,256]{2,1,0:T(8,128)}, f32[2,256,256]{2,1,0:T(8,128)}, u32[]{:S(2)}, u32[]{:S(2)}) collective-permute-start(f32[2,256,256]{2,1,0:T(8,128)} %add.40), channel_id=1, source_target_pairs={{0,1},{1,2},{2,3},{3,4},{4,5},{5,6},{6,7},{8,9},{9,10},{10,11},{11... | collective-permute-start | bytes 1572872 | tf_op jit(solution)/shard_map/ppermute | solution.py:596
  123.8 48.2 %conditional.2 = (f32[2,2,2,2,16,256]{5,4,1,0,3,2:T(8,128)S(1)}, f32[2,512,512]{2,1,0:T(8,128)S(1)}, f32[2,512,256]{2,1,0:T(8,128)}, f32[2,256,256]{2,1,0:T(8,12...) conditional(s32[]{:T(128)} %bitcast.9, () %tuple.29, (f32[2,2,4,2,2,16,256]{6,5,4,3,2,1,0:T(8,128)}, ...), branch_computations={%region_0.0_spmd, %region_1.2_spmd} | conditional | flops 60000591872 | bytes 30748300 | solution.py:685
  123.8 11.5 %propagate_home.1 = (f32[2,2,256,256]{3,2,1,0:T(8,128)}, f32[2,512,512]{2,1,0:T(8,128)S(1)}, f32[2,512,256]{2,1,0:T(8,128)}, f32[2,256,256]{2,1,0:T(8,128)}, f32...) custom-call(s32[16]{0:T(128)S(1)} %get-tuple-element.25.scalars, f32[6,2,256,256]{3,2,1,0:T(8,128)} %get-tuple-element.26.win, ...), custom_call_target="tpu_custom_call" | custom-call | flops 60000002048 | bytes 20000000 | tf_op jit(solution)/shard_map/cond/branch_1_fun/propagate_home/pallas_call | solution.py:535
  137.5 5.8 %collective-permute-start = (f32[4,2,2,2,16,256]{5,4,1,0,3,2:T(8,128)}, f32[4,2,2,2,16,256]{5,4,1,0,3,2:T(8,128)}, u32[]{:S(2)}, u32[]{:S(2)}) collective-permute-start(f32[4,2,2,2,16,256]{5,4,1,0,3,2:T(8,128)} %select_bitcast_fusion), channel_id=1, source_target_pairs={{0,8},{1,9},{2,10},{3,11},{4,12},{5,13},{6,14},{7,15},{8,0},{9,1},... | collective-permute-start | bytes 1572872 | tf_op jit(solution)/shard_map/cond/branch_1_fun/ppermute | solution.py:596
  146.4 18.5 %collective-permute-start.1 = (f32[2,2,2,2,16,256]{5,4,1,0,3,2:T(8,128)S(1)}, f32[2,2,2,2,16,256]{5,4,1,0,3,2:T(8,128)S(1)}, u32[]{:S(2)}, u32[]{:S(2)}) collective-permute-start(f32[2,2,2,2,16,256]{5,4,1,0,3,2:T(8,128)S(1)} %slice_select_fusion), channel_id=1, source_target_pairs={{0,64},{1,65},{2,66},{3,67},{4,68},{5,69},{6,70},{7,71},{8,72},{9,... | collective-permute-start | bytes 786440 | tf_op jit(solution)/shard_map/cond/branch_1_fun/ppermute | solution.py:596
  164.9 6.8 %collective-permute-done.1 = f32[2,2,2,2,16,256]{5,4,1,0,3,2:T(8,128)S(1)} collective-permute-done((f32[2,2,2,2,16,256]{5,4,1,0,3,2:T(8,128)S(1)}, f32[2,2,2,2,16,256]{5,4,1,0,3,2:T(8,128)S(1)}, u32[]{:S(2)}, u32[]{:S(2)}) %collective-permute-start.1) | collective-permute-done | bytes 262176 | tf_op jit(solution)/shard_map/cond/branch_1_fun/ppermute | solution.py:596
  176.6 2.4 %collective-permute-start.31 = (f32[2,256,256]{2,1,0:T(8,128)}, f32[2,256,256]{2,1,0:T(8,128)}, u32[]{:S(2)}, u32[]{:S(2)}) collective-permute-start(f32[2,256,256]{2,1,0:T(8,128)} %get-tuple-element.126), channel_id=1, source_target_pairs={{0,1},{1,2},{2,3},{3,4},{4,5},{5,6},{6,7},{8,9},{9,10},{10,11},{11... | collective-permute-start | bytes 1572872 | tf_op jit(solution)/shard_map/ppermute | solution.py:596
  179.0 1.9 add.41
  181.0 2.2 collective-permute-start.30
  183.2 37.3 %conditional.3 = (f32[2,2,16,256]{3,2,1,0:T(8,128)S(1)}, f32[2,2,512,512]{3,2,1,0:T(8,128)}) conditional(s32[]{:T(128)} %bitcast.9, () %tuple.36, (f32[2,2,2,2,16,256]{5,4,1,0,3,2:T(8,128)S(1)}, f32[2,512,512]{2,1,0:T(8,128)}, f32[2,512,256]{2,1,0:T(8,128)}, f32[2,256,256]{2,1,0:T(8,128)}, f32[2,256,256]{2,1,0:T(8,128)}, ...), branch_computations={%region_2.3_spmd, %region_3.4_spmd} | conditional | flops 1229428 | bytes 10457189 | solution.py:696
  183.3 5.0 %collective-permute-done.2 = f32[2,2,2,16,256]{4,3,2,1,0:T(8,128)S(1)} collective-permute-done((f32[2,2,2,16,256]{4,3,2,1,0:T(8,128)S(1)}, f32[2,2,2,16,256]{4,3,2,1,0:T(8,128)S(1)}, u32[]{:S(2)}, u32[]{:S(2)}) %collective-permute-start.2) | collective-permute-done | bytes 131104 | tf_op jit(solution)/shard_map/cond/branch_1_fun/ppermute | solution.py:596
  188.3 7.3 %collective-permute-start.3 = (f32[2,2,2,16,256]{4,3,2,1,0:T(8,128)S(1)}, f32[2,2,2,16,256]{4,3,2,1,0:T(8,128)S(1)}, u32[]{:S(2)}, u32[]{:S(2)}) collective-permute-start(f32[2,2,2,16,256]{4,3,2,1,0:T(8,128)S(1)} %bitcast_add_fusion.1), channel_id=1, source_target_pairs={{0,2},{1,3},{2,0},{3,1},{4,6},{5,7},{6,4},{7,5},{8,10},{9,11},{10,... | collective-permute-start | bytes 393224 | tf_op jit(solution)/shard_map/cond/branch_1_fun/ppermute | solution.py:596
  195.6 4.1 %collective-permute-done.3 = f32[2,2,2,16,256]{4,3,2,1,0:T(8,128)S(1)} collective-permute-done((f32[2,2,2,16,256]{4,3,2,1,0:T(8,128)S(1)}, f32[2,2,2,16,256]{4,3,2,1,0:T(8,128)S(1)}, u32[]{:S(2)}, u32[]{:S(2)}) %collective-permute-start.3) | collective-permute-done | bytes 131104 | tf_op jit(solution)/shard_map/cond/branch_1_fun/ppermute | solution.py:596
  200.2 6.4 %collective-permute-done.4 = f32[2,2,2,16,256]{4,3,2,1,0:T(8,128)S(1)} collective-permute-done((f32[2,2,2,16,256]{4,3,2,1,0:T(8,128)S(1)}, f32[2,2,2,16,256]{4,3,2,1,0:T(8,128)S(1)}, u32[]{:S(2)}, u32[]{:S(2)}) %collective-permute-start.4) | collective-permute-done | bytes 131104 | tf_op jit(solution)/shard_map/cond/branch_1_fun/ppermute | solution.py:596
  206.6 5.8 %collective-permute-start.5 = (f32[2,2,16,256]{3,2,1,0:T(8,128)S(1)}, f32[2,2,16,256]{3,2,1,0:T(8,128)S(1)}, u32[]{:S(2)}, u32[]{:S(2)}) collective-permute-start(f32[2,2,16,256]{3,2,1,0:T(8,128)S(1)} %select_bitcast_fusion.2), channel_id=1, source_target_pairs={{0,17},{1,16},{2,19},{3,18},{4,21},{5,20},{6,23},{7,22},{8,25},{9,... | collective-permute-start | bytes 196616 | tf_op jit(solution)/shard_map/cond/branch_1_fun/ppermute | solution.py:596
  212.5 2.2 collective-permute-done.5
  216.2 4.2 %join_gradients.2 = f32[2,2,512,512]{3,2,1,0:T(8,128)} custom-call(f32[2,512,512]{2,1,0:T(8,128)} %get-tuple-element.38.main, f32[2,512,256]{2,1,0:T(8,128)} %get-tuple-element.39.right, f32[2,256,256]{2,1,0:T(8,128)} %get-tuple-element.40.low_a, f32[2,256,256]{2,1,0:T(8,128)} %get-tuple-element.41.low_b, f32[2,256,256]{2,1,0:T(8,128)} %get-tuple-element.42.diag), custom_call_target="tpu_custom_call" | custom-call | flops 1000000 | bytes 6000000 | tf_op jit(solution)/shard_map/cond/branch_1_fun/join_gradients/pallas_call | solution.py:561
  221.5 3.9 %join_gradients.3 = f32[2,2,512,512]{3,2,1,0:T(8,128)} custom-call(f32[2,512,512]{2,1,0:T(8,128)S(1)} %get-tuple-element.113.main, f32[2,512,256]{2,1,0:T(8,128)} %copy-done, f32[2,256,256]{2,1,0:T(8,128)} %collective-permute-done.30.low_a, f32[2,256,256]{2,1,0:T(8,128)} %collective-permute-done.31.low_b, ...), custom_call_target="tpu_custom_call", output_to_operand_aliasing={{}: (5, {})} | custom-call | flops 1000000 | bytes 6000000 | tf_op jit(solution)/shard_map/join_gradients/pallas_call | solution.py:561
  (84 shorter events, 34.7 us)
Async XLA Ops:
  0.6 9.1 %collective-permute-start.7 = (f32[2,2,16,256]{3,2,1,0:T(8,128)}, f32[2,2,16,256]{3,2,1,0:T(8,128)S(1)}, u32[]{:S(2)}, u32[]{:S(2)}) collective-permute-start(f32[2,2,16,256]{3,2,1,0:T(8,128)} %param.22), channel_id=1, source_target_pairs={{0,32},{1,33},{2,34},{3,35},{4,36},{5,37},{6,38},{7,39},{8,40},{9,... | collective-permute-start | bytes 196616 | tf_op jit(solution)/shard_map/ppermute | solution.py:596
  2.7 7.0 %collective-permute-start.9 = (f32[2,2,16,256]{3,2,1,0:T(8,128)}, f32[2,2,16,256]{3,2,1,0:T(8,128)S(1)}, u32[]{:S(2)}, u32[]{:S(2)}) collective-permute-start(f32[2,2,16,256]{3,2,1,0:T(8,128)} %param.22), channel_id=1, source_target_pairs={{0,96},{1,97},{2,98},{3,99},{4,100},{5,101},{6,102},{7,103},{8,104... | collective-permute-start | bytes 196616 | tf_op jit(solution)/shard_map/ppermute | solution.py:596
  5.2 6.0 %collective-permute-start.8 = (f32[2,2,16,256]{3,2,1,0:T(8,128)}, f32[2,2,16,256]{3,2,1,0:T(8,128)S(1)}, u32[]{:S(2)}, u32[]{:S(2)}) collective-permute-start(f32[2,2,16,256]{3,2,1,0:T(8,128)} %param.22), channel_id=1, source_target_pairs={{0,64},{1,65},{2,66},{3,67},{4,68},{5,69},{6,70},{7,71},{8,72},{9,... | collective-permute-start | bytes 196616 | tf_op jit(solution)/shard_map/ppermute | solution.py:596
  11.3 16.8 %collective-permute-start.10 = (f32[2,256,256]{2,1,0:T(8,128)S(1)}, f32[2,256,256]{2,1,0:T(8,128)}, u32[]{:S(2)}, u32[]{:S(2)}) collective-permute-start(f32[2,256,256]{2,1,0:T(8,128)S(1)} %get-tuple-element.90), channel_id=1, source_target_pairs={{1,0},{2,1},{3,2},{4,3},{5,4},{6,5},{7,6},{9,8},{10,9},{11,10},{12... | collective-permute-start | bytes 1572872 | tf_op jit(solution)/shard_map/ppermute | solution.py:596
  12.6 34.9 %collective-permute-start.11 = (f32[2,512,256]{2,1,0:T(8,128)S(1)}, f32[2,512,256]{2,1,0:T(8,128)}, u32[]{:S(2)}, u32[]{:S(2)}) collective-permute-start(f32[2,512,256]{2,1,0:T(8,128)S(1)} %slice_bitcast_fusion.1), channel_id=1, source_target_pairs={{8,0},{9,1},{10,2},{11,3},{12,4},{13,5},{14,6},{15,7},{16,8},{17,9... | collective-permute-start | bytes 3145736 | tf_op jit(solution)/shard_map/ppermute | solution.py:596
  20.4 27.0 %collective-permute-start.13 = (f32[2,256,256]{2,1,0:T(8,128)S(1)}, f32[2,256,256]{2,1,0:T(8,128)S(1)}, u32[]{:S(2)}, u32[]{:S(2)}) collective-permute-start(f32[2,256,256]{2,1,0:T(8,128)S(1)} %get-tuple-element.90), channel_id=1, source_target_pairs={{17,8},{18,9},{19,10},{20,11},{21,12},{22,13},{23,14},{33,24},{34,... | collective-permute-start | bytes 1572872 | tf_op jit(solution)/shard_map/ppermute | solution.py:596
  21.1 26.3 %collective-permute-start.15 = (f32[4,2,2,16,256]{4,3,2,1,0:T(8,128)S(1)}, f32[4,2,2,16,256]{4,3,2,1,0:T(8,128)}, u32[]{:S(2)}, u32[]{:S(2)}) collective-permute-start(f32[4,2,2,16,256]{4,3,2,1,0:T(8,128)S(1)} %pad_maximum_fusion.mine), channel_id=1, source_target_pairs={{0,17},{1,16},{2,19},{3,18},{4,21},{5,20},{6,23},{7,22},{8,25},{9,... | collective-permute-start | bytes 786440 | tf_op jit(solution)/shard_map/ppermute | solution.py:596
  26.8 20.6 %collective-permute-start.12 = (f32[2,256,256]{2,1,0:T(8,128)}, f32[2,256,256]{2,1,0:T(8,128)S(1)}, u32[]{:S(2)}, u32[]{:S(2)}) collective-permute-start(f32[2,256,256]{2,1,0:T(8,128)} %get-tuple-element.94), channel_id=1, source_target_pairs={{1,0},{2,1},{3,2},{4,3},{5,4},{6,5},{7,6},{9,8},{10,9},{11,10},{12... | collective-permute-start | bytes 1572872 | tf_op jit(solution)/shard_map/ppermute | solution.py:596
  28.1 19.3 %collective-permute-start.14 = (f32[2,256,256]{2,1,0:T(8,128)}, f32[2,256,256]{2,1,0:T(8,128)S(1)}, u32[]{:S(2)}, u32[]{:S(2)}) collective-permute-start(f32[2,256,256]{2,1,0:T(8,128)} %collective-permute-done.10.low_a), channel_id=1, source_target_pairs={{8,0},{9,1},{10,2},{11,3},{12,4},{13,5},{14,6},{15,7},{24,16},{25,... | collective-permute-start | bytes 1572872 | tf_op jit(solution)/shard_map/ppermute | solution.py:596
  47.5 7.7 %collective-permute-start.16 = (f32[4,2,2,16,256]{4,3,2,1,0:T(8,128)S(1)}, f32[4,2,2,16,256]{4,3,2,1,0:T(8,128)}, u32[]{:S(2)}, u32[]{:S(2)}) collective-permute-start(f32[4,2,2,16,256]{4,3,2,1,0:T(8,128)S(1)} %pad_maximum_fusion.mine), channel_id=1, source_target_pairs={{0,8},{1,9},{2,10},{3,11},{4,12},{5,13},{6,14},{7,15},{8,0},{9,1},... | collective-permute-start | bytes 786440 | tf_op jit(solution)/shard_map/ppermute | solution.py:596
  50.9 5.6 %collective-permute-start.17 = (f32[4,2,2,16,256]{4,3,2,1,0:T(8,128)}, f32[4,2,2,16,256]{4,3,2,1,0:T(8,128)}, u32[]{:S(2)}, u32[]{:S(2)}) collective-permute-start(f32[4,2,2,16,256]{4,3,2,1,0:T(8,128)} %collective-permute-done.15.across), channel_id=1, source_target_pairs={{0,8},{1,9},{2,10},{3,11},{4,12},{5,13},{6,14},{7,15},{8,0},{9,1},... | collective-permute-start | bytes 786440 | tf_op jit(solution)/shard_map/ppermute | solution.py:596
  51.9 28.7 %collective-permute-start.21 = (f32[2,256,256]{2,1,0:T(8,128)S(1)}, f32[2,256,256]{2,1,0:T(8,128)S(1)}, u32[]{:S(2)}, u32[]{:S(2)}) collective-permute-start(f32[2,256,256]{2,1,0:T(8,128)S(1)} %get-tuple-element.106), channel_id=1, source_target_pairs={{17,8},{18,9},{19,10},{20,11},{21,12},{22,13},{23,14},{33,24},{34,... | collective-permute-start | bytes 1572872 | tf_op jit(solution)/shard_map/ppermute | solution.py:596
  52.6 16.7 %collective-permute-start.19 = (f32[2,256,256]{2,1,0:T(8,128)S(1)}, f32[2,256,256]{2,1,0:T(8,128)}, u32[]{:S(2)}, u32[]{:S(2)}) collective-permute-start(f32[2,256,256]{2,1,0:T(8,128)S(1)} %get-tuple-element.106), channel_id=1, source_target_pairs={{1,0},{2,1},{3,2},{4,3},{5,4},{6,5},{7,6},{9,8},{10,9},{11,10},{12... | collective-permute-start | bytes 1572872 | tf_op jit(solution)/shard_map/ppermute | solution.py:596
  53.9 26.7 %collective-permute-start.20 = (f32[2,256,256]{2,1,0:T(8,128)S(1)}, f32[2,256,256]{2,1,0:T(8,128)}, u32[]{:S(2)}, u32[]{:S(2)}) collective-permute-start(f32[2,256,256]{2,1,0:T(8,128)S(1)} %get-tuple-element.109), channel_id=1, source_target_pairs={{1,0},{2,1},{3,2},{4,3},{5,4},{6,5},{7,6},{9,8},{10,9},{11,10},{12... | collective-permute-start | bytes 1572872 | tf_op jit(solution)/shard_map/ppermute | solution.py:596
  55.2 25.4 %collective-permute-start.18 = (f32[2,512,256]{2,1,0:T(8,128)S(1)}, f32[2,512,256]{2,1,0:T(8,128)S(1)}, u32[]{:S(2)}, u32[]{:S(2)}) collective-permute-start(f32[2,512,256]{2,1,0:T(8,128)S(1)} %slice_bitcast_fusion), channel_id=1, source_target_pairs={{8,0},{9,1},{10,2},{11,3},{12,4},{13,5},{14,6},{15,7},{16,8},{17,9... | collective-permute-start | bytes 3145736 | tf_op jit(solution)/shard_map/ppermute | solution.py:596
  69.4 11.3 %collective-permute-start.22 = (f32[2,256,256]{2,1,0:T(8,128)}, f32[2,256,256]{2,1,0:T(8,128)}, u32[]{:S(2)}, u32[]{:S(2)}) collective-permute-start(f32[2,256,256]{2,1,0:T(8,128)} %collective-permute-done.19.low_a), channel_id=1, source_target_pairs={{8,0},{9,1},{10,2},{11,3},{12,4},{13,5},{14,6},{15,7},{24,16},{25,... | collective-permute-start | bytes 1572872 | tf_op jit(solution)/shard_map/ppermute | solution.py:596
  99.3 18.4 %collective-permute-start.24 = (f32[2,256,256]{2,1,0:T(8,128)}, f32[2,256,256]{2,1,0:T(8,128)S(1)}, u32[]{:S(2)}, u32[]{:S(2)}) collective-permute-start(f32[2,256,256]{2,1,0:T(8,128)} %get-tuple-element.121), channel_id=1, source_target_pairs={{0,8},{1,9},{2,10},{3,11},{4,12},{5,13},{6,14},{7,15},{16,24},{17,... | collective-permute-start | bytes 1572872 | tf_op jit(solution)/shard_map/ppermute | solution.py:596
  111.8 60.2 %collective-permute-start.23 = (f32[2,512,256]{2,1,0:T(8,128)}, f32[2,512,256]{2,1,0:T(8,128)}, u32[]{:S(2)}, u32[]{:S(2)}) collective-permute-start(f32[2,512,256]{2,1,0:T(8,128)} %get-tuple-element.119), channel_id=1, source_target_pairs={{0,8},{1,9},{2,10},{3,11},{4,12},{5,13},{6,14},{7,15},{8,16},{9,17... | collective-permute-start | bytes 3145736 | tf_op jit(solution)/shard_map/ppermute | solution.py:596
  114.1 57.8 %collective-permute-start.27 = (f32[2,256,256]{2,1,0:T(8,128)}, f32[2,256,256]{2,1,0:T(8,128)}, u32[]{:S(2)}, u32[]{:S(2)}) collective-permute-start(f32[2,256,256]{2,1,0:T(8,128)} %get-tuple-element.121), channel_id=1, source_target_pairs={{8,17},{9,18},{10,19},{11,20},{12,21},{13,22},{14,23},{24,33},{25,... | collective-permute-start | bytes 1572872 | tf_op jit(solution)/shard_map/ppermute | solution.py:596
  115.6 56.4 %collective-permute-start.26 = (f32[2,256,256]{2,1,0:T(8,128)}, f32[2,256,256]{2,1,0:T(8,128)}, u32[]{:S(2)}, u32[]{:S(2)}) collective-permute-start(f32[2,256,256]{2,1,0:T(8,128)} %get-tuple-element.122), channel_id=1, source_target_pairs={{0,1},{1,2},{2,3},{3,4},{4,5},{5,6},{6,7},{8,9},{9,10},{10,11},{11... | collective-permute-start | bytes 1572872 | tf_op jit(solution)/shard_map/ppermute | solution.py:596
  119.6 52.4 %collective-permute-start.25 = (f32[2,256,256]{2,1,0:T(8,128)}, f32[2,256,256]{2,1,0:T(8,128)}, u32[]{:S(2)}, u32[]{:S(2)}) collective-permute-start(f32[2,256,256]{2,1,0:T(8,128)} %add.40), channel_id=1, source_target_pairs={{0,1},{1,2},{2,3},{3,4},{4,5},{5,6},{6,7},{8,9},{9,10},{10,11},{11... | collective-permute-start | bytes 1572872 | tf_op jit(solution)/shard_map/ppermute | solution.py:596
  137.5 7.6 %collective-permute-start = (f32[4,2,2,2,16,256]{5,4,1,0,3,2:T(8,128)}, f32[4,2,2,2,16,256]{5,4,1,0,3,2:T(8,128)}, u32[]{:S(2)}, u32[]{:S(2)}) collective-permute-start(f32[4,2,2,2,16,256]{5,4,1,0,3,2:T(8,128)} %select_bitcast_fusion), channel_id=1, source_target_pairs={{0,8},{1,9},{2,10},{3,11},{4,12},{5,13},{6,14},{7,15},{8,0},{9,1},... | collective-permute-start | bytes 1572872 | tf_op jit(solution)/shard_map/cond/branch_1_fun/ppermute | solution.py:596
  146.4 25.3 %collective-permute-start.1 = (f32[2,2,2,2,16,256]{5,4,1,0,3,2:T(8,128)S(1)}, f32[2,2,2,2,16,256]{5,4,1,0,3,2:T(8,128)S(1)}, u32[]{:S(2)}, u32[]{:S(2)}) collective-permute-start(f32[2,2,2,2,16,256]{5,4,1,0,3,2:T(8,128)S(1)} %slice_select_fusion), channel_id=1, source_target_pairs={{0,64},{1,65},{2,66},{3,67},{4,68},{5,69},{6,70},{7,71},{8,72},{9,... | collective-permute-start | bytes 786440 | tf_op jit(solution)/shard_map/cond/branch_1_fun/ppermute | solution.py:596
  172.0 7.0 %collective-permute-start.29 = (f32[2,256,256]{2,1,0:T(8,128)}, f32[2,256,256]{2,1,0:T(8,128)S(1)}, u32[]{:S(2)}, u32[]{:S(2)}) collective-permute-start(f32[2,256,256]{2,1,0:T(8,128)} %get-tuple-element.125), channel_id=1, source_target_pairs={{0,8},{1,9},{2,10},{3,11},{4,12},{5,13},{6,14},{7,15},{16,24},{17,... | collective-permute-start | bytes 1572872 | tf_op jit(solution)/shard_map/ppermute | solution.py:596
  173.8 46.8 %collective-permute-start.28 = (f32[2,512,256]{2,1,0:T(8,128)}, f32[2,512,256]{2,1,0:T(8,128)S(1)}, u32[]{:S(2)}, u32[]{:S(2)}) collective-permute-start(f32[2,512,256]{2,1,0:T(8,128)} %get-tuple-element.123), channel_id=1, source_target_pairs={{0,8},{1,9},{2,10},{3,11},{4,12},{5,13},{6,14},{7,15},{8,16},{9,17... | collective-permute-start | bytes 3145736 | tf_op jit(solution)/shard_map/ppermute | solution.py:596
  175.1 45.4 %collective-permute-start.32 = (f32[2,256,256]{2,1,0:T(8,128)}, f32[2,256,256]{2,1,0:T(8,128)}, u32[]{:S(2)}, u32[]{:S(2)}) collective-permute-start(f32[2,256,256]{2,1,0:T(8,128)} %get-tuple-element.125), channel_id=1, source_target_pairs={{8,17},{9,18},{10,19},{11,20},{12,21},{13,22},{14,23},{24,33},{25,... | collective-permute-start | bytes 1572872 | tf_op jit(solution)/shard_map/ppermute | solution.py:596
  176.6 43.9 %collective-permute-start.31 = (f32[2,256,256]{2,1,0:T(8,128)}, f32[2,256,256]{2,1,0:T(8,128)}, u32[]{:S(2)}, u32[]{:S(2)}) collective-permute-start(f32[2,256,256]{2,1,0:T(8,128)} %get-tuple-element.126), channel_id=1, source_target_pairs={{0,1},{1,2},{2,3},{3,4},{4,5},{5,6},{6,7},{8,9},{9,10},{10,11},{11... | collective-permute-start | bytes 1572872 | tf_op jit(solution)/shard_map/ppermute | solution.py:596
  181.0 39.6 %collective-permute-start.30 = (f32[2,256,256]{2,1,0:T(8,128)}, f32[2,256,256]{2,1,0:T(8,128)}, u32[]{:S(2)}, u32[]{:S(2)}) collective-permute-start(f32[2,256,256]{2,1,0:T(8,128)} %add.41), channel_id=1, source_target_pairs={{0,1},{1,2},{2,3},{3,4},{4,5},{5,6},{6,7},{8,9},{9,10},{10,11},{11... | collective-permute-start | bytes 1572872 | tf_op jit(solution)/shard_map/ppermute | solution.py:596
  188.3 11.4 %collective-permute-start.3 = (f32[2,2,2,16,256]{4,3,2,1,0:T(8,128)S(1)}, f32[2,2,2,16,256]{4,3,2,1,0:T(8,128)S(1)}, u32[]{:S(2)}, u32[]{:S(2)}) collective-permute-start(f32[2,2,2,16,256]{4,3,2,1,0:T(8,128)S(1)} %bitcast_add_fusion.1), channel_id=1, source_target_pairs={{0,2},{1,3},{2,0},{3,1},{4,6},{5,7},{6,4},{7,5},{8,10},{9,11},{10,... | collective-permute-start | bytes 393224 | tf_op jit(solution)/shard_map/cond/branch_1_fun/ppermute | solution.py:596
  199.7 6.9 %collective-permute-start.4 = (f32[2,2,2,16,256]{4,3,2,1,0:T(8,128)S(1)}, f32[2,2,2,16,256]{4,3,2,1,0:T(8,128)S(1)}, u32[]{:S(2)}, u32[]{:S(2)}) collective-permute-start(f32[2,2,2,16,256]{4,3,2,1,0:T(8,128)S(1)} %add.34), channel_id=1, source_target_pairs={{0,4},{1,5},{2,6},{3,7},{4,0},{5,1},{6,2},{7,3},{8,12},{9,13},{10,... | collective-permute-start | bytes 393224 | tf_op jit(solution)/shard_map/cond/branch_1_fun/ppermute | solution.py:596
  206.6 8.1 %collective-permute-start.5 = (f32[2,2,16,256]{3,2,1,0:T(8,128)S(1)}, f32[2,2,16,256]{3,2,1,0:T(8,128)S(1)}, u32[]{:S(2)}, u32[]{:S(2)}) collective-permute-start(f32[2,2,16,256]{3,2,1,0:T(8,128)S(1)} %select_bitcast_fusion.2), channel_id=1, source_target_pairs={{0,17},{1,16},{2,19},{3,18},{4,21},{5,20},{6,23},{7,22},{8,25},{9,... | collective-permute-start | bytes 196616 | tf_op jit(solution)/shard_map/cond/branch_1_fun/ppermute | solution.py:596
  214.7 5.8 %collective-permute-start.6 = (f32[2,2,16,256]{3,2,1,0:T(8,128)S(1)}, f32[2,2,16,256]{3,2,1,0:T(8,128)S(1)}, u32[]{:S(2)}, u32[]{:S(2)}) collective-permute-start(f32[2,2,16,256]{3,2,1,0:T(8,128)S(1)} %bitcast_add_fusion.2), channel_id=1, source_target_pairs={{0,1},{1,0},{2,3},{3,2},{4,5},{5,4},{6,7},{7,6},{8,9},{9,8},{10,11... | collective-permute-start | bytes 196616 | tf_op jit(solution)/shard_map/cond/branch_1_fun/ppermute | solution.py:596
  (11 other events, 108.2 us)

commit v5 on v4

--- a/solution.py
+++ b/solution.py
@@ -16,7 +16,7 @@
 SLOTS = 6
 F32 = jnp.float32
 BF16 = jnp.bfloat16
-VMEM_LIMIT = 60 * 1024 * 1024
+VMEM_LIMIT = 48 * 1024 * 1024
 
 
 def split_table(mat):
@@ -642,13 +642,15 @@
         give = jnp.where(bit == 0, part[1], part[0])
         return keep + send(give, there)
 
-    def reduce_rest(part):
-        gx = lax.axis_index("gx")
-        z = gx // 4
-        part = halved(part, z % 2, flip(4, 0))
+    def reduce_z(part):
+        z = lax.axis_index("gx") // 4
+        part = halved(part.reshape(2, 2, *part.shape[1:]), z // 2, flip(8, 0))
+        return halved(part, z % 2, flip(4, 0))
+
+    def reduce_xy(part):
         for bit in (2, 4):
             part = part + send(part, flip(0, bit))
-        part = halved(part, gx // 2 % 2, flip(2, 1))
+        part = halved(part, lax.axis_index("gx") // 2 % 2, flip(2, 1))
         return part + send(part, flip(0, 1))
 
     def on_device(obj, probe, positions, counts, amplitudes):
@@ -658,12 +660,12 @@
         )
         pieces_0, mine = lax.optimization_barrier((pieces(obj, 0), gather_probe(probe)))
         halo_0 = bring(*pieces_0)
-        probe_parts = mine, send(mine, flip(2, 1))
+        across = send(mine, flip(2, 1))
+        probe_parts = [mine, across, send(mine, flip(1, 0)), send(across, flip(1, 0))]
         obj_late, low_a = lax.optimization_barrier((obj, halo_0[1]))
         halo_0 = (halo_0[0], low_a, *halo_0[2:], bring_side(low_a))
         amp = permute_amplitudes(amplitudes[0, 0], tables)
         pieces_1, halo_0, amp, probe_parts = lax.optimization_barrier((pieces(obj_late, 1), halo_0, amp, probe_parts))
-        probe_parts = [*probe_parts, *(send(x, flip(1, 0)) for x in probe_parts)]
         right, low_a, *others = bring(*pieces_1)
         psi, win, probe_rows = run_out(scalars, obj, halo_0, probe_parts, tables)
         low_a, psi = lax.optimization_barrier((low_a, psi))
@@ -675,9 +677,7 @@
 
         def home(operands):
             g_probe, *fields = run_home(*operands, tables)
-            part = reduce_chip(g_probe)
-            part = part.reshape(2, 2, *part.shape[1:])
-            return halved(part, lax.axis_index("gx") // 8, flip(8, 0)), *fields
+            return reduce_chip(g_probe), *fields
 
         def idle(operands):
             return tuple(jnp.zeros(x.shape, x.dtype) for x in jax.eval_shape(home, operands))
@@ -688,7 +688,8 @@
 
         def rest(operands):
             part, main, back = operands
-            return reduce_rest(part), run_join(1, main, back, None)
+            part, grad = lax.optimization_barrier((reduce_z(part), run_join(1, main, back, None)))
+            return reduce_xy(part), grad
 
         def nothing(operands):
             return tuple(jnp.zeros(x.shape, x.dtype) for x in jax.eval_shape(rest, operands))

time: 230 us -> 225 us (0.978); the launches traced: 225 us -> 223 us
  waiting for transfers between devices: 53.8 us -> 63.1 us
  Pallas kernels: 56.1 us -> 48.4 us
  starting transfers between devices: 97.8 us -> 92.5 us
  local copies, waits for them, and re-layouts: 9.7 us -> 14 us
  other arithmetic: 6.16 us -> 2.88 us
    ppermute x33, waiting for transfers between devices: 53.8 us -> 63.1 us  [send(): return lax.ppermute(x, axes, pairs)]
    ppermute x33, starting transfers between devices: 97.8 us -> 92.5 us  [send(): return lax.ppermute(x, axes, pairs)]
    pallas_call x1, Pallas kernels: 6.52 us -> 3.66 us  [permute_amplitudes(): pl.pallas_call(amp_kernel, grid=(SLOTS,), in_specs=[pl.BlockSpec((1, n, n...]
  transfers between devices with their start and end apart: 33 -> 33, of which waited for: 10 -> 13; matrix products, arithmetic and copies ran while one was open for 6% -> 5% of each run, Pallas kernels for 15% -> 13%
where the time goes in v5:
time: 225 us; the launch traced here: 223 us
  starting transfers between devices  92.5 us (41%)
  waiting for transfers between devices  63.1 us (28%)
  Pallas kernels  48.4 us (22%)
  local copies, waits for them, and re-layouts  14 us (6%)
  other arithmetic  2.88 us (1%)
    ppermute x33, starting transfers between devices, send(): return lax.ppermute(x, axes, pairs)  92.5 us
    ppermute x33, waiting for transfers between devices, send(): return lax.ppermute(x, axes, pairs)  63.1 us
    pallas_call x1, Pallas kernels, run_far(): pl.pallas_call(far_kernel, grid_spec=pltpu.PrefetchScalarGridSpec(num_sca...  16 us
    pallas_call x1, Pallas kernels, run_home(): pl.pallas_call(home_kernel, grid_spec=pltpu.PrefetchScalarGridSpec(num_sc...  10.4 us
    pallas_call x1, Pallas kernels, run_out(): pl.pallas_call(out_kernel, grid_spec=pltpu.PrefetchScalarGridSpec(num_sca...  10.2 us
    pallas_call x2, Pallas kernels, run_join(): pl.pallas_call(join_kernel, grid=(4,), in_specs=[pl.BlockSpec((2, h, TILE...  8.11 us
    squeeze x4, local copies, waits for them, and re-layouts, pieces(): return (obj[layer, :, :n, :n], obj[layer, :, :, :n], obj[layer, :, :n, n:])  7.17 us
  transfers between devices with their start and end apart: 33, of which 13 were waited for; matrix products, arithmetic and copies ran while one was open for 5% of the time, Pallas kernels for 13%

profile of v5, /device:TPU:0, one launch (start us, length us, event | category | flops | bytes accessed | tf_op | source)
XLA Modules:
  0.0 223.0 jit_solution(3476767749551613582)
XLA Ops:
  0.7 2.1 collective-permute-start.7
  2.7 2.5 %collective-permute-start.9 = (f32[2,2,16,256]{3,2,1,0:T(8,128)}, f32[2,2,16,256]{3,2,1,0:T(8,128)S(1)}, u32[]{:S(2)}, u32[]{:S(2)}) collective-permute-start(f32[2,2,16,256]{3,2,1,0:T(8,128)} %param.22), channel_id=1, source_target_pairs={{0,96},{1,97},{2,98},{3,99},{4,100},{5,101},{6,102},{7,103},{8,104... | collective-permute-start | bytes 196616 | tf_op jit(solution)/shard_map/ppermute | solution.py:596
  6.3 2.3 %slice_bitcast_fusion.1 = f32[2,512,256]{2,1,0:T(8,128)} fusion(f32[2,2,512,512]{3,2,1,0:T(8,128)} %obj.3), kind=kLoop, calls=%fused_computation.10 | loop fusion | bytes 2097152 | tf_op jit(solution)/shard_map/squeeze | solution.py:603
  8.6 2.3 %slice_bitcast_fusion.4 = (f32[2,256,256]{2,1,0:T(8,128)}, f32[2,256,256]{2,1,0:T(8,128)}) fusion(f32[2,2,512,512]{3,2,1,0:T(8,128)} %obj.3), kind=kLoop, calls=%fused_computation.13 | loop fusion | bytes 2097152 | tf_op jit(solution)/shard_map/squeeze | solution.py:603
  18.0 3.7 %order_amplitudes.1.amp = f32[6,256,256]{2,1,0:T(8,128)S(1)} custom-call(f32[6,256,256]{2,1,0:T(8,128)S(1)} %bitcast.41, bf16[256,768]{1,0:T(8,128)(2,1)S(1)} %copy-done.10, bf16[768,256]{1,0:T(8,128)(2,1)S(1)} %copy-done.9), custom_call_target="tpu_custom_call" | custom-call | flops 1200000000 | bytes 4000000 | tf_op jit(solution)/shard_map/order_amplitudes/pallas_call | solution.py:465
  22.8 4.4 %collective-permute-start.15 = (f32[4,2,2,16,256]{4,3,2,1,0:T(8,128)S(1)}, f32[4,2,2,16,256]{4,3,2,1,0:T(8,128)S(1)}, u32[]{:S(2)}, u32[]{:S(2)}) collective-permute-start(f32[4,2,2,16,256]{4,3,2,1,0:T(8,128)S(1)} %pad_maximum_fusion.mine), channel_id=1, source_target_pairs={{0,17},{1,16},{2,19},{3,18},{4,21},{5,20},{6,23},{7,22},{8,25},{9,... | collective-permute-start | bytes 786440 | tf_op jit(solution)/shard_map/ppermute | solution.py:596
  31.8 9.7 %collective-permute-done.15.across = f32[4,2,2,16,256]{4,3,2,1,0:T(8,128)S(1)} collective-permute-done((f32[4,2,2,16,256]{4,3,2,1,0:T(8,128)S(1)}, f32[4,2,2,16,256]{4,3,2,1,0:T(8,128)S(1)}, u32[]{:S(2)}, u32[]{:S(2)}) %collective-permute-start.15) | collective-permute-done | bytes 262176 | tf_op jit(solution)/shard_map/ppermute | solution.py:596
  48.8 10.2 %propagate_out.1 = (f32[6,2,2,256,256]{4,3,2,1,0:T(8,128)}, f32[6,2,256,256]{3,2,1,0:T(8,128)}, f32[2,2,4,2,2,16,256]{6,5,4,3,2,1,0:T(8,128)}) custom-call(s32[16]{0:T(128)S(1)} %concatenate.3.scalars, f32[2,2,512,512]{3,2,1,0:T(8,128)} %obj.3, f32[2,512,256]{2,1,0:T(8,128)S(1)} %collective-permute-done.11.right, ...), custom_call_target="tpu_custom_call" | custom-call | flops 60000002048 | bytes 20000000 | tf_op jit(solution)/shard_map/propagate_out/pallas_call | solution.py:483
  59.0 7.2 %collective-permute-done.19.low_a = f32[2,256,256]{2,1,0:T(8,128)S(1)} collective-permute-done((f32[2,256,256]{2,1,0:T(8,128)S(1)}, f32[2,256,256]{2,1,0:T(8,128)S(1)}, u32[]{:S(2)}, u32[]{:S(2)}) %collective-permute-start.19) | collective-permute-done | bytes 524320 | tf_op jit(solution)/shard_map/ppermute | solution.py:596
  67.6 9.9 %collective-permute-done.20.low_b = f32[2,256,256]{2,1,0:T(8,128)S(1)} collective-permute-done((f32[2,256,256]{2,1,0:T(8,128)S(1)}, f32[2,256,256]{2,1,0:T(8,128)S(1)}, u32[]{:S(2)}, u32[]{:S(2)}) %collective-permute-start.20) | collective-permute-done | bytes 524320 | tf_op jit(solution)/shard_map/ppermute | solution.py:596
  78.6 16.0 %far_field.1 = (f32[6,2,2,256,256]{4,3,2,1,0:T(8,128)}, f32[2,512,512]{2,1,0:T(8,128)}, f32[2,512,256]{2,1,0:T(8,128)}, f32[2,256,256]{2,1,0:T(8,128)S(1)}, f32[...) custom-call(s32[16]{0:T(128)S(1)} %concatenate.3.scalars, f32[2,2,512,512]{3,2,1,0:T(8,128)} %obj.3, ...), custom_call_target="tpu_custom_call" | custom-call | flops 60000002048 | bytes 20000000 | tf_op jit(solution)/shard_map/far_field/pallas_call | solution.py:505
  94.6 15.0 %collective-permute-start.24 = (f32[2,256,256]{2,1,0:T(8,128)S(1)}, f32[2,256,256]{2,1,0:T(8,128)S(1)}, u32[]{:S(2)}, u32[]{:S(2)}) collective-permute-start(f32[2,256,256]{2,1,0:T(8,128)S(1)} %get-tuple-element.127), channel_id=1, source_target_pairs={{0,8},{1,9},{2,10},{3,11},{4,12},{5,13},{6,14},{7,15},{16,24},{17,... | collective-permute-start | bytes 1572872 | tf_op jit(solution)/shard_map/ppermute | solution.py:596
  109.5 2.3 %collective-permute-start.23 = (f32[2,512,256]{2,1,0:T(8,128)}, f32[2,512,256]{2,1,0:T(8,128)}, u32[]{:S(2)}, u32[]{:S(2)}) collective-permute-start(f32[2,512,256]{2,1,0:T(8,128)} %get-tuple-element.125), channel_id=1, source_target_pairs={{0,8},{1,9},{2,10},{3,11},{4,12},{5,13},{6,14},{7,15},{8,16},{9,17... | collective-permute-start | bytes 3145736 | tf_op jit(solution)/shard_map/ppermute | solution.py:596
  113.3 3.2 %collective-permute-start.26 = (f32[2,256,256]{2,1,0:T(8,128)S(1)}, f32[2,256,256]{2,1,0:T(8,128)}, u32[]{:S(2)}, u32[]{:S(2)}) collective-permute-start(f32[2,256,256]{2,1,0:T(8,128)S(1)} %get-tuple-element.128), channel_id=1, source_target_pairs={{0,1},{1,2},{2,3},{3,4},{4,5},{5,6},{6,7},{8,9},{9,10},{10,11},{11... | collective-permute-start | bytes 1572872 | tf_op jit(solution)/shard_map/ppermute | solution.py:596
  117.4 5.4 %collective-permute-start.25 = (f32[2,256,256]{2,1,0:T(8,128)}, f32[2,256,256]{2,1,0:T(8,128)}, u32[]{:S(2)}, u32[]{:S(2)}) collective-permute-start(f32[2,256,256]{2,1,0:T(8,128)} %add.40), channel_id=1, source_target_pairs={{0,1},{1,2},{2,3},{3,4},{4,5},{5,6},{6,7},{8,9},{9,10},{10,11},{11... | collective-permute-start | bytes 1572872 | tf_op jit(solution)/shard_map/ppermute | solution.py:596
  122.9 17.5 %conditional.2 = (f32[4,2,2,2,16,256]{5,4,1,0,3,2:T(8,128)S(1)}, f32[2,512,512]{2,1,0:T(8,128)}, f32[2,512,256]{2,1,0:T(8,128)}, f32[2,256,256]{2,1,0:T(8,128)S(...) conditional(s32[]{:T(128)} %bitcast.9, () %tuple.30, (f32[2,2,4,2,2,16,256]{6,5,4,3,2,1,0:T(8,128)}, ...), branch_computations={%region_0.0_spmd, %region_1.2_spmd} | conditional | flops 60000395264 | bytes 34156064 | solution.py:685
  125.1 10.4 %propagate_home.1 = (f32[2,2,256,256]{3,2,1,0:T(8,128)S(1)}, f32[2,512,512]{2,1,0:T(8,128)}, f32[2,512,256]{2,1,0:T(8,128)}, f32[2,256,256]{2,1,0:T(8,128)S(1)},...) custom-call(s32[16]{0:T(128)S(1)} %get-tuple-element.25.scalars, f32[6,2,256,256]{3,2,1,0:T(8,128)} %get-tuple-element.26.win, ...), custom_call_target="tpu_custom_call" | custom-call | flops 60000002048 | bytes 20000000 | tf_op jit(solution)/shard_map/cond/branch_1_fun/propagate_home/pallas_call | solution.py:535
  135.8 2.7 %collective-permute-start = (f32[4,2,2,2,16,256]{5,4,1,0,3,2:T(8,128)S(1)}, f32[4,2,2,2,16,256]{5,4,1,0,3,2:T(8,128)S(1)}, u32[]{:S(2)}, u32[]{:S(2)}) collective-permute-start(f32[4,2,2,2,16,256]{5,4,1,0,3,2:T(8,128)S(1)} %select_bitcast_fusion), channel_id=1, source_target_pairs={{0,8},{1,9},{2,10},{3,11},{4,12},{5,13},{6,14},{7,15},{8,0},{9,1},... | collective-permute-start | bytes 1572872 | tf_op jit(solution)/shard_map/cond/branch_1_fun/ppermute | solution.py:596
  138.5 1.5 collective-permute-done
  140.4 12.3 %collective-permute-start.29 = (f32[2,256,256]{2,1,0:T(8,128)}, f32[2,256,256]{2,1,0:T(8,128)S(1)}, u32[]{:S(2)}, u32[]{:S(2)}) collective-permute-start(f32[2,256,256]{2,1,0:T(8,128)} %get-tuple-element.131), channel_id=1, source_target_pairs={{0,8},{1,9},{2,10},{3,11},{4,12},{5,13},{6,14},{7,15},{16,24},{17,... | collective-permute-start | bytes 1572872 | tf_op jit(solution)/shard_map/ppermute | solution.py:596
  154.8 4.1 %collective-permute-start.31 = (f32[2,256,256]{2,1,0:T(8,128)}, f32[2,256,256]{2,1,0:T(8,128)S(1)}, u32[]{:S(2)}, u32[]{:S(2)}) collective-permute-start(f32[2,256,256]{2,1,0:T(8,128)} %get-tuple-element.132), channel_id=1, source_target_pairs={{0,1},{1,2},{2,3},{3,4},{4,5},{5,6},{6,7},{8,9},{9,10},{10,11},{11... | collective-permute-start | bytes 1572872 | tf_op jit(solution)/shard_map/ppermute | solution.py:596
  159.8 1.9 collective-permute-start.30
  161.7 57.4 %conditional.3 = (f32[2,2,16,256]{3,2,1,0:T(8,128)S(1)}, f32[2,2,512,512]{3,2,1,0:T(8,128)}) conditional(s32[]{:T(128)} %bitcast.9, () %tuple.37, (f32[4,2,2,2,16,256]{5,4,1,0,3,2:T(8,128)S(1)}, f32[2,512,512]{2,1,0:T(8,128)}, f32[2,512,256]{2,1,0:T(8,128)}, f32[2,256,256]{2,1,0:T(8,128)}, f32[2,256,256]{2,1,0:T(8,128)}, ...), branch_computations={%region_2.3_spmd, %region_3.4_spmd} | conditional | flops 1426045 | bytes 13340902 | solution.py:697
  162.5 10.3 %collective-permute-start.1 = (f32[2,2,2,2,16,256]{5,4,3,2,1,0:T(8,128)}, f32[2,2,2,2,16,256]{5,4,3,2,1,0:T(8,128)S(1)}, u32[]{:S(2)}, u32[]{:S(2)}) collective-permute-start(f32[2,2,2,2,16,256]{5,4,3,2,1,0:T(8,128)} %slice_select_fusion), channel_id=1, source_target_pairs={{0,64},{1,65},{2,66},{3,67},{4,68},{5,69},{6,70},{7,71},{8,72},{9,... | collective-permute-start | bytes 786440 | tf_op jit(solution)/shard_map/cond/branch_1_fun/ppermute | solution.py:596
  172.8 14.9 %collective-permute-done.1 = f32[2,2,2,2,16,256]{5,4,3,2,1,0:T(8,128)S(1)} collective-permute-done((f32[2,2,2,2,16,256]{5,4,3,2,1,0:T(8,128)}, f32[2,2,2,2,16,256]{5,4,3,2,1,0:T(8,128)S(1)}, u32[]{:S(2)}, u32[]{:S(2)}) %collective-permute-start.1) | collective-permute-done | bytes 262176 | tf_op jit(solution)/shard_map/cond/branch_1_fun/ppermute | solution.py:596
  187.9 4.2 %join_gradients.2 = f32[2,2,512,512]{3,2,1,0:T(8,128)} custom-call(f32[2,512,512]{2,1,0:T(8,128)} %get-tuple-element.38.main, f32[2,512,256]{2,1,0:T(8,128)} %get-tuple-element.39.right, f32[2,256,256]{2,1,0:T(8,128)} %get-tuple-element.40.low_a, f32[2,256,256]{2,1,0:T(8,128)} %get-tuple-element.41.low_b, f32[2,256,256]{2,1,0:T(8,128)} %get-tuple-element.42.diag), custom_call_target="tpu_custom_call" | custom-call | flops 1000000 | bytes 6000000 | tf_op jit(solution)/shard_map/cond/branch_1_fun/join_gradients/pallas_call | solution.py:561
  192.8 6.7 %collective-permute-start.3 = (f32[2,2,2,16,256]{4,3,2,1,0:T(8,128)S(1)}, f32[2,2,2,16,256]{4,3,2,1,0:T(8,128)S(1)}, u32[]{:S(2)}, u32[]{:S(2)}) collective-permute-start(f32[2,2,2,16,256]{4,3,2,1,0:T(8,128)S(1)} %bitcast_add_fusion.1), channel_id=1, source_target_pairs={{0,2},{1,3},{2,0},{3,1},{4,6},{5,7},{6,4},{7,5},{8,10},{9,11},{10,... | collective-permute-start | bytes 393224 | tf_op jit(solution)/shard_map/cond/branch_1_fun/ppermute | solution.py:596
  199.6 3.0 %collective-permute-done.3 = f32[2,2,2,16,256]{4,3,2,1,0:T(8,128)S(1)} collective-permute-done((f32[2,2,2,16,256]{4,3,2,1,0:T(8,128)S(1)}, f32[2,2,2,16,256]{4,3,2,1,0:T(8,128)S(1)}, u32[]{:S(2)}, u32[]{:S(2)}) %collective-permute-start.3) | collective-permute-done | bytes 131104 | tf_op jit(solution)/shard_map/cond/branch_1_fun/ppermute | solution.py:596
  204.1 5.1 %collective-permute-done.4 = f32[2,2,2,16,256]{4,3,2,1,0:T(8,128)S(1)} collective-permute-done((f32[2,2,2,16,256]{4,3,2,1,0:T(8,128)S(1)}, f32[2,2,2,16,256]{4,3,2,1,0:T(8,128)S(1)}, u32[]{:S(2)}, u32[]{:S(2)}) %collective-permute-start.4) | collective-permute-done | bytes 131104 | tf_op jit(solution)/shard_map/cond/branch_1_fun/ppermute | solution.py:596
  209.3 5.5 %collective-permute-done.5 = f32[2,2,16,256]{3,2,1,0:T(8,128)S(1)} collective-permute-done((f32[2,2,16,256]{3,2,1,0:T(8,128)S(1)}, f32[2,2,16,256]{3,2,1,0:T(8,128)S(1)}, u32[]{:S(2)}, u32[]{:S(2)}) %collective-permute-start.5) | collective-permute-done | bytes 65568 | tf_op jit(solution)/shard_map/cond/branch_1_fun/ppermute | solution.py:596
  215.0 4.1 %collective-permute-done.6 = f32[2,2,16,256]{3,2,1,0:T(8,128)S(1)} collective-permute-done((f32[2,2,16,256]{3,2,1,0:T(8,128)S(1)}, f32[2,2,16,256]{3,2,1,0:T(8,128)S(1)}, u32[]{:S(2)}, u32[]{:S(2)}) %collective-permute-start.6) | collective-permute-done | bytes 65568 | tf_op jit(solution)/shard_map/cond/branch_1_fun/ppermute | solution.py:596
  219.2 3.9 %join_gradients.3 = f32[2,2,512,512]{3,2,1,0:T(8,128)} custom-call(f32[2,512,512]{2,1,0:T(8,128)} %get-tuple-element.119.main, f32[2,512,256]{2,1,0:T(8,128)S(1)} %collective-permute-done.28.right, f32[2,256,256]{2,1,0:T(8,128)S(1)} %collective-permute-done.30.low_a, ...), custom_call_target="tpu_custom_call", output_to_operand_aliasing={{}: (5, {})} | custom-call | flops 1000000 | bytes 6000000 | tf_op jit(solution)/shard_map/join_gradients/pallas_call | solution.py:561
  (102 shorter events, 34.1 us)
Async XLA Ops:
  0.7 10.2 %collective-permute-start.7 = (f32[2,2,16,256]{3,2,1,0:T(8,128)}, f32[2,2,16,256]{3,2,1,0:T(8,128)S(1)}, u32[]{:S(2)}, u32[]{:S(2)}) collective-permute-start(f32[2,2,16,256]{3,2,1,0:T(8,128)} %param.22), channel_id=1, source_target_pairs={{0,32},{1,33},{2,34},{3,35},{4,36},{5,37},{6,38},{7,39},{8,40},{9,... | collective-permute-start | bytes 196616 | tf_op jit(solution)/shard_map/ppermute | solution.py:596
  2.7 8.2 %collective-permute-start.9 = (f32[2,2,16,256]{3,2,1,0:T(8,128)}, f32[2,2,16,256]{3,2,1,0:T(8,128)S(1)}, u32[]{:S(2)}, u32[]{:S(2)}) collective-permute-start(f32[2,2,16,256]{3,2,1,0:T(8,128)} %param.22), channel_id=1, source_target_pairs={{0,96},{1,97},{2,98},{3,99},{4,100},{5,101},{6,102},{7,103},{8,104... | collective-permute-start | bytes 196616 | tf_op jit(solution)/shard_map/ppermute | solution.py:596
  5.3 6.0 %collective-permute-start.8 = (f32[2,2,16,256]{3,2,1,0:T(8,128)}, f32[2,2,16,256]{3,2,1,0:T(8,128)S(1)}, u32[]{:S(2)}, u32[]{:S(2)}) collective-permute-start(f32[2,2,16,256]{3,2,1,0:T(8,128)} %param.22), channel_id=1, source_target_pairs={{0,64},{1,65},{2,66},{3,67},{4,68},{5,69},{6,70},{7,71},{8,72},{9,... | collective-permute-start | bytes 196616 | tf_op jit(solution)/shard_map/ppermute | solution.py:596
  11.3 16.6 %collective-permute-start.10 = (f32[2,256,256]{2,1,0:T(8,128)}, f32[2,256,256]{2,1,0:T(8,128)S(1)}, u32[]{:S(2)}, u32[]{:S(2)}) collective-permute-start(f32[2,256,256]{2,1,0:T(8,128)} %get-tuple-element.94), channel_id=1, source_target_pairs={{1,0},{2,1},{3,2},{4,3},{5,4},{6,5},{7,6},{9,8},{10,9},{11,10},{12... | collective-permute-start | bytes 1572872 | tf_op jit(solution)/shard_map/ppermute | solution.py:596
  12.6 31.4 %collective-permute-start.11 = (f32[2,512,256]{2,1,0:T(8,128)}, f32[2,512,256]{2,1,0:T(8,128)S(1)}, u32[]{:S(2)}, u32[]{:S(2)}) collective-permute-start(f32[2,512,256]{2,1,0:T(8,128)} %slice_bitcast_fusion.1), channel_id=1, source_target_pairs={{8,0},{9,1},{10,2},{11,3},{12,4},{13,5},{14,6},{15,7},{16,8},{17,9... | collective-permute-start | bytes 3145736 | tf_op jit(solution)/shard_map/ppermute | solution.py:596
  13.9 15.3 %collective-permute-start.16 = (f32[4,2,2,16,256]{4,3,2,1,0:T(8,128)S(1)}, f32[4,2,2,16,256]{4,3,2,1,0:T(8,128)}, u32[]{:S(2)}, u32[]{:S(2)}) collective-permute-start(f32[4,2,2,16,256]{4,3,2,1,0:T(8,128)S(1)} %pad_maximum_fusion.mine), channel_id=1, source_target_pairs={{0,8},{1,9},{2,10},{3,11},{4,12},{5,13},{6,14},{7,15},{8,0},{9,1},... | collective-permute-start | bytes 786440 | tf_op jit(solution)/shard_map/ppermute | solution.py:596
  22.8 18.7 %collective-permute-start.15 = (f32[4,2,2,16,256]{4,3,2,1,0:T(8,128)S(1)}, f32[4,2,2,16,256]{4,3,2,1,0:T(8,128)S(1)}, u32[]{:S(2)}, u32[]{:S(2)}) collective-permute-start(f32[4,2,2,16,256]{4,3,2,1,0:T(8,128)S(1)} %pad_maximum_fusion.mine), channel_id=1, source_target_pairs={{0,17},{1,16},{2,19},{3,18},{4,21},{5,20},{6,23},{7,22},{8,25},{9,... | collective-permute-start | bytes 786440 | tf_op jit(solution)/shard_map/ppermute | solution.py:596
  27.2 16.8 %collective-permute-start.13 = (f32[2,256,256]{2,1,0:T(8,128)}, f32[2,256,256]{2,1,0:T(8,128)S(1)}, u32[]{:S(2)}, u32[]{:S(2)}) collective-permute-start(f32[2,256,256]{2,1,0:T(8,128)} %get-tuple-element.94), channel_id=1, source_target_pairs={{17,8},{18,9},{19,10},{20,11},{21,12},{22,13},{23,14},{33,24},{34,... | collective-permute-start | bytes 1572872 | tf_op jit(solution)/shard_map/ppermute | solution.py:596
  27.9 16.1 %collective-permute-start.12 = (f32[2,256,256]{2,1,0:T(8,128)S(1)}, f32[2,256,256]{2,1,0:T(8,128)S(1)}, u32[]{:S(2)}, u32[]{:S(2)}) collective-permute-start(f32[2,256,256]{2,1,0:T(8,128)S(1)} %copy-done.14), channel_id=1, source_target_pairs={{1,0},{2,1},{3,2},{4,3},{5,4},{6,5},{7,6},{9,8},{10,9},{11,10},{12... | collective-permute-start | bytes 1572872 | tf_op jit(solution)/shard_map/ppermute | solution.py:596
  29.2 14.8 %collective-permute-start.14 = (f32[2,256,256]{2,1,0:T(8,128)S(1)}, f32[2,256,256]{2,1,0:T(8,128)S(1)}, u32[]{:S(2)}, u32[]{:S(2)}) collective-permute-start(f32[2,256,256]{2,1,0:T(8,128)S(1)} %collective-permute-done.10.low_a), channel_id=1, source_target_pairs={{8,0},{9,1},{10,2},{11,3},{12,4},{13,5},{14,6},{15,7},{24,16},{25,... | collective-permute-start | bytes 1572872 | tf_op jit(solution)/shard_map/ppermute | solution.py:596
  44.0 33.5 %collective-permute-start.21 = (f32[2,256,256]{2,1,0:T(8,128)S(1)}, f32[2,256,256]{2,1,0:T(8,128)S(1)}, u32[]{:S(2)}, u32[]{:S(2)}) collective-permute-start(f32[2,256,256]{2,1,0:T(8,128)S(1)} %get-tuple-element.112), channel_id=1, source_target_pairs={{17,8},{18,9},{19,10},{20,11},{21,12},{22,13},{23,14},{33,24},{34,... | collective-permute-start | bytes 1572872 | tf_op jit(solution)/shard_map/ppermute | solution.py:596
  44.9 21.4 %collective-permute-start.19 = (f32[2,256,256]{2,1,0:T(8,128)S(1)}, f32[2,256,256]{2,1,0:T(8,128)S(1)}, u32[]{:S(2)}, u32[]{:S(2)}) collective-permute-start(f32[2,256,256]{2,1,0:T(8,128)S(1)} %get-tuple-element.112), channel_id=1, source_target_pairs={{1,0},{2,1},{3,2},{4,3},{5,4},{6,5},{7,6},{9,8},{10,9},{11,10},{12... | collective-permute-start | bytes 1572872 | tf_op jit(solution)/shard_map/ppermute | solution.py:596
  46.2 31.3 %collective-permute-start.20 = (f32[2,256,256]{2,1,0:T(8,128)S(1)}, f32[2,256,256]{2,1,0:T(8,128)S(1)}, u32[]{:S(2)}, u32[]{:S(2)}) collective-permute-start(f32[2,256,256]{2,1,0:T(8,128)S(1)} %get-tuple-element.115), channel_id=1, source_target_pairs={{1,0},{2,1},{3,2},{4,3},{5,4},{6,5},{7,6},{9,8},{10,9},{11,10},{12... | collective-permute-start | bytes 1572872 | tf_op jit(solution)/shard_map/ppermute | solution.py:596
  47.5 30.0 %collective-permute-start.18 = (f32[2,512,256]{2,1,0:T(8,128)S(1)}, f32[2,512,256]{2,1,0:T(8,128)S(1)}, u32[]{:S(2)}, u32[]{:S(2)}) collective-permute-start(f32[2,512,256]{2,1,0:T(8,128)S(1)} %slice_bitcast_fusion), channel_id=1, source_target_pairs={{8,0},{9,1},{10,2},{11,3},{12,4},{13,5},{14,6},{15,7},{16,8},{17,9... | collective-permute-start | bytes 3145736 | tf_op jit(solution)/shard_map/ppermute | solution.py:596
  66.3 11.2 %collective-permute-start.22 = (f32[2,256,256]{2,1,0:T(8,128)S(1)}, f32[2,256,256]{2,1,0:T(8,128)S(1)}, u32[]{:S(2)}, u32[]{:S(2)}) collective-permute-start(f32[2,256,256]{2,1,0:T(8,128)S(1)} %collective-permute-done.19.low_a), channel_id=1, source_target_pairs={{8,0},{9,1},{10,2},{11,3},{12,4},{13,5},{14,6},{15,7},{24,16},{25,... | collective-permute-start | bytes 1572872 | tf_op jit(solution)/shard_map/ppermute | solution.py:596
  94.6 22.0 %collective-permute-start.24 = (f32[2,256,256]{2,1,0:T(8,128)S(1)}, f32[2,256,256]{2,1,0:T(8,128)S(1)}, u32[]{:S(2)}, u32[]{:S(2)}) collective-permute-start(f32[2,256,256]{2,1,0:T(8,128)S(1)} %get-tuple-element.127), channel_id=1, source_target_pairs={{0,8},{1,9},{2,10},{3,11},{4,12},{5,13},{6,14},{7,15},{16,24},{17,... | collective-permute-start | bytes 1572872 | tf_op jit(solution)/shard_map/ppermute | solution.py:596
  109.5 30.9 %collective-permute-start.23 = (f32[2,512,256]{2,1,0:T(8,128)}, f32[2,512,256]{2,1,0:T(8,128)}, u32[]{:S(2)}, u32[]{:S(2)}) collective-permute-start(f32[2,512,256]{2,1,0:T(8,128)} %get-tuple-element.125), channel_id=1, source_target_pairs={{0,8},{1,9},{2,10},{3,11},{4,12},{5,13},{6,14},{7,15},{8,16},{9,17... | collective-permute-start | bytes 3145736 | tf_op jit(solution)/shard_map/ppermute | solution.py:596
  111.8 28.5 %collective-permute-start.27 = (f32[2,256,256]{2,1,0:T(8,128)S(1)}, f32[2,256,256]{2,1,0:T(8,128)}, u32[]{:S(2)}, u32[]{:S(2)}) collective-permute-start(f32[2,256,256]{2,1,0:T(8,128)S(1)} %get-tuple-element.127), channel_id=1, source_target_pairs={{8,17},{9,18},{10,19},{11,20},{12,21},{13,22},{14,23},{24,33},{25,... | collective-permute-start | bytes 1572872 | tf_op jit(solution)/shard_map/ppermute | solution.py:596
  113.3 27.1 %collective-permute-start.26 = (f32[2,256,256]{2,1,0:T(8,128)S(1)}, f32[2,256,256]{2,1,0:T(8,128)}, u32[]{:S(2)}, u32[]{:S(2)}) collective-permute-start(f32[2,256,256]{2,1,0:T(8,128)S(1)} %get-tuple-element.128), channel_id=1, source_target_pairs={{0,1},{1,2},{2,3},{3,4},{4,5},{5,6},{6,7},{8,9},{9,10},{10,11},{11... | collective-permute-start | bytes 1572872 | tf_op jit(solution)/shard_map/ppermute | solution.py:596
  117.4 23.0 %collective-permute-start.25 = (f32[2,256,256]{2,1,0:T(8,128)}, f32[2,256,256]{2,1,0:T(8,128)}, u32[]{:S(2)}, u32[]{:S(2)}) collective-permute-start(f32[2,256,256]{2,1,0:T(8,128)} %add.40), channel_id=1, source_target_pairs={{0,1},{1,2},{2,3},{3,4},{4,5},{5,6},{6,7},{8,9},{9,10},{10,11},{11... | collective-permute-start | bytes 1572872 | tf_op jit(solution)/shard_map/ppermute | solution.py:596
  135.8 4.3 %collective-permute-start = (f32[4,2,2,2,16,256]{5,4,1,0,3,2:T(8,128)S(1)}, f32[4,2,2,2,16,256]{5,4,1,0,3,2:T(8,128)S(1)}, u32[]{:S(2)}, u32[]{:S(2)}) collective-permute-start(f32[4,2,2,2,16,256]{5,4,1,0,3,2:T(8,128)S(1)} %select_bitcast_fusion), channel_id=1, source_target_pairs={{0,8},{1,9},{2,10},{3,11},{4,12},{5,13},{6,14},{7,15},{8,0},{9,1},... | collective-permute-start | bytes 1572872 | tf_op jit(solution)/shard_map/cond/branch_1_fun/ppermute | solution.py:596
  140.4 18.5 %collective-permute-start.29 = (f32[2,256,256]{2,1,0:T(8,128)}, f32[2,256,256]{2,1,0:T(8,128)S(1)}, u32[]{:S(2)}, u32[]{:S(2)}) collective-permute-start(f32[2,256,256]{2,1,0:T(8,128)} %get-tuple-element.131), channel_id=1, source_target_pairs={{0,8},{1,9},{2,10},{3,11},{4,12},{5,13},{6,14},{7,15},{16,24},{17,... | collective-permute-start | bytes 1572872 | tf_op jit(solution)/shard_map/ppermute | solution.py:596
  152.7 66.5 %collective-permute-start.28 = (f32[2,512,256]{2,1,0:T(8,128)}, f32[2,512,256]{2,1,0:T(8,128)S(1)}, u32[]{:S(2)}, u32[]{:S(2)}) collective-permute-start(f32[2,512,256]{2,1,0:T(8,128)} %get-tuple-element.129), channel_id=1, source_target_pairs={{0,8},{1,9},{2,10},{3,11},{4,12},{5,13},{6,14},{7,15},{8,16},{9,17... | collective-permute-start | bytes 3145736 | tf_op jit(solution)/shard_map/ppermute | solution.py:596
  154.1 65.1 %collective-permute-start.32 = (f32[2,256,256]{2,1,0:T(8,128)}, f32[2,256,256]{2,1,0:T(8,128)S(1)}, u32[]{:S(2)}, u32[]{:S(2)}) collective-permute-start(f32[2,256,256]{2,1,0:T(8,128)} %get-tuple-element.131), channel_id=1, source_target_pairs={{8,17},{9,18},{10,19},{11,20},{12,21},{13,22},{14,23},{24,33},{25,... | collective-permute-start | bytes 1572872 | tf_op jit(solution)/shard_map/ppermute | solution.py:596
  154.8 64.4 %collective-permute-start.31 = (f32[2,256,256]{2,1,0:T(8,128)}, f32[2,256,256]{2,1,0:T(8,128)S(1)}, u32[]{:S(2)}, u32[]{:S(2)}) collective-permute-start(f32[2,256,256]{2,1,0:T(8,128)} %get-tuple-element.132), channel_id=1, source_target_pairs={{0,1},{1,2},{2,3},{3,4},{4,5},{5,6},{6,7},{8,9},{9,10},{10,11},{11... | collective-permute-start | bytes 1572872 | tf_op jit(solution)/shard_map/ppermute | solution.py:596
  159.8 59.4 %collective-permute-start.30 = (f32[2,256,256]{2,1,0:T(8,128)}, f32[2,256,256]{2,1,0:T(8,128)S(1)}, u32[]{:S(2)}, u32[]{:S(2)}) collective-permute-start(f32[2,256,256]{2,1,0:T(8,128)} %add.41), channel_id=1, source_target_pairs={{0,1},{1,2},{2,3},{3,4},{4,5},{5,6},{6,7},{8,9},{9,10},{10,11},{11... | collective-permute-start | bytes 1572872 | tf_op jit(solution)/shard_map/ppermute | solution.py:596
  162.5 25.2 %collective-permute-start.1 = (f32[2,2,2,2,16,256]{5,4,3,2,1,0:T(8,128)}, f32[2,2,2,2,16,256]{5,4,3,2,1,0:T(8,128)S(1)}, u32[]{:S(2)}, u32[]{:S(2)}) collective-permute-start(f32[2,2,2,2,16,256]{5,4,3,2,1,0:T(8,128)} %slice_select_fusion), channel_id=1, source_target_pairs={{0,64},{1,65},{2,66},{3,67},{4,68},{5,69},{6,70},{7,71},{8,72},{9,... | collective-permute-start | bytes 786440 | tf_op jit(solution)/shard_map/cond/branch_1_fun/ppermute | solution.py:596
  187.8 5.0 %collective-permute-start.2 = (f32[2,2,2,16,256]{4,3,2,1,0:T(8,128)S(1)}, f32[2,2,2,16,256]{4,3,2,1,0:T(8,128)S(1)}, u32[]{:S(2)}, u32[]{:S(2)}) collective-permute-start(f32[2,2,2,16,256]{4,3,2,1,0:T(8,128)S(1)} %select_bitcast_fusion.1), channel_id=1, source_target_pairs={{0,32},{1,33},{2,34},{3,35},{4,36},{5,37},{6,38},{7,39},{8,40},{9,... | collective-permute-start | bytes 393224 | tf_op jit(solution)/shard_map/cond/branch_1_fun/ppermute | solution.py:596
  192.8 9.7 %collective-permute-start.3 = (f32[2,2,2,16,256]{4,3,2,1,0:T(8,128)S(1)}, f32[2,2,2,16,256]{4,3,2,1,0:T(8,128)S(1)}, u32[]{:S(2)}, u32[]{:S(2)}) collective-permute-start(f32[2,2,2,16,256]{4,3,2,1,0:T(8,128)S(1)} %bitcast_add_fusion.1), channel_id=1, source_target_pairs={{0,2},{1,3},{2,0},{3,1},{4,6},{5,7},{6,4},{7,5},{8,10},{9,11},{10,... | collective-permute-start | bytes 393224 | tf_op jit(solution)/shard_map/cond/branch_1_fun/ppermute | solution.py:596
  202.6 6.6 %collective-permute-start.4 = (f32[2,2,2,16,256]{4,3,2,1,0:T(8,128)S(1)}, f32[2,2,2,16,256]{4,3,2,1,0:T(8,128)S(1)}, u32[]{:S(2)}, u32[]{:S(2)}) collective-permute-start(f32[2,2,2,16,256]{4,3,2,1,0:T(8,128)S(1)} %add.34), channel_id=1, source_target_pairs={{0,4},{1,5},{2,6},{3,7},{4,0},{5,1},{6,2},{7,3},{8,12},{9,13},{10,... | collective-permute-start | bytes 393224 | tf_op jit(solution)/shard_map/cond/branch_1_fun/ppermute | solution.py:596
  209.2 5.6 %collective-permute-start.5 = (f32[2,2,16,256]{3,2,1,0:T(8,128)S(1)}, f32[2,2,16,256]{3,2,1,0:T(8,128)S(1)}, u32[]{:S(2)}, u32[]{:S(2)}) collective-permute-start(f32[2,2,16,256]{3,2,1,0:T(8,128)S(1)} %select_bitcast_fusion.2), channel_id=1, source_target_pairs={{0,17},{1,16},{2,19},{3,18},{4,21},{5,20},{6,23},{7,22},{8,25},{9,... | collective-permute-start | bytes 196616 | tf_op jit(solution)/shard_map/cond/branch_1_fun/ppermute | solution.py:596
  214.8 4.3 %collective-permute-start.6 = (f32[2,2,16,256]{3,2,1,0:T(8,128)S(1)}, f32[2,2,16,256]{3,2,1,0:T(8,128)S(1)}, u32[]{:S(2)}, u32[]{:S(2)}) collective-permute-start(f32[2,2,16,256]{3,2,1,0:T(8,128)S(1)} %bitcast_add_fusion.2), channel_id=1, source_target_pairs={{0,1},{1,0},{2,3},{3,2},{4,5},{5,4},{6,7},{7,6},{8,9},{9,8},{10,11... | collective-permute-start | bytes 196616 | tf_op jit(solution)/shard_map/cond/branch_1_fun/ppermute | solution.py:596
  (20 other events, 331.6 us)

commit v6 on v5

--- a/solution.py
+++ b/solution.py
@@ -172,13 +172,12 @@
     field[at] = field[at] + x
 
 
-def fetch_field(layer, core, obj, right, low_a, low_b, diag, side, field, sems, meanwhile=None):
-    n, t = PROBE, TILE
+def fetch_field(layer, core, obj, right, low, diag, side, field, sems, meanwhile=None):
+    t = TILE
     copies = [
         pltpu.make_async_copy(obj.at[layer], field.at[:, :t, :t], sems.at[0]),
         pltpu.make_async_copy(right, field.at[:, :t, t:], sems.at[1]),
-        pltpu.make_async_copy(low_a, field.at[:, t:, :n], sems.at[2]),
-        pltpu.make_async_copy(low_b, field.at[:, t:, n:t], sems.at[3]),
+        pltpu.make_async_copy(low, field.at[:, t:, :t], sems.at[2]),
     ]
     for copy in copies:
         copy.start()
@@ -187,13 +186,13 @@
 
     @pl.when(core == 0)
     def _():
-        copy = pltpu.make_async_copy(side, field.at[:, t:, t:], sems.at[4])
+        copy = pltpu.make_async_copy(side, field.at[:, t:, t:], sems.at[3])
         copy.start()
         copy.wait()
 
     @pl.when(core != 0)
     def _():
-        copy = pltpu.make_async_copy(diag, field.at[:, t:, t:], sems.at[4])
+        copy = pltpu.make_async_copy(diag, field.at[:, t:, t:], sems.at[3])
         copy.start()
         copy.wait()
 
@@ -224,7 +223,7 @@
 
 
 def out_kernel(
-    scalars, obj, right, low_a, low_b, diag, side, mine, across, mine_other, across_other, table_l, table_r,
+    scalars, obj, right, low, diag, side, mine, across, mine_other, across_other, table_l, table_r,
     psi, win, probe_rows, field, sems, probe_sem,
 ):
     slot = pl.program_id(0)
@@ -245,7 +244,7 @@
         ]
         for copy in copies:
             copy.start()
-        fetch_field(0, core, obj, right, low_a, low_b, diag, side, field, sems)
+        fetch_field(0, core, obj, right, low, diag, side, field, sems)
         for copy in copies:
             copy.wait()
 
@@ -268,7 +267,7 @@
 
 
 def far_kernel(
-    scalars, obj, right, low_a, low_b, diag, side, psi, amp, four_l, four_r, ruof_l, ruof_r, tw_row, tw_col,
+    scalars, obj, right, low, diag, side, psi, amp, four_l, four_r, ruof_l, ruof_r, tw_row, tw_col,
     g_psi, g_main, g_right, g_low_a, g_low_b, g_corner, field, grad, win, gwin, sems,
 ):
     slot = pl.program_id(0)
@@ -291,7 +290,7 @@
             grad[...] = jnp.zeros_like(grad)
             gwin[...] = jnp.zeros_like(gwin)
 
-        fetch_field(1, scalars[13], obj, right, low_a, low_b, diag, side, field, sems, clear)
+        fetch_field(1, scalars[13], obj, right, low, diag, side, field, sems, clear)
         load_window(0)
 
     @pl.when(slot < used)
@@ -449,8 +448,8 @@
     return pl.CostEstimate(flops=int(flops), bytes_accessed=int(data), transcendentals=0)
 
 
-def params():
-    return pltpu.CompilerParams(vmem_limit_bytes=VMEM_LIMIT)
+def params(limit=VMEM_LIMIT):
+    return pltpu.CompilerParams(vmem_limit_bytes=limit)
 
 
 FIELD_PARTS = [(2, TILE, TILE), (2, TILE, PROBE), (2, PROBE, PROBE), (2, PROBE, PROBE), (2, PROBE, PROBE)]
@@ -472,7 +471,7 @@
         ],
         out_specs=pl.BlockSpec((1, n, n), lambda j: (j, 0, 0)),
         out_shape=sds((SLOTS, n, n)),
-        compiler_params=params(),
+        compiler_params=params(60 * 1024 * 1024),
         cost_estimate=cost(1.2e9, 4e6),
         name="order_amplitudes",
     )(amp, tables["perm_l"], tables["perm_r"])
@@ -485,7 +484,7 @@
         grid_spec=pltpu.PrefetchScalarGridSpec(
             num_scalar_prefetch=1,
             grid=(SLOTS,),
-            in_specs=[any_spec()] * 10 + [held()] * 2,
+            in_specs=[any_spec()] * 9 + [held()] * 2,
             out_specs=[of_slot((2, 2, n, n)), of_slot((2, n, n)), whole((2, 2, 4, 2, 2, 16, n))],
             scratch_shapes=[
                 pltpu.VMEM((2, 3 * n, 3 * n), F32),
@@ -494,7 +493,7 @@
             ],
         ),
         out_shape=[sds((SLOTS, 2, 2, n, n)), sds((SLOTS, 2, n, n)), sds((2, 2, 4, 2, 2, 16, n))],
-        compiler_params=params(),
+        compiler_params=params(60 * 1024 * 1024),
         cost_estimate=cost(6e10, 2e7),
         name="propagate_out",
     )(scalars, obj, *halo, *probe, tables["prop_l"], tables["prop_r"])
@@ -507,7 +506,7 @@
         grid_spec=pltpu.PrefetchScalarGridSpec(
             num_scalar_prefetch=1,
             grid=(SLOTS,),
-            in_specs=[any_spec()] * 6
+            in_specs=[any_spec()] * 5
             + [of_slot((2, 2, n, n)), of_slot((n, n))]
             + [held()] * 6,
             out_specs=[of_slot((2, 2, n, n))] + [any_spec()] * 5,
@@ -600,17 +599,16 @@
 
     def pieces(obj, layer):
         n = PROBE
-        return obj[layer, :, :n, :n], obj[layer, :, :, :n], obj[layer, :, :n, n:]
+        return obj[layer, :, :n, :n], obj[layer, :, :, :n], obj[layer, :, :n]
 
     def bring(corner, edge, low):
-        low_a = send(corner, lambda gx, gy: (gx, gy - 1))
         right = send(edge, lambda gx, gy: (gx - 1, gy))
-        low_b = send(low, lambda gx, gy: (gx, gy - 1))
+        low = send(low, lambda gx, gy: (gx, gy - 1))
         diag = send(corner, lambda gx, gy: (gx - 1, gy - 1) if gx % 2 == 0 else None)
-        return right, low_a, low_b, diag
-
-    def bring_side(low_a):
-        return send(low_a, lambda gx, gy: (gx - 1, gy) if gx % 2 == 1 else None)
+        return right, low, diag
+
+    def bring_side(low):
+        return send(low[:, :, :PROBE], lambda gx, gy: (gx - 1, gy) if gx % 2 == 1 else None)
 
     def take_back(right, low_a, low_b, corner):
         side = send(corner, lambda gx, gy: (gx + 1, gy) if gx % 2 == 0 else None)
@@ -662,14 +660,14 @@
         halo_0 = bring(*pieces_0)
         across = send(mine, flip(2, 1))
         probe_parts = [mine, across, send(mine, flip(1, 0)), send(across, flip(1, 0))]
-        obj_late, low_a = lax.optimization_barrier((obj, halo_0[1]))
-        halo_0 = (halo_0[0], low_a, *halo_0[2:], bring_side(low_a))
+        obj_late, diag = lax.optimization_barrier((obj, halo_0[2]))
+        halo_0 = (*halo_0[:2], diag)
         amp = permute_amplitudes(amplitudes[0, 0], tables)
         pieces_1, halo_0, amp, probe_parts = lax.optimization_barrier((pieces(obj_late, 1), halo_0, amp, probe_parts))
-        right, low_a, *others = bring(*pieces_1)
-        psi, win, probe_rows = run_out(scalars, obj, halo_0, probe_parts, tables)
-        low_a, psi = lax.optimization_barrier((low_a, psi))
-        halo_1 = (right, low_a, *others, bring_side(low_a))
+        halo_1 = bring(*pieces_1)
+        psi, win, probe_rows = run_out(scalars, obj, (*halo_0, bring_side(halo_0[1])), probe_parts, tables)
+        low, psi = lax.optimization_barrier((halo_1[1], psi))
+        halo_1 = (halo_1[0], low, halo_1[2], bring_side(low))
         probe_full = probe_rows.reshape(2, 2, PROBE, PROBE)
         g_psi, main_1, *edges_1 = run_far(scalars, obj, halo_1, psi, amp, tables)
         back_1 = take_back(*edges_1)

time: 225 us -> 237 us (1.053)
  starting transfers between devices: 92.5 us -> 105 us
  local copies, waits for them, and re-layouts: 14 us -> 16.5 us
    ppermute x33 -> x31, starting transfers between devices: 92.5 us -> 105 us  [send(): return lax.ppermute(x, axes, pairs)]
    slice x0 -> x2, local copies, waits for them, and re-layouts: none -> 2.95 us  [bring_side(): low[:, :, :PROBE]]
    pallas_call x1, Pallas kernels: 3.66 us -> 6.52 us  [permute_amplitudes(): pl.pallas_call(amp_kernel, grid=(SLOTS,), in_specs=[pl.BlockSpec((1, n, n...]
    pallas_call x1, Pallas kernels: 16 us -> 13.4 us  [run_far(): pl.pallas_call(far_kernel, grid_spec=pltpu.PrefetchScalarGridSpec(num_sca...]
    squeeze x4 -> x6, local copies, waits for them, and re-layouts: 7.17 us -> 9.12 us  [pieces(): return (obj[layer, :, :n, :n], obj[layer, :, :, :n], obj[layer, :, :n])]
    ppermute x33 -> x31, waiting for transfers between devices: 63.1 us -> 63 us  [send(): return lax.ppermute(x, axes, pairs)]
  transfers between devices with their start and end apart: 33 -> 31, of which waited for: 13 -> 12; matrix products, arithmetic and copies ran while one was open for 5% -> 6% of each run, Pallas kernels for 13% -> 13%
where the time goes in v6:
time: 237 us; the launch traced here: 236 us
  starting transfers between devices  105 us (44%)
  waiting for transfers between devices  63 us (27%)
  Pallas kernels  47.1 us (20%)
  local copies, waits for them, and re-layouts  16.5 us (7%)
  other arithmetic  2.89 us (1%)
    ppermute x31, starting transfers between devices, send(): return lax.ppermute(x, axes, pairs)  105 us
    ppermute x31, waiting for transfers between devices, send(): return lax.ppermute(x, axes, pairs)  63 us
    pallas_call x1, Pallas kernels, run_far(): pl.pallas_call(far_kernel, grid_spec=pltpu.PrefetchScalarGridSpec(num_sca...  13.4 us
    pallas_call x1, Pallas kernels, run_out(): pl.pallas_call(out_kernel, grid_spec=pltpu.PrefetchScalarGridSpec(num_sca...  10.4 us
    squeeze x6, local copies, waits for them, and re-layouts, pieces(): return (obj[layer, :, :n, :n], obj[layer, :, :, :n], obj[layer, :, :n])  9.12 us
    pallas_call x1, Pallas kernels, run_home(): pl.pallas_call(home_kernel, grid_spec=pltpu.PrefetchScalarGridSpec(num_sc...  8.63 us
    pallas_call x2, Pallas kernels, run_join(): pl.pallas_call(join_kernel, grid=(4,), in_specs=[pl.BlockSpec((2, h, TILE...  8.11 us
    pallas_call x1, Pallas kernels, permute_amplitudes(): pl.pallas_call(amp_kernel, grid=(SLOTS,), in_specs=[pl.BlockSpec((1, n, n...  6.52 us
  transfers between devices with their start and end apart: 31, of which 12 were waited for; matrix products, arithmetic and copies ran while one was open for 6% of the time, Pallas kernels for 13%

profile of v6, /device:TPU:0, one launch (start us, length us, event | category | flops | bytes accessed | tf_op | source)
XLA Modules:
  0.0 236.4 jit_solution(4831874706240991367)
XLA Ops:
  0.6 2.1 collective-permute-start.7
  2.7 2.5 %collective-permute-start.9 = (f32[2,2,16,256]{3,2,1,0:T(8,128)}, f32[2,2,16,256]{3,2,1,0:T(8,128)S(1)}, u32[]{:S(2)}, u32[]{:S(2)}) collective-permute-start(f32[2,2,16,256]{3,2,1,0:T(8,128)} %param.22), channel_id=1, source_target_pairs={{0,96},{1,97},{2,98},{3,99},{4,100},{5,101},{6,102},{7,103},{8,104... | collective-permute-start | bytes 196616 | tf_op jit(solution)/shard_map/ppermute | solution.py:595
  7.6 2.3 slice_bitcast_fusion.3
  12.0 3.7 %collective-permute-start.13 = (f32[4,2,2,16,256]{4,3,2,1,0:T(8,128)S(1)}, f32[4,2,2,16,256]{4,3,2,1,0:T(8,128)}, u32[]{:S(2)}, u32[]{:S(2)}) collective-permute-start(f32[4,2,2,16,256]{4,3,2,1,0:T(8,128)S(1)} %pad_maximum_fusion.mine), channel_id=1, source_target_pairs={{0,17},{1,16},{2,19},{3,18},{4,21},{5,20},{6,23},{7,22},{8,25},{9,... | collective-permute-start | bytes 786440 | tf_op jit(solution)/shard_map/ppermute | solution.py:595
  18.3 6.5 %order_amplitudes.1.amp = f32[6,256,256]{2,1,0:T(8,128)} custom-call(f32[6,256,256]{2,1,0:T(8,128)} %bitcast.47, bf16[256,768]{1,0:T(8,128)(2,1)} %constant.115.clone.perm_l, bf16[768,256]{1,0:T(8,128)(2,1)} %constant.116.clone.perm_r), custom_call_target="tpu_custom_call" | custom-call | flops 1200000000 | bytes 4000000 | tf_op jit(solution)/shard_map/order_amplitudes/pallas_call | solution.py:464
  25.9 4.1 %collective-permute-done.13.across = f32[4,2,2,16,256]{4,3,2,1,0:T(8,128)} collective-permute-done((f32[4,2,2,16,256]{4,3,2,1,0:T(8,128)S(1)}, f32[4,2,2,16,256]{4,3,2,1,0:T(8,128)}, u32[]{:S(2)}, u32[]{:S(2)}) %collective-permute-start.13) | collective-permute-done | bytes 262176 | tf_op jit(solution)/shard_map/ppermute | solution.py:595
  33.4 1.9 slice_bitcast_fusion.4
  35.4 9.5 %collective-permute-done.12.low = f32[2,256,512]{2,1,0:T(8,128)} collective-permute-done((f32[2,256,512]{2,1,0:T(8,128)S(1)}, f32[2,256,512]{2,1,0:T(8,128)}, u32[]{:S(2)}, u32[]{:S(2)}) %collective-permute-start.12) | collective-permute-done | bytes 1048608 | tf_op jit(solution)/shard_map/ppermute | solution.py:595
  52.4 7.4 %collective-permute-done.16.side = f32[2,256,256]{2,1,0:T(8,128)} collective-permute-done((f32[2,256,256]{2,1,0:T(8,128)}, f32[2,256,256]{2,1,0:T(8,128)}, u32[]{:S(2)}, u32[]{:S(2)}) %collective-permute-start.16) | collective-permute-done | bytes 524320 | tf_op jit(solution)/shard_map/ppermute | solution.py:595
  59.8 10.4 %propagate_out.1 = (f32[6,2,2,256,256]{4,3,2,1,0:T(8,128)}, f32[6,2,256,256]{3,2,1,0:T(8,128)}, f32[2,2,4,2,2,16,256]{6,5,4,3,2,1,0:T(8,128)}) custom-call(s32[16]{0:T(128)S(1)} %concatenate.3.scalars, f32[2,2,512,512]{3,2,1,0:T(8,128)} %obj.3, f32[2,512,256]{2,1,0:T(8,128)} %collective-permute-done.11.right, f32[2,256,512]{2,1,0:T(8,128)} %collective-permute-done.12.low, ...), custom_call_target="tpu_custom_call" | custom-call | flops 60000002048 | bytes 20000000 | tf_op jit(solution)/shard_map/propagate_out/pallas_call | solution.py:482
  72.6 10.1 %collective-permute-done.20.side = f32[2,256,256]{2,1,0:T(8,128)S(1)} collective-permute-done((f32[2,256,256]{2,1,0:T(8,128)S(1)}, f32[2,256,256]{2,1,0:T(8,128)S(1)}, u32[]{:S(2)}, u32[]{:S(2)}) %collective-permute-start.20) | collective-permute-done | bytes 524320 | tf_op jit(solution)/shard_map/ppermute | solution.py:595
  83.7 13.4 %far_field.1 = (f32[6,2,2,256,256]{4,3,2,1,0:T(8,128)}, f32[2,512,512]{2,1,0:T(8,128)}, f32[2,512,256]{2,1,0:T(8,128)S(1)}, f32[2,256,256]{2,1,0:T(8,128)S(1)}, ...) custom-call(s32[16]{0:T(128)S(1)} %concatenate.3.scalars, f32[2,2,512,512]{3,2,1,0:T(8,128)} %obj.3, ...), custom_call_target="tpu_custom_call" | custom-call | flops 60000002048 | bytes 20000000 | tf_op jit(solution)/shard_map/far_field/pallas_call | solution.py:504
  97.2 23.5 %collective-permute-start.22 = (f32[2,256,256]{2,1,0:T(8,128)S(1)}, f32[2,256,256]{2,1,0:T(8,128)S(1)}, u32[]{:S(2)}, u32[]{:S(2)}) collective-permute-start(f32[2,256,256]{2,1,0:T(8,128)S(1)} %get-tuple-element.123), channel_id=1, source_target_pairs={{0,8},{1,9},{2,10},{3,11},{4,12},{5,13},{6,14},{7,15},{16,24},{17,... | collective-permute-start | bytes 1572872 | tf_op jit(solution)/shard_map/ppermute | solution.py:595
  120.6 2.3 collective-permute-start.21
  124.4 2.1 collective-permute-start.24
  127.4 2.1 collective-permute-start.23
  129.5 32.7 %conditional.2 = (f32[4,2,2,2,16,256]{5,4,1,0,3,2:T(8,128)S(1)}, f32[2,512,512]{2,1,0:T(8,128)}, f32[2,512,256]{2,1,0:T(8,128)}, f32[2,256,256]{2,1,0:T(8,128)S(...) conditional(s32[]{:T(128)} %bitcast.9, () %tuple.30, (f32[2,2,4,2,2,16,256]{6,5,4,3,2,1,0:T(8,128)}, ...), branch_computations={%region_0.0_spmd, %region_1.2_spmd} | conditional | flops 60000395264 | bytes 34156064 | solution.py:683
  131.7 8.6 %propagate_home.1 = (f32[2,2,256,256]{3,2,1,0:T(8,128)S(1)}, f32[2,512,512]{2,1,0:T(8,128)}, f32[2,512,256]{2,1,0:T(8,128)}, f32[2,256,256]{2,1,0:T(8,128)S(1)},...) custom-call(s32[16]{0:T(128)S(1)} %get-tuple-element.25.scalars, f32[6,2,256,256]{3,2,1,0:T(8,128)} %get-tuple-element.26.win, ...), custom_call_target="tpu_custom_call" | custom-call | flops 60000002048 | bytes 20000000 | tf_op jit(solution)/shard_map/cond/branch_1_fun/propagate_home/pallas_call | solution.py:534
  140.5 19.7 %collective-permute-start = (f32[4,2,2,2,16,256]{5,4,1,0,3,2:T(8,128)S(1)}, f32[4,2,2,2,16,256]{5,4,1,0,3,2:T(8,128)S(1)}, u32[]{:S(2)}, u32[]{:S(2)}) collective-permute-start(f32[4,2,2,2,16,256]{5,4,1,0,3,2:T(8,128)S(1)} %select_bitcast_fusion), channel_id=1, source_target_pairs={{0,8},{1,9},{2,10},{3,11},{4,12},{5,13},{6,14},{7,15},{8,0},{9,1},... | collective-permute-start | bytes 1572872 | tf_op jit(solution)/shard_map/cond/branch_1_fun/ppermute | solution.py:595
  162.2 2.3 collective-permute-start.27
  166.6 2.2 collective-permute-start.29
  169.7 1.9 collective-permute-start.28
  171.6 60.8 %conditional.3 = (f32[2,2,16,256]{3,2,1,0:T(8,128)S(1)}, f32[2,2,512,512]{3,2,1,0:T(8,128)}) conditional(s32[]{:T(128)} %bitcast.9, () %tuple.37, (f32[4,2,2,2,16,256]{5,4,1,0,3,2:T(8,128)S(1)}, f32[2,512,512]{2,1,0:T(8,128)}, f32[2,512,256]{2,1,0:T(8,128)}, f32[2,256,256]{2,1,0:T(8,128)}, f32[2,256,256]{2,1,0:T(8,128)}, ...), branch_computations={%region_2.3_spmd, %region_3.4_spmd} | conditional | flops 1426045 | bytes 13340902 | solution.py:695
  172.4 15.4 %collective-permute-start.1 = (f32[2,2,2,2,16,256]{5,4,3,2,1,0:T(8,128)}, f32[2,2,2,2,16,256]{5,4,3,2,1,0:T(8,128)S(1)}, u32[]{:S(2)}, u32[]{:S(2)}) collective-permute-start(f32[2,2,2,2,16,256]{5,4,3,2,1,0:T(8,128)} %slice_select_fusion), channel_id=1, source_target_pairs={{0,64},{1,65},{2,66},{3,67},{4,68},{5,69},{6,70},{7,71},{8,72},{9,... | collective-permute-start | bytes 786440 | tf_op jit(solution)/shard_map/cond/branch_1_fun/ppermute | solution.py:595
  187.8 10.6 %collective-permute-done.1 = f32[2,2,2,2,16,256]{5,4,3,2,1,0:T(8,128)S(1)} collective-permute-done((f32[2,2,2,2,16,256]{5,4,3,2,1,0:T(8,128)}, f32[2,2,2,2,16,256]{5,4,3,2,1,0:T(8,128)S(1)}, u32[]{:S(2)}, u32[]{:S(2)}) %collective-permute-start.1) | collective-permute-done | bytes 262176 | tf_op jit(solution)/shard_map/cond/branch_1_fun/ppermute | solution.py:595
  198.6 4.2 %join_gradients.2 = f32[2,2,512,512]{3,2,1,0:T(8,128)} custom-call(f32[2,512,512]{2,1,0:T(8,128)} %get-tuple-element.38.main, f32[2,512,256]{2,1,0:T(8,128)} %get-tuple-element.39.right, f32[2,256,256]{2,1,0:T(8,128)} %get-tuple-element.40.low_a, f32[2,256,256]{2,1,0:T(8,128)} %get-tuple-element.41.low_b, f32[2,256,256]{2,1,0:T(8,128)} %get-tuple-element.42.diag), custom_call_target="tpu_custom_call" | custom-call | flops 1000000 | bytes 6000000 | tf_op jit(solution)/shard_map/cond/branch_1_fun/join_gradients/pallas_call | solution.py:560
  204.6 8.2 %collective-permute-start.3 = (f32[2,2,2,16,256]{4,3,2,1,0:T(8,128)S(1)}, f32[2,2,2,16,256]{4,3,2,1,0:T(8,128)S(1)}, u32[]{:S(2)}, u32[]{:S(2)}) collective-permute-start(f32[2,2,2,16,256]{4,3,2,1,0:T(8,128)S(1)} %bitcast_add_fusion.1), channel_id=1, source_target_pairs={{0,2},{1,3},{2,0},{3,1},{4,6},{5,7},{6,4},{7,5},{8,10},{9,11},{10,... | collective-permute-start | bytes 393224 | tf_op jit(solution)/shard_map/cond/branch_1_fun/ppermute | solution.py:595
  212.8 3.1 %collective-permute-done.3 = f32[2,2,2,16,256]{4,3,2,1,0:T(8,128)S(1)} collective-permute-done((f32[2,2,2,16,256]{4,3,2,1,0:T(8,128)S(1)}, f32[2,2,2,16,256]{4,3,2,1,0:T(8,128)S(1)}, u32[]{:S(2)}, u32[]{:S(2)}) %collective-permute-start.3) | collective-permute-done | bytes 131104 | tf_op jit(solution)/shard_map/cond/branch_1_fun/ppermute | solution.py:595
  217.4 5.0 %collective-permute-done.4 = f32[2,2,2,16,256]{4,3,2,1,0:T(8,128)S(1)} collective-permute-done((f32[2,2,2,16,256]{4,3,2,1,0:T(8,128)S(1)}, f32[2,2,2,16,256]{4,3,2,1,0:T(8,128)S(1)}, u32[]{:S(2)}, u32[]{:S(2)}) %collective-permute-start.4) | collective-permute-done | bytes 131104 | tf_op jit(solution)/shard_map/cond/branch_1_fun/ppermute | solution.py:595
  222.6 5.5 %collective-permute-done.5 = f32[2,2,16,256]{3,2,1,0:T(8,128)S(1)} collective-permute-done((f32[2,2,16,256]{3,2,1,0:T(8,128)S(1)}, f32[2,2,16,256]{3,2,1,0:T(8,128)S(1)}, u32[]{:S(2)}, u32[]{:S(2)}) %collective-permute-start.5) | collective-permute-done | bytes 65568 | tf_op jit(solution)/shard_map/cond/branch_1_fun/ppermute | solution.py:595
  228.2 4.3 %collective-permute-done.6 = f32[2,2,16,256]{3,2,1,0:T(8,128)S(1)} collective-permute-done((f32[2,2,16,256]{3,2,1,0:T(8,128)S(1)}, f32[2,2,16,256]{3,2,1,0:T(8,128)S(1)}, u32[]{:S(2)}, u32[]{:S(2)}) %collective-permute-start.6) | collective-permute-done | bytes 65568 | tf_op jit(solution)/shard_map/cond/branch_1_fun/ppermute | solution.py:595
  232.5 3.9 %join_gradients.3 = f32[2,2,512,512]{3,2,1,0:T(8,128)} custom-call(f32[2,512,512]{2,1,0:T(8,128)} %get-tuple-element.115.main, f32[2,512,256]{2,1,0:T(8,128)S(1)} %collective-permute-done.26.right, f32[2,256,256]{2,1,0:T(8,128)S(1)} %collective-permute-done.28.low_a, ...), custom_call_target="tpu_custom_call", output_to_operand_aliasing={{}: (5, {})} | custom-call | flops 1000000 | bytes 6000000 | tf_op jit(solution)/shard_map/join_gradients/pallas_call | solution.py:560
  (94 shorter events, 35.5 us)
Async XLA Ops:
  0.6 10.3 %collective-permute-start.7 = (f32[2,2,16,256]{3,2,1,0:T(8,128)}, f32[2,2,16,256]{3,2,1,0:T(8,128)S(1)}, u32[]{:S(2)}, u32[]{:S(2)}) collective-permute-start(f32[2,2,16,256]{3,2,1,0:T(8,128)} %param.22), channel_id=1, source_target_pairs={{0,32},{1,33},{2,34},{3,35},{4,36},{5,37},{6,38},{7,39},{8,40},{9,... | collective-permute-start | bytes 196616 | tf_op jit(solution)/shard_map/ppermute | solution.py:595
  2.7 8.2 %collective-permute-start.9 = (f32[2,2,16,256]{3,2,1,0:T(8,128)}, f32[2,2,16,256]{3,2,1,0:T(8,128)S(1)}, u32[]{:S(2)}, u32[]{:S(2)}) collective-permute-start(f32[2,2,16,256]{3,2,1,0:T(8,128)} %param.22), channel_id=1, source_target_pairs={{0,96},{1,97},{2,98},{3,99},{4,100},{5,101},{6,102},{7,103},{8,104... | collective-permute-start | bytes 196616 | tf_op jit(solution)/shard_map/ppermute | solution.py:595
  5.2 6.0 %collective-permute-start.8 = (f32[2,2,16,256]{3,2,1,0:T(8,128)}, f32[2,2,16,256]{3,2,1,0:T(8,128)S(1)}, u32[]{:S(2)}, u32[]{:S(2)}) collective-permute-start(f32[2,2,16,256]{3,2,1,0:T(8,128)} %param.22), channel_id=1, source_target_pairs={{0,64},{1,65},{2,66},{3,67},{4,68},{5,69},{6,70},{7,71},{8,72},{9,... | collective-permute-start | bytes 196616 | tf_op jit(solution)/shard_map/ppermute | solution.py:595
  11.3 18.8 %collective-permute-start.10 = (f32[2,256,256]{2,1,0:T(8,128)S(1)}, f32[2,256,256]{2,1,0:T(8,128)S(1)}, u32[]{:S(2)}, u32[]{:S(2)}) collective-permute-start(f32[2,256,256]{2,1,0:T(8,128)S(1)} %slice_bitcast_fusion.5), channel_id=1, source_target_pairs={{17,8},{18,9},{19,10},{20,11},{21,12},{22,13},{23,14},{33,24},{34,... | collective-permute-start | bytes 1572872 | tf_op jit(solution)/shard_map/ppermute | solution.py:595
  12.0 18.0 %collective-permute-start.13 = (f32[4,2,2,16,256]{4,3,2,1,0:T(8,128)S(1)}, f32[4,2,2,16,256]{4,3,2,1,0:T(8,128)}, u32[]{:S(2)}, u32[]{:S(2)}) collective-permute-start(f32[4,2,2,16,256]{4,3,2,1,0:T(8,128)S(1)} %pad_maximum_fusion.mine), channel_id=1, source_target_pairs={{0,17},{1,16},{2,19},{3,18},{4,21},{5,20},{6,23},{7,22},{8,25},{9,... | collective-permute-start | bytes 786440 | tf_op jit(solution)/shard_map/ppermute | solution.py:595
  15.7 19.7 %collective-permute-start.11 = (f32[2,512,256]{2,1,0:T(8,128)}, f32[2,512,256]{2,1,0:T(8,128)}, u32[]{:S(2)}, u32[]{:S(2)}) collective-permute-start(f32[2,512,256]{2,1,0:T(8,128)} %slice_bitcast_fusion.3), channel_id=1, source_target_pairs={{8,0},{9,1},{10,2},{11,3},{12,4},{13,5},{14,6},{15,7},{16,8},{17,9... | collective-permute-start | bytes 3145736 | tf_op jit(solution)/shard_map/ppermute | solution.py:595
  17.0 27.9 %collective-permute-start.12 = (f32[2,256,512]{2,1,0:T(8,128)S(1)}, f32[2,256,512]{2,1,0:T(8,128)}, u32[]{:S(2)}, u32[]{:S(2)}) collective-permute-start(f32[2,256,512]{2,1,0:T(8,128)S(1)} %slice_bitcast_fusion.2), channel_id=1, source_target_pairs={{1,0},{2,1},{3,2},{4,3},{5,4},{6,5},{7,6},{9,8},{10,9},{11,10},{12... | collective-permute-start | bytes 3145736 | tf_op jit(solution)/shard_map/ppermute | solution.py:595
  24.8 10.5 %collective-permute-start.14 = (f32[4,2,2,16,256]{4,3,2,1,0:T(8,128)S(1)}, f32[4,2,2,16,256]{4,3,2,1,0:T(8,128)S(1)}, u32[]{:S(2)}, u32[]{:S(2)}) collective-permute-start(f32[4,2,2,16,256]{4,3,2,1,0:T(8,128)S(1)} %pad_maximum_fusion.mine), channel_id=1, source_target_pairs={{0,8},{1,9},{2,10},{3,11},{4,12},{5,13},{6,14},{7,15},{8,0},{9,1},... | collective-permute-start | bytes 786440 | tf_op jit(solution)/shard_map/ppermute | solution.py:595
  30.0 5.3 %collective-permute-start.15 = (f32[4,2,2,16,256]{4,3,2,1,0:T(8,128)}, f32[4,2,2,16,256]{4,3,2,1,0:T(8,128)S(1)}, u32[]{:S(2)}, u32[]{:S(2)}) collective-permute-start(f32[4,2,2,16,256]{4,3,2,1,0:T(8,128)} %collective-permute-done.13.across), channel_id=1, source_target_pairs={{0,8},{1,9},{2,10},{3,11},{4,12},{5,13},{6,14},{7,15},{8,0},{9,1},... | collective-permute-start | bytes 786440 | tf_op jit(solution)/shard_map/ppermute | solution.py:595
  46.7 13.0 %collective-permute-start.16 = (f32[2,256,256]{2,1,0:T(8,128)}, f32[2,256,256]{2,1,0:T(8,128)}, u32[]{:S(2)}, u32[]{:S(2)}) collective-permute-start(f32[2,256,256]{2,1,0:T(8,128)} %slice.64), channel_id=1, source_target_pairs={{8,0},{9,1},{10,2},{11,3},{12,4},{13,5},{14,6},{15,7},{24,16},{25,... | collective-permute-start | bytes 1572872 | tf_op jit(solution)/shard_map/ppermute | solution.py:595
  48.9 33.8 %copy-start.6 = (f32[2,128,256]{2,1,0:T(8,128)S(1)}, f32[2,128,256]{2,1,0:T(8,128)}, u32[]{:S(2)}) copy-start(f32[2,128,256]{2,1,0:T(8,128)} %constant.123.clone.tw_row) | copy-start | bytes 786436
  49.0 23.6 %collective-permute-start.19 = (f32[2,256,256]{2,1,0:T(8,128)}, f32[2,256,256]{2,1,0:T(8,128)S(1)}, u32[]{:S(2)}, u32[]{:S(2)}) collective-permute-start(f32[2,256,256]{2,1,0:T(8,128)} %slice_bitcast_fusion.4), channel_id=1, source_target_pairs={{17,8},{18,9},{19,10},{20,11},{21,12},{22,13},{23,14},{33,24},{34,... | collective-permute-start | bytes 1572872 | tf_op jit(solution)/shard_map/ppermute | solution.py:595
  49.8 22.8 %collective-permute-start.17 = (f32[2,512,256]{2,1,0:T(8,128)S(1)}, f32[2,512,256]{2,1,0:T(8,128)}, u32[]{:S(2)}, u32[]{:S(2)}) collective-permute-start(f32[2,512,256]{2,1,0:T(8,128)S(1)} %slice_bitcast_fusion.1), channel_id=1, source_target_pairs={{8,0},{9,1},{10,2},{11,3},{12,4},{13,5},{14,6},{15,7},{16,8},{17,9... | collective-permute-start | bytes 3145736 | tf_op jit(solution)/shard_map/ppermute | solution.py:595
  51.1 19.1 %collective-permute-start.18 = (f32[2,256,512]{2,1,0:T(8,128)S(1)}, f32[2,256,512]{2,1,0:T(8,128)}, u32[]{:S(2)}, u32[]{:S(2)}) collective-permute-start(f32[2,256,512]{2,1,0:T(8,128)S(1)} %slice_bitcast_fusion), channel_id=1, source_target_pairs={{1,0},{2,1},{3,2},{4,3},{5,4},{6,5},{7,6},{9,8},{10,9},{11,10},{12... | collective-permute-start | bytes 3145736 | tf_op jit(solution)/shard_map/ppermute | solution.py:595
  71.3 11.4 %collective-permute-start.20 = (f32[2,256,256]{2,1,0:T(8,128)S(1)}, f32[2,256,256]{2,1,0:T(8,128)S(1)}, u32[]{:S(2)}, u32[]{:S(2)}) collective-permute-start(f32[2,256,256]{2,1,0:T(8,128)S(1)} %slice.65), channel_id=1, source_target_pairs={{8,0},{9,1},{10,2},{11,3},{12,4},{13,5},{14,6},{15,7},{24,16},{25,... | collective-permute-start | bytes 1572872 | tf_op jit(solution)/shard_map/ppermute | solution.py:595
  97.2 29.4 %collective-permute-start.22 = (f32[2,256,256]{2,1,0:T(8,128)S(1)}, f32[2,256,256]{2,1,0:T(8,128)S(1)}, u32[]{:S(2)}, u32[]{:S(2)}) collective-permute-start(f32[2,256,256]{2,1,0:T(8,128)S(1)} %get-tuple-element.123), channel_id=1, source_target_pairs={{0,8},{1,9},{2,10},{3,11},{4,12},{5,13},{6,14},{7,15},{16,24},{17,... | collective-permute-start | bytes 1572872 | tf_op jit(solution)/shard_map/ppermute | solution.py:595
  120.6 41.6 %collective-permute-start.21 = (f32[2,512,256]{2,1,0:T(8,128)S(1)}, f32[2,512,256]{2,1,0:T(8,128)}, u32[]{:S(2)}, u32[]{:S(2)}) collective-permute-start(f32[2,512,256]{2,1,0:T(8,128)S(1)} %get-tuple-element.121), channel_id=1, source_target_pairs={{0,8},{1,9},{2,10},{3,11},{4,12},{5,13},{6,14},{7,15},{8,16},{9,17... | collective-permute-start | bytes 3145736 | tf_op jit(solution)/shard_map/ppermute | solution.py:595
  122.9 39.3 %collective-permute-start.25 = (f32[2,256,256]{2,1,0:T(8,128)S(1)}, f32[2,256,256]{2,1,0:T(8,128)}, u32[]{:S(2)}, u32[]{:S(2)}) collective-permute-start(f32[2,256,256]{2,1,0:T(8,128)S(1)} %get-tuple-element.123), channel_id=1, source_target_pairs={{8,17},{9,18},{10,19},{11,20},{12,21},{13,22},{14,23},{24,33},{25,... | collective-permute-start | bytes 1572872 | tf_op jit(solution)/shard_map/ppermute | solution.py:595
  124.4 37.8 %collective-permute-start.24 = (f32[2,256,256]{2,1,0:T(8,128)S(1)}, f32[2,256,256]{2,1,0:T(8,128)}, u32[]{:S(2)}, u32[]{:S(2)}) collective-permute-start(f32[2,256,256]{2,1,0:T(8,128)S(1)} %get-tuple-element.124), channel_id=1, source_target_pairs={{0,1},{1,2},{2,3},{3,4},{4,5},{5,6},{6,7},{8,9},{9,10},{10,11},{11... | collective-permute-start | bytes 1572872 | tf_op jit(solution)/shard_map/ppermute | solution.py:595
  127.4 34.9 %collective-permute-start.23 = (f32[2,256,256]{2,1,0:T(8,128)}, f32[2,256,256]{2,1,0:T(8,128)}, u32[]{:S(2)}, u32[]{:S(2)}) collective-permute-start(f32[2,256,256]{2,1,0:T(8,128)} %add.40), channel_id=1, source_target_pairs={{0,1},{1,2},{2,3},{3,4},{4,5},{5,6},{6,7},{8,9},{9,10},{10,11},{11... | collective-permute-start | bytes 1572872 | tf_op jit(solution)/shard_map/ppermute | solution.py:595
  140.5 21.3 %collective-permute-start = (f32[4,2,2,2,16,256]{5,4,1,0,3,2:T(8,128)S(1)}, f32[4,2,2,2,16,256]{5,4,1,0,3,2:T(8,128)S(1)}, u32[]{:S(2)}, u32[]{:S(2)}) collective-permute-start(f32[4,2,2,2,16,256]{5,4,1,0,3,2:T(8,128)S(1)} %select_bitcast_fusion), channel_id=1, source_target_pairs={{0,8},{1,9},{2,10},{3,11},{4,12},{5,13},{6,14},{7,15},{8,0},{9,1},... | collective-permute-start | bytes 1572872 | tf_op jit(solution)/shard_map/cond/branch_1_fun/ppermute | solution.py:595
  162.2 6.6 %collective-permute-start.27 = (f32[2,256,256]{2,1,0:T(8,128)}, f32[2,256,256]{2,1,0:T(8,128)S(1)}, u32[]{:S(2)}, u32[]{:S(2)}) collective-permute-start(f32[2,256,256]{2,1,0:T(8,128)} %get-tuple-element.127), channel_id=1, source_target_pairs={{0,8},{1,9},{2,10},{3,11},{4,12},{5,13},{6,14},{7,15},{16,24},{17,... | collective-permute-start | bytes 1572872 | tf_op jit(solution)/shard_map/ppermute | solution.py:595
  164.6 67.9 %collective-permute-start.26 = (f32[2,512,256]{2,1,0:T(8,128)}, f32[2,512,256]{2,1,0:T(8,128)S(1)}, u32[]{:S(2)}, u32[]{:S(2)}) collective-permute-start(f32[2,512,256]{2,1,0:T(8,128)} %get-tuple-element.125), channel_id=1, source_target_pairs={{0,8},{1,9},{2,10},{3,11},{4,12},{5,13},{6,14},{7,15},{8,16},{9,17... | collective-permute-start | bytes 3145736 | tf_op jit(solution)/shard_map/ppermute | solution.py:595
  165.9 66.5 %collective-permute-start.30 = (f32[2,256,256]{2,1,0:T(8,128)}, f32[2,256,256]{2,1,0:T(8,128)S(1)}, u32[]{:S(2)}, u32[]{:S(2)}) collective-permute-start(f32[2,256,256]{2,1,0:T(8,128)} %get-tuple-element.127), channel_id=1, source_target_pairs={{8,17},{9,18},{10,19},{11,20},{12,21},{13,22},{14,23},{24,33},{25,... | collective-permute-start | bytes 1572872 | tf_op jit(solution)/shard_map/ppermute | solution.py:595
  166.6 65.8 %collective-permute-start.29 = (f32[2,256,256]{2,1,0:T(8,128)}, f32[2,256,256]{2,1,0:T(8,128)S(1)}, u32[]{:S(2)}, u32[]{:S(2)}) collective-permute-start(f32[2,256,256]{2,1,0:T(8,128)} %get-tuple-element.128), channel_id=1, source_target_pairs={{0,1},{1,2},{2,3},{3,4},{4,5},{5,6},{6,7},{8,9},{9,10},{10,11},{11... | collective-permute-start | bytes 1572872 | tf_op jit(solution)/shard_map/ppermute | solution.py:595
  169.7 62.8 %collective-permute-start.28 = (f32[2,256,256]{2,1,0:T(8,128)}, f32[2,256,256]{2,1,0:T(8,128)S(1)}, u32[]{:S(2)}, u32[]{:S(2)}) collective-permute-start(f32[2,256,256]{2,1,0:T(8,128)} %add.41), channel_id=1, source_target_pairs={{0,1},{1,2},{2,3},{3,4},{4,5},{5,6},{6,7},{8,9},{9,10},{10,11},{11... | collective-permute-start | bytes 1572872 | tf_op jit(solution)/shard_map/ppermute | solution.py:595
  172.4 26.0 %collective-permute-start.1 = (f32[2,2,2,2,16,256]{5,4,3,2,1,0:T(8,128)}, f32[2,2,2,2,16,256]{5,4,3,2,1,0:T(8,128)S(1)}, u32[]{:S(2)}, u32[]{:S(2)}) collective-permute-start(f32[2,2,2,2,16,256]{5,4,3,2,1,0:T(8,128)} %slice_select_fusion), channel_id=1, source_target_pairs={{0,64},{1,65},{2,66},{3,67},{4,68},{5,69},{6,70},{7,71},{8,72},{9,... | collective-permute-start | bytes 786440 | tf_op jit(solution)/shard_map/cond/branch_1_fun/ppermute | solution.py:595
  198.5 6.0 %collective-permute-start.2 = (f32[2,2,2,16,256]{4,3,2,1,0:T(8,128)S(1)}, f32[2,2,2,16,256]{4,3,2,1,0:T(8,128)S(1)}, u32[]{:S(2)}, u32[]{:S(2)}) collective-permute-start(f32[2,2,2,16,256]{4,3,2,1,0:T(8,128)S(1)} %select_bitcast_fusion.1), channel_id=1, source_target_pairs={{0,32},{1,33},{2,34},{3,35},{4,36},{5,37},{6,38},{7,39},{8,40},{9,... | collective-permute-start | bytes 393224 | tf_op jit(solution)/shard_map/cond/branch_1_fun/ppermute | solution.py:595
  204.6 11.3 %collective-permute-start.3 = (f32[2,2,2,16,256]{4,3,2,1,0:T(8,128)S(1)}, f32[2,2,2,16,256]{4,3,2,1,0:T(8,128)S(1)}, u32[]{:S(2)}, u32[]{:S(2)}) collective-permute-start(f32[2,2,2,16,256]{4,3,2,1,0:T(8,128)S(1)} %bitcast_add_fusion.1), channel_id=1, source_target_pairs={{0,2},{1,3},{2,0},{3,1},{4,6},{5,7},{6,4},{7,5},{8,10},{9,11},{10,... | collective-permute-start | bytes 393224 | tf_op jit(solution)/shard_map/cond/branch_1_fun/ppermute | solution.py:595
  215.9 6.6 %collective-permute-start.4 = (f32[2,2,2,16,256]{4,3,2,1,0:T(8,128)S(1)}, f32[2,2,2,16,256]{4,3,2,1,0:T(8,128)S(1)}, u32[]{:S(2)}, u32[]{:S(2)}) collective-permute-start(f32[2,2,2,16,256]{4,3,2,1,0:T(8,128)S(1)} %add.34), channel_id=1, source_target_pairs={{0,4},{1,5},{2,6},{3,7},{4,0},{5,1},{6,2},{7,3},{8,12},{9,13},{10,... | collective-permute-start | bytes 393224 | tf_op jit(solution)/shard_map/cond/branch_1_fun/ppermute | solution.py:595
  222.5 5.6 %collective-permute-start.5 = (f32[2,2,16,256]{3,2,1,0:T(8,128)S(1)}, f32[2,2,16,256]{3,2,1,0:T(8,128)S(1)}, u32[]{:S(2)}, u32[]{:S(2)}) collective-permute-start(f32[2,2,16,256]{3,2,1,0:T(8,128)S(1)} %select_bitcast_fusion.2), channel_id=1, source_target_pairs={{0,17},{1,16},{2,19},{3,18},{4,21},{5,20},{6,23},{7,22},{8,25},{9,... | collective-permute-start | bytes 196616 | tf_op jit(solution)/shard_map/cond/branch_1_fun/ppermute | solution.py:595
  228.1 4.3 %collective-permute-start.6 = (f32[2,2,16,256]{3,2,1,0:T(8,128)S(1)}, f32[2,2,16,256]{3,2,1,0:T(8,128)S(1)}, u32[]{:S(2)}, u32[]{:S(2)}) collective-permute-start(f32[2,2,16,256]{3,2,1,0:T(8,128)S(1)} %bitcast_add_fusion.2), channel_id=1, source_target_pairs={{0,1},{1,0},{2,3},{3,2},{4,5},{5,4},{6,7},{7,6},{8,9},{9,8},{10,11... | collective-permute-start | bytes 196616 | tf_op jit(solution)/shard_map/cond/branch_1_fun/ppermute | solution.py:595
  (14 other events, 220.7 us)

commit v7 on v5

--- a/solution.py
+++ b/solution.py
@@ -413,18 +413,31 @@
 
 def join_kernel(main, right, low_a, low_b, diag, *rest):
     out = rest[-1]
-    n, h = PROBE, HALF
+    n = PROBE
     i = pl.program_id(0)
 
-    @pl.when(i < 2)
+    @pl.when(i < 4)
     def _():
         out[0, :, :, :n] = main[:, :, :n] + right[...] + low_a[...] + diag[...]
         out[0, :, :, n:] = main[:, :, n:] + low_b[...]
 
-    @pl.when(i >= 2)
+    @pl.when(i >= 4)
     def _():
         out[0, :, :, :n] = main[:, :, :n] + right[...]
         out[0, :, :, n:] = main[:, :, n:]
+
+
+def cut_kernel(obj, corner, edge, low, sems):
+    n = PROBE
+    copies = [
+        pltpu.make_async_copy(obj.at[0, :, :n, :n], corner, sems.at[0]),
+        pltpu.make_async_copy(obj.at[0, :, :, :n], edge, sems.at[1]),
+        pltpu.make_async_copy(obj.at[0, :, :n, n:], low, sems.at[2]),
+    ]
+    for copy in copies:
+        copy.start()
+    for copy in copies:
+        copy.wait()
 
 
 def whole(shape):
@@ -458,6 +471,20 @@
 
 def sds(shape):
     return jax.ShapeDtypeStruct(shape, F32)
+
+
+def cut_first(obj):
+    n = PROBE
+    return pl.pallas_call(
+        cut_kernel,
+        in_specs=[pl.BlockSpec(memory_space=pl.ANY)],
+        out_specs=[pl.BlockSpec(memory_space=pl.ANY)] * 3,
+        out_shape=[sds((2, n, n)), sds((2, TILE, n)), sds((2, n, n))],
+        scratch_shapes=[pltpu.SemaphoreType.DMA((3,))],
+        compiler_params=params(),
+        cost_estimate=cost(1e6, 4e6),
+        name="cut_pieces",
+    )(obj)
 
 
 def permute_amplitudes(amp, tables):
@@ -555,12 +582,12 @@
 
 
 def run_join(layer, main, arrived, into):
-    n, h = PROBE, HALF
-    top = lambda i: (0, jnp.minimum(i, 1), 0)
+    n, h = PROBE, HALF // 2
+    top = lambda i: (0, jnp.minimum(i, 3), 0)
     extra = [] if into is None else [into]
     return pl.pallas_call(
         join_kernel,
-        grid=(4,),
+        grid=(8,),
         in_specs=[
             pl.BlockSpec((2, h, TILE), lambda i: (0, i, 0)),
             pl.BlockSpec((2, h, n), lambda i: (0, i, 0)),
@@ -658,7 +685,7 @@
         scalars = jnp.concatenate(
             [positions.reshape(2 * SLOTS), counts.reshape(1), jnp.stack([gx & 1, gx >> 1 & 1, gx >> 2])]
         )
-        pieces_0, mine = lax.optimization_barrier((pieces(obj, 0), gather_probe(probe)))
+        pieces_0, mine = lax.optimization_barrier((cut_first(obj), gather_probe(probe)))
         halo_0 = bring(*pieces_0)
         across = send(mine, flip(2, 1))
         probe_parts = [mine, across, send(mine, flip(1, 0)), send(across, flip(1, 0))]

time: 225 us -> 271 us (1.20); the launches traced: 223 us -> 266 us
  Pallas kernels: 48.4 us -> 121 us
  waiting for transfers between devices: 63.1 us -> 48.9 us
  starting transfers between devices: 92.5 us -> 83.7 us
  local copies, waits for them, and re-layouts: 14 us -> 7.33 us
    pallas_call x2 -> x3, Pallas kernels: 8.11 us -> 60.7 us  [the longest x1 48.8 us: cut_first(): pl.pallas_call(cut_kernel, in_specs=[pl.BlockSpec(memory_space=pl.ANY)],...]
    ppermute x33, waiting for transfers between devices: 63.1 us -> 48.9 us  [send(): return lax.ppermute(x, axes, pairs)]
    ppermute x33, starting transfers between devices: 92.5 us -> 83.7 us  [send(): return lax.ppermute(x, axes, pairs)]
    pallas_call x1, Pallas kernels: 16 us -> 24.7 us  [run_far(): pl.pallas_call(far_kernel, grid_spec=pltpu.PrefetchScalarGridSpec(num_sca...]
    pallas_call x1, Pallas kernels: 10.2 us -> 16.1 us  [run_out(): pl.pallas_call(out_kernel, grid_spec=pltpu.PrefetchScalarGridSpec(num_sca...]
    pallas_call x1, Pallas kernels: 10.4 us -> 16 us  [run_home(): pl.pallas_call(home_kernel, grid_spec=pltpu.PrefetchScalarGridSpec(num_sc...]
    squeeze x4 -> x2, local copies, waits for them, and re-layouts: 7.17 us -> 2.59 us  [pieces(): return (obj[layer, :, :n, :n], obj[layer, :, :, :n], obj[layer, :, :n, n:])]
  transfers between devices with their start and end apart: 33 -> 33, of which waited for: 13 -> 13; matrix products, arithmetic and copies ran while one was open for 5% -> 2% of each run, Pallas kernels for 13% -> 34%
where the time goes in v7:
time: 271 us; the launch traced here: 266 us
  Pallas kernels  121 us (45%)
  starting transfers between devices  83.7 us (31%)
  waiting for transfers between devices  48.9 us (18%)
  local copies, waits for them, and re-layouts  7.33 us (3%)
  other arithmetic  2.87 us (1%)
    ppermute x33, starting transfers between devices, send(): return lax.ppermute(x, axes, pairs)  83.7 us
    ppermute x33, waiting for transfers between devices, send(): return lax.ppermute(x, axes, pairs)  48.9 us
    pallas_call x1, Pallas kernels, cut_first(): pl.pallas_call(cut_kernel, in_specs=[pl.BlockSpec(memory_space=pl.ANY)],...  48.8 us
    pallas_call x1, Pallas kernels, run_far(): pl.pallas_call(far_kernel, grid_spec=pltpu.PrefetchScalarGridSpec(num_sca...  24.7 us
    pallas_call x1, Pallas kernels, run_out(): pl.pallas_call(out_kernel, grid_spec=pltpu.PrefetchScalarGridSpec(num_sca...  16.1 us
    pallas_call x1, Pallas kernels, run_home(): pl.pallas_call(home_kernel, grid_spec=pltpu.PrefetchScalarGridSpec(num_sc...  16 us
    pallas_call x2, Pallas kernels, run_join(): pl.pallas_call(join_kernel, grid=(8,), in_specs=[pl.BlockSpec((2, h, TILE...  11.9 us
  transfers between devices with their start and end apart: 33, of which 13 were waited for; matrix products, arithmetic and copies ran while one was open for 2% of the time, Pallas kernels for 34%

profile of v7, /device:TPU:0, one launch (start us, length us, event | category | flops | bytes accessed | tf_op | source)
XLA Modules:
  0.0 266.0 jit_solution(7114566595908222499)
XLA Ops:
  0.7 2.1 collective-permute-start.7
  2.7 2.5 collective-permute-start.9
  6.3 48.8 %cut_pieces.1 = (f32[2,256,256]{2,1,0:T(8,128)}, f32[2,512,256]{2,1,0:T(8,128)}, f32[2,256,256]{2,1,0:T(8,128)S(1)}) custom-call(f32[2,2,512,512]{3,2,1,0:T(8,128)} %obj.5), custom_call_target="tpu_custom_call" | custom-call | flops 1000000 | bytes 4000000 | tf_op jit(solution)/shard_map/cut_pieces/pallas_call | solution.py:478
  62.0 3.7 %order_amplitudes.1.amp = f32[6,256,256]{2,1,0:T(8,128)S(1)} custom-call(f32[6,256,256]{2,1,0:T(8,128)S(1)} %bitcast.35, bf16[256,768]{1,0:T(8,128)(2,1)S(1)} %copy-done.12, bf16[768,256]{1,0:T(8,128)(2,1)S(1)} %copy-done.11), custom_call_target="tpu_custom_call" | custom-call | flops 1200000000 | bytes 4000000 | tf_op jit(solution)/shard_map/order_amplitudes/pallas_call | solution.py:492
  65.7 4.5 %collective-permute-start.15 = (f32[4,2,2,16,256]{4,3,2,1,0:T(8,128)S(1)}, f32[4,2,2,16,256]{4,3,2,1,0:T(8,128)S(1)}, u32[]{:S(2)}, u32[]{:S(2)}) collective-permute-start(f32[4,2,2,16,256]{4,3,2,1,0:T(8,128)S(1)} %pad_maximum_fusion.mine), channel_id=1, source_target_pairs={{0,17},{1,16},{2,19},{3,18},{4,21},{5,20},{6,23},{7,22},{8,25},{9,... | collective-permute-start | bytes 786440 | tf_op jit(solution)/shard_map/ppermute | solution.py:623
  74.7 8.3 %collective-permute-done.15.across = f32[4,2,2,16,256]{4,3,2,1,0:T(8,128)S(1)} collective-permute-done((f32[4,2,2,16,256]{4,3,2,1,0:T(8,128)S(1)}, f32[4,2,2,16,256]{4,3,2,1,0:T(8,128)S(1)}, u32[]{:S(2)}, u32[]{:S(2)}) %collective-permute-start.15) | collective-permute-done | bytes 262176 | tf_op jit(solution)/shard_map/ppermute | solution.py:623
  84.6 2.3 collective-permute-done.12.low_b
  91.7 16.1 %propagate_out.1 = (f32[6,2,2,256,256]{4,3,2,1,0:T(8,128)}, f32[6,2,256,256]{3,2,1,0:T(8,128)}, f32[2,2,4,2,2,16,256]{6,5,4,3,2,1,0:T(8,128)}) custom-call(s32[16]{0:T(128)S(1)} %concatenate.3.scalars, f32[2,2,512,512]{3,2,1,0:T(8,128)} %obj.5, f32[2,512,256]{2,1,0:T(8,128)S(1)} %collective-permute-done.11.right, ...), custom_call_target="tpu_custom_call" | custom-call | flops 60000002048 | bytes 20000000 | tf_op jit(solution)/shard_map/propagate_out/pallas_call | solution.py:510
  109.2 9.9 %collective-permute-done.20.low_b = f32[2,256,256]{2,1,0:T(8,128)S(1)} collective-permute-done((f32[2,256,256]{2,1,0:T(8,128)S(1)}, f32[2,256,256]{2,1,0:T(8,128)S(1)}, u32[]{:S(2)}, u32[]{:S(2)}) %collective-permute-start.20) | collective-permute-done | bytes 524320 | tf_op jit(solution)/shard_map/ppermute | solution.py:623
  119.1 1.8 collective-permute-done.22.side
  120.9 24.7 %far_field.1 = (f32[6,2,2,256,256]{4,3,2,1,0:T(8,128)}, f32[2,512,512]{2,1,0:T(8,128)}, f32[2,512,256]{2,1,0:T(8,128)}, f32[2,256,256]{2,1,0:T(8,128)S(1)}, f32[...) custom-call(s32[16]{0:T(128)S(1)} %concatenate.3.scalars, f32[2,2,512,512]{3,2,1,0:T(8,128)} %obj.5, ...), custom_call_target="tpu_custom_call" | custom-call | flops 60000002048 | bytes 20000000 | tf_op jit(solution)/shard_map/far_field/pallas_call | solution.py:532
  145.6 19.7 %collective-permute-start.24 = (f32[2,256,256]{2,1,0:T(8,128)S(1)}, f32[2,256,256]{2,1,0:T(8,128)S(1)}, u32[]{:S(2)}, u32[]{:S(2)}) collective-permute-start(f32[2,256,256]{2,1,0:T(8,128)S(1)} %get-tuple-element.133), channel_id=1, source_target_pairs={{0,8},{1,9},{2,10},{3,11},{4,12},{5,13},{6,14},{7,15},{16,24},{17,... | collective-permute-start | bytes 1572872 | tf_op jit(solution)/shard_map/ppermute | solution.py:623
  165.3 2.3 collective-permute-start.23
  169.1 2.1 collective-permute-start.26
  172.0 2.1 collective-permute-start.25
  174.1 20.8 %conditional.2 = (f32[4,2,2,2,16,256]{5,4,1,0,3,2:T(8,128)S(1)}, f32[2,512,512]{2,1,0:T(8,128)}, f32[2,512,256]{2,1,0:T(8,128)}, f32[2,256,256]{2,1,0:T(8,128)S(...) conditional(s32[]{:T(128)} %bitcast.9, () %tuple.30, (f32[2,2,4,2,2,16,256]{6,5,4,3,2,1,0:T(8,128)}, ...), branch_computations={%region_0.0_spmd, %region_1.2_spmd} | conditional | flops 60000395264 | bytes 34156064 | solution.py:712
  176.4 16.0 %propagate_home.1 = (f32[2,2,256,256]{3,2,1,0:T(8,128)S(1)}, f32[2,512,512]{2,1,0:T(8,128)}, f32[2,512,256]{2,1,0:T(8,128)}, f32[2,256,256]{2,1,0:T(8,128)S(1)},...) custom-call(s32[16]{0:T(128)S(1)} %get-tuple-element.25.scalars, f32[6,2,256,256]{3,2,1,0:T(8,128)} %get-tuple-element.26.win, ...), custom_call_target="tpu_custom_call" | custom-call | flops 60000002048 | bytes 20000000 | tf_op jit(solution)/shard_map/cond/branch_1_fun/propagate_home/pallas_call | solution.py:562
  192.6 1.9 collective-permute-done
  194.9 8.1 %collective-permute-start.29 = (f32[2,256,256]{2,1,0:T(8,128)}, f32[2,256,256]{2,1,0:T(8,128)S(1)}, u32[]{:S(2)}, u32[]{:S(2)}) collective-permute-start(f32[2,256,256]{2,1,0:T(8,128)} %get-tuple-element.137), channel_id=1, source_target_pairs={{0,8},{1,9},{2,10},{3,11},{4,12},{5,13},{6,14},{7,15},{16,24},{17,... | collective-permute-start | bytes 1572872 | tf_op jit(solution)/shard_map/ppermute | solution.py:623
  205.1 4.1 %collective-permute-start.31 = (f32[2,256,256]{2,1,0:T(8,128)}, f32[2,256,256]{2,1,0:T(8,128)S(1)}, u32[]{:S(2)}, u32[]{:S(2)}) collective-permute-start(f32[2,256,256]{2,1,0:T(8,128)} %get-tuple-element.138), channel_id=1, source_target_pairs={{0,1},{1,2},{2,3},{3,4},{4,5},{5,6},{6,7},{8,9},{9,10},{10,11},{11... | collective-permute-start | bytes 1572872 | tf_op jit(solution)/shard_map/ppermute | solution.py:623
  210.1 1.9 collective-permute-start.30
  212.0 48.2 %conditional.3 = (f32[2,2,16,256]{3,2,1,0:T(8,128)S(1)}, f32[2,2,512,512]{3,2,1,0:T(8,128)}) conditional(s32[]{:T(128)} %bitcast.9, () %tuple.37, (f32[4,2,2,2,16,256]{5,4,1,0,3,2:T(8,128)S(1)}, f32[2,512,512]{2,1,0:T(8,128)}, f32[2,512,256]{2,1,0:T(8,128)}, f32[2,256,256]{2,1,0:T(8,128)}, f32[2,256,256]{2,1,0:T(8,128)}, ...), branch_computations={%region_2.3_spmd, %region_3.4_spmd} | conditional | flops 1426045 | bytes 13340902 | solution.py:724
  212.8 2.1 collective-permute-start.1
  214.9 8.4 %collective-permute-done.1 = f32[2,2,2,2,16,256]{5,4,3,2,1,0:T(8,128)S(1)} collective-permute-done((f32[2,2,2,2,16,256]{5,4,3,2,1,0:T(8,128)}, f32[2,2,2,2,16,256]{5,4,3,2,1,0:T(8,128)S(1)}, u32[]{:S(2)}, u32[]{:S(2)}) %collective-permute-start.1) | collective-permute-done | bytes 262176 | tf_op jit(solution)/shard_map/cond/branch_1_fun/ppermute | solution.py:623
  223.5 6.2 %join_gradients.2 = f32[2,2,512,512]{3,2,1,0:T(8,128)} custom-call(f32[2,512,512]{2,1,0:T(8,128)} %get-tuple-element.38.main, f32[2,512,256]{2,1,0:T(8,128)} %get-tuple-element.39.right, f32[2,256,256]{2,1,0:T(8,128)} %get-tuple-element.40.low_a, f32[2,256,256]{2,1,0:T(8,128)} %get-tuple-element.41.low_b, f32[2,256,256]{2,1,0:T(8,128)} %get-tuple-element.42.diag), custom_call_target="tpu_custom_call" | custom-call | flops 1000000 | bytes 6000000 | tf_op jit(solution)/shard_map/cond/branch_1_fun/join_gradients/pallas_call | solution.py:588
  230.1 7.2 %collective-permute-start.3 = (f32[2,2,2,16,256]{4,3,2,1,0:T(8,128)S(1)}, f32[2,2,2,16,256]{4,3,2,1,0:T(8,128)S(1)}, u32[]{:S(2)}, u32[]{:S(2)}) collective-permute-start(f32[2,2,2,16,256]{4,3,2,1,0:T(8,128)S(1)} %bitcast_add_fusion.1), channel_id=1, source_target_pairs={{0,2},{1,3},{2,0},{3,1},{4,6},{5,7},{6,4},{7,5},{8,10},{9,11},{10,... | collective-permute-start | bytes 393224 | tf_op jit(solution)/shard_map/cond/branch_1_fun/ppermute | solution.py:623
  237.2 4.2 %collective-permute-done.3 = f32[2,2,2,16,256]{4,3,2,1,0:T(8,128)S(1)} collective-permute-done((f32[2,2,2,16,256]{4,3,2,1,0:T(8,128)S(1)}, f32[2,2,2,16,256]{4,3,2,1,0:T(8,128)S(1)}, u32[]{:S(2)}, u32[]{:S(2)}) %collective-permute-start.3) | collective-permute-done | bytes 131104 | tf_op jit(solution)/shard_map/cond/branch_1_fun/ppermute | solution.py:623
  241.5 5.8 %collective-permute-start.4 = (f32[2,2,2,16,256]{4,3,2,1,0:T(8,128)S(1)}, f32[2,2,2,16,256]{4,3,2,1,0:T(8,128)S(1)}, u32[]{:S(2)}, u32[]{:S(2)}) collective-permute-start(f32[2,2,2,16,256]{4,3,2,1,0:T(8,128)S(1)} %add.34), channel_id=1, source_target_pairs={{0,4},{1,5},{2,6},{3,7},{4,0},{5,1},{6,2},{7,3},{8,12},{9,13},{10,... | collective-permute-start | bytes 393224 | tf_op jit(solution)/shard_map/cond/branch_1_fun/ppermute | solution.py:623
  247.3 2.9 %collective-permute-done.4 = f32[2,2,2,16,256]{4,3,2,1,0:T(8,128)S(1)} collective-permute-done((f32[2,2,2,16,256]{4,3,2,1,0:T(8,128)S(1)}, f32[2,2,2,16,256]{4,3,2,1,0:T(8,128)S(1)}, u32[]{:S(2)}, u32[]{:S(2)}) %collective-permute-start.4) | collective-permute-done | bytes 131104 | tf_op jit(solution)/shard_map/cond/branch_1_fun/ppermute | solution.py:623
  250.4 5.5 %collective-permute-done.5 = f32[2,2,16,256]{3,2,1,0:T(8,128)S(1)} collective-permute-done((f32[2,2,16,256]{3,2,1,0:T(8,128)S(1)}, f32[2,2,16,256]{3,2,1,0:T(8,128)S(1)}, u32[]{:S(2)}, u32[]{:S(2)}) %collective-permute-start.5) | collective-permute-done | bytes 65568 | tf_op jit(solution)/shard_map/cond/branch_1_fun/ppermute | solution.py:623
  257.2 3.0 %collective-permute-done.6 = f32[2,2,16,256]{3,2,1,0:T(8,128)S(1)} collective-permute-done((f32[2,2,16,256]{3,2,1,0:T(8,128)S(1)}, f32[2,2,16,256]{3,2,1,0:T(8,128)S(1)}, u32[]{:S(2)}, u32[]{:S(2)}) %collective-permute-start.6) | collective-permute-done | bytes 65568 | tf_op jit(solution)/shard_map/cond/branch_1_fun/ppermute | solution.py:623
  260.3 5.7 %join_gradients.3 = f32[2,2,512,512]{3,2,1,0:T(8,128)} custom-call(f32[2,512,512]{2,1,0:T(8,128)} %get-tuple-element.125.main, f32[2,512,256]{2,1,0:T(8,128)S(1)} %collective-permute-done.28.right, f32[2,256,256]{2,1,0:T(8,128)S(1)} %collective-permute-done.30.low_a, ...), custom_call_target="tpu_custom_call", output_to_operand_aliasing={{}: (5, {})} | custom-call | flops 1000000 | bytes 6000000 | tf_op jit(solution)/shard_map/join_gradients/pallas_call | solution.py:588
  (103 shorter events, 30.2 us)
Async XLA Ops:
  0.7 54.5 %collective-permute-start.7 = (f32[2,2,16,256]{3,2,1,0:T(8,128)}, f32[2,2,16,256]{3,2,1,0:T(8,128)S(1)}, u32[]{:S(2)}, u32[]{:S(2)}) collective-permute-start(f32[2,2,16,256]{3,2,1,0:T(8,128)} %param.22), channel_id=1, source_target_pairs={{0,32},{1,33},{2,34},{3,35},{4,36},{5,37},{6,38},{7,39},{8,40},{9,... | collective-permute-start | bytes 196616 | tf_op jit(solution)/shard_map/ppermute | solution.py:623
  2.7 52.4 %collective-permute-start.9 = (f32[2,2,16,256]{3,2,1,0:T(8,128)}, f32[2,2,16,256]{3,2,1,0:T(8,128)S(1)}, u32[]{:S(2)}, u32[]{:S(2)}) collective-permute-start(f32[2,2,16,256]{3,2,1,0:T(8,128)} %param.22), channel_id=1, source_target_pairs={{0,96},{1,97},{2,98},{3,99},{4,100},{5,101},{6,102},{7,103},{8,104... | collective-permute-start | bytes 196616 | tf_op jit(solution)/shard_map/ppermute | solution.py:623
  5.3 49.9 %collective-permute-start.8 = (f32[2,2,16,256]{3,2,1,0:T(8,128)}, f32[2,2,16,256]{3,2,1,0:T(8,128)S(1)}, u32[]{:S(2)}, u32[]{:S(2)}) collective-permute-start(f32[2,2,16,256]{3,2,1,0:T(8,128)} %param.22), channel_id=1, source_target_pairs={{0,64},{1,65},{2,66},{3,67},{4,68},{5,69},{6,70},{7,71},{8,72},{9,... | collective-permute-start | bytes 196616 | tf_op jit(solution)/shard_map/ppermute | solution.py:623
  55.2 15.6 %collective-permute-start.10 = (f32[2,256,256]{2,1,0:T(8,128)}, f32[2,256,256]{2,1,0:T(8,128)S(1)}, u32[]{:S(2)}, u32[]{:S(2)}) collective-permute-start(f32[2,256,256]{2,1,0:T(8,128)} %get-tuple-element.100), channel_id=1, source_target_pairs={{1,0},{2,1},{3,2},{4,3},{5,4},{6,5},{7,6},{9,8},{10,9},{11,10},{12... | collective-permute-start | bytes 1572872 | tf_op jit(solution)/shard_map/ppermute | solution.py:623
  56.5 30.4 %collective-permute-start.11 = (f32[2,512,256]{2,1,0:T(8,128)}, f32[2,512,256]{2,1,0:T(8,128)S(1)}, u32[]{:S(2)}, u32[]{:S(2)}) collective-permute-start(f32[2,512,256]{2,1,0:T(8,128)} %get-tuple-element.102), channel_id=1, source_target_pairs={{8,0},{9,1},{10,2},{11,3},{12,4},{13,5},{14,6},{15,7},{16,8},{17,9... | collective-permute-start | bytes 3145736 | tf_op jit(solution)/shard_map/ppermute | solution.py:623
  57.8 14.3 %collective-permute-start.16 = (f32[4,2,2,16,256]{4,3,2,1,0:T(8,128)S(1)}, f32[4,2,2,16,256]{4,3,2,1,0:T(8,128)}, u32[]{:S(2)}, u32[]{:S(2)}) collective-permute-start(f32[4,2,2,16,256]{4,3,2,1,0:T(8,128)S(1)} %pad_maximum_fusion.mine), channel_id=1, source_target_pairs={{0,8},{1,9},{2,10},{3,11},{4,12},{5,13},{6,14},{7,15},{8,0},{9,1},... | collective-permute-start | bytes 786440 | tf_op jit(solution)/shard_map/ppermute | solution.py:623
  65.7 17.4 %collective-permute-start.15 = (f32[4,2,2,16,256]{4,3,2,1,0:T(8,128)S(1)}, f32[4,2,2,16,256]{4,3,2,1,0:T(8,128)S(1)}, u32[]{:S(2)}, u32[]{:S(2)}) collective-permute-start(f32[4,2,2,16,256]{4,3,2,1,0:T(8,128)S(1)} %pad_maximum_fusion.mine), channel_id=1, source_target_pairs={{0,17},{1,16},{2,19},{3,18},{4,21},{5,20},{6,23},{7,22},{8,25},{9,... | collective-permute-start | bytes 786440 | tf_op jit(solution)/shard_map/ppermute | solution.py:623
  70.1 16.8 %collective-permute-start.13 = (f32[2,256,256]{2,1,0:T(8,128)}, f32[2,256,256]{2,1,0:T(8,128)S(1)}, u32[]{:S(2)}, u32[]{:S(2)}) collective-permute-start(f32[2,256,256]{2,1,0:T(8,128)} %get-tuple-element.100), channel_id=1, source_target_pairs={{17,8},{18,9},{19,10},{20,11},{21,12},{22,13},{23,14},{33,24},{34,... | collective-permute-start | bytes 1572872 | tf_op jit(solution)/shard_map/ppermute | solution.py:623
  70.8 16.1 %collective-permute-start.12 = (f32[2,256,256]{2,1,0:T(8,128)S(1)}, f32[2,256,256]{2,1,0:T(8,128)S(1)}, u32[]{:S(2)}, u32[]{:S(2)}) collective-permute-start(f32[2,256,256]{2,1,0:T(8,128)S(1)} %copy-done.2), channel_id=1, source_target_pairs={{1,0},{2,1},{3,2},{4,3},{5,4},{6,5},{7,6},{9,8},{10,9},{11,10},{12... | collective-permute-start | bytes 1572872 | tf_op jit(solution)/shard_map/ppermute | solution.py:623
  72.1 14.8 %collective-permute-start.14 = (f32[2,256,256]{2,1,0:T(8,128)S(1)}, f32[2,256,256]{2,1,0:T(8,128)S(1)}, u32[]{:S(2)}, u32[]{:S(2)}) collective-permute-start(f32[2,256,256]{2,1,0:T(8,128)S(1)} %collective-permute-done.10.low_a), channel_id=1, source_target_pairs={{8,0},{9,1},{10,2},{11,3},{12,4},{13,5},{14,6},{15,7},{24,16},{25,... | collective-permute-start | bytes 1572872 | tf_op jit(solution)/shard_map/ppermute | solution.py:623
  87.0 32.1 %collective-permute-start.21 = (f32[2,256,256]{2,1,0:T(8,128)S(1)}, f32[2,256,256]{2,1,0:T(8,128)S(1)}, u32[]{:S(2)}, u32[]{:S(2)}) collective-permute-start(f32[2,256,256]{2,1,0:T(8,128)S(1)} %get-tuple-element.118), channel_id=1, source_target_pairs={{17,8},{18,9},{19,10},{20,11},{21,12},{22,13},{23,14},{33,24},{34,... | collective-permute-start | bytes 1572872 | tf_op jit(solution)/shard_map/ppermute | solution.py:623
  87.8 20.1 %collective-permute-start.19 = (f32[2,256,256]{2,1,0:T(8,128)S(1)}, f32[2,256,256]{2,1,0:T(8,128)S(1)}, u32[]{:S(2)}, u32[]{:S(2)}) collective-permute-start(f32[2,256,256]{2,1,0:T(8,128)S(1)} %get-tuple-element.118), channel_id=1, source_target_pairs={{1,0},{2,1},{3,2},{4,3},{5,4},{6,5},{7,6},{9,8},{10,9},{11,10},{12... | collective-permute-start | bytes 1572872 | tf_op jit(solution)/shard_map/ppermute | solution.py:623
  89.1 30.0 %collective-permute-start.20 = (f32[2,256,256]{2,1,0:T(8,128)S(1)}, f32[2,256,256]{2,1,0:T(8,128)S(1)}, u32[]{:S(2)}, u32[]{:S(2)}) collective-permute-start(f32[2,256,256]{2,1,0:T(8,128)S(1)} %get-tuple-element.121), channel_id=1, source_target_pairs={{1,0},{2,1},{3,2},{4,3},{5,4},{6,5},{7,6},{9,8},{10,9},{11,10},{12... | collective-permute-start | bytes 1572872 | tf_op jit(solution)/shard_map/ppermute | solution.py:623
  90.4 28.7 %collective-permute-start.18 = (f32[2,512,256]{2,1,0:T(8,128)S(1)}, f32[2,512,256]{2,1,0:T(8,128)S(1)}, u32[]{:S(2)}, u32[]{:S(2)}) collective-permute-start(f32[2,512,256]{2,1,0:T(8,128)S(1)} %slice_bitcast_fusion), channel_id=1, source_target_pairs={{8,0},{9,1},{10,2},{11,3},{12,4},{13,5},{14,6},{15,7},{16,8},{17,9... | collective-permute-start | bytes 3145736 | tf_op jit(solution)/shard_map/ppermute | solution.py:623
  107.9 13.0 %collective-permute-start.22 = (f32[2,256,256]{2,1,0:T(8,128)S(1)}, f32[2,256,256]{2,1,0:T(8,128)S(1)}, u32[]{:S(2)}, u32[]{:S(2)}) collective-permute-start(f32[2,256,256]{2,1,0:T(8,128)S(1)} %collective-permute-done.19.low_a), channel_id=1, source_target_pairs={{8,0},{9,1},{10,2},{11,3},{12,4},{13,5},{14,6},{15,7},{24,16},{25,... | collective-permute-start | bytes 1572872 | tf_op jit(solution)/shard_map/ppermute | solution.py:623
  145.6 25.5 %collective-permute-start.24 = (f32[2,256,256]{2,1,0:T(8,128)S(1)}, f32[2,256,256]{2,1,0:T(8,128)S(1)}, u32[]{:S(2)}, u32[]{:S(2)}) collective-permute-start(f32[2,256,256]{2,1,0:T(8,128)S(1)} %get-tuple-element.133), channel_id=1, source_target_pairs={{0,8},{1,9},{2,10},{3,11},{4,12},{5,13},{6,14},{7,15},{16,24},{17,... | collective-permute-start | bytes 1572872 | tf_op jit(solution)/shard_map/ppermute | solution.py:623
  165.3 29.6 %collective-permute-start.23 = (f32[2,512,256]{2,1,0:T(8,128)}, f32[2,512,256]{2,1,0:T(8,128)}, u32[]{:S(2)}, u32[]{:S(2)}) collective-permute-start(f32[2,512,256]{2,1,0:T(8,128)} %get-tuple-element.131), channel_id=1, source_target_pairs={{0,8},{1,9},{2,10},{3,11},{4,12},{5,13},{6,14},{7,15},{8,16},{9,17... | collective-permute-start | bytes 3145736 | tf_op jit(solution)/shard_map/ppermute | solution.py:623
  167.6 27.3 %collective-permute-start.27 = (f32[2,256,256]{2,1,0:T(8,128)S(1)}, f32[2,256,256]{2,1,0:T(8,128)}, u32[]{:S(2)}, u32[]{:S(2)}) collective-permute-start(f32[2,256,256]{2,1,0:T(8,128)S(1)} %get-tuple-element.133), channel_id=1, source_target_pairs={{8,17},{9,18},{10,19},{11,20},{12,21},{13,22},{14,23},{24,33},{25,... | collective-permute-start | bytes 1572872 | tf_op jit(solution)/shard_map/ppermute | solution.py:623
  169.1 25.8 %collective-permute-start.26 = (f32[2,256,256]{2,1,0:T(8,128)S(1)}, f32[2,256,256]{2,1,0:T(8,128)}, u32[]{:S(2)}, u32[]{:S(2)}) collective-permute-start(f32[2,256,256]{2,1,0:T(8,128)S(1)} %get-tuple-element.134), channel_id=1, source_target_pairs={{0,1},{1,2},{2,3},{3,4},{4,5},{5,6},{6,7},{8,9},{9,10},{10,11},{11... | collective-permute-start | bytes 1572872 | tf_op jit(solution)/shard_map/ppermute | solution.py:623
  172.0 22.9 %collective-permute-start.25 = (f32[2,256,256]{2,1,0:T(8,128)}, f32[2,256,256]{2,1,0:T(8,128)}, u32[]{:S(2)}, u32[]{:S(2)}) collective-permute-start(f32[2,256,256]{2,1,0:T(8,128)} %add.40), channel_id=1, source_target_pairs={{0,1},{1,2},{2,3},{3,4},{4,5},{5,6},{6,7},{8,9},{9,10},{10,11},{11... | collective-permute-start | bytes 1572872 | tf_op jit(solution)/shard_map/ppermute | solution.py:623
  192.5 2.0 collective-permute-start
  194.9 14.3 %collective-permute-start.29 = (f32[2,256,256]{2,1,0:T(8,128)}, f32[2,256,256]{2,1,0:T(8,128)S(1)}, u32[]{:S(2)}, u32[]{:S(2)}) collective-permute-start(f32[2,256,256]{2,1,0:T(8,128)} %get-tuple-element.137), channel_id=1, source_target_pairs={{0,8},{1,9},{2,10},{3,11},{4,12},{5,13},{6,14},{7,15},{16,24},{17,... | collective-permute-start | bytes 1572872 | tf_op jit(solution)/shard_map/ppermute | solution.py:623
  203.0 57.3 %collective-permute-start.28 = (f32[2,512,256]{2,1,0:T(8,128)}, f32[2,512,256]{2,1,0:T(8,128)S(1)}, u32[]{:S(2)}, u32[]{:S(2)}) collective-permute-start(f32[2,512,256]{2,1,0:T(8,128)} %get-tuple-element.135), channel_id=1, source_target_pairs={{0,8},{1,9},{2,10},{3,11},{4,12},{5,13},{6,14},{7,15},{8,16},{9,17... | collective-permute-start | bytes 3145736 | tf_op jit(solution)/shard_map/ppermute | solution.py:623
  204.4 55.9 %collective-permute-start.32 = (f32[2,256,256]{2,1,0:T(8,128)}, f32[2,256,256]{2,1,0:T(8,128)S(1)}, u32[]{:S(2)}, u32[]{:S(2)}) collective-permute-start(f32[2,256,256]{2,1,0:T(8,128)} %get-tuple-element.137), channel_id=1, source_target_pairs={{8,17},{9,18},{10,19},{11,20},{12,21},{13,22},{14,23},{24,33},{25,... | collective-permute-start | bytes 1572872 | tf_op jit(solution)/shard_map/ppermute | solution.py:623
  205.1 55.2 %collective-permute-start.31 = (f32[2,256,256]{2,1,0:T(8,128)}, f32[2,256,256]{2,1,0:T(8,128)S(1)}, u32[]{:S(2)}, u32[]{:S(2)}) collective-permute-start(f32[2,256,256]{2,1,0:T(8,128)} %get-tuple-element.138), channel_id=1, source_target_pairs={{0,1},{1,2},{2,3},{3,4},{4,5},{5,6},{6,7},{8,9},{9,10},{10,11},{11... | collective-permute-start | bytes 1572872 | tf_op jit(solution)/shard_map/ppermute | solution.py:623
  210.1 50.2 %collective-permute-start.30 = (f32[2,256,256]{2,1,0:T(8,128)}, f32[2,256,256]{2,1,0:T(8,128)S(1)}, u32[]{:S(2)}, u32[]{:S(2)}) collective-permute-start(f32[2,256,256]{2,1,0:T(8,128)} %add.41), channel_id=1, source_target_pairs={{0,1},{1,2},{2,3},{3,4},{4,5},{5,6},{6,7},{8,9},{9,10},{10,11},{11... | collective-permute-start | bytes 1572872 | tf_op jit(solution)/shard_map/ppermute | solution.py:623
  212.8 10.4 %collective-permute-start.1 = (f32[2,2,2,2,16,256]{5,4,3,2,1,0:T(8,128)}, f32[2,2,2,2,16,256]{5,4,3,2,1,0:T(8,128)S(1)}, u32[]{:S(2)}, u32[]{:S(2)}) collective-permute-start(f32[2,2,2,2,16,256]{5,4,3,2,1,0:T(8,128)} %slice_select_fusion), channel_id=1, source_target_pairs={{0,64},{1,65},{2,66},{3,67},{4,68},{5,69},{6,70},{7,71},{8,72},{9,... | collective-permute-start | bytes 786440 | tf_op jit(solution)/shard_map/cond/branch_1_fun/ppermute | solution.py:623
  223.3 6.7 %collective-permute-start.2 = (f32[2,2,2,16,256]{4,3,2,1,0:T(8,128)S(1)}, f32[2,2,2,16,256]{4,3,2,1,0:T(8,128)S(1)}, u32[]{:S(2)}, u32[]{:S(2)}) collective-permute-start(f32[2,2,2,16,256]{4,3,2,1,0:T(8,128)S(1)} %select_bitcast_fusion.1), channel_id=1, source_target_pairs={{0,32},{1,33},{2,34},{3,35},{4,36},{5,37},{6,38},{7,39},{8,40},{9,... | collective-permute-start | bytes 393224 | tf_op jit(solution)/shard_map/cond/branch_1_fun/ppermute | solution.py:623
  230.1 11.4 %collective-permute-start.3 = (f32[2,2,2,16,256]{4,3,2,1,0:T(8,128)S(1)}, f32[2,2,2,16,256]{4,3,2,1,0:T(8,128)S(1)}, u32[]{:S(2)}, u32[]{:S(2)}) collective-permute-start(f32[2,2,2,16,256]{4,3,2,1,0:T(8,128)S(1)} %bitcast_add_fusion.1), channel_id=1, source_target_pairs={{0,2},{1,3},{2,0},{3,1},{4,6},{5,7},{6,4},{7,5},{8,10},{9,11},{10,... | collective-permute-start | bytes 393224 | tf_op jit(solution)/shard_map/cond/branch_1_fun/ppermute | solution.py:623
  241.5 8.8 %collective-permute-start.4 = (f32[2,2,2,16,256]{4,3,2,1,0:T(8,128)S(1)}, f32[2,2,2,16,256]{4,3,2,1,0:T(8,128)S(1)}, u32[]{:S(2)}, u32[]{:S(2)}) collective-permute-start(f32[2,2,2,16,256]{4,3,2,1,0:T(8,128)S(1)} %add.34), channel_id=1, source_target_pairs={{0,4},{1,5},{2,6},{3,7},{4,0},{5,1},{6,2},{7,3},{8,12},{9,13},{10,... | collective-permute-start | bytes 393224 | tf_op jit(solution)/shard_map/cond/branch_1_fun/ppermute | solution.py:623
  250.3 5.6 %collective-permute-start.5 = (f32[2,2,16,256]{3,2,1,0:T(8,128)S(1)}, f32[2,2,16,256]{3,2,1,0:T(8,128)S(1)}, u32[]{:S(2)}, u32[]{:S(2)}) collective-permute-start(f32[2,2,16,256]{3,2,1,0:T(8,128)S(1)} %select_bitcast_fusion.2), channel_id=1, source_target_pairs={{0,17},{1,16},{2,19},{3,18},{4,21},{5,20},{6,23},{7,22},{8,25},{9,... | collective-permute-start | bytes 196616 | tf_op jit(solution)/shard_map/cond/branch_1_fun/ppermute | solution.py:623
  255.9 4.3 %collective-permute-start.6 = (f32[2,2,16,256]{3,2,1,0:T(8,128)S(1)}, f32[2,2,16,256]{3,2,1,0:T(8,128)S(1)}, u32[]{:S(2)}, u32[]{:S(2)}) collective-permute-start(f32[2,2,16,256]{3,2,1,0:T(8,128)S(1)} %bitcast_add_fusion.2), channel_id=1, source_target_pairs={{0,1},{1,0},{2,3},{3,2},{4,5},{5,4},{6,7},{7,6},{8,9},{9,8},{10,11... | collective-permute-start | bytes 196616 | tf_op jit(solution)/shard_map/cond/branch_1_fun/ppermute | solution.py:623
  (21 other events, 483.0 us)

commit v8 on v5

--- a/solution.py
+++ b/solution.py
@@ -413,15 +413,15 @@
 
 def join_kernel(main, right, low_a, low_b, diag, *rest):
     out = rest[-1]
-    n, h = PROBE, HALF
+    n = PROBE
     i = pl.program_id(0)
 
-    @pl.when(i < 2)
+    @pl.when(i < 1)
     def _():
         out[0, :, :, :n] = main[:, :, :n] + right[...] + low_a[...] + diag[...]
         out[0, :, :, n:] = main[:, :, n:] + low_b[...]
 
-    @pl.when(i >= 2)
+    @pl.when(i >= 1)
     def _():
         out[0, :, :, :n] = main[:, :, :n] + right[...]
         out[0, :, :, n:] = main[:, :, n:]
@@ -555,12 +555,12 @@
 
 
 def run_join(layer, main, arrived, into):
-    n, h = PROBE, HALF
-    top = lambda i: (0, jnp.minimum(i, 1), 0)
+    n, h = PROBE, PROBE
+    top = lambda i: (0, 0, 0)
     extra = [] if into is None else [into]
     return pl.pallas_call(
         join_kernel,
-        grid=(4,),
+        grid=(2,),
         in_specs=[
             pl.BlockSpec((2, h, TILE), lambda i: (0, i, 0)),
             pl.BlockSpec((2, h, n), lambda i: (0, i, 0)),

time: 225 us -> 223 us (level)
  starting transfers between devices: 92.5 us -> 103 us
  Pallas kernels: 48.4 us -> 39.8 us
  waiting for transfers between devices: 63.1 us -> 58.4 us
    ppermute x33, starting transfers between devices: 92.5 us -> 103 us  [send(): return lax.ppermute(x, axes, pairs)]
    ppermute x33, waiting for transfers between devices: 63.1 us -> 58.4 us  [send(): return lax.ppermute(x, axes, pairs)]
    pallas_call x1, Pallas kernels: 16 us -> 13.2 us  [run_far(): pl.pallas_call(far_kernel, grid_spec=pltpu.PrefetchScalarGridSpec(num_sca...]
  transfers between devices with their start and end apart: 33 -> 33, of which waited for: 13 -> 13; matrix products, arithmetic and copies ran while one was open for 5% -> 5% of each run, Pallas kernels for 13% -> 11%
where the time goes in v8:
time: 223 us; the launch traced here: 220 us
  starting transfers between devices  103 us (46%)
  waiting for transfers between devices  58.4 us (26%)
  Pallas kernels  39.8 us (18%)
  local copies, waits for them, and re-layouts  14 us (6%)
  other arithmetic  2.88 us (1%)
    ppermute x33, starting transfers between devices, send(): return lax.ppermute(x, axes, pairs)  103 us
    ppermute x33, waiting for transfers between devices, send(): return lax.ppermute(x, axes, pairs)  58.4 us
    pallas_call x1, Pallas kernels, run_far(): pl.pallas_call(far_kernel, grid_spec=pltpu.PrefetchScalarGridSpec(num_sca...  13.2 us
    pallas_call x1, Pallas kernels, run_home(): pl.pallas_call(home_kernel, grid_spec=pltpu.PrefetchScalarGridSpec(num_sc...  8.58 us
    pallas_call x1, Pallas kernels, run_out(): pl.pallas_call(out_kernel, grid_spec=pltpu.PrefetchScalarGridSpec(num_sca...  8.29 us
    squeeze x4, local copies, waits for them, and re-layouts, pieces(): return (obj[layer, :, :n, :n], obj[layer, :, :, :n], obj[layer, :, :n, n:])  7.17 us
    pallas_call x2, Pallas kernels, run_join(): pl.pallas_call(join_kernel, grid=(2,), in_specs=[pl.BlockSpec((2, h, TILE...  6.11 us
  transfers between devices with their start and end apart: 33, of which 13 were waited for; matrix products, arithmetic and copies ran while one was open for 5% of the time, Pallas kernels for 11%

profile of v8, /device:TPU:0, one launch (start us, length us, event | category | flops | bytes accessed | tf_op | source)
XLA Modules:
  0.0 220.1 jit_solution(17108721377736460703)
XLA Ops:
  0.7 2.1 collective-permute-start.7
  2.7 2.5 %collective-permute-start.9 = (f32[2,2,16,256]{3,2,1,0:T(8,128)}, f32[2,2,16,256]{3,2,1,0:T(8,128)S(1)}, u32[]{:S(2)}, u32[]{:S(2)}) collective-permute-start(f32[2,2,16,256]{3,2,1,0:T(8,128)} %param.22), channel_id=1, source_target_pairs={{0,96},{1,97},{2,98},{3,99},{4,100},{5,101},{6,102},{7,103},{8,104... | collective-permute-start | bytes 196616 | tf_op jit(solution)/shard_map/ppermute | solution.py:596
  6.3 2.3 %slice_bitcast_fusion.1 = f32[2,512,256]{2,1,0:T(8,128)} fusion(f32[2,2,512,512]{3,2,1,0:T(8,128)} %obj.3), kind=kLoop, calls=%fused_computation.10 | loop fusion | bytes 2097152 | tf_op jit(solution)/shard_map/squeeze | solution.py:603
  8.6 2.3 %slice_bitcast_fusion.4 = (f32[2,256,256]{2,1,0:T(8,128)}, f32[2,256,256]{2,1,0:T(8,128)}) fusion(f32[2,2,512,512]{3,2,1,0:T(8,128)} %obj.3), kind=kLoop, calls=%fused_computation.13 | loop fusion | bytes 2097152 | tf_op jit(solution)/shard_map/squeeze | solution.py:603
  18.0 3.7 %order_amplitudes.1.amp = f32[6,256,256]{2,1,0:T(8,128)S(1)} custom-call(f32[6,256,256]{2,1,0:T(8,128)S(1)} %bitcast.41, bf16[256,768]{1,0:T(8,128)(2,1)S(1)} %copy-done.10, bf16[768,256]{1,0:T(8,128)(2,1)S(1)} %copy-done.9), custom_call_target="tpu_custom_call" | custom-call | flops 1200000000 | bytes 4000000 | tf_op jit(solution)/shard_map/order_amplitudes/pallas_call | solution.py:465
  22.8 4.4 %collective-permute-start.15 = (f32[4,2,2,16,256]{4,3,2,1,0:T(8,128)S(1)}, f32[4,2,2,16,256]{4,3,2,1,0:T(8,128)S(1)}, u32[]{:S(2)}, u32[]{:S(2)}) collective-permute-start(f32[4,2,2,16,256]{4,3,2,1,0:T(8,128)S(1)} %pad_maximum_fusion.mine), channel_id=1, source_target_pairs={{0,17},{1,16},{2,19},{3,18},{4,21},{5,20},{6,23},{7,22},{8,25},{9,... | collective-permute-start | bytes 786440 | tf_op jit(solution)/shard_map/ppermute | solution.py:596
  31.8 9.7 %collective-permute-done.15.across = f32[4,2,2,16,256]{4,3,2,1,0:T(8,128)S(1)} collective-permute-done((f32[4,2,2,16,256]{4,3,2,1,0:T(8,128)S(1)}, f32[4,2,2,16,256]{4,3,2,1,0:T(8,128)S(1)}, u32[]{:S(2)}, u32[]{:S(2)}) %collective-permute-start.15) | collective-permute-done | bytes 262176 | tf_op jit(solution)/shard_map/ppermute | solution.py:596
  48.8 8.3 %propagate_out.1 = (f32[6,2,2,256,256]{4,3,2,1,0:T(8,128)}, f32[6,2,256,256]{3,2,1,0:T(8,128)}, f32[2,2,4,2,2,16,256]{6,5,4,3,2,1,0:T(8,128)}) custom-call(s32[16]{0:T(128)S(1)} %concatenate.3.scalars, f32[2,2,512,512]{3,2,1,0:T(8,128)} %obj.3, f32[2,512,256]{2,1,0:T(8,128)S(1)} %collective-permute-done.11.right, ...), custom_call_target="tpu_custom_call" | custom-call | flops 60000002048 | bytes 20000000 | tf_op jit(solution)/shard_map/propagate_out/pallas_call | solution.py:483
  57.1 9.2 %collective-permute-done.19.low_a = f32[2,256,256]{2,1,0:T(8,128)S(1)} collective-permute-done((f32[2,256,256]{2,1,0:T(8,128)S(1)}, f32[2,256,256]{2,1,0:T(8,128)S(1)}, u32[]{:S(2)}, u32[]{:S(2)}) %collective-permute-start.19) | collective-permute-done | bytes 524320 | tf_op jit(solution)/shard_map/ppermute | solution.py:596
  67.6 9.9 %collective-permute-done.20.low_b = f32[2,256,256]{2,1,0:T(8,128)S(1)} collective-permute-done((f32[2,256,256]{2,1,0:T(8,128)S(1)}, f32[2,256,256]{2,1,0:T(8,128)S(1)}, u32[]{:S(2)}, u32[]{:S(2)}) %collective-permute-start.20) | collective-permute-done | bytes 524320 | tf_op jit(solution)/shard_map/ppermute | solution.py:596
  78.6 13.2 %far_field.1 = (f32[6,2,2,256,256]{4,3,2,1,0:T(8,128)}, f32[2,512,512]{2,1,0:T(8,128)}, f32[2,512,256]{2,1,0:T(8,128)}, f32[2,256,256]{2,1,0:T(8,128)S(1)}, f32[...) custom-call(s32[16]{0:T(128)S(1)} %concatenate.3.scalars, f32[2,2,512,512]{3,2,1,0:T(8,128)} %obj.3, ...), custom_call_target="tpu_custom_call" | custom-call | flops 60000002048 | bytes 20000000 | tf_op jit(solution)/shard_map/far_field/pallas_call | solution.py:505
  91.7 20.7 %collective-permute-start.24 = (f32[2,256,256]{2,1,0:T(8,128)S(1)}, f32[2,256,256]{2,1,0:T(8,128)S(1)}, u32[]{:S(2)}, u32[]{:S(2)}) collective-permute-start(f32[2,256,256]{2,1,0:T(8,128)S(1)} %get-tuple-element.127), channel_id=1, source_target_pairs={{0,8},{1,9},{2,10},{3,11},{4,12},{5,13},{6,14},{7,15},{16,24},{17,... | collective-permute-start | bytes 1572872 | tf_op jit(solution)/shard_map/ppermute | solution.py:596
  112.4 2.3 %collective-permute-start.23 = (f32[2,512,256]{2,1,0:T(8,128)}, f32[2,512,256]{2,1,0:T(8,128)}, u32[]{:S(2)}, u32[]{:S(2)}) collective-permute-start(f32[2,512,256]{2,1,0:T(8,128)} %get-tuple-element.125), channel_id=1, source_target_pairs={{0,8},{1,9},{2,10},{3,11},{4,12},{5,13},{6,14},{7,15},{8,16},{9,17... | collective-permute-start | bytes 3145736 | tf_op jit(solution)/shard_map/ppermute | solution.py:596
  116.2 2.1 collective-permute-start.26
  119.1 6.6 %collective-permute-start.25 = (f32[2,256,256]{2,1,0:T(8,128)}, f32[2,256,256]{2,1,0:T(8,128)}, u32[]{:S(2)}, u32[]{:S(2)}) collective-permute-start(f32[2,256,256]{2,1,0:T(8,128)} %add.40), channel_id=1, source_target_pairs={{0,1},{1,2},{2,3},{3,4},{4,5},{5,6},{6,7},{8,9},{9,10},{10,11},{11... | collective-permute-start | bytes 1572872 | tf_op jit(solution)/shard_map/ppermute | solution.py:596
  125.7 16.5 %conditional.2 = (f32[4,2,2,2,16,256]{5,4,1,0,3,2:T(8,128)S(1)}, f32[2,512,512]{2,1,0:T(8,128)}, f32[2,512,256]{2,1,0:T(8,128)}, f32[2,256,256]{2,1,0:T(8,128)S(...) conditional(s32[]{:T(128)} %bitcast.9, () %tuple.30, (f32[2,2,4,2,2,16,256]{6,5,4,3,2,1,0:T(8,128)}, ...), branch_computations={%region_0.0_spmd, %region_1.2_spmd} | conditional | flops 60000395264 | bytes 34156064 | solution.py:685
  128.0 8.6 %propagate_home.1 = (f32[2,2,256,256]{3,2,1,0:T(8,128)S(1)}, f32[2,512,512]{2,1,0:T(8,128)}, f32[2,512,256]{2,1,0:T(8,128)}, f32[2,256,256]{2,1,0:T(8,128)S(1)},...) custom-call(s32[16]{0:T(128)S(1)} %get-tuple-element.25.scalars, f32[6,2,256,256]{3,2,1,0:T(8,128)} %get-tuple-element.26.win, ...), custom_call_target="tpu_custom_call" | custom-call | flops 60000002048 | bytes 20000000 | tf_op jit(solution)/shard_map/cond/branch_1_fun/propagate_home/pallas_call | solution.py:535
  136.8 3.6 %collective-permute-start = (f32[4,2,2,2,16,256]{5,4,1,0,3,2:T(8,128)S(1)}, f32[4,2,2,2,16,256]{5,4,1,0,3,2:T(8,128)S(1)}, u32[]{:S(2)}, u32[]{:S(2)}) collective-permute-start(f32[4,2,2,2,16,256]{5,4,1,0,3,2:T(8,128)S(1)} %select_bitcast_fusion), channel_id=1, source_target_pairs={{0,8},{1,9},{2,10},{3,11},{4,12},{5,13},{6,14},{7,15},{8,0},{9,1},... | collective-permute-start | bytes 1572872 | tf_op jit(solution)/shard_map/cond/branch_1_fun/ppermute | solution.py:596
  142.3 7.9 %collective-permute-start.29 = (f32[2,256,256]{2,1,0:T(8,128)}, f32[2,256,256]{2,1,0:T(8,128)S(1)}, u32[]{:S(2)}, u32[]{:S(2)}) collective-permute-start(f32[2,256,256]{2,1,0:T(8,128)} %get-tuple-element.131), channel_id=1, source_target_pairs={{0,8},{1,9},{2,10},{3,11},{4,12},{5,13},{6,14},{7,15},{16,24},{17,... | collective-permute-start | bytes 1572872 | tf_op jit(solution)/shard_map/ppermute | solution.py:596
  152.2 4.1 %collective-permute-start.31 = (f32[2,256,256]{2,1,0:T(8,128)}, f32[2,256,256]{2,1,0:T(8,128)S(1)}, u32[]{:S(2)}, u32[]{:S(2)}) collective-permute-start(f32[2,256,256]{2,1,0:T(8,128)} %get-tuple-element.132), channel_id=1, source_target_pairs={{0,1},{1,2},{2,3},{3,4},{4,5},{5,6},{6,7},{8,9},{9,10},{10,11},{11... | collective-permute-start | bytes 1572872 | tf_op jit(solution)/shard_map/ppermute | solution.py:596
  157.2 4.8 %collective-permute-start.30 = (f32[2,256,256]{2,1,0:T(8,128)}, f32[2,256,256]{2,1,0:T(8,128)S(1)}, u32[]{:S(2)}, u32[]{:S(2)}) collective-permute-start(f32[2,256,256]{2,1,0:T(8,128)} %add.41), channel_id=1, source_target_pairs={{0,1},{1,2},{2,3},{3,4},{4,5},{5,6},{6,7},{8,9},{9,10},{10,11},{11... | collective-permute-start | bytes 1572872 | tf_op jit(solution)/shard_map/ppermute | solution.py:596
  162.0 55.3 %conditional.3 = (f32[2,2,16,256]{3,2,1,0:T(8,128)S(1)}, f32[2,2,512,512]{3,2,1,0:T(8,128)}) conditional(s32[]{:T(128)} %bitcast.9, () %tuple.37, (f32[4,2,2,2,16,256]{5,4,1,0,3,2:T(8,128)S(1)}, f32[2,512,512]{2,1,0:T(8,128)}, f32[2,512,256]{2,1,0:T(8,128)}, f32[2,256,256]{2,1,0:T(8,128)}, f32[2,256,256]{2,1,0:T(8,128)}, ...), branch_computations={%region_2.3_spmd, %region_3.4_spmd} | conditional | flops 1426045 | bytes 13340902 | solution.py:697
  162.8 5.8 %collective-permute-start.1 = (f32[2,2,2,2,16,256]{5,4,3,2,1,0:T(8,128)}, f32[2,2,2,2,16,256]{5,4,3,2,1,0:T(8,128)S(1)}, u32[]{:S(2)}, u32[]{:S(2)}) collective-permute-start(f32[2,2,2,2,16,256]{5,4,3,2,1,0:T(8,128)} %slice_select_fusion), channel_id=1, source_target_pairs={{0,64},{1,65},{2,66},{3,67},{4,68},{5,69},{6,70},{7,71},{8,72},{9,... | collective-permute-start | bytes 786440 | tf_op jit(solution)/shard_map/cond/branch_1_fun/ppermute | solution.py:596
  168.6 9.4 %collective-permute-done.1 = f32[2,2,2,2,16,256]{5,4,3,2,1,0:T(8,128)S(1)} collective-permute-done((f32[2,2,2,2,16,256]{5,4,3,2,1,0:T(8,128)}, f32[2,2,2,2,16,256]{5,4,3,2,1,0:T(8,128)S(1)}, u32[]{:S(2)}, u32[]{:S(2)}) %collective-permute-start.1) | collective-permute-done | bytes 262176 | tf_op jit(solution)/shard_map/cond/branch_1_fun/ppermute | solution.py:596
  178.1 3.4 %join_gradients.2 = f32[2,2,512,512]{3,2,1,0:T(8,128)} custom-call(f32[2,512,512]{2,1,0:T(8,128)} %get-tuple-element.38.main, f32[2,512,256]{2,1,0:T(8,128)} %get-tuple-element.39.right, f32[2,256,256]{2,1,0:T(8,128)} %get-tuple-element.40.low_a, f32[2,256,256]{2,1,0:T(8,128)} %get-tuple-element.41.low_b, f32[2,256,256]{2,1,0:T(8,128)} %get-tuple-element.42.diag), custom_call_target="tpu_custom_call" | custom-call | flops 1000000 | bytes 6000000 | tf_op jit(solution)/shard_map/cond/branch_1_fun/join_gradients/pallas_call | solution.py:561
  183.1 9.2 %collective-permute-start.3 = (f32[2,2,2,16,256]{4,3,2,1,0:T(8,128)S(1)}, f32[2,2,2,16,256]{4,3,2,1,0:T(8,128)S(1)}, u32[]{:S(2)}, u32[]{:S(2)}) collective-permute-start(f32[2,2,2,16,256]{4,3,2,1,0:T(8,128)S(1)} %bitcast_add_fusion.1), channel_id=1, source_target_pairs={{0,2},{1,3},{2,0},{3,1},{4,6},{5,7},{6,4},{7,5},{8,10},{9,11},{10,... | collective-permute-start | bytes 393224 | tf_op jit(solution)/shard_map/cond/branch_1_fun/ppermute | solution.py:596
  192.3 2.9 %collective-permute-done.3 = f32[2,2,2,16,256]{4,3,2,1,0:T(8,128)S(1)} collective-permute-done((f32[2,2,2,16,256]{4,3,2,1,0:T(8,128)S(1)}, f32[2,2,2,16,256]{4,3,2,1,0:T(8,128)S(1)}, u32[]{:S(2)}, u32[]{:S(2)}) %collective-permute-start.3) | collective-permute-done | bytes 131104 | tf_op jit(solution)/shard_map/cond/branch_1_fun/ppermute | solution.py:596
  195.3 9.1 %collective-permute-start.4 = (f32[2,2,2,16,256]{4,3,2,1,0:T(8,128)S(1)}, f32[2,2,2,16,256]{4,3,2,1,0:T(8,128)S(1)}, u32[]{:S(2)}, u32[]{:S(2)}) collective-permute-start(f32[2,2,2,16,256]{4,3,2,1,0:T(8,128)S(1)} %add.34), channel_id=1, source_target_pairs={{0,4},{1,5},{2,6},{3,7},{4,0},{5,1},{6,2},{7,3},{8,12},{9,13},{10,... | collective-permute-start | bytes 393224 | tf_op jit(solution)/shard_map/cond/branch_1_fun/ppermute | solution.py:596
  204.4 2.9 %collective-permute-done.4 = f32[2,2,2,16,256]{4,3,2,1,0:T(8,128)S(1)} collective-permute-done((f32[2,2,2,16,256]{4,3,2,1,0:T(8,128)S(1)}, f32[2,2,2,16,256]{4,3,2,1,0:T(8,128)S(1)}, u32[]{:S(2)}, u32[]{:S(2)}) %collective-permute-start.4) | collective-permute-done | bytes 131104 | tf_op jit(solution)/shard_map/cond/branch_1_fun/ppermute | solution.py:596
  207.5 5.5 %collective-permute-done.5 = f32[2,2,16,256]{3,2,1,0:T(8,128)S(1)} collective-permute-done((f32[2,2,16,256]{3,2,1,0:T(8,128)S(1)}, f32[2,2,16,256]{3,2,1,0:T(8,128)S(1)}, u32[]{:S(2)}, u32[]{:S(2)}) %collective-permute-start.5) | collective-permute-done | bytes 65568 | tf_op jit(solution)/shard_map/cond/branch_1_fun/ppermute | solution.py:596
  213.0 4.3 %collective-permute-done.6 = f32[2,2,16,256]{3,2,1,0:T(8,128)S(1)} collective-permute-done((f32[2,2,16,256]{3,2,1,0:T(8,128)S(1)}, f32[2,2,16,256]{3,2,1,0:T(8,128)S(1)}, u32[]{:S(2)}, u32[]{:S(2)}) %collective-permute-start.6) | collective-permute-done | bytes 65568 | tf_op jit(solution)/shard_map/cond/branch_1_fun/ppermute | solution.py:596
  217.4 2.7 %join_gradients.3 = f32[2,2,512,512]{3,2,1,0:T(8,128)} custom-call(f32[2,512,512]{2,1,0:T(8,128)} %get-tuple-element.119.main, f32[2,512,256]{2,1,0:T(8,128)S(1)} %collective-permute-done.28.right, f32[2,256,256]{2,1,0:T(8,128)S(1)} %collective-permute-done.30.low_a, ...), custom_call_target="tpu_custom_call", output_to_operand_aliasing={{}: (5, {})} | custom-call | flops 1000000 | bytes 6000000 | tf_op jit(solution)/shard_map/join_gradients/pallas_call | solution.py:561
  (102 shorter events, 34.8 us)
Async XLA Ops:
  0.7 10.2 %collective-permute-start.7 = (f32[2,2,16,256]{3,2,1,0:T(8,128)}, f32[2,2,16,256]{3,2,1,0:T(8,128)S(1)}, u32[]{:S(2)}, u32[]{:S(2)}) collective-permute-start(f32[2,2,16,256]{3,2,1,0:T(8,128)} %param.22), channel_id=1, source_target_pairs={{0,32},{1,33},{2,34},{3,35},{4,36},{5,37},{6,38},{7,39},{8,40},{9,... | collective-permute-start | bytes 196616 | tf_op jit(solution)/shard_map/ppermute | solution.py:596
  2.7 8.2 %collective-permute-start.9 = (f32[2,2,16,256]{3,2,1,0:T(8,128)}, f32[2,2,16,256]{3,2,1,0:T(8,128)S(1)}, u32[]{:S(2)}, u32[]{:S(2)}) collective-permute-start(f32[2,2,16,256]{3,2,1,0:T(8,128)} %param.22), channel_id=1, source_target_pairs={{0,96},{1,97},{2,98},{3,99},{4,100},{5,101},{6,102},{7,103},{8,104... | collective-permute-start | bytes 196616 | tf_op jit(solution)/shard_map/ppermute | solution.py:596
  5.3 6.0 %collective-permute-start.8 = (f32[2,2,16,256]{3,2,1,0:T(8,128)}, f32[2,2,16,256]{3,2,1,0:T(8,128)S(1)}, u32[]{:S(2)}, u32[]{:S(2)}) collective-permute-start(f32[2,2,16,256]{3,2,1,0:T(8,128)} %param.22), channel_id=1, source_target_pairs={{0,64},{1,65},{2,66},{3,67},{4,68},{5,69},{6,70},{7,71},{8,72},{9,... | collective-permute-start | bytes 196616 | tf_op jit(solution)/shard_map/ppermute | solution.py:596
  11.3 16.6 %collective-permute-start.10 = (f32[2,256,256]{2,1,0:T(8,128)}, f32[2,256,256]{2,1,0:T(8,128)S(1)}, u32[]{:S(2)}, u32[]{:S(2)}) collective-permute-start(f32[2,256,256]{2,1,0:T(8,128)} %get-tuple-element.94), channel_id=1, source_target_pairs={{1,0},{2,1},{3,2},{4,3},{5,4},{6,5},{7,6},{9,8},{10,9},{11,10},{12... | collective-permute-start | bytes 1572872 | tf_op jit(solution)/shard_map/ppermute | solution.py:596
  12.6 31.4 %collective-permute-start.11 = (f32[2,512,256]{2,1,0:T(8,128)}, f32[2,512,256]{2,1,0:T(8,128)S(1)}, u32[]{:S(2)}, u32[]{:S(2)}) collective-permute-start(f32[2,512,256]{2,1,0:T(8,128)} %slice_bitcast_fusion.1), channel_id=1, source_target_pairs={{8,0},{9,1},{10,2},{11,3},{12,4},{13,5},{14,6},{15,7},{16,8},{17,9... | collective-permute-start | bytes 3145736 | tf_op jit(solution)/shard_map/ppermute | solution.py:596
  13.9 15.3 %collective-permute-start.16 = (f32[4,2,2,16,256]{4,3,2,1,0:T(8,128)S(1)}, f32[4,2,2,16,256]{4,3,2,1,0:T(8,128)}, u32[]{:S(2)}, u32[]{:S(2)}) collective-permute-start(f32[4,2,2,16,256]{4,3,2,1,0:T(8,128)S(1)} %pad_maximum_fusion.mine), channel_id=1, source_target_pairs={{0,8},{1,9},{2,10},{3,11},{4,12},{5,13},{6,14},{7,15},{8,0},{9,1},... | collective-permute-start | bytes 786440 | tf_op jit(solution)/shard_map/ppermute | solution.py:596
  22.8 18.7 %collective-permute-start.15 = (f32[4,2,2,16,256]{4,3,2,1,0:T(8,128)S(1)}, f32[4,2,2,16,256]{4,3,2,1,0:T(8,128)S(1)}, u32[]{:S(2)}, u32[]{:S(2)}) collective-permute-start(f32[4,2,2,16,256]{4,3,2,1,0:T(8,128)S(1)} %pad_maximum_fusion.mine), channel_id=1, source_target_pairs={{0,17},{1,16},{2,19},{3,18},{4,21},{5,20},{6,23},{7,22},{8,25},{9,... | collective-permute-start | bytes 786440 | tf_op jit(solution)/shard_map/ppermute | solution.py:596
  27.2 16.8 %collective-permute-start.13 = (f32[2,256,256]{2,1,0:T(8,128)}, f32[2,256,256]{2,1,0:T(8,128)S(1)}, u32[]{:S(2)}, u32[]{:S(2)}) collective-permute-start(f32[2,256,256]{2,1,0:T(8,128)} %get-tuple-element.94), channel_id=1, source_target_pairs={{17,8},{18,9},{19,10},{20,11},{21,12},{22,13},{23,14},{33,24},{34,... | collective-permute-start | bytes 1572872 | tf_op jit(solution)/shard_map/ppermute | solution.py:596
  27.9 16.1 %collective-permute-start.12 = (f32[2,256,256]{2,1,0:T(8,128)S(1)}, f32[2,256,256]{2,1,0:T(8,128)S(1)}, u32[]{:S(2)}, u32[]{:S(2)}) collective-permute-start(f32[2,256,256]{2,1,0:T(8,128)S(1)} %copy-done.14), channel_id=1, source_target_pairs={{1,0},{2,1},{3,2},{4,3},{5,4},{6,5},{7,6},{9,8},{10,9},{11,10},{12... | collective-permute-start | bytes 1572872 | tf_op jit(solution)/shard_map/ppermute | solution.py:596
  29.2 14.8 %collective-permute-start.14 = (f32[2,256,256]{2,1,0:T(8,128)S(1)}, f32[2,256,256]{2,1,0:T(8,128)S(1)}, u32[]{:S(2)}, u32[]{:S(2)}) collective-permute-start(f32[2,256,256]{2,1,0:T(8,128)S(1)} %collective-permute-done.10.low_a), channel_id=1, source_target_pairs={{8,0},{9,1},{10,2},{11,3},{12,4},{13,5},{14,6},{15,7},{24,16},{25,... | collective-permute-start | bytes 1572872 | tf_op jit(solution)/shard_map/ppermute | solution.py:596
  44.0 33.5 %collective-permute-start.21 = (f32[2,256,256]{2,1,0:T(8,128)S(1)}, f32[2,256,256]{2,1,0:T(8,128)S(1)}, u32[]{:S(2)}, u32[]{:S(2)}) collective-permute-start(f32[2,256,256]{2,1,0:T(8,128)S(1)} %get-tuple-element.112), channel_id=1, source_target_pairs={{17,8},{18,9},{19,10},{20,11},{21,12},{22,13},{23,14},{33,24},{34,... | collective-permute-start | bytes 1572872 | tf_op jit(solution)/shard_map/ppermute | solution.py:596
  44.9 21.4 %collective-permute-start.19 = (f32[2,256,256]{2,1,0:T(8,128)S(1)}, f32[2,256,256]{2,1,0:T(8,128)S(1)}, u32[]{:S(2)}, u32[]{:S(2)}) collective-permute-start(f32[2,256,256]{2,1,0:T(8,128)S(1)} %get-tuple-element.112), channel_id=1, source_target_pairs={{1,0},{2,1},{3,2},{4,3},{5,4},{6,5},{7,6},{9,8},{10,9},{11,10},{12... | collective-permute-start | bytes 1572872 | tf_op jit(solution)/shard_map/ppermute | solution.py:596
  46.2 31.3 %collective-permute-start.20 = (f32[2,256,256]{2,1,0:T(8,128)S(1)}, f32[2,256,256]{2,1,0:T(8,128)S(1)}, u32[]{:S(2)}, u32[]{:S(2)}) collective-permute-start(f32[2,256,256]{2,1,0:T(8,128)S(1)} %get-tuple-element.115), channel_id=1, source_target_pairs={{1,0},{2,1},{3,2},{4,3},{5,4},{6,5},{7,6},{9,8},{10,9},{11,10},{12... | collective-permute-start | bytes 1572872 | tf_op jit(solution)/shard_map/ppermute | solution.py:596
  47.5 30.0 %collective-permute-start.18 = (f32[2,512,256]{2,1,0:T(8,128)S(1)}, f32[2,512,256]{2,1,0:T(8,128)S(1)}, u32[]{:S(2)}, u32[]{:S(2)}) collective-permute-start(f32[2,512,256]{2,1,0:T(8,128)S(1)} %slice_bitcast_fusion), channel_id=1, source_target_pairs={{8,0},{9,1},{10,2},{11,3},{12,4},{13,5},{14,6},{15,7},{16,8},{17,9... | collective-permute-start | bytes 3145736 | tf_op jit(solution)/shard_map/ppermute | solution.py:596
  66.3 11.2 %collective-permute-start.22 = (f32[2,256,256]{2,1,0:T(8,128)S(1)}, f32[2,256,256]{2,1,0:T(8,128)S(1)}, u32[]{:S(2)}, u32[]{:S(2)}) collective-permute-start(f32[2,256,256]{2,1,0:T(8,128)S(1)} %collective-permute-done.19.low_a), channel_id=1, source_target_pairs={{8,0},{9,1},{10,2},{11,3},{12,4},{13,5},{14,6},{15,7},{24,16},{25,... | collective-permute-start | bytes 1572872 | tf_op jit(solution)/shard_map/ppermute | solution.py:596
  91.7 26.5 %collective-permute-start.24 = (f32[2,256,256]{2,1,0:T(8,128)S(1)}, f32[2,256,256]{2,1,0:T(8,128)S(1)}, u32[]{:S(2)}, u32[]{:S(2)}) collective-permute-start(f32[2,256,256]{2,1,0:T(8,128)S(1)} %get-tuple-element.127), channel_id=1, source_target_pairs={{0,8},{1,9},{2,10},{3,11},{4,12},{5,13},{6,14},{7,15},{16,24},{17,... | collective-permute-start | bytes 1572872 | tf_op jit(solution)/shard_map/ppermute | solution.py:596
  112.4 29.8 %collective-permute-start.23 = (f32[2,512,256]{2,1,0:T(8,128)}, f32[2,512,256]{2,1,0:T(8,128)}, u32[]{:S(2)}, u32[]{:S(2)}) collective-permute-start(f32[2,512,256]{2,1,0:T(8,128)} %get-tuple-element.125), channel_id=1, source_target_pairs={{0,8},{1,9},{2,10},{3,11},{4,12},{5,13},{6,14},{7,15},{8,16},{9,17... | collective-permute-start | bytes 3145736 | tf_op jit(solution)/shard_map/ppermute | solution.py:596
  114.7 27.5 %collective-permute-start.27 = (f32[2,256,256]{2,1,0:T(8,128)S(1)}, f32[2,256,256]{2,1,0:T(8,128)}, u32[]{:S(2)}, u32[]{:S(2)}) collective-permute-start(f32[2,256,256]{2,1,0:T(8,128)S(1)} %get-tuple-element.127), channel_id=1, source_target_pairs={{8,17},{9,18},{10,19},{11,20},{12,21},{13,22},{14,23},{24,33},{25,... | collective-permute-start | bytes 1572872 | tf_op jit(solution)/shard_map/ppermute | solution.py:596
  116.2 26.0 %collective-permute-start.26 = (f32[2,256,256]{2,1,0:T(8,128)S(1)}, f32[2,256,256]{2,1,0:T(8,128)}, u32[]{:S(2)}, u32[]{:S(2)}) collective-permute-start(f32[2,256,256]{2,1,0:T(8,128)S(1)} %get-tuple-element.128), channel_id=1, source_target_pairs={{0,1},{1,2},{2,3},{3,4},{4,5},{5,6},{6,7},{8,9},{9,10},{10,11},{11... | collective-permute-start | bytes 1572872 | tf_op jit(solution)/shard_map/ppermute | solution.py:596
  119.1 23.1 %collective-permute-start.25 = (f32[2,256,256]{2,1,0:T(8,128)}, f32[2,256,256]{2,1,0:T(8,128)}, u32[]{:S(2)}, u32[]{:S(2)}) collective-permute-start(f32[2,256,256]{2,1,0:T(8,128)} %add.40), channel_id=1, source_target_pairs={{0,1},{1,2},{2,3},{3,4},{4,5},{5,6},{6,7},{8,9},{9,10},{10,11},{11... | collective-permute-start | bytes 1572872 | tf_op jit(solution)/shard_map/ppermute | solution.py:596
  136.8 5.1 %collective-permute-start = (f32[4,2,2,2,16,256]{5,4,1,0,3,2:T(8,128)S(1)}, f32[4,2,2,2,16,256]{5,4,1,0,3,2:T(8,128)S(1)}, u32[]{:S(2)}, u32[]{:S(2)}) collective-permute-start(f32[4,2,2,2,16,256]{5,4,1,0,3,2:T(8,128)S(1)} %select_bitcast_fusion), channel_id=1, source_target_pairs={{0,8},{1,9},{2,10},{3,11},{4,12},{5,13},{6,14},{7,15},{8,0},{9,1},... | collective-permute-start | bytes 1572872 | tf_op jit(solution)/shard_map/cond/branch_1_fun/ppermute | solution.py:596
  142.3 14.1 %collective-permute-start.29 = (f32[2,256,256]{2,1,0:T(8,128)}, f32[2,256,256]{2,1,0:T(8,128)S(1)}, u32[]{:S(2)}, u32[]{:S(2)}) collective-permute-start(f32[2,256,256]{2,1,0:T(8,128)} %get-tuple-element.131), channel_id=1, source_target_pairs={{0,8},{1,9},{2,10},{3,11},{4,12},{5,13},{6,14},{7,15},{16,24},{17,... | collective-permute-start | bytes 1572872 | tf_op jit(solution)/shard_map/ppermute | solution.py:596
  150.1 67.2 %collective-permute-start.28 = (f32[2,512,256]{2,1,0:T(8,128)}, f32[2,512,256]{2,1,0:T(8,128)S(1)}, u32[]{:S(2)}, u32[]{:S(2)}) collective-permute-start(f32[2,512,256]{2,1,0:T(8,128)} %get-tuple-element.129), channel_id=1, source_target_pairs={{0,8},{1,9},{2,10},{3,11},{4,12},{5,13},{6,14},{7,15},{8,16},{9,17... | collective-permute-start | bytes 3145736 | tf_op jit(solution)/shard_map/ppermute | solution.py:596
  151.5 65.8 %collective-permute-start.32 = (f32[2,256,256]{2,1,0:T(8,128)}, f32[2,256,256]{2,1,0:T(8,128)S(1)}, u32[]{:S(2)}, u32[]{:S(2)}) collective-permute-start(f32[2,256,256]{2,1,0:T(8,128)} %get-tuple-element.131), channel_id=1, source_target_pairs={{8,17},{9,18},{10,19},{11,20},{12,21},{13,22},{14,23},{24,33},{25,... | collective-permute-start | bytes 1572872 | tf_op jit(solution)/shard_map/ppermute | solution.py:596
  152.2 65.1 %collective-permute-start.31 = (f32[2,256,256]{2,1,0:T(8,128)}, f32[2,256,256]{2,1,0:T(8,128)S(1)}, u32[]{:S(2)}, u32[]{:S(2)}) collective-permute-start(f32[2,256,256]{2,1,0:T(8,128)} %get-tuple-element.132), channel_id=1, source_target_pairs={{0,1},{1,2},{2,3},{3,4},{4,5},{5,6},{6,7},{8,9},{9,10},{10,11},{11... | collective-permute-start | bytes 1572872 | tf_op jit(solution)/shard_map/ppermute | solution.py:596
  157.2 60.2 %collective-permute-start.30 = (f32[2,256,256]{2,1,0:T(8,128)}, f32[2,256,256]{2,1,0:T(8,128)S(1)}, u32[]{:S(2)}, u32[]{:S(2)}) collective-permute-start(f32[2,256,256]{2,1,0:T(8,128)} %add.41), channel_id=1, source_target_pairs={{0,1},{1,2},{2,3},{3,4},{4,5},{5,6},{6,7},{8,9},{9,10},{10,11},{11... | collective-permute-start | bytes 1572872 | tf_op jit(solution)/shard_map/ppermute | solution.py:596
  162.8 15.2 %collective-permute-start.1 = (f32[2,2,2,2,16,256]{5,4,3,2,1,0:T(8,128)}, f32[2,2,2,2,16,256]{5,4,3,2,1,0:T(8,128)S(1)}, u32[]{:S(2)}, u32[]{:S(2)}) collective-permute-start(f32[2,2,2,2,16,256]{5,4,3,2,1,0:T(8,128)} %slice_select_fusion), channel_id=1, source_target_pairs={{0,64},{1,65},{2,66},{3,67},{4,68},{5,69},{6,70},{7,71},{8,72},{9,... | collective-permute-start | bytes 786440 | tf_op jit(solution)/shard_map/cond/branch_1_fun/ppermute | solution.py:596
  178.0 5.0 %collective-permute-start.2 = (f32[2,2,2,16,256]{4,3,2,1,0:T(8,128)S(1)}, f32[2,2,2,16,256]{4,3,2,1,0:T(8,128)S(1)}, u32[]{:S(2)}, u32[]{:S(2)}) collective-permute-start(f32[2,2,2,16,256]{4,3,2,1,0:T(8,128)S(1)} %select_bitcast_fusion.1), channel_id=1, source_target_pairs={{0,32},{1,33},{2,34},{3,35},{4,36},{5,37},{6,38},{7,39},{8,40},{9,... | collective-permute-start | bytes 393224 | tf_op jit(solution)/shard_map/cond/branch_1_fun/ppermute | solution.py:596
  183.1 12.2 %collective-permute-start.3 = (f32[2,2,2,16,256]{4,3,2,1,0:T(8,128)S(1)}, f32[2,2,2,16,256]{4,3,2,1,0:T(8,128)S(1)}, u32[]{:S(2)}, u32[]{:S(2)}) collective-permute-start(f32[2,2,2,16,256]{4,3,2,1,0:T(8,128)S(1)} %bitcast_add_fusion.1), channel_id=1, source_target_pairs={{0,2},{1,3},{2,0},{3,1},{4,6},{5,7},{6,4},{7,5},{8,10},{9,11},{10,... | collective-permute-start | bytes 393224 | tf_op jit(solution)/shard_map/cond/branch_1_fun/ppermute | solution.py:596
  195.3 12.1 %collective-permute-start.4 = (f32[2,2,2,16,256]{4,3,2,1,0:T(8,128)S(1)}, f32[2,2,2,16,256]{4,3,2,1,0:T(8,128)S(1)}, u32[]{:S(2)}, u32[]{:S(2)}) collective-permute-start(f32[2,2,2,16,256]{4,3,2,1,0:T(8,128)S(1)} %add.34), channel_id=1, source_target_pairs={{0,4},{1,5},{2,6},{3,7},{4,0},{5,1},{6,2},{7,3},{8,12},{9,13},{10,... | collective-permute-start | bytes 393224 | tf_op jit(solution)/shard_map/cond/branch_1_fun/ppermute | solution.py:596
  207.4 5.6 %collective-permute-start.5 = (f32[2,2,16,256]{3,2,1,0:T(8,128)S(1)}, f32[2,2,16,256]{3,2,1,0:T(8,128)S(1)}, u32[]{:S(2)}, u32[]{:S(2)}) collective-permute-start(f32[2,2,16,256]{3,2,1,0:T(8,128)S(1)} %select_bitcast_fusion.2), channel_id=1, source_target_pairs={{0,17},{1,16},{2,19},{3,18},{4,21},{5,20},{6,23},{7,22},{8,25},{9,... | collective-permute-start | bytes 196616 | tf_op jit(solution)/shard_map/cond/branch_1_fun/ppermute | solution.py:596
  213.0 4.3 %collective-permute-start.6 = (f32[2,2,16,256]{3,2,1,0:T(8,128)S(1)}, f32[2,2,16,256]{3,2,1,0:T(8,128)S(1)}, u32[]{:S(2)}, u32[]{:S(2)}) collective-permute-start(f32[2,2,16,256]{3,2,1,0:T(8,128)S(1)} %bitcast_add_fusion.2), channel_id=1, source_target_pairs={{0,1},{1,0},{2,3},{3,2},{4,5},{5,4},{6,7},{7,6},{8,9},{9,8},{10,11... | collective-permute-start | bytes 196616 | tf_op jit(solution)/shard_map/cond/branch_1_fun/ppermute | solution.py:596
  (20 other events, 330.5 us)
